TPU v7x, 32 devices: a whole 2x2x4 slice. The times are simulated.
32 devices in a mesh: row: 4 (over y, x), col: 8 (over z, core).
Axes of the slice: x: 2, y: 2, z: 4, core: 2. Of those that a mesh axis runs over, the one named last changes fastest.
Arguments:
- amplitudes: bfloat16 [8, 8, 512, 512], P('row', None, 'col'), may hold values from -6 to 6
- intermediate: bfloat16 [8, 512, 8, 512], P('row', None, 'col'), may hold values from -0.09375 to 0.09375
Outputs:
- update: bfloat16 [8, 8, 512, 512], P('row', None, 'col')
All inputs are finite; a program needn't handle non-finite values.
Results may differ from a plain program's by a relative error of at most 0.0051.
Values may be sent and summed in bfloat16 or wider, within the bound.
No kernel may reach another device: no remote copies, remote signals or barrier semaphores. Data moves between devices by JAX's collectives and lax.ppermute only.
A program may use at most 128 MiB of HBM per device.

v0:
```python
import jax
import jax.numpy as jnp
from jax import lax
from jax.sharding import PartitionSpec as P


def contract(panel_part, weight_part):
    return jnp.einsum(
        "kica,kcjb->ijab", panel_part, weight_part, preferred_element_type=jnp.float32
    )


def local(amplitudes, intermediate):
    panel = lax.all_to_all(
        lax.all_to_all(amplitudes, "row", split_axis=1, concat_axis=0, tiled=True),
        "col",
        split_axis=0,
        concat_axis=2,
        tiled=True,
    )
    weights = lax.all_gather(intermediate, "row", axis=0, tiled=True)
    cycle = contract(lax.all_gather(panel, "col", axis=0, tiled=True), weights)
    cycle = cycle.astype(jnp.bfloat16)
    first = lax.all_to_all(cycle, "col", split_axis=2, concat_axis=1, tiled=True)
    swapped = lax.all_to_all(
        lax.all_to_all(first, "row", split_axis=1, concat_axis=0, tiled=True),
        "col",
        split_axis=3,
        concat_axis=2,
        tiled=True,
    )
    second = jnp.transpose(swapped, (1, 0, 3, 2))
    return (first.astype(jnp.float32) + second.astype(jnp.float32)).astype(jnp.bfloat16)


def solution(mesh):
    placed = (P("row", None, "col", None), P("row", None, "col", None))
    return jax.shard_map(
        local, mesh=mesh, in_specs=placed, out_specs=P("row", None, "col", None), check_vma=False
    )
```

profile of v0, /device:TPU:0, one launch (start us, length us, event | category | flops | bytes accessed | tf_op | source)
XLA Modules:
  0.0 277.3 jit_solution(11022857380694620984)
XLA Ops:
  6.5 0.7 all-gather.3.cloned.1.call-update
  7.3 1.3 copy.34
  8.6 24.7 %all_to_all.75 = bf16[2,8,64,512]{3,2,0,1:T(8,128)(2,1)S(1)} all-to-all(bf16[2,8,64,512]{3,2,0,1:T(8,128)(2,1)S(1)} %copy.34), channel_id=1, replica_groups=mesh['row'=4,'col'=8] {'row'}, dimensions={1} | all-to-all | bytes 2097152 | tf_op jit(solution)/shard_map/all_to_all | solution.py:15
  33.3 0.1 copy.35
  33.4 31.5 %all_to_all.76 = bf16[8,2,64,512]{3,2,1,0:T(8,128)(2,1)S(1)} all-to-all(bf16[8,2,64,512]{3,2,1,0:T(8,128)(2,1)S(1)} %bitcast.53), channel_id=1, replica_groups=mesh['row'=4,'col'=8] {'col'}, dimensions={0} | all-to-all | bytes 2097152 | tf_op jit(solution)/shard_map/all_to_all | solution.py:14
  64.9 1.1 copy.36
  66.0 3.1 %all-gather.3.cloned.1.call-done = bf16[8,512,1,512]{3,1,2,0:T(8,128)(2,1)} async-done(((bf16[2,512,1,512]{3,1,2,0:T(8,128)(2,1)}), bf16[8,512,1,512]{3,1,2,0:T(8,128)(2,1)}) %all-gather.3.cloned.1.call-update) | async-done | bytes 4194320 | tf_op jit(solution)/shard_map/all_gather | solution.py:21
  69.2 83.7 %all-gather.5.cloned.1.call-done = bf16[8,2,512,512]{3,2,0,1:T(8,128)(2,1)} async-done(((bf16[1,2,512,512]{3,2,0,1:T(8,128)(2,1)}), bf16[8,2,512,512]{3,2,0,1:T(8,128)(2,1)}) %all-gather.5.cloned.1.call-update) | async-done | bytes 8388624 | tf_op jit(solution)/shard_map/all_gather | solution.py:22
  152.9 9.2 %fusion.5 = bf16[2,1,512,512]{2,3,0,1:T(8,128)(2,1)S(1)} fusion(bf16[8,2,512,512]{3,2,0,1:T(8,128)(2,1)} %all-gather.5.cloned.1.call-done, bf16[8,512,1,512]{3,1,2,0:T(8,128)(2,1)} %all-gather.3.cloned.1.call-done), kind=kOutput, calls=%fused_computation.5 | convolution fusion | flops 4295491584 | bytes 13631488 | tf_op jit(solution)/shard_map/kica,kcjb->ijab/dot_general | solution.py:8
  162.0 1.0 copy.37
  163.0 29.0 %all_to_all.77 = bf16[2,1,512,512]{3,0,1,2:T(2,128)(2,1)S(1)} all-to-all(bf16[2,1,512,512]{3,0,1,2:T(2,128)(2,1)S(1)} %copy.37), channel_id=1, replica_groups=mesh['row'=4,'col'=8] {'col'}, dimensions={2} | all-to-all | bytes 2097152 | tf_op jit(solution)/shard_map/all_to_all | solution.py:24
  192.0 0.2 copy.38
  192.2 0.1 copy.39
  192.3 17.2 %all_to_all.78 = bf16[2,8,64,512]{3,2,0,1:T(8,128)(2,1)S(1)} all-to-all(bf16[2,8,64,512]{3,2,0,1:T(8,128)(2,1)S(1)} %copy.39), channel_id=1, replica_groups=mesh['row'=4,'col'=8] {'row'}, dimensions={1} | all-to-all | bytes 2097152 | tf_op jit(solution)/shard_map/all_to_all | solution.py:26
  209.5 1.1 copy.41
  210.6 4.7 %copy.42 = bf16[8,2,64,512]{2,1,0,3:T(2,128)(2,1)S(1)} copy(bf16[8,2,64,512]{3,2,1,0:T(8,128)(2,1)} %bitcast.50) | data formatting | bytes 2097152 | tf_op jit(solution)/shard_map/all_to_all | solution.py:26
  215.3 2.7 reshape.17
  218.0 30.8 %all_to_all.79 = bf16[8,2,32768]{2,1,0:T(2,128)(2,1)} all-to-all(bf16[8,2,32768]{2,1,0:T(2,128)(2,1)} %reshape.17), channel_id=1, replica_groups=mesh['row'=4,'col'=8] {'col'}, dimensions={0} | all-to-all | bytes 2097152 | tf_op jit(solution)/shard_map/all_to_all | solution.py:25
  248.8 3.1 %reshape.18 = bf16[512,8,2,64]{3,2,1,0:T(2,128)(2,1)S(1)} reshape(bf16[8,2,32768]{2,1,0:T(2,128)(2,1)} %all_to_all.79) | data formatting | bytes 2097152
  251.9 4.3 %copy.43 = bf16[8,2,64,512]{3,2,1,0:T(8,128)(2,1)} copy(bf16[8,2,64,512]{2,1,0,3:T(2,128)(2,1)S(1)} %bitcast.49) | data formatting | bytes 2097152 | tf_op jit(solution)/shard_map/all_to_all | solution.py:25
  256.2 4.0 %reshape.14 = f32[8,2,64,8,64]{4,3,2,1,0:T(8,128)} reshape(bf16[8,2,64,512]{3,2,1,0:T(8,128)(2,1)} %copy.43) | data formatting | bytes 3145728 | tf_op jit(solution)/shard_map/convert_element_type | solution.py:33
  260.2 5.5 %copy.44 = f32[8,2,8,64,64]{3,2,4,0,1:T(8,128)} copy(f32[8,2,8,64,64]{4,2,3,1,0:T(8,128)} %bitcast.45) | data formatting | bytes 4194304 | tf_op jit(solution)/shard_map/convert_element_type | solution.py:33
  265.7 3.4 %reshape.13 = f32[8,2,512,64]{2,3,0,1:T(8,128)S(1)} reshape(f32[8,2,8,64,64]{3,2,4,0,1:T(8,128)} %copy.44) | data formatting | bytes 4194304 | tf_op jit(solution)/shard_map/convert_element_type | solution.py:33
  269.1 1.3 fusion.2
  (3 shorter events, 0.1 us)
Async XLA Ops:
  6.5 62.6 %all-gather.3.cloned.1.call-start = ((), (), s32[]{:S(2)}) async-start(), calls=%async_computation.5 | async-start | bytes 5242880 | tf_op jit(solution)/shard_map/all_gather | solution.py:21
  7.3 145.6 %all-gather.5.cloned.1.call-start = ((), (), s32[]{:S(2)}) async-start(), calls=%async_computation.6 | async-start | bytes 9437184 | tf_op jit(solution)/shard_map/all_gather | solution.py:22
Sparse Core Ops, SparseCore 0:
  9.2 59.9 all-gather.2
  70.8 82.0 all-gather.4
where the time goes:
time: 278 us; the launch traced here: 277 us
  blocking collectives  133 us (48%)
  waiting for transfers between devices  87.6 us (32%)
  local copies, waits for them, and re-layouts  32.5 us (12%)
  between operations  13.5 us (5%)
  matrix products  9.16 us (3%)
    all_gather x1, waiting for transfers between devices, local(): cycle = contract(lax.all_gather(panel, 'col', axis=0, tiled=True), weights)  83.7 us
    all_to_all x1, blocking collectives, local(): lax.all_to_all(lax.all_to_all(amplitudes, 'row', split_axis=1, concat_axi...  31.5 us
    all_to_all x1, blocking collectives, local(): lax.all_to_all(lax.all_to_all(first, 'row', split_axis=1, concat_axis=0,...  30.8 us
    all_to_all x1, blocking collectives, local(): lax.all_to_all(cycle, 'col', split_axis=2, concat_axis=1, tiled=True)  29 us
    all_to_all x1, blocking collectives, local(): lax.all_to_all(amplitudes, 'row', split_axis=1, concat_axis=0, tiled=True)  24.7 us
    all_to_all x1, blocking collectives, local(): lax.all_to_all(first, 'row', split_axis=1, concat_axis=0, tiled=True)  17.2 us
    convert_element_type x3, local copies, waits for them, and re-layouts, local(): second.astype(jnp.float32)  12.9 us
    dot_general x1, matrix products, contract(): jnp.einsum('kica,kcjb->ijab', panel_part, weight_part, preferred_element_...  9.16 us
  transfers between devices with their start and end apart: 2, of which 2 were waited for; matrix products, arithmetic and copies ran while one was open for 1% of the time, Pallas kernels for 0%

commit v1 on v0

v1 whole, which is shorter than its diff:
```python
import jax
import jax.numpy as jnp
from jax import lax
from jax.sharding import PartitionSpec as P


def swap_cores(x, ncol):
    return lax.ppermute(x, "col", [(s, s ^ 1) for s in range(ncol)])


def solution(mesh):
    nrow, ncol = mesh.shape["row"], mesh.shape["col"]

    def local(amplitudes, intermediate):
        kk, occ, cs, v = amplitudes.shape
        ai = occ // nrow
        vs = v // ncol
        row = lax.axis_index("row")
        core = lax.axis_index("col") % 2

        w = intermediate[:, :, 0, :]
        own = lax.dynamic_index_in_dim(w, core, 0, keepdims=False)
        other = swap_cores(lax.dynamic_index_in_dim(w, 1 - core, 0, keepdims=False), ncol)
        gathered = []
        for q in range(2):
            part = jnp.where(core == q, own, other)
            g = lax.all_gather(part, "col", axis=0, tiled=False)
            gathered.append(g.reshape(ncol // 2, kk, v, v))

        blocks = amplitudes.reshape(kk, occ, cs, ncol, vs)
        blocks = jnp.transpose(blocks, (3, 0, 2, 1, 4)).reshape(ncol, kk, cs, occ * vs)
        panel = lax.all_to_all(blocks, "col", 0, 0, tiled=True)
        panel = jnp.transpose(panel, (1, 0, 2, 3)).reshape(kk, v, nrow, ai * vs)

        firsts, seconds = [], []
        for q in range(2):
            total = None
            for t in range(nrow):
                mine = lax.dynamic_index_in_dim(panel, row ^ t, 2, keepdims=False)
                part = jnp.einsum(
                    "kcm,jkcb->mjb", mine, gathered[q], preferred_element_type=jnp.float32
                )
                if t > 0:
                    part = lax.ppermute(
                        part.astype(jnp.bfloat16), "row", [(r, r ^ t) for r in range(nrow)]
                    ).astype(jnp.float32)
                total = part if total is None else total + part
            first = total.astype(jnp.bfloat16)
            firsts.append(first)
            turned = jnp.transpose(first, (1, 2, 0)).reshape(nrow * ncol, vs, ai * vs)
            seconds.append(lax.all_to_all(turned, ("row", "col"), 0, 0, tiled=True))

        first = jnp.stack([f.reshape(ai, vs, nrow, v) for f in firsts], 0)
        first = jnp.transpose(first, (1, 3, 0, 2, 4)).reshape(ai, occ, vs, v)
        second = jnp.stack(
            [s.reshape(nrow, ncol, vs, ai, vs).transpose(0, 3, 2, 1, 4) for s in seconds], 0
        ).reshape(ai, occ, vs, v)
        return (first.astype(jnp.float32) + second.astype(jnp.float32)).astype(jnp.bfloat16)

    placed = P("row", None, "col", None)
    return jax.shard_map(
        local, mesh=mesh, in_specs=(placed, placed), out_specs=placed, check_vma=False
    )
```

time: 278 us -> 213 us (0.77)
  blocking collectives: 133 us -> 0 us
  waiting for transfers between devices: 87.6 us -> 129 us
  starting transfers between devices: 0.04 us -> 21.3 us
  matrix products: 9.16 us -> 16.4 us
  local copies, waits for them, and re-layouts: 32.5 us -> 28 us
  other arithmetic: 1.34 us -> 4.61 us
    all_to_all x5 -> x0, blocking collectives: 133 us -> none  [the longest x1 31.5 us: local(): lax.all_to_all(lax.all_to_all(amplitudes, 'row', split_axis=1, concat_axi...]
    all_to_all x0 -> x3, waiting for transfers between devices: none -> 62.2 us  [the longest x1 52.9 us: local(): panel = lax.all_to_all(blocks, 'col', 0, 0, tiled=True)]
    all_gather x2, waiting for transfers between devices: 86.8 us -> 38.3 us  [local(): g = lax.all_gather(part, 'col', axis=0, tiled=False)]
    ppermute x0 -> x7, waiting for transfers between devices: none -> 27.4 us  [the longest x6 25.8 us: local(): lax.ppermute(part.astype(jnp.bfloat16), 'row', [(r, r ^ t) for r in range...]
    convert_element_type x4 -> x1, local copies, waits for them, and re-layouts: 13.9 us -> 0.21 us  [local(): first.astype(jnp.float32) + second.astype(jnp.float32)]
    all_to_all x0 -> x3, starting transfers between devices: none -> 13.7 us  [the longest x2 7.41 us: local(): seconds.append(lax.all_to_all(turned, ('row', 'col'), 0, 0, tiled=True))]
    reshape x0 -> x6, local copies, waits for them, and re-layouts: none -> 12.3 us  [the longest x2 5.05 us: local(): blocks = amplitudes.reshape(kk, occ, cs, ncol, vs)]
    all_to_all x7 -> x0, local copies, waits for them, and re-layouts: 11.5 us -> none  [the longest x2 5.81 us: local(): lax.all_to_all(first, 'row', split_axis=1, concat_axis=0, tiled=True)]
  transfers between devices with their start and end apart: 2 -> 12, of which waited for: 2 -> 8; matrix products, arithmetic and copies ran while one was open for 1% -> 16% of each run, Pallas kernels for 0% -> 0%
where the time goes in v1:
time: 213 us; the launch traced here: 212 us
  waiting for transfers between devices  129 us (61%)
  local copies, waits for them, and re-layouts  28 us (13%)
  starting transfers between devices  21.3 us (10%)
  matrix products  16.4 us (8%)
  between operations  13.6 us (6%)
  other arithmetic  4.61 us (2%)
    all_to_all x1, waiting for transfers between devices, local(): panel = lax.all_to_all(blocks, 'col', 0, 0, tiled=True)  52.9 us
    all_gather x2, waiting for transfers between devices, local(): g = lax.all_gather(part, 'col', axis=0, tiled=False)  38.3 us
    ppermute x6, waiting for transfers between devices, local(): lax.ppermute(part.astype(jnp.bfloat16), 'row', [(r, r ^ t) for r in range...  25.8 us
    dot_general x8, matrix products, local(): jnp.einsum('kcm,jkcb->mjb', mine, gathered[q], preferred_element_type=jnp...  16.4 us
    all_to_all x2, waiting for transfers between devices, local(): seconds.append(lax.all_to_all(turned, ('row', 'col'), 0, 0, tiled=True))  9.29 us
    all_to_all x2, starting transfers between devices, local(): seconds.append(lax.all_to_all(turned, ('row', 'col'), 0, 0, tiled=True))  7.41 us
    ppermute x6, starting transfers between devices, local(): lax.ppermute(part.astype(jnp.bfloat16), 'row', [(r, r ^ t) for r in range...  7.04 us
    all_to_all x1, starting transfers between devices, local(): panel = lax.all_to_all(blocks, 'col', 0, 0, tiled=True)  6.25 us
  transfers between devices with their start and end apart: 12, of which 8 were waited for; matrix products, arithmetic and copies ran while one was open for 16% of the time, Pallas kernels for 0%

profile of v1, /device:TPU:0, one launch (start us, length us, event | category | flops | bytes accessed | tf_op | source)
XLA Modules:
  0.0 212.4 jit_solution(16629524815709732097)
XLA Ops:
  9.8 2.1 bitcast_select_fusion.1
  12.6 2.1 reshape.39
  14.8 2.9 %copy.33 = bf16[2,8,64,8,64]{4,1,2,0,3:T(8,128)(2,1)S(1)} copy(bf16[2,8,64,8,64]{4,3,2,1,0:T(8,128)(2,1)} %reshape.39) | data formatting | bytes 2097152 | tf_op jit(solution)/shard_map/reshape | solution.py:30
  17.7 2.0 reshape.40
  19.7 6.2 %all-to-all-start = ((bf16[8,2,64,512]{3,2,1,0:T(8,128)(2,1)}), bf16[8,2,64,512]{3,2,1,0:T(8,128)(2,1)S(1)}, u32[]{:S(2)}, u32[]{:S(2)}) async-start(bf16[8,2,64,512]{3,2,1,0:T(8,128)(2,1)} %reshape.40), calls=%async_computation | async-start | bytes 2097152 | tf_op jit(solution)/shard_map/all_to_all | solution.py:32
  26.0 52.9 %all-to-all-done = bf16[8,2,64,512]{3,2,1,0:T(8,128)(2,1)S(1)} async-done(((bf16[8,2,64,512]{3,2,1,0:T(8,128)(2,1)}), bf16[8,2,64,512]{3,2,1,0:T(8,128)(2,1)S(1)}, u32[]{:S(2)}, u32[]{:S(2)}) %all-to-all-start) | async-done | bytes 1048608 | tf_op jit(solution)/shard_map/all_to_all | solution.py:32
  79.3 2.2 %constant_dynamic-slice_fusion.3 = (bf16[2,512,1,128]{3,2,1,0:T(2,128)(2,1)S(1)}, bf16[2,512,1,128]{3,2,1,0:T(2,128)(2,1)S(1)}, bf16[2,512,1,128]{3,2,1,0:T(2,128)(2,1)S(1)}, bf16[2,512,1,128]{3,2,1,0:T(2,128)(2,1)S(1)}) fusion(bf16[2,512,4,128]{3,2,1,0:T(4,128)(2,1)S(1)} %reshape.41, s32[]{:T(128)S(6)} %select_n.45, s32[]{:T(128)S(6)} %select_n.53, ...), kind=kLoop, calls=%fused_computation.39 | loop fusion | bytes 2097168 | tf_op jit(solution)/shard_map/jit(dynamic_index_in_dim)/dynamic_slice | solution.py:39
  84.1 3.8 %fusion.11 = bf16[128,4,512]{2,0,1:T(8,128)(2,1)} fusion(bf16[4,2,512,512]{3,2,1,0:T(8,128)(2,1)} %bitcast.120, bf16[2,512,1,128]{1,3,0,2:T(8,128)(2,1)S(1)} %copy.18), kind=kOutput, calls=%fused_computation.22 | convolution fusion | flops 537133056 | bytes 4980736 | tf_op jit(solution)/shard_map/kcm,jkcb->mjb/dot_general | solution.py:40
  87.9 2.4 %collective-permute-start.6 = (bf16[128,4,512]{2,0,1:T(8,128)(2,1)}, bf16[128,4,512]{2,0,1:T(8,128)(2,1)S(1)}, u32[]{:S(2)}, u32[]{:S(2)}) collective-permute-start(bf16[128,4,512]{2,0,1:T(8,128)(2,1)} %fusion.11), channel_id=1, source_target_pairs={{0,24},{8,16},{16,8},{24,0},{1,25},{9,17},{17,9},{25,1},{2,26},{10... | collective-permute-start | bytes 1572872 | tf_op jit(solution)/shard_map/ppermute | solution.py:44
  94.5 37.1 %all-gather.5.cloned.1.call-done = bf16[4096,512]{1,0:T(8,128)(2,1)} async-done(((bf16[512,512]{1,0:T(8,128)(2,1)}), bf16[4096,512]{1,0:T(8,128)(2,1)}) %all-gather.5.cloned.1.call-update) | async-done | bytes 4194320 | tf_op jit(solution)/shard_map/all_gather | solution.py:27
  131.6 3.1 %fusion.8 = bf16[128,4,512]{2,0,1:T(8,128)(2,1)S(1)} fusion(bf16[4,2,512,512]{3,2,1,0:T(8,128)(2,1)} %bitcast.116, bf16[2,512,1,128]{1,3,0,2:T(8,128)(2,1)S(1)} %copy.18), kind=kOutput, calls=%fused_computation.19 | convolution fusion | flops 537133056 | bytes 4980736 | tf_op jit(solution)/shard_map/kcm,jkcb->mjb/dot_general | solution.py:40
  136.3 1.9 fusion.12
  139.2 3.5 %all-to-all-start.2 = ((bf16[32,64,128]{2,1,0:T(8,128)(2,1)}), bf16[32,64,128]{2,1,0:T(8,128)(2,1)S(1)}, u32[]{:S(2)}, u32[]{:S(2)}) async-start(bf16[32,64,128]{2,1,0:T(8,128)(2,1)} %bitcast.38), calls=%async_computation.2 | async-start | bytes 1048576 | tf_op jit(solution)/shard_map/all_to_all | solution.py:51
  142.7 3.1 %fusion.6 = bf16[128,4,512]{2,0,1:T(8,128)(2,1)S(1)} fusion(bf16[4,2,512,512]{3,2,1,0:T(8,128)(2,1)} %bitcast.117, bf16[2,512,1,128]{1,3,0,2:T(8,128)(2,1)S(1)} %copy.16), kind=kOutput, calls=%fused_computation.17 | convolution fusion | flops 537133056 | bytes 4980736 | tf_op jit(solution)/shard_map/kcm,jkcb->mjb/dot_general | solution.py:40
  145.8 2.6 %collective-permute-start.3 = (bf16[128,4,512]{2,0,1:T(8,128)(2,1)S(1)}, bf16[128,4,512]{2,0,1:T(8,128)(2,1)S(1)}, u32[]{:S(2)}, u32[]{:S(2)}) collective-permute-start(bf16[128,4,512]{2,0,1:T(8,128)(2,1)S(1)} %fusion.8), channel_id=1, source_target_pairs={{0,24},{8,16},{16,8},{24,0},{1,25},{9,17},{17,9},{25,1},{2,26},{10... | collective-permute-start | bytes 1572872 | tf_op jit(solution)/shard_map/ppermute | solution.py:44
  149.3 15.3 %collective-permute-done.3 = bf16[128,4,512]{2,0,1:T(8,128)(2,1)S(1)} collective-permute-done((bf16[128,4,512]{2,0,1:T(8,128)(2,1)S(1)}, bf16[128,4,512]{2,0,1:T(8,128)(2,1)S(1)}, u32[]{:S(2)}, u32[]{:S(2)}) %collective-permute-start.3) | collective-permute-done | bytes 524320 | tf_op jit(solution)/shard_map/ppermute | solution.py:44
  164.6 10.1 %collective-permute-done.2 = bf16[128,4,512]{2,0,1:T(8,128)(2,1)S(1)} collective-permute-done((bf16[128,4,512]{2,0,1:T(8,128)(2,1)S(1)}, bf16[128,4,512]{2,0,1:T(8,128)(2,1)S(1)}, u32[]{:S(2)}, u32[]{:S(2)}) %collective-permute-start.2) | collective-permute-done | bytes 524320 | tf_op jit(solution)/shard_map/ppermute | solution.py:44
  177.0 3.9 %all-to-all-start.1 = ((bf16[32,64,128]{2,1,0:T(8,128)(2,1)}), bf16[32,64,128]{2,1,0:T(8,128)(2,1)}, u32[]{:S(2)}, u32[]{:S(2)}) async-start(bf16[32,64,128]{2,1,0:T(8,128)(2,1)} %bitcast.35), calls=%async_computation.1 | async-start | bytes 1048576 | tf_op jit(solution)/shard_map/all_to_all | solution.py:51
  181.3 2.5 %reshape.47 = bf16[4,8,64,2,64]{4,3,2,1,0:T(2,128)(2,1)S(1)} reshape(bf16[32,64,128]{2,1,0:T(8,128)(2,1)} %copy-done.4) | data formatting | bytes 1048576 | tf_op jit(solution)/shard_map/reshape | solution.py:56
  185.4 2.6 %stack.14 = bf16[1,8,64,512]{3,2,1,0:T(8,128)(2,1)} reshape(bf16[4,2,64,8,64]{4,3,2,1,0:T(8,128)(2,1)} %copy.23) | data formatting | bytes 1048576 | tf_op jit(solution)/shard_map/stack | solution.py:55
  188.0 9.3 %all-to-all-done.1 = bf16[32,64,128]{2,1,0:T(8,128)(2,1)} async-done(((bf16[32,64,128]{2,1,0:T(8,128)(2,1)}), bf16[32,64,128]{2,1,0:T(8,128)(2,1)}, u32[]{:S(2)}, u32[]{:S(2)}) %all-to-all-start.1) | async-done | bytes 524320 | tf_op jit(solution)/shard_map/all_to_all | solution.py:51
  197.2 2.4 %reshape.45 = bf16[4,8,64,2,64]{4,3,2,1,0:T(2,128)(2,1)S(1)} reshape(bf16[32,64,128]{2,1,0:T(8,128)(2,1)} %all-to-all-done.1) | data formatting | bytes 1048576 | tf_op jit(solution)/shard_map/reshape | solution.py:56
  201.3 1.9 stack.13
  203.2 2.4 %add_convert_fusion = bf16[2,8,64,512]{3,2,1,0:T(8,128)(2,1)} fusion(f32[2,8,64,512]{3,2,1,0:T(8,128)S(1)} %bitcast.124, bf16[1,8,64,512]{3,2,1,0:T(8,128)(2,1)} %stack.14, bf16[1,8,64,512]{3,2,1,0:T(8,128)(2,1)S(1)} %stack.13), kind=kLoop, calls=%fused_computation.2 | loop fusion | flops 2097152 | bytes 4194304 | tf_op jit(solution)/shard_map/convert_element_type | solution.py:58
  (45 shorter events, 20.7 us)
Async XLA Ops:
  6.5 6.1 %copy-start.5 = (bf16[2,8,64,512]{3,2,1,0:T(8,128)(2,1)S(1)}, bf16[2,8,64,512]{3,2,1,0:T(8,128)(2,1)}, u32[]{:S(2)}) copy-start(bf16[2,8,64,512]{3,2,1,0:T(8,128)(2,1)} %param.2) | copy-start | bytes 3145732
  6.5 77.5 %all-gather.7.cloned.1.call-start = ((), (), s32[]{:S(2)}) async-start(), calls=%async_computation.4 | async-start | bytes 4718592 | tf_op jit(solution)/shard_map/all_gather | solution.py:27
  7.7 2.1 collective-permute-start
  11.9 119.7 %all-gather.5.cloned.1.call-start = ((), (), s32[]{:S(2)}) async-start(), calls=%async_computation.3 | async-start | bytes 4718592 | tf_op jit(solution)/shard_map/all_gather | solution.py:27
  19.7 59.1 %all-to-all-start = ((bf16[8,2,64,512]{3,2,1,0:T(8,128)(2,1)}), bf16[8,2,64,512]{3,2,1,0:T(8,128)(2,1)S(1)}, u32[]{:S(2)}, u32[]{:S(2)}) async-start(bf16[8,2,64,512]{3,2,1,0:T(8,128)(2,1)} %reshape.40), calls=%async_computation | async-start | bytes 2097152 | tf_op jit(solution)/shard_map/all_to_all | solution.py:32
  84.1 6.2 %copy-start.2 = (bf16[4096,512]{1,0:T(8,128)(2,1)S(1)}, bf16[4096,512]{1,0:T(8,128)(2,1)}, u32[]{:S(2)}) copy-start(bf16[4096,512]{1,0:T(8,128)(2,1)} %all-gather.7.cloned.1.call-done) | copy-start | bytes 12582916
  87.9 47.8 %collective-permute-start.6 = (bf16[128,4,512]{2,0,1:T(8,128)(2,1)}, bf16[128,4,512]{2,0,1:T(8,128)(2,1)S(1)}, u32[]{:S(2)}, u32[]{:S(2)}) collective-permute-start(bf16[128,4,512]{2,0,1:T(8,128)(2,1)} %fusion.11), channel_id=1, source_target_pairs={{0,24},{8,16},{16,8},{24,0},{1,25},{9,17},{17,9},{25,1},{2,26},{10... | collective-permute-start | bytes 1572872 | tf_op jit(solution)/shard_map/ppermute | solution.py:44
  91.9 43.9 %collective-permute-start.5 = (bf16[128,4,512]{2,0,1:T(8,128)(2,1)}, bf16[128,4,512]{2,0,1:T(8,128)(2,1)S(1)}, u32[]{:S(2)}, u32[]{:S(2)}) collective-permute-start(bf16[128,4,512]{2,0,1:T(8,128)(2,1)} %fusion.10), channel_id=1, source_target_pairs={{0,16},{8,24},{16,0},{24,8},{1,17},{9,25},{17,1},{25,9},{2,18},{10... | collective-permute-start | bytes 1572872 | tf_op jit(solution)/shard_map/ppermute | solution.py:44
  93.9 41.8 %collective-permute-start.4 = (bf16[128,4,512]{2,0,1:T(8,128)(2,1)}, bf16[128,4,512]{2,0,1:T(8,128)(2,1)}, u32[]{:S(2)}, u32[]{:S(2)}) collective-permute-start(bf16[128,4,512]{2,0,1:T(8,128)(2,1)} %fusion.9), channel_id=1, source_target_pairs={{0,8},{8,0},{16,24},{24,16},{1,9},{9,1},{17,25},{25,17},{2,10},{10... | collective-permute-start | bytes 1572872 | tf_op jit(solution)/shard_map/ppermute | solution.py:44
  131.6 3.4 %copy-start = (bf16[4096,512]{1,0:T(8,128)(2,1)S(1)}, bf16[4096,512]{1,0:T(8,128)(2,1)}, u32[]{:S(2)}) copy-start(bf16[4096,512]{1,0:T(8,128)(2,1)} %all-gather.5.cloned.1.call-done) | copy-start | bytes 12582916
  131.6 4.7 %copy-start.3 = (bf16[4096,512]{1,0:T(8,128)(2,1)S(1)}, bf16[4096,512]{1,0:T(8,128)(2,1)}, u32[]{:S(2)}) copy-start(bf16[4096,512]{1,0:T(8,128)(2,1)} %all-gather.7.cloned.1.call-done) | copy-start | bytes 12582916
  139.2 37.8 %all-to-all-start.2 = ((bf16[32,64,128]{2,1,0:T(8,128)(2,1)}), bf16[32,64,128]{2,1,0:T(8,128)(2,1)S(1)}, u32[]{:S(2)}, u32[]{:S(2)}) async-start(bf16[32,64,128]{2,1,0:T(8,128)(2,1)} %bitcast.38), calls=%async_computation.2 | async-start | bytes 1048576 | tf_op jit(solution)/shard_map/all_to_all | solution.py:51
  142.7 32.4 %copy-start.1 = (bf16[4096,512]{1,0:T(8,128)(2,1)S(1)}, bf16[4096,512]{1,0:T(8,128)(2,1)}, u32[]{:S(2)}) copy-start(bf16[4096,512]{1,0:T(8,128)(2,1)} %all-gather.5.cloned.1.call-done) | copy-start | bytes 12582916
  145.8 18.8 %collective-permute-start.3 = (bf16[128,4,512]{2,0,1:T(8,128)(2,1)S(1)}, bf16[128,4,512]{2,0,1:T(8,128)(2,1)S(1)}, u32[]{:S(2)}, u32[]{:S(2)}) collective-permute-start(bf16[128,4,512]{2,0,1:T(8,128)(2,1)S(1)} %fusion.8), channel_id=1, source_target_pairs={{0,24},{8,16},{16,8},{24,0},{1,25},{9,17},{17,9},{25,1},{2,26},{10... | collective-permute-start | bytes 1572872 | tf_op jit(solution)/shard_map/ppermute | solution.py:44
  148.3 26.4 %collective-permute-start.2 = (bf16[128,4,512]{2,0,1:T(8,128)(2,1)S(1)}, bf16[128,4,512]{2,0,1:T(8,128)(2,1)S(1)}, u32[]{:S(2)}, u32[]{:S(2)}) collective-permute-start(bf16[128,4,512]{2,0,1:T(8,128)(2,1)S(1)} %fusion.7), channel_id=1, source_target_pairs={{0,16},{8,24},{16,0},{24,8},{1,17},{9,25},{17,1},{25,9},{2,18},{10... | collective-permute-start | bytes 1572872 | tf_op jit(solution)/shard_map/ppermute | solution.py:44
  148.9 26.2 %collective-permute-start.1 = (bf16[128,4,512]{2,0,1:T(8,128)(2,1)S(1)}, bf16[128,4,512]{2,0,1:T(8,128)(2,1)S(1)}, u32[]{:S(2)}, u32[]{:S(2)}) collective-permute-start(bf16[128,4,512]{2,0,1:T(8,128)(2,1)S(1)} %fusion.6), channel_id=1, source_target_pairs={{0,8},{8,0},{16,24},{24,16},{1,9},{9,1},{17,25},{25,17},{2,10},{10... | collective-permute-start | bytes 1572872 | tf_op jit(solution)/shard_map/ppermute | solution.py:44
  177.0 3.9 %copy-start.4 = (bf16[32,64,128]{2,1,0:T(8,128)(2,1)}, bf16[32,64,128]{2,1,0:T(8,128)(2,1)S(1)}, u32[]{:S(2)}) copy-start(bf16[32,64,128]{2,1,0:T(8,128)(2,1)S(1)} %all-to-all-done.2) | copy-start | bytes 1572868
  177.0 20.2 %all-to-all-start.1 = ((bf16[32,64,128]{2,1,0:T(8,128)(2,1)}), bf16[32,64,128]{2,1,0:T(8,128)(2,1)}, u32[]{:S(2)}, u32[]{:S(2)}) async-start(bf16[32,64,128]{2,1,0:T(8,128)(2,1)} %bitcast.35), calls=%async_computation.1 | async-start | bytes 1048576 | tf_op jit(solution)/shard_map/all_to_all | solution.py:51
Sparse Core Ops, SparseCore 0:
  12.0 72.0 all-gather.6
  85.7 45.8 all-gather.4

commit v2 on v1

v2 whole, which is shorter than its diff:
```python
import jax
import jax.numpy as jnp
from jax import lax
from jax.sharding import PartitionSpec as P

F32, BF16 = jnp.float32, jnp.bfloat16


def solution(mesh):
    nrow, ncol = mesh.shape["row"], mesh.shape["col"]
    nz = ncol // 2
    half = nz // 2

    def across(x):
        return lax.ppermute(x, "col", [(s, s ^ 1) for s in range(ncol)])

    def along(x, pairs):
        both = [(2 * a + c, 2 * b + c) for a, b in pairs for c in range(2)]
        return lax.ppermute(x, "col", both)

    def local(amplitudes, intermediate):
        kk, occ, cs, v = amplitudes.shape
        ai = occ // nrow
        vs = v // ncol
        rows = ai * vs
        row = lax.axis_index("row")
        col = lax.axis_index("col")
        z, core = col // 2, col % 2

        def by_core(x):
            return [lax.dynamic_index_in_dim(x, c, 0, keepdims=False) for c in (core, 1 - core)]

        w = intermediate[:, :, 0, :]
        mine, theirs = by_core(w), by_core(across(w))
        own = [[jnp.where(core == q, a, b) for a, b in zip(mine, theirs)] for q in range(2)]

        blocks = amplitudes.reshape(kk, occ, cs, ncol, vs)
        blocks = jnp.transpose(blocks, (3, 0, 2, 1, 4)).reshape(ncol, kk, cs, occ * vs)
        panel = lax.all_to_all(blocks, "col", 0, 0, tiled=True)
        panel = jnp.transpose(panel, (1, 0, 2, 3)).reshape(kk, v, nrow, rows)
        panel = jnp.stack(by_core(panel), 0)
        panel = [lax.dynamic_index_in_dim(panel, row ^ t, 2, keepdims=False) for t in range(nrow)]

        def product(parts):
            mats = jnp.stack([jnp.stack(p, 0) for p in parts], 0)
            total = None
            sent = []
            for t in range(1, nrow):
                part = jnp.einsum("kcm,nkcb->nmb", panel[t], mats, preferred_element_type=F32)
                sent.append(
                    lax.ppermute(part.astype(BF16), "row", [(r, r ^ t) for r in range(nrow)])
                )
            total = jnp.einsum("kcm,nkcb->nmb", panel[0], mats, preferred_element_type=F32)
            for s in sent:
                total = total + s.astype(F32)
            return total.astype(BF16)

        firsts, seconds = [], []
        for q in range(2):
            arrivals = [(z, own[q])]
            up = down = merged = own[q][0]
            for t in range(1, nz):
                if t < half:
                    up = along(up, [(a, a + 1) for a in range(t - 1, nz - 1)])
                    down = along(down, [(a, a - 1) for a in range(1, nz - t + 1)])
                    arrivals.append((jnp.where(z >= t, z - t, nz), [up, across(up)]))
                    arrivals.append((jnp.where(z < nz - t, z + t, nz), [down, across(down)]))
                    continue
                if t == half:
                    up = along(up, [(a, a + 1) for a in range(t - 1, nz - 1)])
                    down = along(down, [(a, a - 1) for a in range(1, nz - t + 1)])
                    merged = jnp.where(z >= t, up, down)
                else:
                    pairs = [(a, a + 1) for a in range(t - 1, nz - 1)]
                    pairs += [(a, a - 1) for a in range(1, nz - t + 1)]
                    merged = along(merged, pairs)
                slot = jnp.where(z >= t, z - t, jnp.where(z < nz - t, z + t, nz))
                arrivals.append((slot, [merged, across(merged)]))
            groups = [arrivals] if q == 0 else [arrivals[:-1], arrivals[-1:]]
            first = jnp.zeros((nz + 1, rows, v), BF16)
            turned = jnp.zeros((nz + 1, v, rows), BF16)
            for group in groups:
                block = product([m for _, m in group])
                flipped = jnp.transpose(block, (0, 2, 1))
                for n, (slot, _) in enumerate(group):
                    first = lax.dynamic_update_index_in_dim(first, block[n], slot, 0)
                    turned = lax.dynamic_update_index_in_dim(turned, flipped[n], slot, 0)
            firsts.append(first[:nz])
            turned = turned[:nz].reshape(nrow * ncol, vs, rows)
            seconds.append(lax.all_to_all(turned, ("row", "col"), 0, 0, tiled=True))

        first = jnp.stack([f.reshape(nrow, ai, vs, v) for f in firsts], 1)
        first = jnp.transpose(first, (2, 0, 1, 3, 4)).reshape(ai, occ, vs, v)
        second = jnp.stack(
            [s.reshape(nrow, ncol, vs, ai, vs).transpose(0, 3, 2, 1, 4) for s in seconds], 0
        ).reshape(ai, occ, vs, v)
        return (first.astype(F32) + second.astype(F32)).astype(BF16)

    placed = P("row", None, "col", None)
    return jax.shard_map(
        local, mesh=mesh, in_specs=(placed, placed), out_specs=placed, check_vma=False
    )
```

time: 213 us -> 211 us (level)
  waiting for transfers between devices: 129 us -> 82 us
  starting transfers between devices: 21.3 us -> 45.8 us
  other arithmetic: 4.61 us -> 19.2 us
  between operations: 13.6 us -> 0.79 us
  local copies, waits for them, and re-layouts: 28 us -> 39.5 us
  matrix products: 16.4 us -> 22.8 us
    all_to_all x1, waiting for transfers between devices: 52.9 us -> 0.01 us  [local(): panel = lax.all_to_all(blocks, 'col', 0, 0, tiled=True)]
    ppermute x7 -> x28, waiting for transfers between devices: 27.4 us -> 67.3 us  [the longest x10 51.2 us: along(): return lax.ppermute(x, 'col', both)]
    all_gather x2 -> x0, waiting for transfers between devices: 38.3 us -> none  [local(): g = lax.all_gather(part, 'col', axis=0, tiled=False)]
    ppermute x7 -> x28, starting transfers between devices: 7.56 us -> 33.2 us  [the longest x10 20.7 us: along(): return lax.ppermute(x, 'col', both)]
    slice x0 -> x15, local copies, waits for them, and re-layouts: none -> 8.77 us  [the longest x11 7.04 us: local(): first = lax.dynamic_update_index_in_dim(first, block[n], slot, 0)]
    another operation x0 -> x6, other arithmetic: none -> 6.65 us  [the longest x5 3.61 us: product(): mats = jnp.stack([jnp.stack(p, 0) for p in parts], 0)]
    dot_general x8 -> x12, matrix products: 16.4 us -> 22.8 us  [the longest x9 15.1 us: product(): jnp.einsum('kcm,nkcb->nmb', panel[t], mats, preferred_element_type=F32)]
    all_to_all x2, waiting for transfers between devices: 9.29 us -> 14.8 us  [local(): seconds.append(lax.all_to_all(turned, ('row', 'col'), 0, 0, tiled=True))]
  transfers between devices with their start and end apart: 12 -> 31, of which waited for: 8 -> 11; matrix products, arithmetic and copies ran while one was open for 16% -> 34% of each run, Pallas kernels for 0% -> 0%
where the time goes in v2:
time: 211 us; the launch traced here: 210 us
  waiting for transfers between devices  82 us (39%)
  starting transfers between devices  45.8 us (22%)
  local copies, waits for them, and re-layouts  39.5 us (19%)
  matrix products  22.8 us (11%)
  other arithmetic  19.2 us (9%)
    ppermute x10, waiting for transfers between devices, along(): return lax.ppermute(x, 'col', both)  51.2 us
    ppermute x10, starting transfers between devices, along(): return lax.ppermute(x, 'col', both)  20.7 us
    ppermute x9, waiting for transfers between devices, product(): lax.ppermute(part.astype(BF16), 'row', [(r, r ^ t) for r in range(nrow)])  16 us
    dot_general x9, matrix products, product(): jnp.einsum('kcm,nkcb->nmb', panel[t], mats, preferred_element_type=F32)  15.1 us
    all_to_all x2, waiting for transfers between devices, local(): seconds.append(lax.all_to_all(turned, ('row', 'col'), 0, 0, tiled=True))  14.8 us
    ppermute x9, starting transfers between devices, product(): lax.ppermute(part.astype(BF16), 'row', [(r, r ^ t) for r in range(nrow)])  10.7 us
    dot_general x3, matrix products, product(): jnp.einsum('kcm,nkcb->nmb', panel[0], mats, preferred_element_type=F32)  7.75 us
    slice x11, local copies, waits for them, and re-layouts, local(): first = lax.dynamic_update_index_in_dim(first, block[n], slot, 0)  7.04 us
  transfers between devices with their start and end apart: 31, of which 11 were waited for; matrix products, arithmetic and copies ran while one was open for 34% of the time, Pallas kernels for 0%

profile of v2, /device:TPU:0, one launch (start us, length us, event | category | flops | bytes accessed | tf_op | source)
XLA Modules:
  0.0 210.1 jit_solution(11862113606625783177)
XLA Ops:
  2.7 3.9 %reshape.53 = bf16[2,8,64,8,64]{4,3,2,1,0:T(8,128)(2,1)} reshape(bf16[2,8,64,512]{3,2,1,0:T(8,128)(2,1)} %param.2) | data formatting | bytes 2097152 | tf_op jit(solution)/shard_map/reshape | solution.py:37
  6.6 3.0 %copy.110 = bf16[2,8,64,8,64]{4,1,2,0,3:T(8,128)(2,1)S(1)} copy(bf16[2,8,64,8,64]{4,3,2,1,0:T(8,128)(2,1)} %reshape.53) | data formatting | bytes 2097152 | tf_op jit(solution)/shard_map/reshape | solution.py:37
  11.7 6.0 %all-to-all-start = ((bf16[8,2,64,512]{3,2,1,0:T(8,128)(2,1)}), bf16[8,2,64,512]{3,2,1,0:T(8,128)(2,1)S(1)}, u32[]{:S(2)}, u32[]{:S(2)}) async-start(bf16[8,2,64,512]{3,2,1,0:T(8,128)(2,1)} %reshape.54), calls=%async_computation | async-start | bytes 2097152 | tf_op jit(solution)/shard_map/all_to_all | solution.py:39
  21.2 4.7 %collective-permute-start.1 = (bf16[512,512]{0,1:T(8,128)(2,1)S(1)}, bf16[512,512]{0,1:T(8,128)(2,1)}, u32[]{:S(2)}, u32[]{:S(2)}) collective-permute-start(bf16[512,512]{0,1:T(8,128)(2,1)S(1)} %get-tuple-element.5), channel_id=1, source_target_pairs={{0,2},{1,3},{2,4},{3,5},{4,6},{5,7},{8,10},{9,11},{10,12},{11,13},... | collective-permute-start | bytes 1572872 | tf_op jit(solution)/shard_map/ppermute | solution.py:19
  27.2 5.4 %collective-permute-start.13 = (bf16[512,512]{0,1:T(8,128)(2,1)S(1)}, bf16[512,512]{0,1:T(8,128)(2,1)}, u32[]{:S(2)}, u32[]{:S(2)}) collective-permute-start(bf16[512,512]{0,1:T(8,128)(2,1)S(1)} %get-tuple-element.6), channel_id=1, source_target_pairs={{0,2},{1,3},{2,4},{3,5},{4,6},{5,7},{8,10},{9,11},{10,12},{11,13},... | collective-permute-start | bytes 1572872 | tf_op jit(solution)/shard_map/ppermute | solution.py:19
  37.5 9.7 %collective-permute-done.1 = bf16[512,512]{0,1:T(8,128)(2,1)} collective-permute-done((bf16[512,512]{0,1:T(8,128)(2,1)S(1)}, bf16[512,512]{0,1:T(8,128)(2,1)}, u32[]{:S(2)}, u32[]{:S(2)}) %collective-permute-start.1) | collective-permute-done | bytes 524320 | tf_op jit(solution)/shard_map/ppermute | solution.py:19
  51.1 7.1 %collective-permute-done.13 = bf16[512,512]{0,1:T(8,128)(2,1)} collective-permute-done((bf16[512,512]{0,1:T(8,128)(2,1)S(1)}, bf16[512,512]{0,1:T(8,128)(2,1)}, u32[]{:S(2)}, u32[]{:S(2)}) %collective-permute-start.13) | collective-permute-done | bytes 524320 | tf_op jit(solution)/shard_map/ppermute | solution.py:19
  62.4 3.0 %fusion.29 = (bf16[2,512,1,128]{3,2,1,0:T(2,128)(2,1)S(1)}, bf16[2,512,1,128]{3,2,1,0:T(2,128)(2,1)S(1)}, bf16[2,512,1,128]{3,2,1,0:T(2,128)(2,1)S(1)}, bf16[2,512,1,128]{3,2,1,0:T(2,128)(2,1)S(1)}) fusion(s32[]{:T(128)S(6)} %select_n.149, bf16[1,512,4,128]{3,2,1,0:T(4,128)(2,1)S(1)} %get-tuple-element.20, ...), kind=kLoop, calls=%fused_computation.65 | loop fusion | flops 2097152 | bytes 2097168 | tf_op jit(solution)/shard_map/stack | solution.py:41
  65.6 8.7 %collective-permute-done.6 = bf16[512,512]{0,1:T(8,128)(2,1)} collective-permute-done((bf16[512,512]{0,1:T(8,128)(2,1)}, bf16[512,512]{0,1:T(8,128)(2,1)}, u32[]{:S(2)}, u32[]{:S(2)}) %collective-permute-start.6) | collective-permute-done | bytes 524320 | tf_op jit(solution)/shard_map/ppermute | solution.py:19
  76.0 9.1 %collective-permute-done.18 = bf16[512,512]{0,1:T(8,128)(2,1)} collective-permute-done((bf16[512,512]{0,1:T(8,128)(2,1)}, bf16[512,512]{0,1:T(8,128)(2,1)}, u32[]{:S(2)}, u32[]{:S(2)}) %collective-permute-start.18) | collective-permute-done | bytes 524320 | tf_op jit(solution)/shard_map/ppermute | solution.py:19
  102.6 4.2 %collective-permute-done.8 = bf16[512,512]{0,1:T(8,128)(2,1)S(1)} collective-permute-done((bf16[512,512]{0,1:T(8,128)(2,1)S(1)}, bf16[512,512]{0,1:T(8,128)(2,1)S(1)}, u32[]{:S(2)}, u32[]{:S(2)}) %collective-permute-start.8) | collective-permute-done | bytes 524320 | tf_op jit(solution)/shard_map/ppermute | solution.py:19
  106.9 10.5 %collective-permute-done.23 = bf16[512,512]{0,1:T(8,128)(2,1)S(1)} collective-permute-done((bf16[512,512]{0,1:T(8,128)(2,1)S(1)}, bf16[512,512]{0,1:T(8,128)(2,1)S(1)}, u32[]{:S(2)}, u32[]{:S(2)}) %collective-permute-start.23) | collective-permute-done | bytes 524320 | tf_op jit(solution)/shard_map/ppermute | solution.py:19
  118.8 2.5 %fusion.8 = bf16[5,128,512]{1,2,0:T(8,128)(2,1)} fusion(bf16[5,2,512,512]{2,3,1,0:T(8,128)(2,1)S(1)} %fusion.26, bf16[2,512,1,128]{3,2,1,0:T(2,128)(2,1)S(1)} %get-tuple-element.13), kind=kOutput, calls=%fused_computation.21 | convolution fusion | flops 671416320 | bytes 6160384 | tf_op jit(solution)/shard_map/kcm,nkcb->nmb/dot_general | solution.py:49
  139.3 4.0 %convolution_bitcast_fusion.3 = f32[5,128,512]{1,2,0:T(8,128)S(1)} fusion(bf16[5,2,512,512]{2,3,1,0:T(8,128)(2,1)} %copy-done, bf16[2,512,1,128]{3,2,1,0:T(2,128)(2,1)S(1)} %get-tuple-element.14), kind=kOutput, calls=%fused_computation.7 | convolution fusion | flops 671088640 | bytes 6815744 | tf_op jit(solution)/shard_map/kcm,nkcb->nmb/dot_general | solution.py:53
  143.9 16.0 %collective-permute-done.11 = bf16[5,128,512]{1,2,0:T(8,128)(2,1)} collective-permute-done((bf16[5,128,512]{1,2,0:T(8,128)(2,1)}, bf16[5,128,512]{1,2,0:T(8,128)(2,1)}, u32[]{:S(2)}, u32[]{:S(2)}) %collective-permute-start.11) | collective-permute-done | bytes 655392 | tf_op jit(solution)/shard_map/ppermute | solution.py:51
  162.6 3.3 %all-to-all-start.1 = ((bf16[32,64,128]{2,1,0:T(8,128)(2,1)}), bf16[32,64,128]{2,1,0:T(8,128)(2,1)S(1)}, u32[]{:S(2)}, u32[]{:S(2)}) async-start(bf16[32,64,128]{2,1,0:T(8,128)(2,1)} %bitcast.73), calls=%async_computation.1 | async-start | bytes 1048576 | tf_op jit(solution)/shard_map/all_to_all | solution.py:90
  169.6 2.5 %bitcast_dynamic-update-slice_fusion = (bf16[5,512,128]{2,1,0:T(8,128)(2,1)S(1)}, bf16[1,128,512]{1,2,0:T(8,128)(2,1)}) fusion(bf16[5,512,128]{2,1,0:T(8,128)(2,1)S(1)} %slice_dynamic-update-slice_fusion, s32[]{:T(128)S(6)} %select_n.162, bf16[1,128,512]{1,2,0:T(8,128)(2,1)} %collective-permute-done.27, bf16[1,128,512]{1,2,0:T(8,128)(2,1)} %collective-permute-done.26, ...), kind=kOutput, calls=%fused_computation.96 | convolution fusion | flops 135200768 | bytes 2228228 | tf_op jit(solution)/shard_map/kcm,nkcb->nmb/dot_general | solution.py:53
  172.9 9.2 %all-to-all-done.1 = bf16[32,64,128]{2,1,0:T(8,128)(2,1)S(1)} async-done(((bf16[32,64,128]{2,1,0:T(8,128)(2,1)}), bf16[32,64,128]{2,1,0:T(8,128)(2,1)S(1)}, u32[]{:S(2)}, u32[]{:S(2)}) %all-to-all-start.1) | async-done | bytes 524320 | tf_op jit(solution)/shard_map/all_to_all | solution.py:90
  182.1 3.3 %all-to-all-start.2 = ((bf16[32,64,128]{2,1,0:T(8,128)(2,1)}), bf16[32,64,128]{2,1,0:T(8,128)(2,1)}, u32[]{:S(2)}, u32[]{:S(2)}) async-start(bf16[32,64,128]{2,1,0:T(8,128)(2,1)} %bitcast.77), calls=%async_computation.2 | async-start | bytes 1048576 | tf_op jit(solution)/shard_map/all_to_all | solution.py:90
  189.5 2.5 %reshape.57 = bf16[4,8,64,2,64]{4,3,2,1,0:T(2,128)(2,1)S(1)} reshape(bf16[32,64,128]{2,1,0:T(8,128)(2,1)} %copy-done.2) | data formatting | bytes 1048576 | tf_op jit(solution)/shard_map/reshape | solution.py:95
  193.6 2.5 %stack.172 = bf16[1,8,64,512]{3,2,1,0:T(8,128)(2,1)} reshape(bf16[4,2,64,8,64]{4,3,2,1,0:T(8,128)(2,1)} %copy.41) | data formatting | bytes 1048576 | tf_op jit(solution)/shard_map/stack | solution.py:94
  196.2 5.6 %all-to-all-done.2 = bf16[32,64,128]{2,1,0:T(8,128)(2,1)} async-done(((bf16[32,64,128]{2,1,0:T(8,128)(2,1)}), bf16[32,64,128]{2,1,0:T(8,128)(2,1)}, u32[]{:S(2)}, u32[]{:S(2)}) %all-to-all-start.2) | async-done | bytes 524320 | tf_op jit(solution)/shard_map/all_to_all | solution.py:90
  201.8 2.4 %reshape.59 = bf16[4,8,64,2,64]{4,3,2,1,0:T(2,128)(2,1)S(1)} reshape(bf16[32,64,128]{2,1,0:T(8,128)(2,1)} %all-to-all-done.2) | data formatting | bytes 1048576 | tf_op jit(solution)/shard_map/reshape | solution.py:95
  207.8 2.4 %add_convert_fusion = bf16[2,8,64,512]{3,2,1,0:T(8,128)(2,1)} fusion(f32[2,8,64,512]{3,2,1,0:T(8,128)S(1)} %bitcast.229, bf16[1,8,64,512]{3,2,1,0:T(8,128)(2,1)S(1)} %stack.173, bf16[1,8,64,512]{3,2,1,0:T(8,128)(2,1)} %stack.172), kind=kLoop, calls=%fused_computation.3 | loop fusion | flops 2097152 | bytes 4194304 | tf_op jit(solution)/shard_map/convert_element_type | solution.py:97
  (151 shorter events, 77.8 us)
Async XLA Ops:
  2.3 17.8 %collective-permute-start = (bf16[2,512,512]{1,2,0:T(8,128)(2,1)}, bf16[2,512,512]{1,2,0:T(8,128)(2,1)}, u32[]{:S(2)}, u32[]{:S(2)}) collective-permute-start(bf16[2,512,512]{1,2,0:T(8,128)(2,1)} %bitcast.1), channel_id=1, source_target_pairs={{0,1},{1,0},{2,3},{3,2},{4,5},{5,4},{6,7},{7,6},{8,9},{9,8},{10,11... | collective-permute-start | bytes 3145736 | tf_op jit(solution)/shard_map/ppermute | solution.py:15
  11.7 49.9 %all-to-all-start = ((bf16[8,2,64,512]{3,2,1,0:T(8,128)(2,1)}), bf16[8,2,64,512]{3,2,1,0:T(8,128)(2,1)S(1)}, u32[]{:S(2)}, u32[]{:S(2)}) async-start(bf16[8,2,64,512]{3,2,1,0:T(8,128)(2,1)} %reshape.54), calls=%async_computation | async-start | bytes 2097152 | tf_op jit(solution)/shard_map/all_to_all | solution.py:39
  21.2 25.9 %collective-permute-start.1 = (bf16[512,512]{0,1:T(8,128)(2,1)S(1)}, bf16[512,512]{0,1:T(8,128)(2,1)}, u32[]{:S(2)}, u32[]{:S(2)}) collective-permute-start(bf16[512,512]{0,1:T(8,128)(2,1)S(1)} %get-tuple-element.5), channel_id=1, source_target_pairs={{0,2},{1,3},{2,4},{3,5},{4,6},{5,7},{8,10},{9,11},{10,12},{11,13},... | collective-permute-start | bytes 1572872 | tf_op jit(solution)/shard_map/ppermute | solution.py:19
  26.0 23.8 %collective-permute-start.3 = (bf16[512,512]{0,1:T(8,128)(2,1)S(1)}, bf16[512,512]{0,1:T(8,128)(2,1)}, u32[]{:S(2)}, u32[]{:S(2)}) collective-permute-start(bf16[512,512]{0,1:T(8,128)(2,1)S(1)} %get-tuple-element.5), channel_id=1, source_target_pairs={{2,0},{3,1},{4,2},{5,3},{6,4},{7,5},{10,8},{11,9},{12,10},{13,11},... | collective-permute-start | bytes 1572872 | tf_op jit(solution)/shard_map/ppermute | solution.py:19
  27.2 30.9 %collective-permute-start.13 = (bf16[512,512]{0,1:T(8,128)(2,1)S(1)}, bf16[512,512]{0,1:T(8,128)(2,1)}, u32[]{:S(2)}, u32[]{:S(2)}) collective-permute-start(bf16[512,512]{0,1:T(8,128)(2,1)S(1)} %get-tuple-element.6), channel_id=1, source_target_pairs={{0,2},{1,3},{2,4},{3,5},{4,6},{5,7},{8,10},{9,11},{10,12},{11,13},... | collective-permute-start | bytes 1572872 | tf_op jit(solution)/shard_map/ppermute | solution.py:19
  32.7 27.7 %collective-permute-start.15 = (bf16[512,512]{0,1:T(8,128)(2,1)S(1)}, bf16[512,512]{0,1:T(8,128)(2,1)}, u32[]{:S(2)}, u32[]{:S(2)}) collective-permute-start(bf16[512,512]{0,1:T(8,128)(2,1)S(1)} %get-tuple-element.6), channel_id=1, source_target_pairs={{2,0},{3,1},{4,2},{5,3},{6,4},{7,5},{10,8},{11,9},{12,10},{13,11},... | collective-permute-start | bytes 1572872 | tf_op jit(solution)/shard_map/ppermute | solution.py:19
  47.1 43.4 %collective-permute-start.2 = (bf16[512,512]{0,1:T(8,128)(2,1)}, bf16[512,512]{0,1:T(8,128)(2,1)}, u32[]{:S(2)}, u32[]{:S(2)}) collective-permute-start(bf16[512,512]{0,1:T(8,128)(2,1)} %collective-permute-done.1), channel_id=1, source_target_pairs={{0,1},{1,0},{2,3},{3,2},{4,5},{5,4},{6,7},{7,6},{8,9},{9,8},{10,11... | collective-permute-start | bytes 1572872 | tf_op jit(solution)/shard_map/ppermute | solution.py:15
  47.1 18.4 %collective-permute-start.5 = (bf16[512,512]{0,1:T(8,128)(2,1)}, bf16[512,512]{0,1:T(8,128)(2,1)}, u32[]{:S(2)}, u32[]{:S(2)}) collective-permute-start(bf16[512,512]{0,1:T(8,128)(2,1)} %collective-permute-done.1), channel_id=1, source_target_pairs={{2,4},{3,5},{4,6},{5,7},{10,12},{11,13},{12,14},{13,15},{18,20},{1... | collective-permute-start | bytes 1572872 | tf_op jit(solution)/shard_map/ppermute | solution.py:19
  49.8 24.5 %collective-permute-start.6 = (bf16[512,512]{0,1:T(8,128)(2,1)}, bf16[512,512]{0,1:T(8,128)(2,1)}, u32[]{:S(2)}, u32[]{:S(2)}) collective-permute-start(bf16[512,512]{0,1:T(8,128)(2,1)} %collective-permute-done.3), channel_id=1, source_target_pairs={{2,0},{3,1},{4,2},{5,3},{10,8},{11,9},{12,10},{13,11},{18,16},{19,... | collective-permute-start | bytes 1572872 | tf_op jit(solution)/shard_map/ppermute | solution.py:19
  60.4 24.8 %collective-permute-start.18 = (bf16[512,512]{0,1:T(8,128)(2,1)}, bf16[512,512]{0,1:T(8,128)(2,1)}, u32[]{:S(2)}, u32[]{:S(2)}) collective-permute-start(bf16[512,512]{0,1:T(8,128)(2,1)} %collective-permute-done.15), channel_id=1, source_target_pairs={{2,0},{3,1},{4,2},{5,3},{10,8},{11,9},{12,10},{13,11},{18,16},{19,... | collective-permute-start | bytes 1572872 | tf_op jit(solution)/shard_map/ppermute | solution.py:19
  65.5 20.7 %collective-permute-start.14 = (bf16[512,512]{0,1:T(8,128)(2,1)}, bf16[512,512]{0,1:T(8,128)(2,1)S(1)}, u32[]{:S(2)}, u32[]{:S(2)}) collective-permute-start(bf16[512,512]{0,1:T(8,128)(2,1)} %collective-permute-done.13), channel_id=1, source_target_pairs={{0,1},{1,0},{2,3},{3,2},{4,5},{5,4},{6,7},{7,6},{8,9},{9,8},{10,11... | collective-permute-start | bytes 1572872 | tf_op jit(solution)/shard_map/ppermute | solution.py:15
  88.0 18.8 %collective-permute-start.8 = (bf16[512,512]{0,1:T(8,128)(2,1)S(1)}, bf16[512,512]{0,1:T(8,128)(2,1)S(1)}, u32[]{:S(2)}, u32[]{:S(2)}) collective-permute-start(bf16[512,512]{0,1:T(8,128)(2,1)S(1)} %broadcast_select_fusion.1), channel_id=1, source_target_pairs={{4,6},{5,7},{2,0},{3,1},{12,14},{13,15},{10,8},{11,9},{20,22},{21,... | collective-permute-start | bytes 1572872 | tf_op jit(solution)/shard_map/ppermute | solution.py:19
  90.5 26.9 %collective-permute-start.23 = (bf16[512,512]{0,1:T(8,128)(2,1)S(1)}, bf16[512,512]{0,1:T(8,128)(2,1)S(1)}, u32[]{:S(2)}, u32[]{:S(2)}) collective-permute-start(bf16[512,512]{0,1:T(8,128)(2,1)S(1)} %broadcast_select_fusion), channel_id=1, source_target_pairs={{4,6},{5,7},{2,0},{3,1},{12,14},{13,15},{10,8},{11,9},{20,22},{21,... | collective-permute-start | bytes 1572872 | tf_op jit(solution)/shard_map/ppermute | solution.py:19
  96.0 35.2 %collective-permute-start.20 = (bf16[4,128,512]{1,2,0:T(8,128)(2,1)S(1)}, bf16[4,128,512]{1,2,0:T(8,128)(2,1)S(1)}, u32[]{:S(2)}, u32[]{:S(2)}) collective-permute-start(bf16[4,128,512]{1,2,0:T(8,128)(2,1)S(1)} %fusion.11), channel_id=1, source_target_pairs={{0,8},{8,0},{16,24},{24,16},{1,9},{9,1},{17,25},{25,17},{2,10},{10... | collective-permute-start | bytes 1572872 | tf_op jit(solution)/shard_map/ppermute | solution.py:51
  99.0 32.7 %collective-permute-start.21 = (bf16[4,128,512]{1,2,0:T(8,128)(2,1)S(1)}, bf16[4,128,512]{1,2,0:T(8,128)(2,1)S(1)}, u32[]{:S(2)}, u32[]{:S(2)}) collective-permute-start(bf16[4,128,512]{1,2,0:T(8,128)(2,1)S(1)} %fusion.10), channel_id=1, source_target_pairs={{0,16},{8,24},{16,0},{24,8},{1,17},{9,25},{17,1},{25,9},{2,18},{10... | collective-permute-start | bytes 1572872 | tf_op jit(solution)/shard_map/ppermute | solution.py:51
  102.1 29.7 %collective-permute-start.22 = (bf16[4,128,512]{1,2,0:T(8,128)(2,1)S(1)}, bf16[4,128,512]{1,2,0:T(8,128)(2,1)S(1)}, u32[]{:S(2)}, u32[]{:S(2)}) collective-permute-start(bf16[4,128,512]{1,2,0:T(8,128)(2,1)S(1)} %fusion.9), channel_id=1, source_target_pairs={{0,24},{8,16},{16,8},{24,0},{1,25},{9,17},{17,9},{25,1},{2,26},{10... | collective-permute-start | bytes 1572872 | tf_op jit(solution)/shard_map/ppermute | solution.py:51
  121.3 22.0 %collective-permute-start.10 = (bf16[5,128,512]{1,2,0:T(8,128)(2,1)}, bf16[5,128,512]{1,2,0:T(8,128)(2,1)}, u32[]{:S(2)}, u32[]{:S(2)}) collective-permute-start(bf16[5,128,512]{1,2,0:T(8,128)(2,1)} %fusion.8), channel_id=1, source_target_pairs={{0,8},{8,0},{16,24},{24,16},{1,9},{9,1},{17,25},{25,17},{2,10},{10... | collective-permute-start | bytes 1966088 | tf_op jit(solution)/shard_map/ppermute | solution.py:51
  125.2 34.7 %collective-permute-start.11 = (bf16[5,128,512]{1,2,0:T(8,128)(2,1)}, bf16[5,128,512]{1,2,0:T(8,128)(2,1)}, u32[]{:S(2)}, u32[]{:S(2)}) collective-permute-start(bf16[5,128,512]{1,2,0:T(8,128)(2,1)} %fusion.7), channel_id=1, source_target_pairs={{0,16},{8,24},{16,0},{24,8},{1,17},{9,25},{17,1},{25,9},{2,18},{10... | collective-permute-start | bytes 1966088 | tf_op jit(solution)/shard_map/ppermute | solution.py:51
  131.3 28.7 %collective-permute-start.12 = (bf16[5,128,512]{1,2,0:T(8,128)(2,1)}, bf16[5,128,512]{1,2,0:T(8,128)(2,1)S(1)}, u32[]{:S(2)}, u32[]{:S(2)}) collective-permute-start(bf16[5,128,512]{1,2,0:T(8,128)(2,1)} %fusion.6), channel_id=1, source_target_pairs={{0,24},{8,16},{16,8},{24,0},{1,25},{9,17},{17,9},{25,1},{2,26},{10... | collective-permute-start | bytes 1966088 | tf_op jit(solution)/shard_map/ppermute | solution.py:51
  134.7 34.9 %collective-permute-start.25 = (bf16[1,128,512]{1,2,0:T(8,128)(2,1)}, bf16[1,128,512]{1,2,0:T(8,128)(2,1)}, u32[]{:S(2)}, u32[]{:S(2)}) collective-permute-start(bf16[1,128,512]{1,2,0:T(8,128)(2,1)} %fusion.21), channel_id=1, source_target_pairs={{0,8},{8,0},{16,24},{24,16},{1,9},{9,1},{17,25},{25,17},{2,10},{10... | collective-permute-start | bytes 393224 | tf_op jit(solution)/shard_map/ppermute | solution.py:51
  136.2 33.4 %collective-permute-start.26 = (bf16[1,128,512]{1,2,0:T(8,128)(2,1)}, bf16[1,128,512]{1,2,0:T(8,128)(2,1)}, u32[]{:S(2)}, u32[]{:S(2)}) collective-permute-start(bf16[1,128,512]{1,2,0:T(8,128)(2,1)} %fusion.20), channel_id=1, source_target_pairs={{0,16},{8,24},{16,0},{24,8},{1,17},{9,25},{17,1},{25,9},{2,18},{10... | collective-permute-start | bytes 393224 | tf_op jit(solution)/shard_map/ppermute | solution.py:51
  143.4 26.2 %collective-permute-start.27 = (bf16[1,128,512]{1,2,0:T(8,128)(2,1)}, bf16[1,128,512]{1,2,0:T(8,128)(2,1)}, u32[]{:S(2)}, u32[]{:S(2)}) collective-permute-start(bf16[1,128,512]{1,2,0:T(8,128)(2,1)} %fusion.19), channel_id=1, source_target_pairs={{0,24},{8,16},{16,8},{24,0},{1,25},{9,17},{17,9},{25,1},{2,26},{10... | collective-permute-start | bytes 393224 | tf_op jit(solution)/shard_map/ppermute | solution.py:51
  162.6 19.4 %all-to-all-start.1 = ((bf16[32,64,128]{2,1,0:T(8,128)(2,1)}), bf16[32,64,128]{2,1,0:T(8,128)(2,1)S(1)}, u32[]{:S(2)}, u32[]{:S(2)}) async-start(bf16[32,64,128]{2,1,0:T(8,128)(2,1)} %bitcast.73), calls=%async_computation.1 | async-start | bytes 1048576 | tf_op jit(solution)/shard_map/all_to_all | solution.py:90
  182.1 19.7 %all-to-all-start.2 = ((bf16[32,64,128]{2,1,0:T(8,128)(2,1)}), bf16[32,64,128]{2,1,0:T(8,128)(2,1)}, u32[]{:S(2)}, u32[]{:S(2)}) async-start(bf16[32,64,128]{2,1,0:T(8,128)(2,1)} %bitcast.77), calls=%async_computation.2 | async-start | bytes 1048576 | tf_op jit(solution)/shard_map/all_to_all | solution.py:90
  (21 other events, 319.8 us)

commit v3 on v1

v3 whole, which is shorter than its diff:
```python
import functools

import jax
import jax.numpy as jnp
from jax import lax
from jax.experimental import pallas as pl
from jax.experimental.pallas import tpu as pltpu
from jax.sharding import PartitionSpec as P

F32, BF16 = jnp.float32, jnp.bfloat16
VMEM = pl.BlockSpec(memory_space=pltpu.VMEM)
SMEM = pl.BlockSpec(memory_space=pltpu.SMEM)
PARAMS = pltpu.CompilerParams(vmem_limit_bytes=40 * 1024 * 1024)


def spread_kernel(nrow, ncol, row_ref, a_ref, out_ref):
    kk, occ, _, v = a_ref.shape
    ai, vs = occ // nrow, v // ncol
    for k in range(kk):
        tiles = [a_ref[k, (row_ref[0] ^ t) * ai + i] for t in range(nrow) for i in range(ai)]
        for s in range(ncol):
            piece = [tile[:, s * vs : (s + 1) * vs] for tile in tiles]
            out_ref[s, k] = jnp.concatenate(piece, axis=1)


def product_kernel(count, nrow, flag_ref, panel_ref, *refs):
    blocks, outs = refs[: 2 * count], refs[2 * count :]
    rows = outs[0].shape[1]

    def run(pick):
        for n in range(count):
            prod = jnp.dot(panel_ref[...], blocks[2 * n + pick][...], preferred_element_type=F32)
            outs[0][n] = prod[:rows]
            for t in range(1, nrow):
                outs[t][n] = prod[t * rows : (t + 1) * rows].astype(BF16)

    @pl.when(flag_ref[0] == 1)
    def _():
        run(0)

    @pl.when(flag_ref[0] == 0)
    def _():
        run(1)


def sum_kernel(groups, nrow, slot_ref, *refs):
    first_ref, turned_ref = refs[-2:]
    at = 0
    for g in range(groups):
        parts = refs[g * nrow : (g + 1) * nrow]
        for n in range(parts[0].shape[0]):
            total = parts[0][n]
            for other in parts[1:]:
                total = total + other[n].astype(F32)
            total = total.astype(BF16)
            first_ref[slot_ref[at]] = total
            turned_ref[slot_ref[at]] = total.astype(F32).T.astype(BF16)
            at += 1


def final_kernel(nrow, ncol, first0, first1, second0, second1, out_ref):
    ai, occ, vs, v = out_ref.shape
    firsts, seconds = (first0, first1), (second0, second1)
    for i in range(ai):
        for r in range(nrow):
            tiles = [seconds[i][r * ncol + s].astype(F32) for s in range(ncol)]
            for q in range(ai):
                second = jnp.concatenate([x[:, q * vs : (q + 1) * vs] for x in tiles], axis=1)
                first = firsts[q][r, i * vs : (i + 1) * vs, :].astype(F32)
                out_ref[i, r * ai + q] = (first + second).astype(BF16)


def solution(mesh):
    nrow, ncol = mesh.shape["row"], mesh.shape["col"]
    nz = ncol // 2
    order = []
    for z in range(nz):
        seq = []
        for t in range(1, nz):
            seq += [(t, 1)] if z >= t else []
            seq += [(t, -1)] if z + t < nz else []
        order.append(seq)

    def core_copy(x, p):
        return lax.ppermute(x, "col", [(2 * a + p, 2 * a + 1 - p) for a in range(nz)])

    def along(x, pairs, p):
        return lax.ppermute(x, "col", [(2 * a + p, 2 * b + p) for a, b in pairs])

    def local(amplitudes, intermediate):
        kk, occ, cs, v = amplitudes.shape
        ai = occ // nrow
        vs = v // ncol
        rows = ai * vs
        row = lax.axis_index("row")
        col = lax.axis_index("col")
        z, core = col // 2, col % 2

        w = intermediate.reshape(kk * v, v)
        other = lax.ppermute(w, "col", [(s, s ^ 1) for s in range(ncol)])

        blocks = pl.pallas_call(
            functools.partial(spread_kernel, nrow, ncol),
            out_shape=jax.ShapeDtypeStruct((ncol, kk, cs, occ * vs), BF16),
            in_specs=[SMEM, VMEM],
            out_specs=VMEM,
            compiler_params=PARAMS,
        )(row.reshape(1), amplitudes)
        panel = lax.all_to_all(blocks, "col", 0, 0, tiled=True)
        panel = jnp.transpose(panel, (3, 1, 0, 2)).reshape(nrow * rows, kk * v)

        def product(p, pairs):
            n = len(pairs)
            flag = (core == p).astype(jnp.int32).reshape(1)
            sent = [jax.ShapeDtypeStruct((n, rows, v), BF16)] * (nrow - 1)
            parts = pl.pallas_call(
                functools.partial(product_kernel, n, nrow),
                out_shape=[jax.ShapeDtypeStruct((n, rows, v), F32)] + sent,
                in_specs=[SMEM] + [VMEM] * (1 + 2 * n),
                out_specs=[VMEM] * nrow,
                compiler_params=PARAMS,
            )(flag, panel, *[x for pair in pairs for x in pair])
            return [parts[0]] + [
                lax.ppermute(parts[t], "row", [(r, r ^ t) for r in range(nrow)])
                for t in range(1, nrow)
            ]

        def chain(p, start):
            got = {}
            blocks = []
            up = down = start
            for t in range(1, nz):
                up = along(up, [(a, a + 1) for a in range(t - 1, nz - 1)], p)
                down = along(down, [(a, a - 1) for a in range(1, nz - t + 1)], p)
                got[t, 1], got[t, -1] = up, down
                picks = [seq[t - 1] for seq in order]
                block = got[picks[0]]
                for pick in sorted(set(picks) - {picks[0]}):
                    hit = functools.reduce(
                        jnp.logical_or, [z == a for a in range(nz) if picks[a] == pick]
                    )
                    block = jnp.where(hit, got[pick], block)
                blocks.append((block, core_copy(block, p)))
            return blocks

        def slots():
            table = []
            for seq in order:
                a = len(table)
                table.append([a] + [a - t * d for t, d in seq])
            return jnp.array(table, jnp.int32)[z]

        where = slots()
        firsts, seconds = [], []
        start = w
        for p in range(2):
            arrived = chain(p, start)
            if p == 0:
                start, _ = lax.optimization_barrier((w, arrived[0][1]))
            here = (w, other)
            groups = [product(p, [here, arrived[0]])]
            groups += [product(p, [pair]) for pair in arrived[1:]]
            first, turned = pl.pallas_call(
                functools.partial(sum_kernel, len(groups), nrow),
                out_shape=[
                    jax.ShapeDtypeStruct((nz, rows, v), BF16),
                    jax.ShapeDtypeStruct((nz, v, rows), BF16),
                ],
                in_specs=[SMEM] + [VMEM] * (len(groups) * nrow),
                out_specs=[VMEM] * 2,
                compiler_params=PARAMS,
            )(where, *[x for g in groups for x in g])
            firsts.append(first)
            turned = turned.reshape(nrow * ncol, vs, rows)
            seconds.append(lax.all_to_all(turned, ("row", "col"), 0, 0, tiled=True))

        return pl.pallas_call(
            functools.partial(final_kernel, nrow, ncol),
            out_shape=jax.ShapeDtypeStruct((ai, occ, vs, v), BF16),
            in_specs=[VMEM] * 4,
            out_specs=VMEM,
            compiler_params=PARAMS,
        )(*firsts, *seconds)

    placed = P("row", None, "col", None)
    return jax.shard_map(
        local, mesh=mesh, in_specs=(placed, placed), out_specs=placed, check_vma=False
    )
```

time: 213 us -> 240 us (1.13)
  starting transfers between devices: 21.3 us -> 78.5 us
  waiting for transfers between devices: 129 us -> 90 us
  blocking collectives: 0 us -> 21.2 us
  Pallas kernels: 0 us -> 19.9 us
  matrix products: 16.4 us -> 0 us
  between operations: 13.6 us -> 0.37 us
  local copies, waits for them, and re-layouts: 28 us -> 21.5 us
  other arithmetic: 4.61 us -> 7.79 us
    ppermute x7 -> x37, starting transfers between devices: 7.56 us -> 55.4 us  [the longest x18 22.4 us: product(): lax.ppermute(parts[t], 'row', [(r, r ^ t) for r in range(nrow)])]
    ppermute x7 -> x37, waiting for transfers between devices: 27.4 us -> 71.8 us  [the longest x12 44 us: along(): return lax.ppermute(x, 'col', [(2 * a + p, 2 * b + p) for a, b in pairs])]
    all_gather x2 -> x0, waiting for transfers between devices: 38.3 us -> none  [local(): g = lax.all_gather(part, 'col', axis=0, tiled=False)]
    all_to_all x1, waiting for transfers between devices: 52.9 us -> 18.2 us  [local(): panel = lax.all_to_all(blocks, 'col', 0, 0, tiled=True)]
    all_to_all x0 -> x1, blocking collectives: none -> 21.2 us  [local(): seconds.append(lax.all_to_all(turned, ('row', 'col'), 0, 0, tiled=True))]
    pallas_call x0 -> x10, Pallas kernels: none -> 19.9 us  [the longest x6 13.8 us: product(): pl.pallas_call(functools.partial(product_kernel, n, nrow), out_shape=[jax...]
    unnamed x12 -> x52, local copies, waits for them, and re-layouts: 0.92 us -> 18.2 us
    dot_general x8 -> x0, matrix products: 16.4 us -> none  [local(): jnp.einsum('kcm,jkcb->mjb', mine, gathered[q], preferred_element_type=jnp...]
  transfers between devices with their start and end apart: 12 -> 39, of which waited for: 8 -> 11; matrix products, arithmetic and copies ran while one was open for 16% -> 3% of each run, Pallas kernels for 0% -> 7%
where the time goes in v3:
time: 240 us; the launch traced here: 239 us
  waiting for transfers between devices  90 us (38%)
  starting transfers between devices  78.5 us (33%)
  local copies, waits for them, and re-layouts  21.5 us (9%)
  blocking collectives  21.2 us (9%)
  Pallas kernels  19.9 us (8%)
  other arithmetic  7.79 us (3%)
    ppermute x12, waiting for transfers between devices, along(): return lax.ppermute(x, 'col', [(2 * a + p, 2 * b + p) for a, b in pairs])  44 us
    ppermute x18, waiting for transfers between devices, product(): lax.ppermute(parts[t], 'row', [(r, r ^ t) for r in range(nrow)])  26.6 us
    ppermute x18, starting transfers between devices, product(): lax.ppermute(parts[t], 'row', [(r, r ^ t) for r in range(nrow)])  22.4 us
    ppermute x12, starting transfers between devices, along(): return lax.ppermute(x, 'col', [(2 * a + p, 2 * b + p) for a, b in pairs])  22.1 us
    all_to_all x1, blocking collectives, local(): seconds.append(lax.all_to_all(turned, ('row', 'col'), 0, 0, tiled=True))  21.2 us
    unnamed x52, local copies, waits for them, and re-layouts  18.2 us
    all_to_all x1, waiting for transfers between devices, local(): panel = lax.all_to_all(blocks, 'col', 0, 0, tiled=True)  18.2 us
    all_to_all x1, starting transfers between devices, local(): panel = lax.all_to_all(blocks, 'col', 0, 0, tiled=True)  16.5 us
  transfers between devices with their start and end apart: 39, of which 11 were waited for; matrix products, arithmetic and copies ran while one was open for 3% of the time, Pallas kernels for 7%

profile of v3, /device:TPU:0, one launch (start us, length us, event | category | flops | bytes accessed | tf_op | source)
XLA Modules:
  0.0 239.2 jit_solution(10199316759096959)
XLA Ops:
  0.0 5.0 %collective-permute-start.1 = (bf16[1024,512]{1,0:T(8,128)(2,1)}, bf16[1024,512]{1,0:T(8,128)(2,1)S(1)}, u32[]{:S(2)}, u32[]{:S(2)}) collective-permute-start(bf16[1024,512]{1,0:T(8,128)(2,1)} %bitcast.10), channel_id=1, source_target_pairs={{0,2},{2,4},{4,6},{8,10},{10,12},{12,14},{16,18},{18,20},{20,22},{... | collective-permute-start | bytes 3145736 | tf_op jit(solution)/shard_map/ppermute | solution.py:88
  6.3 11.2 %collective-permute-done.1 = bf16[1024,512]{1,0:T(8,128)(2,1)S(1)} collective-permute-done((bf16[1024,512]{1,0:T(8,128)(2,1)}, bf16[1024,512]{1,0:T(8,128)(2,1)S(1)}, u32[]{:S(2)}, u32[]{:S(2)}) %collective-permute-start.1) | collective-permute-done | bytes 1048608 | tf_op jit(solution)/shard_map/ppermute | solution.py:88
  19.2 2.7 %collective-permute-done.2 = bf16[1024,512]{1,0:T(8,128)(2,1)S(1)} collective-permute-done((bf16[1024,512]{1,0:T(8,128)(2,1)}, bf16[1024,512]{1,0:T(8,128)(2,1)S(1)}, u32[]{:S(2)}, u32[]{:S(2)}) %collective-permute-start.2) | collective-permute-done | bytes 1048608 | tf_op jit(solution)/shard_map/ppermute | solution.py:88
  24.8 14.3 %collective-permute-done.8 = bf16[1024,512]{1,0:T(8,128)(2,1)} collective-permute-done((bf16[1024,512]{1,0:T(8,128)(2,1)S(1)}, bf16[1024,512]{1,0:T(8,128)(2,1)}, u32[]{:S(2)}, u32[]{:S(2)}) %collective-permute-start.8) | collective-permute-done | bytes 1048608 | tf_op jit(solution)/shard_map/ppermute | solution.py:88
  40.5 15.6 %collective-permute-done.14 = bf16[1024,512]{1,0:T(8,128)(2,1)} collective-permute-done((bf16[1024,512]{1,0:T(8,128)(2,1)}, bf16[1024,512]{1,0:T(8,128)(2,1)}, u32[]{:S(2)}, u32[]{:S(2)}) %collective-permute-start.14) | collective-permute-done | bytes 1048608 | tf_op jit(solution)/shard_map/ppermute | solution.py:88
  56.2 3.8 %select_select_fusion.2 = (bf16[1024,512]{1,0:T(8,128)(2,1)}, bf16[1024,512]{1,0:T(8,128)(2,1)}, bf16[1024,512]{1,0:T(8,128)(2,1)S(1)}) fusion(bf16[1024,512]{1,0:T(8,128)(2,1)} %collective-permute-done.13, bf16[1024,512]{1,0:T(8,128)(2,1)} %collective-permute-done.7, bf16[1024,512]{1,0:T(8,128)(2,1)} %collective-permute-done.8, ...), kind=kLoop, calls=%fused_computation.2 | loop fusion | flops 3145728 | bytes 9437189 | tf_op jit(solution)/shard_map/jit(_where)/select_n | solution.py:142
  72.4 16.5 %all-to-all-start = ((bf16[8,2,64,512]{3,2,1,0:T(8,128)(2,1)}), bf16[8,2,64,512]{3,2,1,0:T(8,128)(2,1)S(1)}, u32[]{:S(2)}, u32[]{:S(2)}) async-start(bf16[8,2,64,512]{3,2,1,0:T(8,128)(2,1)} %shard_map.37), calls=%async_computation | async-start | bytes 2097152 | tf_op jit(solution)/shard_map/all_to_all | solution.py:109
  89.4 3.0 %collective-permute-start.9 = (bf16[1024,512]{1,0:T(8,128)(2,1)}, bf16[1024,512]{1,0:T(8,128)(2,1)}, u32[]{:S(2)}, u32[]{:S(2)}) collective-permute-start(bf16[1024,512]{1,0:T(8,128)(2,1)} %get-tuple-element.66.refs_0_), channel_id=1, source_target_pairs={{0,1},{2,3},{4,5},{6,7},{8,9},{10,11},{12,13},{14,15},{16,17},{18,... | collective-permute-start | bytes 3145736 | tf_op jit(solution)/shard_map/ppermute | solution.py:85
  92.4 2.3 collective-permute-start.15
  98.1 18.2 %all-to-all-done = bf16[8,2,64,512]{3,2,1,0:T(8,128)(2,1)S(1)} async-done(((bf16[8,2,64,512]{3,2,1,0:T(8,128)(2,1)}), bf16[8,2,64,512]{3,2,1,0:T(8,128)(2,1)S(1)}, u32[]{:S(2)}, u32[]{:S(2)}) %all-to-all-start) | async-done | bytes 1048608 | tf_op jit(solution)/shard_map/all_to_all | solution.py:109
  121.3 2.1 shard_map.38
  125.7 2.2 shard_map.39
  130.7 2.2 shard_map.40
  135.0 4.0 %select_select_fusion = (bf16[1024,512]{1,0:T(8,128)(2,1)}, bf16[1024,512]{1,0:T(8,128)(2,1)}, bf16[1024,512]{1,0:T(8,128)(2,1)}) fusion(bf16[1024,512]{1,0:T(8,128)(2,1)} %collective-permute-done.31, bf16[1024,512]{1,0:T(8,128)(2,1)} %collective-permute-done.25, bf16[1024,512]{1,0:T(8,128)(2,1)} %collective-permute-done.26, ...), kind=kLoop, calls=%fused_computation | loop fusion | flops 3145728 | bytes 9437189 | tf_op jit(solution)/shard_map/jit(_where)/select_n | solution.py:142
  150.7 2.0 collective-permute-start.6
  153.4 9.4 %collective-permute-done.5.refs_2_ = bf16[2,128,512]{2,1,0:T(8,128)(2,1)} collective-permute-done((bf16[2,128,512]{2,1,0:T(8,128)(2,1)}, bf16[2,128,512]{2,1,0:T(8,128)(2,1)}, u32[]{:S(2)}, u32[]{:S(2)}) %collective-permute-start.5) | collective-permute-done | bytes 262176 | tf_op jit(solution)/shard_map/ppermute | solution.py:124
  173.2 6.5 %all-to-all-start.1 = ((bf16[32,64,128]{2,1,0:T(8,128)(2,1)}), bf16[32,64,128]{2,1,0:T(8,128)(2,1)}, u32[]{:S(2)}, u32[]{:S(2)}) async-start(bf16[32,64,128]{2,1,0:T(8,128)(2,1)} %bitcast.17), calls=%async_computation.1 | async-start | bytes 1048576 | tf_op jit(solution)/shard_map/all_to_all | solution.py:175
  179.7 2.2 shard_map.43
  185.2 2.8 %shard_map.42 = (f32[2,128,512]{2,1,0:T(8,128)S(1)}, bf16[2,128,512]{2,1,0:T(8,128)(2,1)S(1)}, bf16[2,128,512]{2,1,0:T(8,128)(2,1)S(1)}, bf16[2,128,512]{2,1,0:T(8,128)(2,1)S(1)}) custom-call(s32[1]{0:T(128)} %bitcast.6.flag_ref, bf16[512,1024]{1,0:T(8,128)(2,1)S(1)} %copy.6.panel_ref, bf16[1024,512]{1,0:T(8,128)(2,1)S(1)} %bitcast.16, ...), custom_call_target="tpu_custom_call" | custom-call | tf_op jit(solution)/shard_map/pallas_call | solution.py:116
  190.1 2.2 shard_map.44
  195.9 5.6 %collective-permute-done.30.refs_7_ = bf16[1,128,512]{2,1,0:T(8,128)(2,1)S(1)} collective-permute-done((bf16[1,128,512]{2,1,0:T(8,128)(2,1)S(1)}, bf16[1,128,512]{2,1,0:T(8,128)(2,1)S(1)}, u32[]{:S(2)}, u32[]{:S(2)}) %collective-permute-start.30) | collective-permute-done | bytes 131104 | tf_op jit(solution)/shard_map/ppermute | solution.py:124
  204.9 9.6 %collective-permute-done.35.refs_10_ = bf16[1,128,512]{2,1,0:T(8,128)(2,1)S(1)} collective-permute-done((bf16[1,128,512]{2,1,0:T(8,128)(2,1)S(1)}, bf16[1,128,512]{2,1,0:T(8,128)(2,1)S(1)}, u32[]{:S(2)}, u32[]{:S(2)}) %collective-permute-start.35) | collective-permute-done | bytes 131104 | tf_op jit(solution)/shard_map/ppermute | solution.py:124
  215.4 21.2 %all_to_all.15.second1 = bf16[32,64,128]{2,1,0:T(8,128)(2,1)S(1)} all-to-all(bf16[32,64,128]{2,1,0:T(8,128)(2,1)S(1)} %bitcast.18), channel_id=1, replica_groups=mesh['row'=4,'col'=8] {'row','col'}, dimensions={0} | all-to-all | bytes 1048576 | tf_op jit(solution)/shard_map/all_to_all | solution.py:175
  236.6 2.5 %shard_map.46 = bf16[2,8,64,512]{3,2,1,0:T(8,128)(2,1)} custom-call(bf16[4,128,512]{2,1,0:T(8,128)(2,1)S(1)} %copy-done.8, bf16[4,128,512]{2,1,0:T(8,128)(2,1)S(1)} %get-tuple-element.60.first1, bf16[32,64,128]{2,1,0:T(8,128)(2,1)} %all-to-all-done.1.second0, bf16[32,64,128]{2,1,0:T(8,128)(2,1)S(1)} %all_to_all.15.second1), custom_call_target="tpu_custom_call" | custom-call | tf_op jit(solution)/shard_map/pallas_call | solution.py:177
  (122 shorter events, 71.5 us)
Async XLA Ops:
  0.0 17.5 %collective-permute-start.1 = (bf16[1024,512]{1,0:T(8,128)(2,1)}, bf16[1024,512]{1,0:T(8,128)(2,1)S(1)}, u32[]{:S(2)}, u32[]{:S(2)}) collective-permute-start(bf16[1024,512]{1,0:T(8,128)(2,1)} %bitcast.10), channel_id=1, source_target_pairs={{0,2},{2,4},{4,6},{8,10},{10,12},{12,14},{16,18},{18,20},{20,22},{... | collective-permute-start | bytes 3145736 | tf_op jit(solution)/shard_map/ppermute | solution.py:88
  5.0 16.9 %collective-permute-start.2 = (bf16[1024,512]{1,0:T(8,128)(2,1)}, bf16[1024,512]{1,0:T(8,128)(2,1)S(1)}, u32[]{:S(2)}, u32[]{:S(2)}) collective-permute-start(bf16[1024,512]{1,0:T(8,128)(2,1)} %bitcast.11), channel_id=1, source_target_pairs={{2,0},{4,2},{6,4},{10,8},{12,10},{14,12},{18,16},{20,18},{22,20},{... | collective-permute-start | bytes 3145736 | tf_op jit(solution)/shard_map/ppermute | solution.py:88
  21.9 17.3 %collective-permute-start.8 = (bf16[1024,512]{1,0:T(8,128)(2,1)S(1)}, bf16[1024,512]{1,0:T(8,128)(2,1)}, u32[]{:S(2)}, u32[]{:S(2)}) collective-permute-start(bf16[1024,512]{1,0:T(8,128)(2,1)S(1)} %collective-permute-done.2), channel_id=1, source_target_pairs={{2,0},{4,2},{10,8},{12,10},{18,16},{20,18},{26,24},{28,26}} | collective-permute-start | bytes 3145736 | tf_op jit(solution)/shard_map/ppermute | solution.py:88
  23.2 17.3 %collective-permute-start.13 = (bf16[1024,512]{1,0:T(8,128)(2,1)}, bf16[1024,512]{1,0:T(8,128)(2,1)}, u32[]{:S(2)}, u32[]{:S(2)}) collective-permute-start(bf16[1024,512]{1,0:T(8,128)(2,1)} %collective-permute-done.7), channel_id=1, source_target_pairs={{4,6},{12,14},{20,22},{28,30}} | collective-permute-start | bytes 3145736 | tf_op jit(solution)/shard_map/ppermute | solution.py:88
  39.2 17.0 %collective-permute-start.14 = (bf16[1024,512]{1,0:T(8,128)(2,1)}, bf16[1024,512]{1,0:T(8,128)(2,1)}, u32[]{:S(2)}, u32[]{:S(2)}) collective-permute-start(bf16[1024,512]{1,0:T(8,128)(2,1)} %collective-permute-done.8), channel_id=1, source_target_pairs={{2,0},{10,8},{18,16},{26,24}} | collective-permute-start | bytes 3145736 | tf_op jit(solution)/shard_map/ppermute | solution.py:88
  67.8 26.8 %collective-permute-start.25 = (bf16[1024,512]{1,0:T(8,128)(2,1)}, bf16[1024,512]{1,0:T(8,128)(2,1)}, u32[]{:S(2)}, u32[]{:S(2)}) collective-permute-start(bf16[1024,512]{1,0:T(8,128)(2,1)} %collective-permute-done.19), channel_id=1, source_target_pairs={{3,5},{5,7},{11,13},{13,15},{19,21},{21,23},{27,29},{29,31}} | collective-permute-start | bytes 3145736 | tf_op jit(solution)/shard_map/ppermute | solution.py:88
  69.5 26.9 %collective-permute-start.26 = (bf16[1024,512]{1,0:T(8,128)(2,1)}, bf16[1024,512]{1,0:T(8,128)(2,1)}, u32[]{:S(2)}, u32[]{:S(2)}) collective-permute-start(bf16[1024,512]{1,0:T(8,128)(2,1)} %collective-permute-done.20), channel_id=1, source_target_pairs={{3,1},{5,3},{11,9},{13,11},{19,17},{21,19},{27,25},{29,27}} | collective-permute-start | bytes 3145736 | tf_op jit(solution)/shard_map/ppermute | solution.py:88
  72.4 43.9 %all-to-all-start = ((bf16[8,2,64,512]{3,2,1,0:T(8,128)(2,1)}), bf16[8,2,64,512]{3,2,1,0:T(8,128)(2,1)S(1)}, u32[]{:S(2)}, u32[]{:S(2)}) async-start(bf16[8,2,64,512]{3,2,1,0:T(8,128)(2,1)} %shard_map.37), calls=%async_computation | async-start | bytes 2097152 | tf_op jit(solution)/shard_map/all_to_all | solution.py:109
  88.9 29.9 %collective-permute-start = (bf16[1024,512]{1,0:T(8,128)(2,1)S(1)}, bf16[1024,512]{1,0:T(8,128)(2,1)S(1)}, u32[]{:S(2)}, u32[]{:S(2)}) collective-permute-start(bf16[1024,512]{1,0:T(8,128)(2,1)S(1)} %bitcast.14), channel_id=1, source_target_pairs={{0,1},{1,0},{2,3},{3,2},{4,5},{5,4},{6,7},{7,6},{8,9},{9,8},{10,11... | collective-permute-start | bytes 3145736 | tf_op jit(solution)/shard_map/ppermute | solution.py:100
  89.4 36.2 %collective-permute-start.9 = (bf16[1024,512]{1,0:T(8,128)(2,1)}, bf16[1024,512]{1,0:T(8,128)(2,1)}, u32[]{:S(2)}, u32[]{:S(2)}) collective-permute-start(bf16[1024,512]{1,0:T(8,128)(2,1)} %get-tuple-element.66.refs_0_), channel_id=1, source_target_pairs={{0,1},{2,3},{4,5},{6,7},{8,9},{10,11},{12,13},{14,15},{16,17},{18,... | collective-permute-start | bytes 3145736 | tf_op jit(solution)/shard_map/ppermute | solution.py:85
  92.4 36.8 %collective-permute-start.15 = (bf16[1024,512]{1,0:T(8,128)(2,1)}, bf16[1024,512]{1,0:T(8,128)(2,1)}, u32[]{:S(2)}, u32[]{:S(2)}) collective-permute-start(bf16[1024,512]{1,0:T(8,128)(2,1)} %get-tuple-element.65.refs_0_), channel_id=1, source_target_pairs={{0,1},{2,3},{4,5},{6,7},{8,9},{10,11},{12,13},{14,15},{16,17},{18,... | collective-permute-start | bytes 3145736 | tf_op jit(solution)/shard_map/ppermute | solution.py:85
  94.7 38.3 %collective-permute-start.31 = (bf16[1024,512]{1,0:T(8,128)(2,1)}, bf16[1024,512]{1,0:T(8,128)(2,1)}, u32[]{:S(2)}, u32[]{:S(2)}) collective-permute-start(bf16[1024,512]{1,0:T(8,128)(2,1)} %collective-permute-done.25), channel_id=1, source_target_pairs={{5,7},{13,15},{21,23},{29,31}} | collective-permute-start | bytes 3145736 | tf_op jit(solution)/shard_map/ppermute | solution.py:88
  96.3 38.1 %collective-permute-start.32 = (bf16[1024,512]{1,0:T(8,128)(2,1)}, bf16[1024,512]{1,0:T(8,128)(2,1)}, u32[]{:S(2)}, u32[]{:S(2)}) collective-permute-start(bf16[1024,512]{1,0:T(8,128)(2,1)} %collective-permute-done.26), channel_id=1, source_target_pairs={{3,1},{11,9},{19,17},{27,25}} | collective-permute-start | bytes 3145736 | tf_op jit(solution)/shard_map/ppermute | solution.py:88
  124.2 26.6 %collective-permute-start.4 = (bf16[2,128,512]{2,1,0:T(8,128)(2,1)S(1)}, bf16[2,128,512]{2,1,0:T(8,128)(2,1)S(1)}, u32[]{:S(2)}, u32[]{:S(2)}) collective-permute-start(bf16[2,128,512]{2,1,0:T(8,128)(2,1)S(1)} %get-tuple-element.35), channel_id=1, source_target_pairs={{0,8},{8,0},{16,24},{24,16},{1,9},{9,1},{17,25},{25,17},{2,10},{10... | collective-permute-start | bytes 786440 | tf_op jit(solution)/shard_map/ppermute | solution.py:124
  141.2 38.5 %collective-permute-start.27 = (bf16[1024,512]{1,0:T(8,128)(2,1)}, bf16[1024,512]{1,0:T(8,128)(2,1)}, u32[]{:S(2)}, u32[]{:S(2)}) collective-permute-start(bf16[1024,512]{1,0:T(8,128)(2,1)} %get-tuple-element.64.refs_0_), channel_id=1, source_target_pairs={{1,0},{3,2},{5,4},{7,6},{9,8},{11,10},{13,12},{15,14},{17,16},{19,... | collective-permute-start | bytes 3145736 | tf_op jit(solution)/shard_map/ppermute | solution.py:85
  145.3 39.9 %collective-permute-start.21 = (bf16[1024,512]{1,0:T(8,128)(2,1)}, bf16[1024,512]{1,0:T(8,128)(2,1)}, u32[]{:S(2)}, u32[]{:S(2)}) collective-permute-start(bf16[1024,512]{1,0:T(8,128)(2,1)} %get-tuple-element.68.refs_2_), channel_id=1, source_target_pairs={{1,0},{3,2},{5,4},{7,6},{9,8},{11,10},{13,12},{15,14},{17,16},{19,... | collective-permute-start | bytes 3145736 | tf_op jit(solution)/shard_map/ppermute | solution.py:85
  147.2 42.9 %collective-permute-start.33 = (bf16[1024,512]{1,0:T(8,128)(2,1)}, bf16[1024,512]{1,0:T(8,128)(2,1)}, u32[]{:S(2)}, u32[]{:S(2)}) collective-permute-start(bf16[1024,512]{1,0:T(8,128)(2,1)} %get-tuple-element.63.refs_0_), channel_id=1, source_target_pairs={{1,0},{3,2},{5,4},{7,6},{9,8},{11,10},{13,12},{15,14},{17,16},{19,... | collective-permute-start | bytes 3145736 | tf_op jit(solution)/shard_map/ppermute | solution.py:85
  149.7 13.0 %collective-permute-start.5 = (bf16[2,128,512]{2,1,0:T(8,128)(2,1)}, bf16[2,128,512]{2,1,0:T(8,128)(2,1)}, u32[]{:S(2)}, u32[]{:S(2)}) collective-permute-start(bf16[2,128,512]{2,1,0:T(8,128)(2,1)} %get-tuple-element.36), channel_id=1, source_target_pairs={{0,16},{8,24},{16,0},{24,8},{1,17},{9,25},{17,1},{25,9},{2,18},{10... | collective-permute-start | bytes 786440 | tf_op jit(solution)/shard_map/ppermute | solution.py:124
  173.2 42.2 %all-to-all-start.1 = ((bf16[32,64,128]{2,1,0:T(8,128)(2,1)}), bf16[32,64,128]{2,1,0:T(8,128)(2,1)}, u32[]{:S(2)}, u32[]{:S(2)}) async-start(bf16[32,64,128]{2,1,0:T(8,128)(2,1)} %bitcast.17), calls=%async_computation.1 | async-start | bytes 1048576 | tf_op jit(solution)/shard_map/all_to_all | solution.py:175
  188.0 26.5 %collective-permute-start.22 = (bf16[2,128,512]{2,1,0:T(8,128)(2,1)S(1)}, bf16[2,128,512]{2,1,0:T(8,128)(2,1)S(1)}, u32[]{:S(2)}, u32[]{:S(2)}) collective-permute-start(bf16[2,128,512]{2,1,0:T(8,128)(2,1)S(1)} %get-tuple-element.49), channel_id=1, source_target_pairs={{0,8},{8,0},{16,24},{24,16},{1,9},{9,1},{17,25},{25,17},{2,10},{10... | collective-permute-start | bytes 786440 | tf_op jit(solution)/shard_map/ppermute | solution.py:124
  188.6 12.9 %collective-permute-start.30 = (bf16[1,128,512]{2,1,0:T(8,128)(2,1)S(1)}, bf16[1,128,512]{2,1,0:T(8,128)(2,1)S(1)}, u32[]{:S(2)}, u32[]{:S(2)}) collective-permute-start(bf16[1,128,512]{2,1,0:T(8,128)(2,1)S(1)} %get-tuple-element.55), channel_id=1, source_target_pairs={{0,24},{8,16},{16,8},{24,0},{1,25},{9,17},{17,9},{25,1},{2,26},{10... | collective-permute-start | bytes 393224 | tf_op jit(solution)/shard_map/ppermute | solution.py:124
  192.8 21.8 %collective-permute-start.23 = (bf16[2,128,512]{2,1,0:T(8,128)(2,1)S(1)}, bf16[2,128,512]{2,1,0:T(8,128)(2,1)S(1)}, u32[]{:S(2)}, u32[]{:S(2)}) collective-permute-start(bf16[2,128,512]{2,1,0:T(8,128)(2,1)S(1)} %get-tuple-element.50), channel_id=1, source_target_pairs={{0,16},{8,24},{16,0},{24,8},{1,17},{9,25},{17,1},{25,9},{2,18},{10... | collective-permute-start | bytes 786440 | tf_op jit(solution)/shard_map/ppermute | solution.py:124
  194.5 20.1 %collective-permute-start.24 = (bf16[2,128,512]{2,1,0:T(8,128)(2,1)S(1)}, bf16[2,128,512]{2,1,0:T(8,128)(2,1)S(1)}, u32[]{:S(2)}, u32[]{:S(2)}) collective-permute-start(bf16[2,128,512]{2,1,0:T(8,128)(2,1)S(1)} %get-tuple-element.51), channel_id=1, source_target_pairs={{0,24},{8,16},{16,8},{24,0},{1,25},{9,17},{17,9},{25,1},{2,26},{10... | collective-permute-start | bytes 786440 | tf_op jit(solution)/shard_map/ppermute | solution.py:124
  201.6 13.0 %collective-permute-start.35 = (bf16[1,128,512]{2,1,0:T(8,128)(2,1)S(1)}, bf16[1,128,512]{2,1,0:T(8,128)(2,1)S(1)}, u32[]{:S(2)}, u32[]{:S(2)}) collective-permute-start(bf16[1,128,512]{2,1,0:T(8,128)(2,1)S(1)} %get-tuple-element.58), channel_id=1, source_target_pairs={{0,16},{8,24},{16,0},{24,8},{1,17},{9,25},{17,1},{25,9},{2,18},{10... | collective-permute-start | bytes 393224 | tf_op jit(solution)/shard_map/ppermute | solution.py:124
  (41 other events, 245.2 us)

commit v4 on v0

v4 whole, which is shorter than its diff:
```python
import functools

import jax
import jax.numpy as jnp
from jax import lax
from jax.experimental import pallas as pl
from jax.experimental.pallas import tpu as pltpu
from jax.sharding import PartitionSpec as P

F32, BF16 = jnp.float32, jnp.bfloat16
VMEM = pl.BlockSpec(memory_space=pltpu.VMEM)
SMEM = pl.BlockSpec(memory_space=pltpu.SMEM)
PARAMS = pltpu.CompilerParams(vmem_limit_bytes=16 * 1024 * 1024)


def spread_kernel(ncol, a_ref, out_ref):
    kk, occ, _, v = a_ref.shape
    vs = v // ncol
    for k in range(kk):
        tiles = [a_ref[k, i] for i in range(occ)]
        for s in range(ncol):
            piece = [tile[:, s * vs : (s + 1) * vs] for tile in tiles]
            out_ref[s, k] = jnp.concatenate(piece, axis=1)


def product_kernel(count, core_ref, panel_ref, *refs):
    blocks, out_ref = refs[:-1], refs[-1]
    nrow, _, rows, _ = out_ref.shape
    core = core_ref[0]
    for m in range(count):
        for c in range(2):
            n = 2 * m + (core ^ c)
            block = blocks[2 * m + c]
            prod = jnp.dot(panel_ref[...], block[...], preferred_element_type=F32).astype(BF16)
            for r in range(nrow):
                out_ref[r, n] = prod[r * rows : (r + 1) * rows]


def turn_kernel(groups, ncol, slot_ref, *refs):
    first_ref, turned_ref = refs[-2:]
    vs = turned_ref.shape[2]
    at = 0
    for ref in refs[:groups]:
        for m in range(ref.shape[0] // 2):
            slot = slot_ref[at]
            at += 1
            for p in range(2):
                total = ref[2 * m + p]
                first_ref[2 * slot + p] = total
                turned = total.astype(F32).T.astype(BF16)
                for s in range(ncol):
                    turned_ref[slot * ncol + s, p] = turned[s * vs : (s + 1) * vs]


def final_kernel(nrow, ncol, first_ref, second_ref, out_ref):
    ai, _, vs, _ = out_ref.shape
    for i in range(ai):
        for r in range(nrow):
            tiles = [second_ref[r * ncol + s, i].astype(F32) for s in range(ncol)]
            for q in range(ai):
                second = jnp.concatenate([x[:, q * vs : (q + 1) * vs] for x in tiles], axis=1)
                first = first_ref[r * ai + q, i * vs : (i + 1) * vs, :].astype(F32)
                out_ref[i, r * ai + q] = (first + second).astype(BF16)


def solution(mesh):
    nrow, ncol = mesh.shape["row"], mesh.shape["col"]
    nz = ncol // 2

    def across(x):
        return lax.ppermute(x, "col", [(s, s ^ 1) for s in range(ncol)])

    def along(x, pairs):
        return lax.ppermute(x, "col", [(2 * a + c, 2 * b + c) for a, b in pairs for c in range(2)])

    def after(x, *earlier):
        return lax.optimization_barrier((x, *earlier))[0]

    def local(amplitudes, intermediate):
        kk, occ, cs, v = amplitudes.shape
        ai = occ // nrow
        vs = v // ncol
        rows = ai * vs
        col = lax.axis_index("col")
        z, core = col // 2, (col % 2).reshape(1)
        end = (z == 0) | (z == nz - 1)

        w = intermediate.reshape(kk * v, v)
        line = nz == 4
        if line:
            swap = [(1, 2), (2, 1)]
            outward = [(1, 0), (2, 3)]
            x1 = along(w, [(a, a ^ 1) for a in range(nz)])
            y2 = along(w, swap)
        own = (w, across(w))

        blocks = pl.pallas_call(
            functools.partial(spread_kernel, ncol),
            out_shape=jax.ShapeDtypeStruct((ncol, kk, cs, occ * vs), BF16),
            in_specs=[VMEM],
            out_specs=VMEM,
            compiler_params=PARAMS,
        )(amplitudes)
        panel = lax.all_to_all(blocks, "col", 0, 0, tiled=True)
        panel = jnp.transpose(panel, (3, 1, 0, 2)).reshape(nrow * rows, kk * v)

        def product(pairs):
            n = 2 * len(pairs)
            return pl.pallas_call(
                functools.partial(product_kernel, len(pairs)),
                out_shape=jax.ShapeDtypeStruct((nrow, n, rows, v), BF16),
                in_specs=[SMEM] + [VMEM] * (1 + n),
                out_specs=VMEM,
                compiler_params=PARAMS,
            )(core, panel, *[x for pair in pairs for x in pair])

        def summed(part):
            n = part.shape[1]
            flat = part.reshape(nrow * n * rows, v)
            flat = lax.psum_scatter(flat, "row", scatter_dimension=0, tiled=True)
            return flat.reshape(n, rows, v)

        if line:
            y3 = along(after(x1, blocks), swap)
            e2 = along(after(y2, blocks), outward)
            part = product([own, (x1, across(x1))])
            e3 = along(after(y3, part), outward)
            groups = [summed(part)]
            for inner, outer in ((y2, e2), (y3, e3)):
                x = jnp.where(end, outer, inner)
                groups.append(summed(product([(after(x, groups[-1]), across(x))])))
            slots = [z, z ^ 1, jnp.where(end, z ^ 2, 3 - z), jnp.where(end, 3 - z, z ^ 2)]
        else:
            groups = [summed(product([own]))]
            for m in range(1, nz):
                x = along(w, [(a, a ^ m) for a in range(nz)])
                groups.append(summed(product([(after(x, groups[-1]), across(x))])))
            slots = [z ^ m for m in range(nz)]

        first, turned = pl.pallas_call(
            functools.partial(turn_kernel, len(groups), ncol),
            out_shape=[
                jax.ShapeDtypeStruct((occ, rows, v), BF16),
                jax.ShapeDtypeStruct((nrow * ncol, ai, vs, rows), BF16),
            ],
            in_specs=[SMEM] + [VMEM] * len(groups),
            out_specs=[VMEM] * 2,
            compiler_params=PARAMS,
        )(jnp.stack(slots).astype(jnp.int32), *groups)
        second = lax.all_to_all(turned, ("row", "col"), 0, 0, tiled=True)

        return pl.pallas_call(
            functools.partial(final_kernel, nrow, ncol),
            out_shape=jax.ShapeDtypeStruct((ai, occ, vs, v), BF16),
            in_specs=[VMEM] * 2,
            out_specs=VMEM,
            compiler_params=PARAMS,
        )(first, second)

    placed = P("row", None, "col", None)
    return jax.shard_map(
        local, mesh=mesh, in_specs=(placed, placed), out_specs=placed, check_vma=False
    )
```

time: 278 us -> 218 us (0.78)
  blocking collectives: 133 us -> 32 us
  waiting for transfers between devices: 87.6 us -> 138 us
  local copies, waits for them, and re-layouts: 32.5 us -> 5.77 us
  Pallas kernels: 0 us -> 13.3 us
  starting transfers between devices: 0.04 us -> 12.7 us
  matrix products: 9.16 us -> 0 us
    all_to_all x5 -> x1, blocking collectives: 133 us -> 32 us  [local(): second = lax.all_to_all(turned, ('row', 'col'), 0, 0, tiled=True)]
    ppermute x0 -> x9, waiting for transfers between devices: none -> 95 us  [the longest x5 93.6 us: along(): lax.ppermute(x, 'col', [(2 * a + c, 2 * b + c) for a, b in pairs for c in...]
    all_gather x2 -> x0, waiting for transfers between devices: 86.8 us -> none  [the longest x1 83.7 us: local(): cycle = contract(lax.all_gather(panel, 'col', axis=0, tiled=True), weights)]
    reduce_scatter x0 -> x3, waiting for transfers between devices: none -> 32.6 us  [summed(): flat = lax.psum_scatter(flat, 'row', scatter_dimension=0, tiled=True)]
    convert_element_type x4 -> x0, local copies, waits for them, and re-layouts: 13.9 us -> none  [the longest x3 12.9 us: local(): second.astype(jnp.float32)]
    pallas_call x0 -> x6, Pallas kernels: none -> 13.3 us  [the longest x3 9.66 us: product(): pl.pallas_call(functools.partial(product_kernel, len(pairs)), out_shape=j...]
    all_to_all x7 -> x0, local copies, waits for them, and re-layouts: 11.5 us -> none  [the longest x2 5.81 us: local(): lax.all_to_all(first, 'row', split_axis=1, concat_axis=0, tiled=True)]
    all_to_all x0 -> x1, waiting for transfers between devices: none -> 10 us  [local(): panel = lax.all_to_all(blocks, 'col', 0, 0, tiled=True)]
  transfers between devices with their start and end apart: 2 -> 13, of which waited for: 2 -> 7; matrix products, arithmetic and copies ran while one was open for 1% -> 2% of each run, Pallas kernels for 0% -> 2%
where the time goes in v4:
time: 218 us; the launch traced here: 217 us
  waiting for transfers between devices  138 us (63%)
  blocking collectives  32 us (15%)
  Pallas kernels  13.3 us (6%)
  between operations  13.3 us (6%)
  starting transfers between devices  12.7 us (6%)
  local copies, waits for them, and re-layouts  5.77 us (3%)
  other arithmetic  2.75 us (1%)
    ppermute x5, waiting for transfers between devices, along(): lax.ppermute(x, 'col', [(2 * a + c, 2 * b + c) for a, b in pairs for c in...  93.6 us
    reduce_scatter x3, waiting for transfers between devices, summed(): flat = lax.psum_scatter(flat, 'row', scatter_dimension=0, tiled=True)  32.6 us
    all_to_all x1, blocking collectives, local(): second = lax.all_to_all(turned, ('row', 'col'), 0, 0, tiled=True)  32 us
    all_to_all x1, waiting for transfers between devices, local(): panel = lax.all_to_all(blocks, 'col', 0, 0, tiled=True)  10 us
    pallas_call x3, Pallas kernels, product(): pl.pallas_call(functools.partial(product_kernel, len(pairs)), out_shape=j...  9.66 us
    ppermute x5, starting transfers between devices, along(): lax.ppermute(x, 'col', [(2 * a + c, 2 * b + c) for a, b in pairs for c in...  8.02 us
  transfers between devices with their start and end apart: 13, of which 7 were waited for; matrix products, arithmetic and copies ran while one was open for 2% of the time, Pallas kernels for 2%

profile of v4, /device:TPU:0, one launch (start us, length us, event | category | flops | bytes accessed | tf_op | source)
XLA Modules:
  0.0 217.4 jit_solution(7811297098794289115)
XLA Ops:
  6.5 3.0 %collective-permute-start.1 = (bf16[1024,512]{1,0:T(8,128)(2,1)}, bf16[1024,512]{1,0:T(8,128)(2,1)}, u32[]{:S(2)}, u32[]{:S(2)}) collective-permute-start(bf16[1024,512]{1,0:T(8,128)(2,1)} %bitcast.14), channel_id=1, source_target_pairs={{0,2},{1,3},{2,0},{3,1},{4,6},{5,7},{6,4},{7,5},{8,10},{9,11},{10,... | collective-permute-start | bytes 3145736 | tf_op jit(solution)/shard_map/ppermute | solution.py:74
  9.6 1.2 copy-done
  10.8 1.3 shard_map.28
  12.1 3.9 %all-to-all-start = ((bf16[8,2,64,512]{3,2,1,0:T(8,128)(2,1)}), bf16[8,2,64,512]{3,2,1,0:T(8,128)(2,1)S(1)}, u32[]{:S(2)}, u32[]{:S(2)}) async-start(bf16[8,2,64,512]{3,2,1,0:T(8,128)(2,1)} %shard_map.28), calls=%async_computation | async-start | bytes 2097152 | tf_op jit(solution)/shard_map/all_to_all | solution.py:104
  16.5 23.2 %collective-permute-done.1.refs_2_ = bf16[1024,512]{1,0:T(8,128)(2,1)} collective-permute-done((bf16[1024,512]{1,0:T(8,128)(2,1)}, bf16[1024,512]{1,0:T(8,128)(2,1)}, u32[]{:S(2)}, u32[]{:S(2)}) %collective-permute-start.1) | collective-permute-done | bytes 1048608 | tf_op jit(solution)/shard_map/ppermute | solution.py:74
  39.7 10.0 %all-to-all-done = bf16[8,2,64,512]{3,2,1,0:T(8,128)(2,1)S(1)} async-done(((bf16[8,2,64,512]{3,2,1,0:T(8,128)(2,1)}), bf16[8,2,64,512]{3,2,1,0:T(8,128)(2,1)S(1)}, u32[]{:S(2)}, u32[]{:S(2)}) %all-to-all-start) | async-done | bytes 1048608 | tf_op jit(solution)/shard_map/all_to_all | solution.py:104
  49.8 1.1 copy.4
  50.8 1.5 copy.5.panel_ref
  52.4 5.2 %shard_map.29 = bf16[4,4,128,512]{3,2,1,0:T(8,128)(2,1)} custom-call(s32[1]{0:T(128)} %bitcast.4.core_ref, bf16[512,1024]{1,0:T(8,128)(2,1)S(1)} %copy.5.panel_ref, bf16[1024,512]{1,0:T(8,128)(2,1)S(1)} %bitcast.16, bf16[1024,512]{1,0:T(8,128)(2,1)S(1)} %collective-permute-done.refs_1_, bf16[1024,512]{1,0:T(8,128)(2,1)} %collective-permute-done.1.refs_2_, ...), custom_call_target="tpu_custom_call" | custom-call | tf_op jit(solution)/shard_map/pallas_call | solution.py:109
  58.4 1.3 collective-permute-start.4
  59.7 1.7 collective-permute-start.6
  61.4 47.6 %collective-permute-done.4 = bf16[1024,512]{1,0:T(8,128)(2,1)} collective-permute-done((bf16[1024,512]{1,0:T(8,128)(2,1)S(1)}, bf16[1024,512]{1,0:T(8,128)(2,1)}, u32[]{:S(2)}, u32[]{:S(2)}) %collective-permute-start.4) | collective-permute-done | bytes 1048608 | tf_op jit(solution)/shard_map/ppermute | solution.py:74
  109.0 1.3 broadcast_select_fusion.1.refs_0_
  110.4 1.3 collective-permute-start.7
  111.8 1.3 collective-permute-done.5.refs_1_
  113.1 2.2 %shard_map.30 = bf16[4,2,128,512]{3,2,1,0:T(8,128)(2,1)} custom-call(s32[1]{0:T(128)} %bitcast.4.core_ref, bf16[512,1024]{1,0:T(8,128)(2,1)S(1)} %copy.5.panel_ref, bf16[1024,512]{1,0:T(8,128)(2,1)S(1)} %broadcast_select_fusion.1.refs_0_, bf16[1024,512]{1,0:T(8,128)(2,1)S(1)} %collective-permute-done.5.refs_1_), custom_call_target="tpu_custom_call" | custom-call | tf_op jit(solution)/shard_map/pallas_call | solution.py:109
  115.4 22.8 %collective-permute-done.7 = bf16[1024,512]{1,0:T(8,128)(2,1)} collective-permute-done((bf16[1024,512]{1,0:T(8,128)(2,1)}, bf16[1024,512]{1,0:T(8,128)(2,1)}, u32[]{:S(2)}, u32[]{:S(2)}) %collective-permute-start.7) | collective-permute-done | bytes 1048608 | tf_op jit(solution)/shard_map/ppermute | solution.py:74
  138.2 1.3 broadcast_select_fusion.refs_0_
  139.6 4.3 %reduce-scatter.6.cloned.1.call-done = bf16[256,512]{1,0:T(8,128)(2,1)} async-done(((bf16[1024,512]{1,0:T(8,128)(2,1)}), bf16[256,512]{1,0:T(8,128)(2,1)}) %reduce-scatter.6.cloned.1.call-update) | async-done | bytes 262160 | tf_op jit(solution)/shard_map/reduce_scatter | solution.py:120
  143.9 2.2 %shard_map.31 = bf16[4,2,128,512]{3,2,1,0:T(8,128)(2,1)} custom-call(s32[1]{0:T(128)} %bitcast.4.core_ref, bf16[512,1024]{1,0:T(8,128)(2,1)S(1)} %copy.5.panel_ref, bf16[1024,512]{1,0:T(8,128)(2,1)S(1)} %broadcast_select_fusion.refs_0_, bf16[1024,512]{1,0:T(8,128)(2,1)S(1)} %collective-permute-done.8.refs_1_), custom_call_target="tpu_custom_call" | custom-call | tf_op jit(solution)/shard_map/pallas_call | solution.py:109
  146.2 28.3 %reduce-scatter.8.cloned.1.call-done = bf16[256,512]{1,0:T(8,128)(2,1)} async-done(((bf16[1024,512]{1,0:T(8,128)(2,1)}), bf16[256,512]{1,0:T(8,128)(2,1)}) %reduce-scatter.8.cloned.1.call-update) | async-done | bytes 262160 | tf_op jit(solution)/shard_map/reduce_scatter | solution.py:120
  174.5 1.0 copy-done.2
  177.4 32.0 %all_to_all.10.second_ref = bf16[32,2,64,128]{3,2,1,0:T(8,128)(2,1)S(1)} all-to-all(bf16[32,2,64,128]{3,2,1,0:T(8,128)(2,1)S(1)} %get-tuple-element.18), channel_id=1, replica_groups=mesh['row'=4,'col'=8] {'row','col'}, dimensions={0} | all-to-all | bytes 2097152 | tf_op jit(solution)/shard_map/all_to_all | solution.py:150
  209.4 1.5 shard_map.33
  (27 shorter events, 3.5 us)
Async XLA Ops:
  6.5 33.2 %collective-permute-start.1 = (bf16[1024,512]{1,0:T(8,128)(2,1)}, bf16[1024,512]{1,0:T(8,128)(2,1)}, u32[]{:S(2)}, u32[]{:S(2)}) collective-permute-start(bf16[1024,512]{1,0:T(8,128)(2,1)} %bitcast.14), channel_id=1, source_target_pairs={{0,2},{1,3},{2,0},{3,1},{4,6},{5,7},{6,4},{7,5},{8,10},{9,11},{10,... | collective-permute-start | bytes 3145736 | tf_op jit(solution)/shard_map/ppermute | solution.py:74
  9.6 1.2 copy-start
  10.8 5.2 %copy-start.1 = (bf16[2,512,1,512]{3,1,2,0:T(8,128)(2,1)S(1)}, bf16[2,512,1,512]{3,1,2,0:T(8,128)(2,1)}, u32[]{:S(2)}) copy-start(bf16[2,512,1,512]{3,1,2,0:T(8,128)(2,1)} %param.3) | copy-start | bytes 3145732
  12.1 37.7 %all-to-all-start = ((bf16[8,2,64,512]{3,2,1,0:T(8,128)(2,1)}), bf16[8,2,64,512]{3,2,1,0:T(8,128)(2,1)S(1)}, u32[]{:S(2)}, u32[]{:S(2)}) async-start(bf16[8,2,64,512]{3,2,1,0:T(8,128)(2,1)} %shard_map.28), calls=%async_computation | async-start | bytes 2097152 | tf_op jit(solution)/shard_map/all_to_all | solution.py:104
  16.0 95.8 %reduce-scatter.4.cloned.1.call-start = ((), (), s32[]{:S(2)}) async-start(), calls=%async_computation.5 | async-start | bytes 2621440 | tf_op jit(solution)/shard_map/reduce_scatter | solution.py:120
  16.0 36.3 %collective-permute-start = (bf16[1024,512]{1,0:T(8,128)(2,1)S(1)}, bf16[1024,512]{1,0:T(8,128)(2,1)S(1)}, u32[]{:S(2)}, u32[]{:S(2)}) collective-permute-start(bf16[1024,512]{1,0:T(8,128)(2,1)S(1)} %bitcast.15), channel_id=1, source_target_pairs={{0,1},{1,0},{2,3},{3,2},{4,5},{5,4},{6,7},{7,6},{8,9},{9,8},{10,11... | collective-permute-start | bytes 3145736 | tf_op jit(solution)/shard_map/ppermute | solution.py:71
  39.7 12.6 %collective-permute-start.2 = (bf16[1024,512]{1,0:T(8,128)(2,1)}, bf16[1024,512]{1,0:T(8,128)(2,1)}, u32[]{:S(2)}, u32[]{:S(2)}) collective-permute-start(bf16[1024,512]{1,0:T(8,128)(2,1)} %collective-permute-done.1.refs_2_), channel_id=1, source_target_pairs={{0,1},{1,0},{2,3},{3,2},{4,5},{5,4},{6,7},{7,6},{8,9},{9,8},{10,11... | collective-permute-start | bytes 3145736 | tf_op jit(solution)/shard_map/ppermute | solution.py:71
  57.6 86.3 %reduce-scatter.6.cloned.1.call-start = ((), (), s32[]{:S(2)}) async-start(), calls=%async_computation.6 | async-start | bytes 1310720 | tf_op jit(solution)/shard_map/reduce_scatter | solution.py:120
  57.7 0.7 collective-permute-start.3
  58.4 50.6 %collective-permute-start.4 = (bf16[1024,512]{1,0:T(8,128)(2,1)S(1)}, bf16[1024,512]{1,0:T(8,128)(2,1)}, u32[]{:S(2)}, u32[]{:S(2)}) collective-permute-start(bf16[1024,512]{1,0:T(8,128)(2,1)S(1)} %collective-permute-done.3), channel_id=1, source_target_pairs={{2,0},{3,1},{4,6},{5,7},{10,8},{11,9},{12,14},{13,15},{18,16},{19,... | collective-permute-start | bytes 3145736 | tf_op jit(solution)/shard_map/ppermute | solution.py:74
  59.7 50.7 %collective-permute-start.6 = (bf16[1024,512]{1,0:T(8,128)(2,1)}, bf16[1024,512]{1,0:T(8,128)(2,1)}, u32[]{:S(2)}, u32[]{:S(2)}) collective-permute-start(bf16[1024,512]{1,0:T(8,128)(2,1)} %collective-permute-done.1.refs_2_), channel_id=1, source_target_pairs={{2,4},{3,5},{4,2},{5,3},{10,12},{11,13},{12,10},{13,11},{18,20},{1... | collective-permute-start | bytes 3145736 | tf_op jit(solution)/shard_map/ppermute | solution.py:74
  110.4 2.7 %collective-permute-start.5 = (bf16[1024,512]{1,0:T(8,128)(2,1)S(1)}, bf16[1024,512]{1,0:T(8,128)(2,1)S(1)}, u32[]{:S(2)}, u32[]{:S(2)}) collective-permute-start(bf16[1024,512]{1,0:T(8,128)(2,1)S(1)} %broadcast_select_fusion.1.refs_0_), channel_id=1, source_target_pairs={{0,1},{1,0},{2,3},{3,2},{4,5},{5,4},{6,7},{7,6},{8,9},{9,8},{10,11... | collective-permute-start | bytes 3145736 | tf_op jit(solution)/shard_map/ppermute | solution.py:71
  110.4 27.8 %collective-permute-start.7 = (bf16[1024,512]{1,0:T(8,128)(2,1)}, bf16[1024,512]{1,0:T(8,128)(2,1)}, u32[]{:S(2)}, u32[]{:S(2)}) collective-permute-start(bf16[1024,512]{1,0:T(8,128)(2,1)} %collective-permute-done.6), channel_id=1, source_target_pairs={{2,0},{3,1},{4,6},{5,7},{10,8},{11,9},{12,14},{13,15},{18,16},{19,... | collective-permute-start | bytes 3145736 | tf_op jit(solution)/shard_map/ppermute | solution.py:74
  115.3 59.2 %reduce-scatter.8.cloned.1.call-start = ((), (), s32[]{:S(2)}) async-start(), calls=%async_computation.7 | async-start | bytes 1310720 | tf_op jit(solution)/shard_map/reduce_scatter | solution.py:120
  139.5 4.3 %collective-permute-start.8 = (bf16[1024,512]{1,0:T(8,128)(2,1)S(1)}, bf16[1024,512]{1,0:T(8,128)(2,1)S(1)}, u32[]{:S(2)}, u32[]{:S(2)}) collective-permute-start(bf16[1024,512]{1,0:T(8,128)(2,1)S(1)} %broadcast_select_fusion.refs_0_), channel_id=1, source_target_pairs={{0,1},{1,0},{2,3},{3,2},{4,5},{5,4},{6,7},{7,6},{8,9},{9,8},{10,11... | collective-permute-start | bytes 3145736 | tf_op jit(solution)/shard_map/ppermute | solution.py:71
  143.9 30.7 %copy-start.3 = (bf16[256,512]{1,0:T(8,128)(2,1)S(1)}, bf16[256,512]{1,0:T(8,128)(2,1)}, u32[]{:S(2)}) copy-start(bf16[256,512]{1,0:T(8,128)(2,1)} %reduce-scatter.6.cloned.1.call-done) | copy-start | bytes 786436
  174.5 1.0 copy-start.2
  175.6 0.9 copy-start.4
Sparse Core Ops, SparseCore 0:
  57.7 36.6 reduce-scatter.3
  115.4 28.3 reduce-scatter.5
  146.8 27.7 reduce-scatter.7

commit v5 on v4

--- a/solution.py
+++ b/solution.py
@@ -13,39 +13,43 @@
 PARAMS = pltpu.CompilerParams(vmem_limit_bytes=16 * 1024 * 1024)
 
 
-def spread_kernel(ncol, a_ref, out_ref):
+def spread_kernel(nrow, ncol, row_ref, a_ref, out_ref):
     kk, occ, _, v = a_ref.shape
-    vs = v // ncol
+    ai, vs = occ // nrow, v // ncol
     for k in range(kk):
-        tiles = [a_ref[k, i] for i in range(occ)]
+        tiles = [a_ref[k, (row_ref[0] ^ t) * ai + i] for t in range(nrow) for i in range(ai)]
         for s in range(ncol):
             piece = [tile[:, s * vs : (s + 1) * vs] for tile in tiles]
             out_ref[s, k] = jnp.concatenate(piece, axis=1)
 
 
 def product_kernel(count, core_ref, panel_ref, *refs):
-    blocks, out_ref = refs[:-1], refs[-1]
-    nrow, _, rows, _ = out_ref.shape
+    blocks, outs = refs[: 2 * count], refs[2 * count :]
+    rows = outs[0].shape[1]
     core = core_ref[0]
     for m in range(count):
         for c in range(2):
             n = 2 * m + (core ^ c)
-            block = blocks[2 * m + c]
-            prod = jnp.dot(panel_ref[...], block[...], preferred_element_type=F32).astype(BF16)
-            for r in range(nrow):
-                out_ref[r, n] = prod[r * rows : (r + 1) * rows]
+            prod = jnp.dot(panel_ref[...], blocks[2 * m + c][...], preferred_element_type=F32)
+            outs[0][n] = prod[:rows]
+            for t in range(1, len(outs)):
+                outs[t][n] = prod[t * rows : (t + 1) * rows].astype(BF16)
 
 
-def turn_kernel(groups, ncol, slot_ref, *refs):
+def turn_kernel(sizes, ncol, slot_ref, *refs):
     first_ref, turned_ref = refs[-2:]
     vs = turned_ref.shape[2]
     at = 0
-    for ref in refs[:groups]:
-        for m in range(ref.shape[0] // 2):
+    for size in sizes:
+        parts, refs = refs[:size], refs[size:]
+        for m in range(parts[0].shape[0] // 2):
             slot = slot_ref[at]
             at += 1
             for p in range(2):
-                total = ref[2 * m + p]
+                total = parts[0][2 * m + p]
+                for other in parts[1:]:
+                    total = total + other[2 * m + p].astype(F32)
+                total = total.astype(BF16)
                 first_ref[2 * slot + p] = total
                 turned = total.astype(F32).T.astype(BF16)
                 for s in range(ncol):
@@ -81,6 +85,7 @@
         ai = occ // nrow
         vs = v // ncol
         rows = ai * vs
+        row = lax.axis_index("row").reshape(1)
         col = lax.axis_index("col")
         z, core = col // 2, (col % 2).reshape(1)
         end = (z == 0) | (z == nz - 1)
@@ -95,58 +100,69 @@
         own = (w, across(w))
 
         blocks = pl.pallas_call(
-            functools.partial(spread_kernel, ncol),
+            functools.partial(spread_kernel, nrow, ncol),
             out_shape=jax.ShapeDtypeStruct((ncol, kk, cs, occ * vs), BF16),
-            in_specs=[VMEM],
+            in_specs=[SMEM, VMEM],
             out_specs=VMEM,
             compiler_params=PARAMS,
-        )(amplitudes)
+        )(row, amplitudes)
         panel = lax.all_to_all(blocks, "col", 0, 0, tiled=True)
         panel = jnp.transpose(panel, (3, 1, 0, 2)).reshape(nrow * rows, kk * v)
 
         def product(pairs):
             n = 2 * len(pairs)
+            sent = [jax.ShapeDtypeStruct((n, rows, v), BF16)] * (nrow - 1)
             return pl.pallas_call(
                 functools.partial(product_kernel, len(pairs)),
-                out_shape=jax.ShapeDtypeStruct((nrow, n, rows, v), BF16),
+                out_shape=[jax.ShapeDtypeStruct((n, rows, v), F32)] + sent,
                 in_specs=[SMEM] + [VMEM] * (1 + n),
-                out_specs=VMEM,
+                out_specs=[VMEM] * nrow,
                 compiler_params=PARAMS,
             )(core, panel, *[x for pair in pairs for x in pair])
 
-        def summed(part):
-            n = part.shape[1]
-            flat = part.reshape(nrow * n * rows, v)
-            flat = lax.psum_scatter(flat, "row", scatter_dimension=0, tiled=True)
-            return flat.reshape(n, rows, v)
+        def exchange(parts):
+            return [parts[0]] + [
+                lax.ppermute(parts[t], "row", [(r, r ^ t) for r in range(nrow)])
+                for t in range(1, nrow)
+            ]
+
+        def summed(group):
+            total = group[0]
+            for part in group[1:]:
+                total = total + part.astype(F32)
+            return total.astype(BF16)
 
         if line:
-            y3 = along(after(x1, blocks), swap)
-            e2 = along(after(y2, blocks), outward)
-            part = product([own, (x1, across(x1))])
-            e3 = along(after(y3, part), outward)
-            groups = [summed(part)]
+            x1, y2, blocks = lax.optimization_barrier((x1, y2, blocks))
+            y3, e2 = along(x1, swap), along(y2, outward)
+            parts = product([own, (x1, across(x1))])
+            groups = [exchange(parts)]
+            e3 = along(after(y3, *parts), outward)
             for inner, outer in ((y2, e2), (y3, e3)):
-                x = jnp.where(end, outer, inner)
-                groups.append(summed(product([(after(x, groups[-1]), across(x))])))
+                groups[-1] = [summed(groups[-1])]
+                x = jnp.where(end, after(outer, *parts), inner)
+                parts = product([(after(x, groups[-1][0]), across(x))])
+                groups.append(exchange(parts))
             slots = [z, z ^ 1, jnp.where(end, z ^ 2, 3 - z), jnp.where(end, 3 - z, z ^ 2)]
         else:
-            groups = [summed(product([own]))]
+            groups = [exchange(product([own]))]
             for m in range(1, nz):
+                groups[-1] = [summed(groups[-1])]
                 x = along(w, [(a, a ^ m) for a in range(nz)])
-                groups.append(summed(product([(after(x, groups[-1]), across(x))])))
+                groups.append(exchange(product([(after(x, groups[-1][0]), across(x))])))
             slots = [z ^ m for m in range(nz)]
 
+        sizes = [len(g) for g in groups]
         first, turned = pl.pallas_call(
-            functools.partial(turn_kernel, len(groups), ncol),
+            functools.partial(turn_kernel, sizes, ncol),
             out_shape=[
                 jax.ShapeDtypeStruct((occ, rows, v), BF16),
                 jax.ShapeDtypeStruct((nrow * ncol, ai, vs, rows), BF16),
             ],
-            in_specs=[SMEM] + [VMEM] * len(groups),
+            in_specs=[SMEM] + [VMEM] * sum(sizes),
             out_specs=[VMEM] * 2,
             compiler_params=PARAMS,
-        )(jnp.stack(slots).astype(jnp.int32), *groups)
+        )(jnp.stack(slots).astype(jnp.int32), *[x for g in groups for x in g])
         second = lax.all_to_all(turned, ("row", "col"), 0, 0, tiled=True)
 
         return pl.pallas_call(

time: 218 us -> 170 us (0.78)
  waiting for transfers between devices: 138 us -> 93.4 us
  between operations: 13.3 us -> 0.14 us
  starting transfers between devices: 12.7 us -> 25 us
  Pallas kernels: 13.3 us -> 10.1 us
  blocking collectives: 32 us -> 35 us
    ppermute x5, waiting for transfers between devices: 93.6 us -> 23 us  [along(): lax.ppermute(x, 'col', [(2 * a + c, 2 * b + c) for a, b in pairs for c in...]
    ppermute x0 -> x9, waiting for transfers between devices: none -> 46.2 us  [exchange(): lax.ppermute(parts[t], 'row', [(r, r ^ t) for r in range(nrow)])]
    reduce_scatter x3 -> x0, waiting for transfers between devices: 32.6 us -> none  [summed(): flat = lax.psum_scatter(flat, 'row', scatter_dimension=0, tiled=True)]
    all_to_all x1, waiting for transfers between devices: 10 us -> 24.1 us  [local(): panel = lax.all_to_all(blocks, 'col', 0, 0, tiled=True)]
    ppermute x0 -> x9, starting transfers between devices: none -> 10.7 us  [exchange(): lax.ppermute(parts[t], 'row', [(r, r ^ t) for r in range(nrow)])]
    pallas_call x5, Pallas kernels: 11.9 us -> 8.66 us  [the longest x3 6.4 us: product(): pl.pallas_call(functools.partial(product_kernel, len(pairs)), out_shape=[...]
    all_to_all x1, blocking collectives: 32 us -> 35 us  [local(): second = lax.all_to_all(turned, ('row', 'col'), 0, 0, tiled=True)]
  transfers between devices with their start and end apart: 13 -> 19, of which waited for: 7 -> 12; matrix products, arithmetic and copies ran while one was open for 2% -> 3% of each run, Pallas kernels for 2% -> 4%
where the time goes in v5:
time: 170 us; the launch traced here: 169 us
  waiting for transfers between devices  93.4 us (55%)
  blocking collectives  35 us (21%)
  starting transfers between devices  25 us (15%)
  Pallas kernels  10.1 us (6%)
  local copies, waits for them, and re-layouts  3.78 us (2%)
  other arithmetic  2.03 us (1%)
    ppermute x9, waiting for transfers between devices, exchange(): lax.ppermute(parts[t], 'row', [(r, r ^ t) for r in range(nrow)])  46.2 us
    all_to_all x1, blocking collectives, local(): second = lax.all_to_all(turned, ('row', 'col'), 0, 0, tiled=True)  35 us
    all_to_all x1, waiting for transfers between devices, local(): panel = lax.all_to_all(blocks, 'col', 0, 0, tiled=True)  24.1 us
    ppermute x5, waiting for transfers between devices, along(): lax.ppermute(x, 'col', [(2 * a + c, 2 * b + c) for a, b in pairs for c in...  23 us
    ppermute x9, starting transfers between devices, exchange(): lax.ppermute(parts[t], 'row', [(r, r ^ t) for r in range(nrow)])  10.7 us
    ppermute x5, starting transfers between devices, along(): lax.ppermute(x, 'col', [(2 * a + c, 2 * b + c) for a, b in pairs for c in...  8.92 us
    pallas_call x3, Pallas kernels, product(): pl.pallas_call(functools.partial(product_kernel, len(pairs)), out_shape=[...  6.4 us
    all_to_all x1, starting transfers between devices, local(): panel = lax.all_to_all(blocks, 'col', 0, 0, tiled=True)  4.81 us
  transfers between devices with their start and end apart: 19, of which 12 were waited for; matrix products, arithmetic and copies ran while one was open for 3% of the time, Pallas kernels for 4%

profile of v5, /device:TPU:0, one launch (start us, length us, event | category | flops | bytes accessed | tf_op | source)
XLA Modules:
  0.0 169.5 jit_solution(4338202347925358257)
XLA Ops:
  0.0 3.0 %collective-permute-start.1 = (bf16[1024,512]{1,0:T(8,128)(2,1)}, bf16[1024,512]{1,0:T(8,128)(2,1)S(1)}, u32[]{:S(2)}, u32[]{:S(2)}) collective-permute-start(bf16[1024,512]{1,0:T(8,128)(2,1)} %bitcast.9), channel_id=1, source_target_pairs={{0,2},{1,3},{2,0},{3,1},{4,6},{5,7},{6,4},{7,5},{8,10},{9,11},{10,... | collective-permute-start | bytes 3145736 | tf_op jit(solution)/shard_map/ppermute | solution.py:78
  3.0 1.7 collective-permute-start.2
  5.9 1.3 shard_map.28
  7.2 4.8 %all-to-all-start = ((bf16[8,2,64,512]{3,2,1,0:T(8,128)(2,1)}), bf16[8,2,64,512]{3,2,1,0:T(8,128)(2,1)S(1)}, u32[]{:S(2)}, u32[]{:S(2)}) async-start(bf16[8,2,64,512]{3,2,1,0:T(8,128)(2,1)} %shard_map.28), calls=%async_computation | async-start | bytes 2097152 | tf_op jit(solution)/shard_map/all_to_all | solution.py:109
  12.5 14.7 %collective-permute-done.1.refs_2_ = bf16[1024,512]{1,0:T(8,128)(2,1)S(1)} collective-permute-done((bf16[1024,512]{1,0:T(8,128)(2,1)}, bf16[1024,512]{1,0:T(8,128)(2,1)S(1)}, u32[]{:S(2)}, u32[]{:S(2)}) %collective-permute-start.1) | collective-permute-done | bytes 1048608 | tf_op jit(solution)/shard_map/ppermute | solution.py:78
  27.2 1.3 collective-permute-start.7
  28.5 1.7 collective-permute-start.12
  30.2 24.1 %all-to-all-done = bf16[8,2,64,512]{3,2,1,0:T(8,128)(2,1)S(1)} async-done(((bf16[8,2,64,512]{3,2,1,0:T(8,128)(2,1)}), bf16[8,2,64,512]{3,2,1,0:T(8,128)(2,1)S(1)}, u32[]{:S(2)}, u32[]{:S(2)}) %all-to-all-start) | async-done | bytes 1048608 | tf_op jit(solution)/shard_map/all_to_all | solution.py:109
  55.3 1.5 copy.5.panel_ref
  56.8 3.9 %shard_map.29 = (f32[4,128,512]{2,1,0:T(8,128)S(1)}, bf16[4,128,512]{2,1,0:T(8,128)(2,1)S(1)}, bf16[4,128,512]{2,1,0:T(8,128)(2,1)S(1)}, bf16[4,128,512]{2,1,0:T(8,128)(2,1)S(1)}) custom-call(s32[1]{0:T(128)} %bitcast.4.core_ref, bf16[512,1024]{1,0:T(8,128)(2,1)S(1)} %copy.5.panel_ref, bf16[1024,512]{1,0:T(8,128)(2,1)S(1)} %bitcast.12, ...), custom_call_target="tpu_custom_call" | custom-call | tf_op jit(solution)/shard_map/pallas_call | solution.py:115
  60.7 7.9 %collective-permute-done.7 = bf16[1024,512]{1,0:T(8,128)(2,1)} collective-permute-done((bf16[1024,512]{1,0:T(8,128)(2,1)}, bf16[1024,512]{1,0:T(8,128)(2,1)}, u32[]{:S(2)}, u32[]{:S(2)}) %collective-permute-start.7) | collective-permute-done | bytes 1048608 | tf_op jit(solution)/shard_map/ppermute | solution.py:78
  68.6 1.3 broadcast_select_fusion.1.refs_0_
  70.1 1.3 collective-permute-start.13
  71.4 2.5 %collective-permute-start.6 = (bf16[4,128,512]{2,1,0:T(8,128)(2,1)S(1)}, bf16[4,128,512]{2,1,0:T(8,128)(2,1)S(1)}, u32[]{:S(2)}, u32[]{:S(2)}) collective-permute-start(bf16[4,128,512]{2,1,0:T(8,128)(2,1)S(1)} %get-tuple-element.30), channel_id=1, source_target_pairs={{0,24},{8,16},{16,8},{24,0},{1,25},{9,17},{17,9},{25,1},{2,26},{10... | collective-permute-start | bytes 1572872 | tf_op jit(solution)/shard_map/ppermute | solution.py:125
  74.9 12.2 %collective-permute-done.6 = bf16[4,128,512]{2,1,0:T(8,128)(2,1)S(1)} collective-permute-done((bf16[4,128,512]{2,1,0:T(8,128)(2,1)S(1)}, bf16[4,128,512]{2,1,0:T(8,128)(2,1)S(1)}, u32[]{:S(2)}, u32[]{:S(2)}) %collective-permute-start.6) | collective-permute-done | bytes 524320 | tf_op jit(solution)/shard_map/ppermute | solution.py:125
  87.1 10.8 %collective-permute-done.5 = bf16[4,128,512]{2,1,0:T(8,128)(2,1)S(1)} collective-permute-done((bf16[4,128,512]{2,1,0:T(8,128)(2,1)S(1)}, bf16[4,128,512]{2,1,0:T(8,128)(2,1)S(1)}, u32[]{:S(2)}, u32[]{:S(2)}) %collective-permute-start.5) | collective-permute-done | bytes 524320 | tf_op jit(solution)/shard_map/ppermute | solution.py:125
  100.2 2.5 %collective-permute-start.11 = (bf16[2,128,512]{2,1,0:T(8,128)(2,1)S(1)}, bf16[2,128,512]{2,1,0:T(8,128)(2,1)S(1)}, u32[]{:S(2)}, u32[]{:S(2)}) collective-permute-start(bf16[2,128,512]{2,1,0:T(8,128)(2,1)S(1)} %get-tuple-element.37), channel_id=1, source_target_pairs={{0,24},{8,16},{16,8},{24,0},{1,25},{9,17},{17,9},{25,1},{2,26},{10... | collective-permute-start | bytes 786440 | tf_op jit(solution)/shard_map/ppermute | solution.py:125
  103.8 6.6 %collective-permute-done.11 = bf16[2,128,512]{2,1,0:T(8,128)(2,1)S(1)} collective-permute-done((bf16[2,128,512]{2,1,0:T(8,128)(2,1)S(1)}, bf16[2,128,512]{2,1,0:T(8,128)(2,1)S(1)}, u32[]{:S(2)}, u32[]{:S(2)}) %collective-permute-start.11) | collective-permute-done | bytes 262176 | tf_op jit(solution)/shard_map/ppermute | solution.py:125
  110.4 5.1 %collective-permute-done.10 = bf16[2,128,512]{2,1,0:T(8,128)(2,1)S(1)} collective-permute-done((bf16[2,128,512]{2,1,0:T(8,128)(2,1)S(1)}, bf16[2,128,512]{2,1,0:T(8,128)(2,1)S(1)}, u32[]{:S(2)}, u32[]{:S(2)}) %collective-permute-start.10) | collective-permute-done | bytes 262176 | tf_op jit(solution)/shard_map/ppermute | solution.py:125
  117.0 1.6 collective-permute-start.15
  120.6 5.6 %collective-permute-done.15.refs_3_ = bf16[2,128,512]{2,1,0:T(8,128)(2,1)S(1)} collective-permute-done((bf16[2,128,512]{2,1,0:T(8,128)(2,1)S(1)}, bf16[2,128,512]{2,1,0:T(8,128)(2,1)S(1)}, u32[]{:S(2)}, u32[]{:S(2)}) %collective-permute-start.15) | collective-permute-done | bytes 262176 | tf_op jit(solution)/shard_map/ppermute | solution.py:125
  126.2 5.8 %collective-permute-done.16.refs_4_ = bf16[2,128,512]{2,1,0:T(8,128)(2,1)S(1)} collective-permute-done((bf16[2,128,512]{2,1,0:T(8,128)(2,1)S(1)}, bf16[2,128,512]{2,1,0:T(8,128)(2,1)S(1)}, u32[]{:S(2)}, u32[]{:S(2)}) %collective-permute-start.16) | collective-permute-done | bytes 262176 | tf_op jit(solution)/shard_map/ppermute | solution.py:125
  133.0 35.0 %all_to_all.10.second_ref = bf16[32,2,64,128]{3,2,1,0:T(8,128)(2,1)S(1)} all-to-all(bf16[32,2,64,128]{3,2,1,0:T(8,128)(2,1)S(1)} %get-tuple-element.46), channel_id=1, replica_groups=mesh['row'=4,'col'=8] {'row','col'}, dimensions={0} | all-to-all | bytes 2097152 | tf_op jit(solution)/shard_map/all_to_all | solution.py:166
  168.0 1.5 shard_map.33
  (32 shorter events, 11.8 us)
Async XLA Ops:
  0.0 27.2 %collective-permute-start.1 = (bf16[1024,512]{1,0:T(8,128)(2,1)}, bf16[1024,512]{1,0:T(8,128)(2,1)S(1)}, u32[]{:S(2)}, u32[]{:S(2)}) collective-permute-start(bf16[1024,512]{1,0:T(8,128)(2,1)} %bitcast.9), channel_id=1, source_target_pairs={{0,2},{1,3},{2,0},{3,1},{4,6},{5,7},{6,4},{7,5},{8,10},{9,11},{10,... | collective-permute-start | bytes 3145736 | tf_op jit(solution)/shard_map/ppermute | solution.py:78
  3.0 24.2 %collective-permute-start.2 = (bf16[1024,512]{1,0:T(8,128)(2,1)}, bf16[1024,512]{1,0:T(8,128)(2,1)}, u32[]{:S(2)}, u32[]{:S(2)}) collective-permute-start(bf16[1024,512]{1,0:T(8,128)(2,1)} %bitcast.10), channel_id=1, source_target_pairs={{2,4},{3,5},{4,2},{5,3},{10,12},{11,13},{12,10},{13,11},{18,20},{1... | collective-permute-start | bytes 3145736 | tf_op jit(solution)/shard_map/ppermute | solution.py:78
  4.7 1.2 copy-start
  7.2 4.8 %copy-start.1 = (bf16[2,512,1,512]{3,1,2,0:T(8,128)(2,1)S(1)}, bf16[2,512,1,512]{3,1,2,0:T(8,128)(2,1)}, u32[]{:S(2)}) copy-start(bf16[2,512,1,512]{3,1,2,0:T(8,128)(2,1)} %param.3) | copy-start | bytes 3145732
  7.2 47.0 %all-to-all-start = ((bf16[8,2,64,512]{3,2,1,0:T(8,128)(2,1)}), bf16[8,2,64,512]{3,2,1,0:T(8,128)(2,1)S(1)}, u32[]{:S(2)}, u32[]{:S(2)}) async-start(bf16[8,2,64,512]{3,2,1,0:T(8,128)(2,1)} %shard_map.28), calls=%async_computation | async-start | bytes 2097152 | tf_op jit(solution)/shard_map/all_to_all | solution.py:109
  12.0 44.8 %collective-permute-start = (bf16[1024,512]{1,0:T(8,128)(2,1)S(1)}, bf16[1024,512]{1,0:T(8,128)(2,1)}, u32[]{:S(2)}, u32[]{:S(2)}) collective-permute-start(bf16[1024,512]{1,0:T(8,128)(2,1)S(1)} %bitcast.11), channel_id=1, source_target_pairs={{0,1},{1,0},{2,3},{3,2},{4,5},{5,4},{6,7},{7,6},{8,9},{9,8},{10,11... | collective-permute-start | bytes 3145736 | tf_op jit(solution)/shard_map/ppermute | solution.py:75
  27.2 29.6 %collective-permute-start.3 = (bf16[1024,512]{1,0:T(8,128)(2,1)S(1)}, bf16[1024,512]{1,0:T(8,128)(2,1)}, u32[]{:S(2)}, u32[]{:S(2)}) collective-permute-start(bf16[1024,512]{1,0:T(8,128)(2,1)S(1)} %collective-permute-done.1.refs_2_), channel_id=1, source_target_pairs={{0,1},{1,0},{2,3},{3,2},{4,5},{5,4},{6,7},{7,6},{8,9},{9,8},{10,11... | collective-permute-start | bytes 3145736 | tf_op jit(solution)/shard_map/ppermute | solution.py:75
  27.2 41.4 %collective-permute-start.7 = (bf16[1024,512]{1,0:T(8,128)(2,1)}, bf16[1024,512]{1,0:T(8,128)(2,1)}, u32[]{:S(2)}, u32[]{:S(2)}) collective-permute-start(bf16[1024,512]{1,0:T(8,128)(2,1)} %collective-permute-done.2), channel_id=1, source_target_pairs={{2,0},{3,1},{4,6},{5,7},{10,8},{11,9},{12,14},{13,15},{18,16},{19,... | collective-permute-start | bytes 3145736 | tf_op jit(solution)/shard_map/ppermute | solution.py:78
  28.5 41.5 %collective-permute-start.12 = (bf16[1024,512]{1,0:T(8,128)(2,1)S(1)}, bf16[1024,512]{1,0:T(8,128)(2,1)}, u32[]{:S(2)}, u32[]{:S(2)}) collective-permute-start(bf16[1024,512]{1,0:T(8,128)(2,1)S(1)} %collective-permute-done.1.refs_2_), channel_id=1, source_target_pairs={{2,4},{3,5},{4,2},{5,3},{10,12},{11,13},{12,10},{13,11},{18,20},{1... | collective-permute-start | bytes 3145736 | tf_op jit(solution)/shard_map/ppermute | solution.py:78
  70.0 28.3 %collective-permute-start.8 = (bf16[1024,512]{1,0:T(8,128)(2,1)S(1)}, bf16[1024,512]{1,0:T(8,128)(2,1)S(1)}, u32[]{:S(2)}, u32[]{:S(2)}) collective-permute-start(bf16[1024,512]{1,0:T(8,128)(2,1)S(1)} %broadcast_select_fusion.1.refs_0_), channel_id=1, source_target_pairs={{0,1},{1,0},{2,3},{3,2},{4,5},{5,4},{6,7},{7,6},{8,9},{9,8},{10,11... | collective-permute-start | bytes 3145736 | tf_op jit(solution)/shard_map/ppermute | solution.py:75
  70.1 30.0 %collective-permute-start.13 = (bf16[1024,512]{1,0:T(8,128)(2,1)}, bf16[1024,512]{1,0:T(8,128)(2,1)S(1)}, u32[]{:S(2)}, u32[]{:S(2)}) collective-permute-start(bf16[1024,512]{1,0:T(8,128)(2,1)} %collective-permute-done.12), channel_id=1, source_target_pairs={{2,0},{3,1},{4,6},{5,7},{10,8},{11,9},{12,14},{13,15},{18,16},{19,... | collective-permute-start | bytes 3145736 | tf_op jit(solution)/shard_map/ppermute | solution.py:78
  71.4 15.7 %collective-permute-start.6 = (bf16[4,128,512]{2,1,0:T(8,128)(2,1)S(1)}, bf16[4,128,512]{2,1,0:T(8,128)(2,1)S(1)}, u32[]{:S(2)}, u32[]{:S(2)}) collective-permute-start(bf16[4,128,512]{2,1,0:T(8,128)(2,1)S(1)} %get-tuple-element.30), channel_id=1, source_target_pairs={{0,24},{8,16},{16,8},{24,0},{1,25},{9,17},{17,9},{25,1},{2,26},{10... | collective-permute-start | bytes 1572872 | tf_op jit(solution)/shard_map/ppermute | solution.py:125
  73.9 24.0 %collective-permute-start.5 = (bf16[4,128,512]{2,1,0:T(8,128)(2,1)S(1)}, bf16[4,128,512]{2,1,0:T(8,128)(2,1)S(1)}, u32[]{:S(2)}, u32[]{:S(2)}) collective-permute-start(bf16[4,128,512]{2,1,0:T(8,128)(2,1)S(1)} %get-tuple-element.29), channel_id=1, source_target_pairs={{0,16},{8,24},{16,0},{24,8},{1,17},{9,25},{17,1},{25,9},{2,18},{10... | collective-permute-start | bytes 1572872 | tf_op jit(solution)/shard_map/ppermute | solution.py:125
  74.4 23.6 %collective-permute-start.4 = (bf16[4,128,512]{2,1,0:T(8,128)(2,1)S(1)}, bf16[4,128,512]{2,1,0:T(8,128)(2,1)S(1)}, u32[]{:S(2)}, u32[]{:S(2)}) collective-permute-start(bf16[4,128,512]{2,1,0:T(8,128)(2,1)S(1)} %get-tuple-element.28), channel_id=1, source_target_pairs={{0,8},{8,0},{16,24},{24,16},{1,9},{9,1},{17,25},{25,17},{2,10},{10... | collective-permute-start | bytes 1572872 | tf_op jit(solution)/shard_map/ppermute | solution.py:125
  100.2 15.6 %collective-permute-start.14 = (bf16[1024,512]{1,0:T(8,128)(2,1)S(1)}, bf16[1024,512]{1,0:T(8,128)(2,1)S(1)}, u32[]{:S(2)}, u32[]{:S(2)}) collective-permute-start(bf16[1024,512]{1,0:T(8,128)(2,1)S(1)} %broadcast_select_fusion.refs_0_), channel_id=1, source_target_pairs={{0,1},{1,0},{2,3},{3,2},{4,5},{5,4},{6,7},{7,6},{8,9},{9,8},{10,11... | collective-permute-start | bytes 3145736 | tf_op jit(solution)/shard_map/ppermute | solution.py:75
  100.2 10.1 %collective-permute-start.11 = (bf16[2,128,512]{2,1,0:T(8,128)(2,1)S(1)}, bf16[2,128,512]{2,1,0:T(8,128)(2,1)S(1)}, u32[]{:S(2)}, u32[]{:S(2)}) collective-permute-start(bf16[2,128,512]{2,1,0:T(8,128)(2,1)S(1)} %get-tuple-element.37), channel_id=1, source_target_pairs={{0,24},{8,16},{16,8},{24,0},{1,25},{9,17},{17,9},{25,1},{2,26},{10... | collective-permute-start | bytes 786440 | tf_op jit(solution)/shard_map/ppermute | solution.py:125
  102.8 12.7 %collective-permute-start.10 = (bf16[2,128,512]{2,1,0:T(8,128)(2,1)S(1)}, bf16[2,128,512]{2,1,0:T(8,128)(2,1)S(1)}, u32[]{:S(2)}, u32[]{:S(2)}) collective-permute-start(bf16[2,128,512]{2,1,0:T(8,128)(2,1)S(1)} %get-tuple-element.36), channel_id=1, source_target_pairs={{0,16},{8,24},{16,0},{24,8},{1,17},{9,25},{17,1},{25,9},{2,18},{10... | collective-permute-start | bytes 786440 | tf_op jit(solution)/shard_map/ppermute | solution.py:125
  103.3 12.3 %collective-permute-start.9 = (bf16[2,128,512]{2,1,0:T(8,128)(2,1)S(1)}, bf16[2,128,512]{2,1,0:T(8,128)(2,1)S(1)}, u32[]{:S(2)}, u32[]{:S(2)}) collective-permute-start(bf16[2,128,512]{2,1,0:T(8,128)(2,1)S(1)} %get-tuple-element.35), channel_id=1, source_target_pairs={{0,8},{8,0},{16,24},{24,16},{1,9},{9,1},{17,25},{25,17},{2,10},{10... | collective-permute-start | bytes 786440 | tf_op jit(solution)/shard_map/ppermute | solution.py:125
  117.0 9.2 %collective-permute-start.15 = (bf16[2,128,512]{2,1,0:T(8,128)(2,1)S(1)}, bf16[2,128,512]{2,1,0:T(8,128)(2,1)S(1)}, u32[]{:S(2)}, u32[]{:S(2)}) collective-permute-start(bf16[2,128,512]{2,1,0:T(8,128)(2,1)S(1)} %get-tuple-element.42), channel_id=1, source_target_pairs={{0,8},{8,0},{16,24},{24,16},{1,9},{9,1},{17,25},{25,17},{2,10},{10... | collective-permute-start | bytes 786440 | tf_op jit(solution)/shard_map/ppermute | solution.py:125
  118.6 13.5 %collective-permute-start.16 = (bf16[2,128,512]{2,1,0:T(8,128)(2,1)S(1)}, bf16[2,128,512]{2,1,0:T(8,128)(2,1)S(1)}, u32[]{:S(2)}, u32[]{:S(2)}) collective-permute-start(bf16[2,128,512]{2,1,0:T(8,128)(2,1)S(1)} %get-tuple-element.43), channel_id=1, source_target_pairs={{0,16},{8,24},{16,0},{24,8},{1,17},{9,25},{17,1},{25,9},{2,18},{10... | collective-permute-start | bytes 786440 | tf_op jit(solution)/shard_map/ppermute | solution.py:125
  119.3 12.8 %collective-permute-start.17 = (bf16[2,128,512]{2,1,0:T(8,128)(2,1)S(1)}, bf16[2,128,512]{2,1,0:T(8,128)(2,1)S(1)}, u32[]{:S(2)}, u32[]{:S(2)}) collective-permute-start(bf16[2,128,512]{2,1,0:T(8,128)(2,1)S(1)} %get-tuple-element.44), channel_id=1, source_target_pairs={{0,24},{8,16},{16,8},{24,0},{1,25},{9,17},{17,9},{25,1},{2,26},{10... | collective-permute-start | bytes 786440 | tf_op jit(solution)/shard_map/ppermute | solution.py:125

commit v6 on v5

v6 whole, which is shorter than its diff:
```python
import functools

import jax
import jax.numpy as jnp
from jax import lax
from jax.experimental import pallas as pl
from jax.experimental.pallas import tpu as pltpu
from jax.sharding import PartitionSpec as P

F32, BF16 = jnp.float32, jnp.bfloat16
VMEM = pl.BlockSpec(memory_space=pltpu.VMEM)
SMEM = pl.BlockSpec(memory_space=pltpu.SMEM)
PARAMS = pltpu.CompilerParams(vmem_limit_bytes=16 * 1024 * 1024)


def spread_kernel(nrow, ncol, row_ref, a_ref, out_ref):
    kk, occ, _, v = a_ref.shape
    ai, vs = occ // nrow, v // ncol
    for k in range(kk):
        tiles = [a_ref[k, (row_ref[0] ^ t) * ai + i] for t in range(nrow) for i in range(ai)]
        for s in range(ncol):
            piece = [tile[:, s * vs : (s + 1) * vs] for tile in tiles]
            out_ref[s, k] = jnp.concatenate(piece, axis=1)


def product_kernel(split, core_ref, panel_ref, here_ref, there_ref, *outs):
    nrow = len(outs) // 2 if split else len(outs)
    rows = outs[0].shape[1]

    def run(order):
        for p, block in enumerate(order):
            prod = jnp.dot(panel_ref[...], block[...], preferred_element_type=F32)
            to, n = (outs[p * nrow : (p + 1) * nrow], 0) if split else (outs, p)
            to[0][n] = prod[:rows]
            for t in range(1, nrow):
                to[t][n] = prod[t * rows : (t + 1) * rows].astype(BF16)

    pl.when(core_ref[0] == 0)(lambda: run((here_ref, there_ref)))
    pl.when(core_ref[0] == 1)(lambda: run((there_ref, here_ref)))


def turn_kernel(p, ncol, count, slot_ref, *refs):
    first_ref, turned_ref = refs[-2:]
    vs = turned_ref.shape[1]
    total = refs[count][0]
    for other in refs[count + 1 : -2]:
        total = total + other[0].astype(F32)
    for m, value in enumerate([ref[p] for ref in refs[:count]] + [total.astype(BF16)]):
        slot = slot_ref[m]
        first_ref[slot] = value
        turned = value.astype(F32).T.astype(BF16)
        for s in range(ncol):
            turned_ref[slot * ncol + s] = turned[s * vs : (s + 1) * vs]


def final_kernel(nrow, ncol, *refs):
    out_ref = refs[-1]
    ai, _, vs, _ = out_ref.shape
    firsts, seconds = refs[:ai], refs[ai:-1]
    for i in range(ai):
        for r in range(nrow):
            tiles = [seconds[i][r * ncol + s].astype(F32) for s in range(ncol)]
            for q in range(ai):
                second = jnp.concatenate([x[:, q * vs : (q + 1) * vs] for x in tiles], axis=1)
                first = firsts[q][r, i * vs : (i + 1) * vs, :].astype(F32)
                out_ref[i, r * ai + q] = (first + second).astype(BF16)


def solution(mesh):
    nrow, ncol = mesh.shape["row"], mesh.shape["col"]
    nz = ncol // 2

    def across(x):
        return lax.ppermute(x, "col", [(s, s ^ 1) for s in range(ncol)])

    def along(x, pairs):
        return lax.ppermute(x, "col", [(2 * a + c, 2 * b + c) for a, b in pairs for c in range(2)])

    def after(x, *earlier):
        return lax.optimization_barrier((x, *earlier))[0]

    def local(amplitudes, intermediate):
        kk, occ, cs, v = amplitudes.shape
        ai = occ // nrow
        vs = v // ncol
        rows = ai * vs
        row = lax.axis_index("row").reshape(1)
        col = lax.axis_index("col")
        z, core = (col // 2).reshape(1), (col % 2).reshape(1)
        end = (z == 0) | (z == nz - 1)

        w = intermediate.reshape(kk * v, v)
        line = nz == 4
        if line:
            swap = [(1, 2), (2, 1)]
            outward = [(1, 0), (2, 3)]
            x1 = along(w, [(a, a ^ 1) for a in range(nz)])
            y2 = along(w, swap)
        own = (w, across(w))

        blocks = pl.pallas_call(
            functools.partial(spread_kernel, nrow, ncol),
            out_shape=jax.ShapeDtypeStruct((ncol, kk, cs, occ * vs), BF16),
            in_specs=[SMEM, VMEM],
            out_specs=VMEM,
            compiler_params=PARAMS,
        )(row, amplitudes)
        panel = lax.all_to_all(blocks, "col", 0, 0, tiled=True)
        panel = jnp.transpose(panel, (3, 1, 0, 2)).reshape(nrow * rows, kk * v)

        def product(here, there, split=False):
            sets, n = (2, 1) if split else (1, 2)
            sent = [jax.ShapeDtypeStruct((n, rows, v), BF16)] * (nrow - 1)
            parts = pl.pallas_call(
                functools.partial(product_kernel, split),
                out_shape=([jax.ShapeDtypeStruct((n, rows, v), F32)] + sent) * sets,
                in_specs=[SMEM] + [VMEM] * 3,
                out_specs=[VMEM] * (nrow * sets),
                compiler_params=PARAMS,
            )(core, panel, here, there)
            return [parts[a * nrow : (a + 1) * nrow] for a in range(sets)]

        def exchange(parts):
            return [parts[0]] + [
                lax.ppermute(parts[t], "row", [(r, r ^ t) for r in range(nrow)])
                for t in range(1, nrow)
            ]

        def summed(parts):
            total = parts[0]
            for part in exchange(parts)[1:]:
                total = total + part.astype(F32)
            return total.astype(BF16)

        if line:
            x1, y2, blocks = lax.optimization_barrier((x1, y2, blocks))
            y3, e2 = along(x1, swap), along(y2, outward)
            sums = [summed(product(*own)[0])]
            sums.append(summed(product(x1, across(x1))[0]))
            e3 = along(after(y3, sums[0]), outward)
            x2 = jnp.where(end, e2, y2)
            parts = product(after(x2, sums[1]), across(x2))[0]
            sums.append(summed(parts))
            x3 = jnp.where(end, after(e3, *parts), y3)
            last = product(after(x3, sums[2]), across(x3), True)
            slots = [z, z ^ 1, jnp.where(end, z ^ 2, 3 - z), jnp.where(end, 3 - z, z ^ 2)]
        else:
            sums = [summed(product(*own)[0])]
            for m in range(1, nz):
                x = along(w, [(a, a ^ m) for a in range(nz)])
                last = product(after(x, sums[-1]), across(x), m == nz - 1)
                if m < nz - 1:
                    sums.append(summed(last[0]))
            slots = [z ^ m for m in range(nz)]
        slots = jnp.concatenate(slots).astype(jnp.int32)

        firsts, seconds = [], []
        for p, group in enumerate(exchange(g) for g in last):
            first, turned = pl.pallas_call(
                functools.partial(turn_kernel, p, ncol, len(sums)),
                out_shape=[
                    jax.ShapeDtypeStruct((nrow, rows, v), BF16),
                    jax.ShapeDtypeStruct((nrow * ncol, vs, rows), BF16),
                ],
                in_specs=[SMEM] + [VMEM] * (len(sums) + nrow),
                out_specs=[VMEM] * 2,
                compiler_params=PARAMS,
            )(slots, *sums, *group)
            firsts.append(first)
            seconds.append(lax.all_to_all(turned, ("row", "col"), 0, 0, tiled=True))

        return pl.pallas_call(
            functools.partial(final_kernel, nrow, ncol),
            out_shape=jax.ShapeDtypeStruct((ai, occ, vs, v), BF16),
            in_specs=[VMEM] * (2 * ai),
            out_specs=VMEM,
            compiler_params=PARAMS,
        )(*firsts, *seconds)

    placed = P("row", None, "col", None)
    return jax.shard_map(
        local, mesh=mesh, in_specs=(placed, placed), out_specs=placed, check_vma=False
    )
```

time: 170 us -> 169 us (level)
  blocking collectives: 35 us -> 19.4 us
  starting transfers between devices: 25 us -> 38 us
  Pallas kernels: 10.1 us -> 12.6 us
    all_to_all x1, blocking collectives: 35 us -> 19.4 us  [local(): seconds.append(lax.all_to_all(turned, ('row', 'col'), 0, 0, tiled=True))]
    ppermute x9 -> x15, starting transfers between devices: 10.7 us -> 19.9 us  [exchange(): lax.ppermute(parts[t], 'row', [(r, r ^ t) for r in range(nrow)])]
    ppermute x9 -> x15, waiting for transfers between devices: 46.2 us -> 39.4 us  [exchange(): lax.ppermute(parts[t], 'row', [(r, r ^ t) for r in range(nrow)])]
    ppermute x5, waiting for transfers between devices: 23 us -> 28.1 us  [along(): lax.ppermute(x, 'col', [(2 * a + c, 2 * b + c) for a, b in pairs for c in...]
    all_to_all x0 -> x1, starting transfers between devices: none -> 3.72 us  [local(): seconds.append(lax.all_to_all(turned, ('row', 'col'), 0, 0, tiled=True))]
    pallas_call x4 -> x6, Pallas kernels: 7.35 us -> 9.84 us  [the longest x4 7.5 us: product(): pl.pallas_call(functools.partial(product_kernel, split), out_shape=([jax....]
  transfers between devices with their start and end apart: 19 -> 26, of which waited for: 12 -> 15; matrix products, arithmetic and copies ran while one was open for 3% -> 3% of each run, Pallas kernels for 4% -> 5%
where the time goes in v6:
time: 169 us
  waiting for transfers between devices  92.7 us (55%)
  starting transfers between devices  38 us (22%)
  blocking collectives  19.4 us (11%)
  Pallas kernels  12.6 us (7%)
  local copies, waits for them, and re-layouts  3.78 us (2%)
  other arithmetic  1.98 us (1%)
    ppermute x15, waiting for transfers between devices, exchange(): lax.ppermute(parts[t], 'row', [(r, r ^ t) for r in range(nrow)])  39.4 us
    ppermute x5, waiting for transfers between devices, along(): lax.ppermute(x, 'col', [(2 * a + c, 2 * b + c) for a, b in pairs for c in...  28.1 us
    all_to_all x1, waiting for transfers between devices, local(): panel = lax.all_to_all(blocks, 'col', 0, 0, tiled=True)  24.1 us
    ppermute x15, starting transfers between devices, exchange(): lax.ppermute(parts[t], 'row', [(r, r ^ t) for r in range(nrow)])  19.9 us
    all_to_all x1, blocking collectives, local(): seconds.append(lax.all_to_all(turned, ('row', 'col'), 0, 0, tiled=True))  19.4 us
    ppermute x5, starting transfers between devices, along(): lax.ppermute(x, 'col', [(2 * a + c, 2 * b + c) for a, b in pairs for c in...  8.87 us
    pallas_call x4, Pallas kernels, product(): pl.pallas_call(functools.partial(product_kernel, split), out_shape=([jax....  7.5 us
    all_to_all x1, starting transfers between devices, local(): panel = lax.all_to_all(blocks, 'col', 0, 0, tiled=True)  4.83 us
  transfers between devices with their start and end apart: 26, of which 15 were waited for; matrix products, arithmetic and copies ran while one was open for 3% of the time, Pallas kernels for 5%

profile of v6, /device:TPU:0, one launch (start us, length us, event | category | flops | bytes accessed | tf_op | source)
XLA Modules:
  0.0 168.6 jit_solution(11170169482261160974)
XLA Ops:
  0.0 3.0 %collective-permute-start.4 = (bf16[1024,512]{1,0:T(8,128)(2,1)}, bf16[1024,512]{1,0:T(8,128)(2,1)S(1)}, u32[]{:S(2)}, u32[]{:S(2)}) collective-permute-start(bf16[1024,512]{1,0:T(8,128)(2,1)} %bitcast.7), channel_id=1, source_target_pairs={{0,2},{1,3},{2,0},{3,1},{4,6},{5,7},{6,4},{7,5},{8,10},{9,11},{10,... | collective-permute-start | bytes 3145736 | tf_op jit(solution)/shard_map/ppermute | solution.py:77
  3.0 1.6 collective-permute-start.5
  7.2 4.8 %all-to-all-start = ((bf16[8,2,64,512]{3,2,1,0:T(8,128)(2,1)}), bf16[8,2,64,512]{3,2,1,0:T(8,128)(2,1)S(1)}, u32[]{:S(2)}, u32[]{:S(2)}) async-start(bf16[8,2,64,512]{3,2,1,0:T(8,128)(2,1)} %shard_map.28), calls=%async_computation | async-start | bytes 2097152 | tf_op jit(solution)/shard_map/all_to_all | solution.py:108
  12.5 14.7 %collective-permute-done.4.here_ref = bf16[1024,512]{1,0:T(8,128)(2,1)S(1)} collective-permute-done((bf16[1024,512]{1,0:T(8,128)(2,1)}, bf16[1024,512]{1,0:T(8,128)(2,1)S(1)}, u32[]{:S(2)}, u32[]{:S(2)}) %collective-permute-start.4) | collective-permute-done | bytes 1048608 | tf_op jit(solution)/shard_map/ppermute | solution.py:77
  28.5 1.6 collective-permute-start.15
  30.2 24.1 %all-to-all-done = bf16[8,2,64,512]{3,2,1,0:T(8,128)(2,1)S(1)} async-done(((bf16[8,2,64,512]{3,2,1,0:T(8,128)(2,1)}), bf16[8,2,64,512]{3,2,1,0:T(8,128)(2,1)S(1)}, u32[]{:S(2)}, u32[]{:S(2)}) %all-to-all-start) | async-done | bytes 1048608 | tf_op jit(solution)/shard_map/all_to_all | solution.py:108
  56.8 2.5 %shard_map.29 = (f32[2,128,512]{2,1,0:T(8,128)S(1)}, bf16[2,128,512]{2,1,0:T(8,128)(2,1)S(1)}, bf16[2,128,512]{2,1,0:T(8,128)(2,1)S(1)}, bf16[2,128,512]{2,1,0:T(8,128)(2,1)S(1)}) custom-call(s32[1]{0:T(128)} %bitcast.1.core_ref, bf16[512,1024]{1,0:T(8,128)(2,1)S(1)} %copy.5.panel_ref, bf16[1024,512]{1,0:T(8,128)(2,1)S(1)} %bitcast.10, ...), custom_call_target="tpu_custom_call" | custom-call | tf_op jit(solution)/shard_map/pallas_call | solution.py:114
  62.4 3.4 %collective-permute-done.10 = bf16[1024,512]{1,0:T(8,128)(2,1)} collective-permute-done((bf16[1024,512]{1,0:T(8,128)(2,1)}, bf16[1024,512]{1,0:T(8,128)(2,1)}, u32[]{:S(2)}, u32[]{:S(2)}) %collective-permute-start.10) | collective-permute-done | bytes 1048608 | tf_op jit(solution)/shard_map/ppermute | solution.py:77
  65.8 2.6 %collective-permute-start.3 = (bf16[2,128,512]{2,1,0:T(8,128)(2,1)S(1)}, bf16[2,128,512]{2,1,0:T(8,128)(2,1)S(1)}, u32[]{:S(2)}, u32[]{:S(2)}) collective-permute-start(bf16[2,128,512]{2,1,0:T(8,128)(2,1)S(1)} %get-tuple-element.38), channel_id=1, source_target_pairs={{0,24},{8,16},{16,8},{24,0},{1,25},{9,17},{17,9},{25,1},{2,26},{10... | collective-permute-start | bytes 786440 | tf_op jit(solution)/shard_map/ppermute | solution.py:125
  70.1 3.0 %collective-permute-done.3 = bf16[2,128,512]{2,1,0:T(8,128)(2,1)S(1)} collective-permute-done((bf16[2,128,512]{2,1,0:T(8,128)(2,1)S(1)}, bf16[2,128,512]{2,1,0:T(8,128)(2,1)S(1)}, u32[]{:S(2)}, u32[]{:S(2)}) %collective-permute-start.3) | collective-permute-done | bytes 262176 | tf_op jit(solution)/shard_map/ppermute | solution.py:125
  74.6 2.5 %shard_map.30 = (f32[2,128,512]{2,1,0:T(8,128)S(1)}, bf16[2,128,512]{2,1,0:T(8,128)(2,1)S(1)}, bf16[2,128,512]{2,1,0:T(8,128)(2,1)S(1)}, bf16[2,128,512]{2,1,0:T(8,128)(2,1)S(1)}) custom-call(s32[1]{0:T(128)} %bitcast.1.core_ref, bf16[512,1024]{1,0:T(8,128)(2,1)S(1)} %copy.5.panel_ref, bf16[1024,512]{1,0:T(8,128)(2,1)S(1)} %collective-permute-done.4.here_ref, ...), custom_call_target="tpu_custom_call" | custom-call | tf_op jit(solution)/shard_map/pallas_call | solution.py:114
  77.1 1.7 %collective-permute-start.7 = (bf16[2,128,512]{2,1,0:T(8,128)(2,1)S(1)}, bf16[2,128,512]{2,1,0:T(8,128)(2,1)S(1)}, u32[]{:S(2)}, u32[]{:S(2)}) collective-permute-start(bf16[2,128,512]{2,1,0:T(8,128)(2,1)S(1)} %get-tuple-element.41), channel_id=1, source_target_pairs={{0,8},{8,0},{16,24},{24,16},{1,9},{9,1},{17,25},{25,17},{2,10},{10... | collective-permute-start | bytes 786440 | tf_op jit(solution)/shard_map/ppermute | solution.py:125
  80.6 4.8 %collective-permute-done.7 = bf16[2,128,512]{2,1,0:T(8,128)(2,1)S(1)} collective-permute-done((bf16[2,128,512]{2,1,0:T(8,128)(2,1)S(1)}, bf16[2,128,512]{2,1,0:T(8,128)(2,1)S(1)}, u32[]{:S(2)}, u32[]{:S(2)}) %collective-permute-start.7) | collective-permute-done | bytes 262176 | tf_op jit(solution)/shard_map/ppermute | solution.py:125
  85.5 3.1 %collective-permute-done.8 = bf16[2,128,512]{2,1,0:T(8,128)(2,1)S(1)} collective-permute-done((bf16[2,128,512]{2,1,0:T(8,128)(2,1)S(1)}, bf16[2,128,512]{2,1,0:T(8,128)(2,1)S(1)}, u32[]{:S(2)}, u32[]{:S(2)}) %collective-permute-start.8) | collective-permute-done | bytes 262176 | tf_op jit(solution)/shard_map/ppermute | solution.py:125
  90.0 10.0 %collective-permute-done.16 = bf16[1024,512]{1,0:T(8,128)(2,1)S(1)} collective-permute-done((bf16[1024,512]{1,0:T(8,128)(2,1)}, bf16[1024,512]{1,0:T(8,128)(2,1)S(1)}, u32[]{:S(2)}, u32[]{:S(2)}) %collective-permute-start.16) | collective-permute-done | bytes 1048608 | tf_op jit(solution)/shard_map/ppermute | solution.py:77
  103.8 5.6 %collective-permute-done.12 = bf16[2,128,512]{2,1,0:T(8,128)(2,1)S(1)} collective-permute-done((bf16[2,128,512]{2,1,0:T(8,128)(2,1)S(1)}, bf16[2,128,512]{2,1,0:T(8,128)(2,1)S(1)}, u32[]{:S(2)}, u32[]{:S(2)}) %collective-permute-start.12) | collective-permute-done | bytes 262176 | tf_op jit(solution)/shard_map/ppermute | solution.py:125
  109.4 6.4 %collective-permute-done.13 = bf16[2,128,512]{2,1,0:T(8,128)(2,1)S(1)} collective-permute-done((bf16[2,128,512]{2,1,0:T(8,128)(2,1)S(1)}, bf16[2,128,512]{2,1,0:T(8,128)(2,1)S(1)}, u32[]{:S(2)}, u32[]{:S(2)}) %collective-permute-start.13) | collective-permute-done | bytes 262176 | tf_op jit(solution)/shard_map/ppermute | solution.py:125
  120.8 2.0 %collective-permute-done.21.refs_4_ = bf16[1,128,512]{2,1,0:T(8,128)(2,1)S(1)} collective-permute-done((bf16[1,128,512]{2,1,0:T(8,128)(2,1)S(1)}, bf16[1,128,512]{2,1,0:T(8,128)(2,1)S(1)}, u32[]{:S(2)}, u32[]{:S(2)}) %collective-permute-start.21) | collective-permute-done | bytes 131104 | tf_op jit(solution)/shard_map/ppermute | solution.py:125
  122.8 3.3 %collective-permute-done.22.refs_5_ = bf16[1,128,512]{2,1,0:T(8,128)(2,1)S(1)} collective-permute-done((bf16[1,128,512]{2,1,0:T(8,128)(2,1)S(1)}, bf16[1,128,512]{2,1,0:T(8,128)(2,1)S(1)}, u32[]{:S(2)}, u32[]{:S(2)}) %collective-permute-start.22) | collective-permute-done | bytes 131104 | tf_op jit(solution)/shard_map/ppermute | solution.py:125
  127.7 3.7 %all-to-all-start.2 = ((bf16[32,64,128]{2,1,0:T(8,128)(2,1)}), bf16[32,64,128]{2,1,0:T(8,128)(2,1)S(1)}, u32[]{:S(2)}, u32[]{:S(2)}) async-start(bf16[32,64,128]{2,1,0:T(8,128)(2,1)} %get-tuple-element.64), calls=%async_computation.2 | async-start | bytes 1048576 | tf_op jit(solution)/shard_map/all_to_all | solution.py:170
  131.4 1.8 %collective-permute-start.18 = (bf16[1,128,512]{2,1,0:T(8,128)(2,1)S(1)}, bf16[1,128,512]{2,1,0:T(8,128)(2,1)S(1)}, u32[]{:S(2)}, u32[]{:S(2)}) collective-permute-start(bf16[1,128,512]{2,1,0:T(8,128)(2,1)S(1)} %get-tuple-element.54), channel_id=1, source_target_pairs={{0,8},{8,0},{16,24},{24,16},{1,9},{9,1},{17,25},{25,17},{2,10},{10... | collective-permute-start | bytes 393224 | tf_op jit(solution)/shard_map/ppermute | solution.py:125
  134.9 6.4 %collective-permute-done.18.refs_4_ = bf16[1,128,512]{2,1,0:T(8,128)(2,1)S(1)} collective-permute-done((bf16[1,128,512]{2,1,0:T(8,128)(2,1)S(1)}, bf16[1,128,512]{2,1,0:T(8,128)(2,1)S(1)}, u32[]{:S(2)}, u32[]{:S(2)}) %collective-permute-start.18) | collective-permute-done | bytes 131104 | tf_op jit(solution)/shard_map/ppermute | solution.py:125
  141.4 4.5 %collective-permute-done.20.refs_6_ = bf16[1,128,512]{2,1,0:T(8,128)(2,1)S(1)} collective-permute-done((bf16[1,128,512]{2,1,0:T(8,128)(2,1)S(1)}, bf16[1,128,512]{2,1,0:T(8,128)(2,1)S(1)}, u32[]{:S(2)}, u32[]{:S(2)}) %collective-permute-start.20) | collective-permute-done | bytes 131104 | tf_op jit(solution)/shard_map/ppermute | solution.py:125
  147.7 19.4 %all_to_all.15.refs_2_ = bf16[32,64,128]{2,1,0:T(8,128)(2,1)S(1)} all-to-all(bf16[32,64,128]{2,1,0:T(8,128)(2,1)S(1)} %get-tuple-element.63), channel_id=1, replica_groups=mesh['row'=4,'col'=8] {'row','col'}, dimensions={0} | all-to-all | bytes 1048576 | tf_op jit(solution)/shard_map/all_to_all | solution.py:170
  (49 shorter events, 31.7 us)
Async XLA Ops:
  0.0 27.2 %collective-permute-start.4 = (bf16[1024,512]{1,0:T(8,128)(2,1)}, bf16[1024,512]{1,0:T(8,128)(2,1)S(1)}, u32[]{:S(2)}, u32[]{:S(2)}) collective-permute-start(bf16[1024,512]{1,0:T(8,128)(2,1)} %bitcast.7), channel_id=1, source_target_pairs={{0,2},{1,3},{2,0},{3,1},{4,6},{5,7},{6,4},{7,5},{8,10},{9,11},{10,... | collective-permute-start | bytes 3145736 | tf_op jit(solution)/shard_map/ppermute | solution.py:77
  3.0 24.2 %collective-permute-start.5 = (bf16[1024,512]{1,0:T(8,128)(2,1)}, bf16[1024,512]{1,0:T(8,128)(2,1)}, u32[]{:S(2)}, u32[]{:S(2)}) collective-permute-start(bf16[1024,512]{1,0:T(8,128)(2,1)} %bitcast.8), channel_id=1, source_target_pairs={{2,4},{3,5},{4,2},{5,3},{10,12},{11,13},{12,10},{13,11},{18,20},{1... | collective-permute-start | bytes 3145736 | tf_op jit(solution)/shard_map/ppermute | solution.py:77
  7.2 47.1 %all-to-all-start = ((bf16[8,2,64,512]{3,2,1,0:T(8,128)(2,1)}), bf16[8,2,64,512]{3,2,1,0:T(8,128)(2,1)S(1)}, u32[]{:S(2)}, u32[]{:S(2)}) async-start(bf16[8,2,64,512]{3,2,1,0:T(8,128)(2,1)} %shard_map.28), calls=%async_computation | async-start | bytes 2097152 | tf_op jit(solution)/shard_map/all_to_all | solution.py:108
  12.0 44.8 %collective-permute-start = (bf16[1024,512]{1,0:T(8,128)(2,1)S(1)}, bf16[1024,512]{1,0:T(8,128)(2,1)}, u32[]{:S(2)}, u32[]{:S(2)}) collective-permute-start(bf16[1024,512]{1,0:T(8,128)(2,1)S(1)} %bitcast.9), channel_id=1, source_target_pairs={{0,1},{1,0},{2,3},{3,2},{4,5},{5,4},{6,7},{7,6},{8,9},{9,8},{10,11... | collective-permute-start | bytes 3145736 | tf_op jit(solution)/shard_map/ppermute | solution.py:74
  27.2 38.6 %collective-permute-start.10 = (bf16[1024,512]{1,0:T(8,128)(2,1)}, bf16[1024,512]{1,0:T(8,128)(2,1)}, u32[]{:S(2)}, u32[]{:S(2)}) collective-permute-start(bf16[1024,512]{1,0:T(8,128)(2,1)} %collective-permute-done.5), channel_id=1, source_target_pairs={{2,0},{3,1},{4,6},{5,7},{10,8},{11,9},{12,14},{13,15},{18,16},{19,... | collective-permute-start | bytes 3145736 | tf_op jit(solution)/shard_map/ppermute | solution.py:77
  28.5 44.8 %collective-permute-start.15 = (bf16[1024,512]{1,0:T(8,128)(2,1)S(1)}, bf16[1024,512]{1,0:T(8,128)(2,1)}, u32[]{:S(2)}, u32[]{:S(2)}) collective-permute-start(bf16[1024,512]{1,0:T(8,128)(2,1)S(1)} %collective-permute-done.4.here_ref), channel_id=1, source_target_pairs={{2,4},{3,5},{4,2},{5,3},{10,12},{11,13},{12,10},{13,11},{18,20},{1... | collective-permute-start | bytes 3145736 | tf_op jit(solution)/shard_map/ppermute | solution.py:77
  30.1 44.4 %collective-permute-start.6 = (bf16[1024,512]{1,0:T(8,128)(2,1)S(1)}, bf16[1024,512]{1,0:T(8,128)(2,1)}, u32[]{:S(2)}, u32[]{:S(2)}) collective-permute-start(bf16[1024,512]{1,0:T(8,128)(2,1)S(1)} %collective-permute-done.4.here_ref), channel_id=1, source_target_pairs={{0,1},{1,0},{2,3},{3,2},{4,5},{5,4},{6,7},{7,6},{8,9},{9,8},{10,11... | collective-permute-start | bytes 3145736 | tf_op jit(solution)/shard_map/ppermute | solution.py:74
  59.3 10.5 %collective-permute-start.1 = (bf16[2,128,512]{2,1,0:T(8,128)(2,1)S(1)}, bf16[2,128,512]{2,1,0:T(8,128)(2,1)S(1)}, u32[]{:S(2)}, u32[]{:S(2)}) collective-permute-start(bf16[2,128,512]{2,1,0:T(8,128)(2,1)S(1)} %get-tuple-element.36), channel_id=1, source_target_pairs={{0,8},{8,0},{16,24},{24,16},{1,9},{9,1},{17,25},{25,17},{2,10},{10... | collective-permute-start | bytes 786440 | tf_op jit(solution)/shard_map/ppermute | solution.py:125
  60.9 9.2 %collective-permute-start.2 = (bf16[2,128,512]{2,1,0:T(8,128)(2,1)S(1)}, bf16[2,128,512]{2,1,0:T(8,128)(2,1)S(1)}, u32[]{:S(2)}, u32[]{:S(2)}) collective-permute-start(bf16[2,128,512]{2,1,0:T(8,128)(2,1)S(1)} %get-tuple-element.37), channel_id=1, source_target_pairs={{0,16},{8,24},{16,0},{24,8},{1,17},{9,25},{17,1},{25,9},{2,18},{10... | collective-permute-start | bytes 786440 | tf_op jit(solution)/shard_map/ppermute | solution.py:125
  65.8 7.3 %collective-permute-start.3 = (bf16[2,128,512]{2,1,0:T(8,128)(2,1)S(1)}, bf16[2,128,512]{2,1,0:T(8,128)(2,1)S(1)}, u32[]{:S(2)}, u32[]{:S(2)}) collective-permute-start(bf16[2,128,512]{2,1,0:T(8,128)(2,1)S(1)} %get-tuple-element.38), channel_id=1, source_target_pairs={{0,24},{8,16},{16,8},{24,0},{1,25},{9,17},{17,9},{25,1},{2,26},{10... | collective-permute-start | bytes 786440 | tf_op jit(solution)/shard_map/ppermute | solution.py:125
  69.8 18.9 %collective-permute-start.11 = (bf16[1024,512]{1,0:T(8,128)(2,1)S(1)}, bf16[1024,512]{1,0:T(8,128)(2,1)S(1)}, u32[]{:S(2)}, u32[]{:S(2)}) collective-permute-start(bf16[1024,512]{1,0:T(8,128)(2,1)S(1)} %broadcast_select_fusion.1.here_ref), channel_id=1, source_target_pairs={{0,1},{1,0},{2,3},{3,2},{4,5},{5,4},{6,7},{7,6},{8,9},{9,8},{10,11... | collective-permute-start | bytes 3145736 | tf_op jit(solution)/shard_map/ppermute | solution.py:74
  73.3 26.7 %collective-permute-start.16 = (bf16[1024,512]{1,0:T(8,128)(2,1)}, bf16[1024,512]{1,0:T(8,128)(2,1)S(1)}, u32[]{:S(2)}, u32[]{:S(2)}) collective-permute-start(bf16[1024,512]{1,0:T(8,128)(2,1)} %collective-permute-done.15), channel_id=1, source_target_pairs={{2,0},{3,1},{4,6},{5,7},{10,8},{11,9},{12,14},{13,15},{18,16},{19,... | collective-permute-start | bytes 3145736 | tf_op jit(solution)/shard_map/ppermute | solution.py:77
  77.1 8.4 %collective-permute-start.7 = (bf16[2,128,512]{2,1,0:T(8,128)(2,1)S(1)}, bf16[2,128,512]{2,1,0:T(8,128)(2,1)S(1)}, u32[]{:S(2)}, u32[]{:S(2)}) collective-permute-start(bf16[2,128,512]{2,1,0:T(8,128)(2,1)S(1)} %get-tuple-element.41), channel_id=1, source_target_pairs={{0,8},{8,0},{16,24},{24,16},{1,9},{9,1},{17,25},{25,17},{2,10},{10... | collective-permute-start | bytes 786440 | tf_op jit(solution)/shard_map/ppermute | solution.py:125
  78.8 9.8 %collective-permute-start.8 = (bf16[2,128,512]{2,1,0:T(8,128)(2,1)S(1)}, bf16[2,128,512]{2,1,0:T(8,128)(2,1)S(1)}, u32[]{:S(2)}, u32[]{:S(2)}) collective-permute-start(bf16[2,128,512]{2,1,0:T(8,128)(2,1)S(1)} %get-tuple-element.42), channel_id=1, source_target_pairs={{0,16},{8,24},{16,0},{24,8},{1,17},{9,25},{17,1},{25,9},{2,18},{10... | collective-permute-start | bytes 786440 | tf_op jit(solution)/shard_map/ppermute | solution.py:125
  80.3 8.2 %collective-permute-start.9 = (bf16[2,128,512]{2,1,0:T(8,128)(2,1)S(1)}, bf16[2,128,512]{2,1,0:T(8,128)(2,1)S(1)}, u32[]{:S(2)}, u32[]{:S(2)}) collective-permute-start(bf16[2,128,512]{2,1,0:T(8,128)(2,1)S(1)} %get-tuple-element.43), channel_id=1, source_target_pairs={{0,24},{8,16},{16,8},{24,0},{1,25},{9,17},{17,9},{25,1},{2,26},{10... | collective-permute-start | bytes 786440 | tf_op jit(solution)/shard_map/ppermute | solution.py:125
  100.1 15.8 %collective-permute-start.17 = (bf16[1024,512]{1,0:T(8,128)(2,1)S(1)}, bf16[1024,512]{1,0:T(8,128)(2,1)S(1)}, u32[]{:S(2)}, u32[]{:S(2)}) collective-permute-start(bf16[1024,512]{1,0:T(8,128)(2,1)S(1)} %broadcast_select_fusion.here_ref), channel_id=1, source_target_pairs={{0,1},{1,0},{2,3},{3,2},{4,5},{5,4},{6,7},{7,6},{8,9},{9,8},{10,11... | collective-permute-start | bytes 3145736 | tf_op jit(solution)/shard_map/ppermute | solution.py:74
  100.2 9.2 %collective-permute-start.12 = (bf16[2,128,512]{2,1,0:T(8,128)(2,1)S(1)}, bf16[2,128,512]{2,1,0:T(8,128)(2,1)S(1)}, u32[]{:S(2)}, u32[]{:S(2)}) collective-permute-start(bf16[2,128,512]{2,1,0:T(8,128)(2,1)S(1)} %get-tuple-element.47), channel_id=1, source_target_pairs={{0,8},{8,0},{16,24},{24,16},{1,9},{9,1},{17,25},{25,17},{2,10},{10... | collective-permute-start | bytes 786440 | tf_op jit(solution)/shard_map/ppermute | solution.py:125
  101.8 14.0 %collective-permute-start.13 = (bf16[2,128,512]{2,1,0:T(8,128)(2,1)S(1)}, bf16[2,128,512]{2,1,0:T(8,128)(2,1)S(1)}, u32[]{:S(2)}, u32[]{:S(2)}) collective-permute-start(bf16[2,128,512]{2,1,0:T(8,128)(2,1)S(1)} %get-tuple-element.48), channel_id=1, source_target_pairs={{0,16},{8,24},{16,0},{24,8},{1,17},{9,25},{17,1},{25,9},{2,18},{10... | collective-permute-start | bytes 786440 | tf_op jit(solution)/shard_map/ppermute | solution.py:125
  103.3 12.5 %collective-permute-start.14 = (bf16[2,128,512]{2,1,0:T(8,128)(2,1)S(1)}, bf16[2,128,512]{2,1,0:T(8,128)(2,1)S(1)}, u32[]{:S(2)}, u32[]{:S(2)}) collective-permute-start(bf16[2,128,512]{2,1,0:T(8,128)(2,1)S(1)} %get-tuple-element.49), channel_id=1, source_target_pairs={{0,24},{8,16},{16,8},{24,0},{1,25},{9,17},{17,9},{25,1},{2,26},{10... | collective-permute-start | bytes 786440 | tf_op jit(solution)/shard_map/ppermute | solution.py:125
  118.5 7.6 %collective-permute-start.22 = (bf16[1,128,512]{2,1,0:T(8,128)(2,1)S(1)}, bf16[1,128,512]{2,1,0:T(8,128)(2,1)S(1)}, u32[]{:S(2)}, u32[]{:S(2)}) collective-permute-start(bf16[1,128,512]{2,1,0:T(8,128)(2,1)S(1)} %get-tuple-element.60), channel_id=1, source_target_pairs={{0,16},{8,24},{16,0},{24,8},{1,17},{9,25},{17,1},{25,9},{2,18},{10... | collective-permute-start | bytes 393224 | tf_op jit(solution)/shard_map/ppermute | solution.py:125
  127.7 20.1 %all-to-all-start.2 = ((bf16[32,64,128]{2,1,0:T(8,128)(2,1)}), bf16[32,64,128]{2,1,0:T(8,128)(2,1)S(1)}, u32[]{:S(2)}, u32[]{:S(2)}) async-start(bf16[32,64,128]{2,1,0:T(8,128)(2,1)} %get-tuple-element.64), calls=%async_computation.2 | async-start | bytes 1048576 | tf_op jit(solution)/shard_map/all_to_all | solution.py:170
  131.4 10.0 %collective-permute-start.18 = (bf16[1,128,512]{2,1,0:T(8,128)(2,1)S(1)}, bf16[1,128,512]{2,1,0:T(8,128)(2,1)S(1)}, u32[]{:S(2)}, u32[]{:S(2)}) collective-permute-start(bf16[1,128,512]{2,1,0:T(8,128)(2,1)S(1)} %get-tuple-element.54), channel_id=1, source_target_pairs={{0,8},{8,0},{16,24},{24,16},{1,9},{9,1},{17,25},{25,17},{2,10},{10... | collective-permute-start | bytes 393224 | tf_op jit(solution)/shard_map/ppermute | solution.py:125
  133.2 8.2 %collective-permute-start.19 = (bf16[1,128,512]{2,1,0:T(8,128)(2,1)S(1)}, bf16[1,128,512]{2,1,0:T(8,128)(2,1)S(1)}, u32[]{:S(2)}, u32[]{:S(2)}) collective-permute-start(bf16[1,128,512]{2,1,0:T(8,128)(2,1)S(1)} %get-tuple-element.55), channel_id=1, source_target_pairs={{0,16},{8,24},{16,0},{24,8},{1,17},{9,25},{17,1},{25,9},{2,18},{10... | collective-permute-start | bytes 393224 | tf_op jit(solution)/shard_map/ppermute | solution.py:125
  134.7 11.2 %collective-permute-start.20 = (bf16[1,128,512]{2,1,0:T(8,128)(2,1)S(1)}, bf16[1,128,512]{2,1,0:T(8,128)(2,1)S(1)}, u32[]{:S(2)}, u32[]{:S(2)}) collective-permute-start(bf16[1,128,512]{2,1,0:T(8,128)(2,1)S(1)} %get-tuple-element.56), channel_id=1, source_target_pairs={{0,24},{8,16},{16,8},{24,0},{1,25},{9,17},{17,9},{25,1},{2,26},{10... | collective-permute-start | bytes 393224 | tf_op jit(solution)/shard_map/ppermute | solution.py:125
  (4 other events, 18.5 us)

commit v7 on v6

v7 whole, which is shorter than its diff:
```python
import functools

import jax
import jax.numpy as jnp
from jax import lax
from jax.experimental import pallas as pl
from jax.experimental.pallas import tpu as pltpu
from jax.sharding import PartitionSpec as P

F32, BF16 = jnp.float32, jnp.bfloat16
VMEM = pl.BlockSpec(memory_space=pltpu.VMEM)
SMEM = pl.BlockSpec(memory_space=pltpu.SMEM)
PARAMS = pltpu.CompilerParams(vmem_limit_bytes=16 * 1024 * 1024)


def spread_kernel(nrow, ncol, row_ref, a_ref, out_ref):
    kk, occ, _, v = a_ref.shape
    ai, vs = occ // nrow, v // ncol
    for k in range(kk):
        tiles = [a_ref[k, (row_ref[0] ^ t) * ai + i] for t in range(nrow) for i in range(ai)]
        for s in range(ncol):
            piece = [tile[:, s * vs : (s + 1) * vs] for tile in tiles]
            out_ref[s, k] = jnp.concatenate(piece, axis=1)


def product_kernel(count, panel_ref, *refs):
    blocks, outs = refs[:count], refs[count:]
    rows = outs[0].shape[1]
    for n, block in enumerate(blocks):
        prod = jnp.dot(panel_ref[...], block[...], preferred_element_type=F32)
        outs[0][n] = prod[:rows]
        for t in range(1, len(outs)):
            outs[t][n] = prod[t * rows : (t + 1) * rows].astype(BF16)


def turn_kernel(half, ncol, count, slot_ref, *refs):
    first_ref, turned_ref = refs[-2:]
    vs = turned_ref.shape[1]
    total = refs[count][0]
    for other in refs[count + 1 : -2]:
        total = total + other[0].astype(F32)
    for m, value in enumerate([ref[half] for ref in refs[:count]] + [total.astype(BF16)]):
        slot = slot_ref[m]
        first_ref[slot] = value
        turned = value.astype(F32).T.astype(BF16)
        for s in range(ncol):
            turned_ref[slot * ncol + s] = turned[s * vs : (s + 1) * vs]


def final_kernel(nrow, ncol, core_ref, *refs):
    out_ref = refs[-1]
    ai, _, vs, _ = out_ref.shape
    firsts, seconds = refs[:ai], refs[ai:-1]

    def run(core):
        for i in range(ai):
            for r in range(nrow):
                tiles = [seconds[i ^ (s % 2)][r * ncol + s].astype(F32) for s in range(ncol)]
                for q in range(ai):
                    second = jnp.concatenate([x[:, q * vs : (q + 1) * vs] for x in tiles], axis=1)
                    first = firsts[q ^ core][r, i * vs : (i + 1) * vs, :].astype(F32)
                    out_ref[i, r * ai + q] = (first + second).astype(BF16)

    for c in range(2):
        pl.when(core_ref[0] == c)(functools.partial(run, c))


def solution(mesh):
    nrow, ncol = mesh.shape["row"], mesh.shape["col"]
    nz = ncol // 2

    def across(x):
        return lax.ppermute(x, "col", [(s, s ^ 1) for s in range(ncol)])

    def along(x, pairs):
        return lax.ppermute(x, "col", [(2 * a + c, 2 * b + c) for a, b in pairs for c in range(2)])

    def after(x, *earlier):
        return lax.optimization_barrier((x, *earlier))[0]

    def local(amplitudes, intermediate):
        kk, occ, cs, v = amplitudes.shape
        ai = occ // nrow
        vs = v // ncol
        rows = ai * vs
        row = lax.axis_index("row").reshape(1)
        col = lax.axis_index("col")
        z, core = (col // 2).reshape(1), (col % 2).reshape(1)
        end = (z == 0) | (z == nz - 1)

        w = intermediate.reshape(kk * v, v)
        line = nz == 4
        if line:
            swap = [(1, 2), (2, 1)]
            outward = [(1, 0), (2, 3)]
            x1 = along(w, [(a, a ^ 1) for a in range(nz)])
            y2 = along(w, swap)
        own = (w, across(w))

        blocks = pl.pallas_call(
            functools.partial(spread_kernel, nrow, ncol),
            out_shape=jax.ShapeDtypeStruct((ncol, kk, cs, occ * vs), BF16),
            in_specs=[SMEM, VMEM],
            out_specs=VMEM,
            compiler_params=PARAMS,
        )(row, amplitudes)
        panel = lax.all_to_all(blocks, "col", 0, 0, tiled=True)
        panel = jnp.transpose(panel, (3, 1, 0, 2)).reshape(nrow * rows, kk * v)

        def product(*given):
            n = len(given)
            sent = [jax.ShapeDtypeStruct((n, rows, v), BF16)] * (nrow - 1)
            return pl.pallas_call(
                functools.partial(product_kernel, n),
                out_shape=[jax.ShapeDtypeStruct((n, rows, v), F32)] + sent,
                in_specs=[VMEM] * (1 + n),
                out_specs=[VMEM] * nrow,
                compiler_params=PARAMS,
            )(panel, *given)

        def exchange(parts):
            return [parts[0]] + [
                lax.ppermute(parts[t], "row", [(r, r ^ t) for r in range(nrow)])
                for t in range(1, nrow)
            ]

        def summed(group):
            total = group[0]
            for part in group[1:]:
                total = total + part.astype(F32)
            return total.astype(BF16)

        if line:
            x1, y2, blocks = lax.optimization_barrier((x1, y2, blocks))
            y3, e2 = along(x1, swap), along(y2, outward)
            group = exchange(product(*own))
            e3 = along(after(y3, *group[1:]), outward)
            sums = [summed(group)]
            sums.append(summed(exchange(product(x1, across(x1)))))
            x2 = jnp.where(end, e2, y2)
            group = exchange(product(after(x2, sums[1]), across(x2)))
            x = jnp.where(end, after(e3, *group[1:]), y3)
            sums.append(summed(group))
            slots = [z, z ^ 1, jnp.where(end, z ^ 2, 3 - z), jnp.where(end, 3 - z, z ^ 2)]
        else:
            sums = [summed(exchange(product(*own)))]
            for m in range(1, nz):
                x = after(along(w, [(a, a ^ m) for a in range(nz)]), sums[-1])
                if m < nz - 1:
                    sums.append(summed(exchange(product(x, across(x)))))
            slots = [z ^ m for m in range(nz)]
        slots = jnp.concatenate(slots).astype(jnp.int32)

        firsts, seconds = [], []
        for half, group in enumerate([exchange(product(x)), exchange(product(across(x)))]):
            first, turned = pl.pallas_call(
                functools.partial(turn_kernel, half, ncol, len(sums)),
                out_shape=[
                    jax.ShapeDtypeStruct((nrow, rows, v), BF16),
                    jax.ShapeDtypeStruct((nrow * ncol, vs, rows), BF16),
                ],
                in_specs=[SMEM] + [VMEM] * (len(sums) + nrow),
                out_specs=[VMEM] * 2,
                compiler_params=PARAMS,
            )(slots, *sums, *group)
            firsts.append(first)
            seconds.append(lax.all_to_all(turned, ("row", "col"), 0, 0, tiled=True))

        return pl.pallas_call(
            functools.partial(final_kernel, nrow, ncol),
            out_shape=jax.ShapeDtypeStruct((ai, occ, vs, v), BF16),
            in_specs=[SMEM] + [VMEM] * (2 * ai),
            out_specs=VMEM,
            compiler_params=PARAMS,
        )(core, *firsts, *seconds)

    placed = P("row", None, "col", None)
    return jax.shard_map(
        local, mesh=mesh, in_specs=(placed, placed), out_specs=placed, check_vma=False
    )
```

time: 169 us -> 170 us (level)
  blocking collectives: 19.4 us -> 0 us
  waiting for transfers between devices: 92.7 us -> 102 us
  starting transfers between devices: 38 us -> 45.6 us
    all_to_all x1 -> x0, blocking collectives: 19.4 us -> none  [local(): seconds.append(lax.all_to_all(turned, ('row', 'col'), 0, 0, tiled=True))]
    all_to_all x1 -> x2, waiting for transfers between devices: 1.08 us -> 16.4 us  [local(): seconds.append(lax.all_to_all(turned, ('row', 'col'), 0, 0, tiled=True))]
    all_to_all x1 -> x2, starting transfers between devices: 3.72 us -> 11.2 us  [local(): seconds.append(lax.all_to_all(turned, ('row', 'col'), 0, 0, tiled=True))]
    ppermute x5, waiting for transfers between devices: 28.1 us -> 22.1 us  [along(): lax.ppermute(x, 'col', [(2 * a + c, 2 * b + c) for a, b in pairs for c in...]
    pallas_call x6 -> x7, Pallas kernels: 9.84 us -> 11.2 us  [the longest x5 8.84 us: product(): pl.pallas_call(functools.partial(product_kernel, n), out_shape=[jax.Shape...]
  transfers between devices with their start and end apart: 26 -> 27, of which waited for: 15 -> 17; matrix products, arithmetic and copies ran while one was open for 3% -> 3% of each run, Pallas kernels for 5% -> 7%
where the time goes in v7:
time: 170 us; the launch traced here: 169 us
  waiting for transfers between devices  102 us (60%)
  starting transfers between devices  45.6 us (27%)
  Pallas kernels  14 us (8%)
  local copies, waits for them, and re-layouts  5.35 us (3%)
  other arithmetic  2.01 us (1%)
    ppermute x15, waiting for transfers between devices, exchange(): lax.ppermute(parts[t], 'row', [(r, r ^ t) for r in range(nrow)])  39.7 us
    all_to_all x1, waiting for transfers between devices, local(): panel = lax.all_to_all(blocks, 'col', 0, 0, tiled=True)  24.1 us
    ppermute x5, waiting for transfers between devices, along(): lax.ppermute(x, 'col', [(2 * a + c, 2 * b + c) for a, b in pairs for c in...  22.1 us
    ppermute x15, starting transfers between devices, exchange(): lax.ppermute(parts[t], 'row', [(r, r ^ t) for r in range(nrow)])  20 us
    all_to_all x2, waiting for transfers between devices, local(): seconds.append(lax.all_to_all(turned, ('row', 'col'), 0, 0, tiled=True))  16.4 us
    all_to_all x2, starting transfers between devices, local(): seconds.append(lax.all_to_all(turned, ('row', 'col'), 0, 0, tiled=True))  11.2 us
    ppermute x5, starting transfers between devices, along(): lax.ppermute(x, 'col', [(2 * a + c, 2 * b + c) for a, b in pairs for c in...  8.87 us
    pallas_call x5, Pallas kernels, product(): pl.pallas_call(functools.partial(product_kernel, n), out_shape=[jax.Shape...  8.84 us
  transfers between devices with their start and end apart: 27, of which 17 were waited for; matrix products, arithmetic and copies ran while one was open for 3% of the time, Pallas kernels for 7%

profile of v7, /device:TPU:0, one launch (start us, length us, event | category | flops | bytes accessed | tf_op | source)
XLA Modules:
  0.0 169.4 jit_solution(10291654660993298594)
XLA Ops:
  0.0 3.0 %collective-permute-start.4 = (bf16[1024,512]{1,0:T(8,128)(2,1)}, bf16[1024,512]{1,0:T(8,128)(2,1)S(1)}, u32[]{:S(2)}, u32[]{:S(2)}) collective-permute-start(bf16[1024,512]{1,0:T(8,128)(2,1)} %bitcast.7), channel_id=1, source_target_pairs={{0,2},{1,3},{2,0},{3,1},{4,6},{5,7},{6,4},{7,5},{8,10},{9,11},{10,... | collective-permute-start | bytes 3145736 | tf_op jit(solution)/shard_map/ppermute | solution.py:76
  7.2 4.8 %all-to-all-start = ((bf16[8,2,64,512]{3,2,1,0:T(8,128)(2,1)}), bf16[8,2,64,512]{3,2,1,0:T(8,128)(2,1)S(1)}, u32[]{:S(2)}, u32[]{:S(2)}) async-start(bf16[8,2,64,512]{3,2,1,0:T(8,128)(2,1)} %shard_map.28), calls=%async_computation | async-start | bytes 2097152 | tf_op jit(solution)/shard_map/all_to_all | solution.py:107
  12.5 14.7 %collective-permute-done.4.refs_0_ = bf16[1024,512]{1,0:T(8,128)(2,1)S(1)} collective-permute-done((bf16[1024,512]{1,0:T(8,128)(2,1)}, bf16[1024,512]{1,0:T(8,128)(2,1)S(1)}, u32[]{:S(2)}, u32[]{:S(2)}) %collective-permute-start.4) | collective-permute-done | bytes 1048608 | tf_op jit(solution)/shard_map/ppermute | solution.py:76
  30.2 24.1 %all-to-all-done = bf16[8,2,64,512]{3,2,1,0:T(8,128)(2,1)S(1)} async-done(((bf16[8,2,64,512]{3,2,1,0:T(8,128)(2,1)}), bf16[8,2,64,512]{3,2,1,0:T(8,128)(2,1)S(1)}, u32[]{:S(2)}, u32[]{:S(2)}) %all-to-all-start) | async-done | bytes 1048608 | tf_op jit(solution)/shard_map/all_to_all | solution.py:107
  56.8 2.5 %shard_map.29 = (f32[2,128,512]{2,1,0:T(8,128)S(1)}, bf16[2,128,512]{2,1,0:T(8,128)(2,1)S(1)}, bf16[2,128,512]{2,1,0:T(8,128)(2,1)S(1)}, bf16[2,128,512]{2,1,0:T(8,128)(2,1)S(1)}) custom-call(bf16[512,1024]{1,0:T(8,128)(2,1)S(1)} %copy.5.panel_ref, bf16[1024,512]{1,0:T(8,128)(2,1)S(1)} %bitcast.10, bf16[1024,512]{1,0:T(8,128)(2,1)} %collective-permute-done.refs_1_), custom_call_target="tpu_custom_call" | custom-call | tf_op jit(solution)/shard_map/pallas_call | solution.py:113
  59.3 2.5 %collective-permute-start.3 = (bf16[2,128,512]{2,1,0:T(8,128)(2,1)S(1)}, bf16[2,128,512]{2,1,0:T(8,128)(2,1)S(1)}, u32[]{:S(2)}, u32[]{:S(2)}) collective-permute-start(bf16[2,128,512]{2,1,0:T(8,128)(2,1)S(1)} %get-tuple-element.37), channel_id=1, source_target_pairs={{0,24},{8,16},{16,8},{24,0},{1,25},{9,17},{17,9},{25,1},{2,26},{10... | collective-permute-start | bytes 786440 | tf_op jit(solution)/shard_map/ppermute | solution.py:123
  61.8 4.0 %collective-permute-done.10 = bf16[1024,512]{1,0:T(8,128)(2,1)} collective-permute-done((bf16[1024,512]{1,0:T(8,128)(2,1)}, bf16[1024,512]{1,0:T(8,128)(2,1)}, u32[]{:S(2)}, u32[]{:S(2)}) %collective-permute-start.10) | collective-permute-done | bytes 1048608 | tf_op jit(solution)/shard_map/ppermute | solution.py:76
  67.2 1.8 %collective-permute-start.2 = (bf16[2,128,512]{2,1,0:T(8,128)(2,1)S(1)}, bf16[2,128,512]{2,1,0:T(8,128)(2,1)S(1)}, u32[]{:S(2)}, u32[]{:S(2)}) collective-permute-start(bf16[2,128,512]{2,1,0:T(8,128)(2,1)S(1)} %get-tuple-element.36), channel_id=1, source_target_pairs={{0,16},{8,24},{16,0},{24,8},{1,17},{9,25},{17,1},{25,9},{2,18},{10... | collective-permute-start | bytes 786440 | tf_op jit(solution)/shard_map/ppermute | solution.py:123
  70.5 5.5 %collective-permute-done.2 = bf16[2,128,512]{2,1,0:T(8,128)(2,1)S(1)} collective-permute-done((bf16[2,128,512]{2,1,0:T(8,128)(2,1)S(1)}, bf16[2,128,512]{2,1,0:T(8,128)(2,1)S(1)}, u32[]{:S(2)}, u32[]{:S(2)}) %collective-permute-start.2) | collective-permute-done | bytes 262176 | tf_op jit(solution)/shard_map/ppermute | solution.py:123
  78.7 2.5 %shard_map.30 = (f32[2,128,512]{2,1,0:T(8,128)S(1)}, bf16[2,128,512]{2,1,0:T(8,128)(2,1)S(1)}, bf16[2,128,512]{2,1,0:T(8,128)(2,1)S(1)}, bf16[2,128,512]{2,1,0:T(8,128)(2,1)S(1)}) custom-call(bf16[512,1024]{1,0:T(8,128)(2,1)S(1)} %copy.5.panel_ref, bf16[1024,512]{1,0:T(8,128)(2,1)S(1)} %collective-permute-done.4.refs_0_, ...), custom_call_target="tpu_custom_call" | custom-call | tf_op jit(solution)/shard_map/pallas_call | solution.py:113
  84.8 6.6 %collective-permute-done.9 = bf16[2,128,512]{2,1,0:T(8,128)(2,1)S(1)} collective-permute-done((bf16[2,128,512]{2,1,0:T(8,128)(2,1)S(1)}, bf16[2,128,512]{2,1,0:T(8,128)(2,1)S(1)}, u32[]{:S(2)}, u32[]{:S(2)}) %collective-permute-start.9) | collective-permute-done | bytes 262176 | tf_op jit(solution)/shard_map/ppermute | solution.py:123
  91.4 3.9 %collective-permute-done.8 = bf16[2,128,512]{2,1,0:T(8,128)(2,1)S(1)} collective-permute-done((bf16[2,128,512]{2,1,0:T(8,128)(2,1)S(1)}, bf16[2,128,512]{2,1,0:T(8,128)(2,1)S(1)}, u32[]{:S(2)}, u32[]{:S(2)}) %collective-permute-start.8) | collective-permute-done | bytes 262176 | tf_op jit(solution)/shard_map/ppermute | solution.py:123
  100.4 3.4 %collective-permute-done.16 = bf16[1024,512]{1,0:T(8,128)(2,1)S(1)} collective-permute-done((bf16[1024,512]{1,0:T(8,128)(2,1)}, bf16[1024,512]{1,0:T(8,128)(2,1)S(1)}, u32[]{:S(2)}, u32[]{:S(2)}) %collective-permute-start.16) | collective-permute-done | bytes 1048608 | tf_op jit(solution)/shard_map/ppermute | solution.py:76
  103.9 3.0 %collective-permute-done.14 = bf16[2,128,512]{2,1,0:T(8,128)(2,1)S(1)} collective-permute-done((bf16[2,128,512]{2,1,0:T(8,128)(2,1)S(1)}, bf16[2,128,512]{2,1,0:T(8,128)(2,1)S(1)}, u32[]{:S(2)}, u32[]{:S(2)}) %collective-permute-start.14) | collective-permute-done | bytes 262176 | tf_op jit(solution)/shard_map/ppermute | solution.py:123
  106.9 4.6 %collective-permute-done.13 = bf16[2,128,512]{2,1,0:T(8,128)(2,1)S(1)} collective-permute-done((bf16[2,128,512]{2,1,0:T(8,128)(2,1)S(1)}, bf16[2,128,512]{2,1,0:T(8,128)(2,1)S(1)}, u32[]{:S(2)}, u32[]{:S(2)}) %collective-permute-start.13) | collective-permute-done | bytes 262176 | tf_op jit(solution)/shard_map/ppermute | solution.py:123
  116.2 2.7 %collective-permute-done.17.refs_4_ = bf16[1,128,512]{2,1,0:T(8,128)(2,1)S(1)} collective-permute-done((bf16[1,128,512]{2,1,0:T(8,128)(2,1)S(1)}, bf16[1,128,512]{2,1,0:T(8,128)(2,1)S(1)}, u32[]{:S(2)}, u32[]{:S(2)}) %collective-permute-start.17) | collective-permute-done | bytes 131104 | tf_op jit(solution)/shard_map/ppermute | solution.py:123
  118.9 2.8 %collective-permute-done.18.refs_5_ = bf16[1,128,512]{2,1,0:T(8,128)(2,1)S(1)} collective-permute-done((bf16[1,128,512]{2,1,0:T(8,128)(2,1)S(1)}, bf16[1,128,512]{2,1,0:T(8,128)(2,1)S(1)}, u32[]{:S(2)}, u32[]{:S(2)}) %collective-permute-start.18) | collective-permute-done | bytes 131104 | tf_op jit(solution)/shard_map/ppermute | solution.py:123
  124.0 7.0 %all-to-all-start.1 = ((bf16[32,64,128]{2,1,0:T(8,128)(2,1)}), bf16[32,64,128]{2,1,0:T(8,128)(2,1)S(1)}, u32[]{:S(2)}, u32[]{:S(2)}) async-start(bf16[32,64,128]{2,1,0:T(8,128)(2,1)} %copy-done.2), calls=%async_computation.1 | async-start | bytes 1048576 | tf_op jit(solution)/shard_map/all_to_all | solution.py:167
  131.0 1.9 %shard_map.34 = (f32[1,128,512]{2,1,0:T(8,128)S(1)}, bf16[1,128,512]{2,1,0:T(8,128)(2,1)S(1)}, bf16[1,128,512]{2,1,0:T(8,128)(2,1)S(1)}, bf16[1,128,512]{2,1,0:T(8,128)(2,1)S(1)}) custom-call(bf16[512,1024]{1,0:T(8,128)(2,1)S(1)} %copy.5.panel_ref, bf16[1024,512]{1,0:T(8,128)(2,1)} %collective-permute-done.20.refs_0_), custom_call_target="tpu_custom_call" | custom-call | tf_op jit(solution)/shard_map/pallas_call | solution.py:113
  132.9 1.8 %collective-permute-start.21 = (bf16[1,128,512]{2,1,0:T(8,128)(2,1)S(1)}, bf16[1,128,512]{2,1,0:T(8,128)(2,1)S(1)}, u32[]{:S(2)}, u32[]{:S(2)}) collective-permute-start(bf16[1,128,512]{2,1,0:T(8,128)(2,1)S(1)} %get-tuple-element.57), channel_id=1, source_target_pairs={{0,8},{8,0},{16,24},{24,16},{1,9},{9,1},{17,25},{25,17},{2,10},{10... | collective-permute-start | bytes 393224 | tf_op jit(solution)/shard_map/ppermute | solution.py:123
  136.5 4.5 %collective-permute-done.21.refs_4_ = bf16[1,128,512]{2,1,0:T(8,128)(2,1)S(1)} collective-permute-done((bf16[1,128,512]{2,1,0:T(8,128)(2,1)S(1)}, bf16[1,128,512]{2,1,0:T(8,128)(2,1)S(1)}, u32[]{:S(2)}, u32[]{:S(2)}) %collective-permute-start.21) | collective-permute-done | bytes 131104 | tf_op jit(solution)/shard_map/ppermute | solution.py:123
  141.0 3.1 %collective-permute-done.22.refs_5_ = bf16[1,128,512]{2,1,0:T(8,128)(2,1)S(1)} collective-permute-done((bf16[1,128,512]{2,1,0:T(8,128)(2,1)S(1)}, bf16[1,128,512]{2,1,0:T(8,128)(2,1)S(1)}, u32[]{:S(2)}, u32[]{:S(2)}) %collective-permute-start.22) | collective-permute-done | bytes 131104 | tf_op jit(solution)/shard_map/ppermute | solution.py:123
  147.4 4.2 %all-to-all-start.2 = ((bf16[32,64,128]{2,1,0:T(8,128)(2,1)}), bf16[32,64,128]{2,1,0:T(8,128)(2,1)S(1)}, u32[]{:S(2)}, u32[]{:S(2)}) async-start(bf16[32,64,128]{2,1,0:T(8,128)(2,1)} %get-tuple-element.62), calls=%async_computation.2 | async-start | bytes 1048576 | tf_op jit(solution)/shard_map/all_to_all | solution.py:167
  151.6 16.3 %all-to-all-done.2.refs_3_ = bf16[32,64,128]{2,1,0:T(8,128)(2,1)S(1)} async-done(((bf16[32,64,128]{2,1,0:T(8,128)(2,1)}), bf16[32,64,128]{2,1,0:T(8,128)(2,1)S(1)}, u32[]{:S(2)}, u32[]{:S(2)}) %all-to-all-start.2) | async-done | bytes 524320 | tf_op jit(solution)/shard_map/all_to_all | solution.py:167
  (57 shorter events, 37.9 us)
Async XLA Ops:
  0.0 27.2 %collective-permute-start.4 = (bf16[1024,512]{1,0:T(8,128)(2,1)}, bf16[1024,512]{1,0:T(8,128)(2,1)S(1)}, u32[]{:S(2)}, u32[]{:S(2)}) collective-permute-start(bf16[1024,512]{1,0:T(8,128)(2,1)} %bitcast.7), channel_id=1, source_target_pairs={{0,2},{1,3},{2,0},{3,1},{4,6},{5,7},{6,4},{7,5},{8,10},{9,11},{10,... | collective-permute-start | bytes 3145736 | tf_op jit(solution)/shard_map/ppermute | solution.py:76
  3.0 24.2 %collective-permute-start.5 = (bf16[1024,512]{1,0:T(8,128)(2,1)}, bf16[1024,512]{1,0:T(8,128)(2,1)}, u32[]{:S(2)}, u32[]{:S(2)}) collective-permute-start(bf16[1024,512]{1,0:T(8,128)(2,1)} %bitcast.8), channel_id=1, source_target_pairs={{2,4},{3,5},{4,2},{5,3},{10,12},{11,13},{12,10},{13,11},{18,20},{1... | collective-permute-start | bytes 3145736 | tf_op jit(solution)/shard_map/ppermute | solution.py:76
  7.2 47.1 %all-to-all-start = ((bf16[8,2,64,512]{3,2,1,0:T(8,128)(2,1)}), bf16[8,2,64,512]{3,2,1,0:T(8,128)(2,1)S(1)}, u32[]{:S(2)}, u32[]{:S(2)}) async-start(bf16[8,2,64,512]{3,2,1,0:T(8,128)(2,1)} %shard_map.28), calls=%async_computation | async-start | bytes 2097152 | tf_op jit(solution)/shard_map/all_to_all | solution.py:107
  12.0 44.8 %collective-permute-start = (bf16[1024,512]{1,0:T(8,128)(2,1)S(1)}, bf16[1024,512]{1,0:T(8,128)(2,1)}, u32[]{:S(2)}, u32[]{:S(2)}) collective-permute-start(bf16[1024,512]{1,0:T(8,128)(2,1)S(1)} %bitcast.9), channel_id=1, source_target_pairs={{0,1},{1,0},{2,3},{3,2},{4,5},{5,4},{6,7},{7,6},{8,9},{9,8},{10,11... | collective-permute-start | bytes 3145736 | tf_op jit(solution)/shard_map/ppermute | solution.py:73
  27.2 38.6 %collective-permute-start.10 = (bf16[1024,512]{1,0:T(8,128)(2,1)}, bf16[1024,512]{1,0:T(8,128)(2,1)}, u32[]{:S(2)}, u32[]{:S(2)}) collective-permute-start(bf16[1024,512]{1,0:T(8,128)(2,1)} %collective-permute-done.5), channel_id=1, source_target_pairs={{2,0},{3,1},{4,6},{5,7},{10,8},{11,9},{12,14},{13,15},{18,16},{19,... | collective-permute-start | bytes 3145736 | tf_op jit(solution)/shard_map/ppermute | solution.py:76
  28.5 48.9 %collective-permute-start.15 = (bf16[1024,512]{1,0:T(8,128)(2,1)S(1)}, bf16[1024,512]{1,0:T(8,128)(2,1)}, u32[]{:S(2)}, u32[]{:S(2)}) collective-permute-start(bf16[1024,512]{1,0:T(8,128)(2,1)S(1)} %collective-permute-done.4.refs_0_), channel_id=1, source_target_pairs={{2,4},{3,5},{4,2},{5,3},{10,12},{11,13},{12,10},{13,11},{18,20},{1... | collective-permute-start | bytes 3145736 | tf_op jit(solution)/shard_map/ppermute | solution.py:76
  30.1 48.5 %collective-permute-start.6 = (bf16[1024,512]{1,0:T(8,128)(2,1)S(1)}, bf16[1024,512]{1,0:T(8,128)(2,1)}, u32[]{:S(2)}, u32[]{:S(2)}) collective-permute-start(bf16[1024,512]{1,0:T(8,128)(2,1)S(1)} %collective-permute-done.4.refs_0_), channel_id=1, source_target_pairs={{0,1},{1,0},{2,3},{3,2},{4,5},{5,4},{6,7},{7,6},{8,9},{9,8},{10,11... | collective-permute-start | bytes 3145736 | tf_op jit(solution)/shard_map/ppermute | solution.py:73
  59.3 9.7 %collective-permute-start.3 = (bf16[2,128,512]{2,1,0:T(8,128)(2,1)S(1)}, bf16[2,128,512]{2,1,0:T(8,128)(2,1)S(1)}, u32[]{:S(2)}, u32[]{:S(2)}) collective-permute-start(bf16[2,128,512]{2,1,0:T(8,128)(2,1)S(1)} %get-tuple-element.37), channel_id=1, source_target_pairs={{0,24},{8,16},{16,8},{24,0},{1,25},{9,17},{17,9},{25,1},{2,26},{10... | collective-permute-start | bytes 786440 | tf_op jit(solution)/shard_map/ppermute | solution.py:123
  67.2 28.3 %collective-permute-start.11 = (bf16[1024,512]{1,0:T(8,128)(2,1)S(1)}, bf16[1024,512]{1,0:T(8,128)(2,1)S(1)}, u32[]{:S(2)}, u32[]{:S(2)}) collective-permute-start(bf16[1024,512]{1,0:T(8,128)(2,1)S(1)} %broadcast_select_fusion.1.refs_0_), channel_id=1, source_target_pairs={{0,1},{1,0},{2,3},{3,2},{4,5},{5,4},{6,7},{7,6},{8,9},{9,8},{10,11... | collective-permute-start | bytes 3145736 | tf_op jit(solution)/shard_map/ppermute | solution.py:73
  67.2 8.7 %collective-permute-start.2 = (bf16[2,128,512]{2,1,0:T(8,128)(2,1)S(1)}, bf16[2,128,512]{2,1,0:T(8,128)(2,1)S(1)}, u32[]{:S(2)}, u32[]{:S(2)}) collective-permute-start(bf16[2,128,512]{2,1,0:T(8,128)(2,1)S(1)} %get-tuple-element.36), channel_id=1, source_target_pairs={{0,16},{8,24},{16,0},{24,8},{1,17},{9,25},{17,1},{25,9},{2,18},{10... | collective-permute-start | bytes 786440 | tf_op jit(solution)/shard_map/ppermute | solution.py:123
  69.0 8.4 %collective-permute-start.1 = (bf16[2,128,512]{2,1,0:T(8,128)(2,1)S(1)}, bf16[2,128,512]{2,1,0:T(8,128)(2,1)S(1)}, u32[]{:S(2)}, u32[]{:S(2)}) collective-permute-start(bf16[2,128,512]{2,1,0:T(8,128)(2,1)S(1)} %get-tuple-element.35), channel_id=1, source_target_pairs={{0,8},{8,0},{16,24},{24,16},{1,9},{9,1},{17,25},{25,17},{2,10},{10... | collective-permute-start | bytes 786440 | tf_op jit(solution)/shard_map/ppermute | solution.py:123
  77.4 26.5 %collective-permute-start.16 = (bf16[1024,512]{1,0:T(8,128)(2,1)}, bf16[1024,512]{1,0:T(8,128)(2,1)S(1)}, u32[]{:S(2)}, u32[]{:S(2)}) collective-permute-start(bf16[1024,512]{1,0:T(8,128)(2,1)} %collective-permute-done.15), channel_id=1, source_target_pairs={{2,0},{3,1},{4,6},{5,7},{10,8},{11,9},{12,14},{13,15},{18,16},{19,... | collective-permute-start | bytes 3145736 | tf_op jit(solution)/shard_map/ppermute | solution.py:76
  81.2 10.3 %collective-permute-start.9 = (bf16[2,128,512]{2,1,0:T(8,128)(2,1)S(1)}, bf16[2,128,512]{2,1,0:T(8,128)(2,1)S(1)}, u32[]{:S(2)}, u32[]{:S(2)}) collective-permute-start(bf16[2,128,512]{2,1,0:T(8,128)(2,1)S(1)} %get-tuple-element.42), channel_id=1, source_target_pairs={{0,24},{8,16},{16,8},{24,0},{1,25},{9,17},{17,9},{25,1},{2,26},{10... | collective-permute-start | bytes 786440 | tf_op jit(solution)/shard_map/ppermute | solution.py:123
  82.7 12.6 %collective-permute-start.8 = (bf16[2,128,512]{2,1,0:T(8,128)(2,1)S(1)}, bf16[2,128,512]{2,1,0:T(8,128)(2,1)S(1)}, u32[]{:S(2)}, u32[]{:S(2)}) collective-permute-start(bf16[2,128,512]{2,1,0:T(8,128)(2,1)S(1)} %get-tuple-element.41), channel_id=1, source_target_pairs={{0,16},{8,24},{16,0},{24,8},{1,17},{9,25},{17,1},{25,9},{2,18},{10... | collective-permute-start | bytes 786440 | tf_op jit(solution)/shard_map/ppermute | solution.py:123
  84.2 11.1 %collective-permute-start.7 = (bf16[2,128,512]{2,1,0:T(8,128)(2,1)S(1)}, bf16[2,128,512]{2,1,0:T(8,128)(2,1)S(1)}, u32[]{:S(2)}, u32[]{:S(2)}) collective-permute-start(bf16[2,128,512]{2,1,0:T(8,128)(2,1)S(1)} %get-tuple-element.40), channel_id=1, source_target_pairs={{0,8},{8,0},{16,24},{24,16},{1,9},{9,1},{17,25},{25,17},{2,10},{10... | collective-permute-start | bytes 786440 | tf_op jit(solution)/shard_map/ppermute | solution.py:123
  96.7 10.2 %collective-permute-start.14 = (bf16[2,128,512]{2,1,0:T(8,128)(2,1)S(1)}, bf16[2,128,512]{2,1,0:T(8,128)(2,1)S(1)}, u32[]{:S(2)}, u32[]{:S(2)}) collective-permute-start(bf16[2,128,512]{2,1,0:T(8,128)(2,1)S(1)} %get-tuple-element.48), channel_id=1, source_target_pairs={{0,24},{8,16},{16,8},{24,0},{1,25},{9,17},{17,9},{25,1},{2,26},{10... | collective-permute-start | bytes 786440 | tf_op jit(solution)/shard_map/ppermute | solution.py:123
  98.3 13.2 %collective-permute-start.13 = (bf16[2,128,512]{2,1,0:T(8,128)(2,1)S(1)}, bf16[2,128,512]{2,1,0:T(8,128)(2,1)S(1)}, u32[]{:S(2)}, u32[]{:S(2)}) collective-permute-start(bf16[2,128,512]{2,1,0:T(8,128)(2,1)S(1)} %get-tuple-element.47), channel_id=1, source_target_pairs={{0,16},{8,24},{16,0},{24,8},{1,17},{9,25},{17,1},{25,9},{2,18},{10... | collective-permute-start | bytes 786440 | tf_op jit(solution)/shard_map/ppermute | solution.py:123
  99.2 12.4 %collective-permute-start.12 = (bf16[2,128,512]{2,1,0:T(8,128)(2,1)S(1)}, bf16[2,128,512]{2,1,0:T(8,128)(2,1)S(1)}, u32[]{:S(2)}, u32[]{:S(2)}) collective-permute-start(bf16[2,128,512]{2,1,0:T(8,128)(2,1)S(1)} %get-tuple-element.46), channel_id=1, source_target_pairs={{0,8},{8,0},{16,24},{24,16},{1,9},{9,1},{17,25},{25,17},{2,10},{10... | collective-permute-start | bytes 786440 | tf_op jit(solution)/shard_map/ppermute | solution.py:123
  112.4 18.6 %collective-permute-start.20 = (bf16[1024,512]{1,0:T(8,128)(2,1)S(1)}, bf16[1024,512]{1,0:T(8,128)(2,1)}, u32[]{:S(2)}, u32[]{:S(2)}) collective-permute-start(bf16[1024,512]{1,0:T(8,128)(2,1)S(1)} %broadcast_select_fusion.refs_0_), channel_id=1, source_target_pairs={{0,1},{1,0},{2,3},{3,2},{4,5},{5,4},{6,7},{7,6},{8,9},{9,8},{10,11... | collective-permute-start | bytes 3145736 | tf_op jit(solution)/shard_map/ppermute | solution.py:73
  113.2 8.4 %collective-permute-start.18 = (bf16[1,128,512]{2,1,0:T(8,128)(2,1)S(1)}, bf16[1,128,512]{2,1,0:T(8,128)(2,1)S(1)}, u32[]{:S(2)}, u32[]{:S(2)}) collective-permute-start(bf16[1,128,512]{2,1,0:T(8,128)(2,1)S(1)} %get-tuple-element.53), channel_id=1, source_target_pairs={{0,16},{8,24},{16,0},{24,8},{1,17},{9,25},{17,1},{25,9},{2,18},{10... | collective-permute-start | bytes 393224 | tf_op jit(solution)/shard_map/ppermute | solution.py:123
  124.0 23.4 %all-to-all-start.1 = ((bf16[32,64,128]{2,1,0:T(8,128)(2,1)}), bf16[32,64,128]{2,1,0:T(8,128)(2,1)S(1)}, u32[]{:S(2)}, u32[]{:S(2)}) async-start(bf16[32,64,128]{2,1,0:T(8,128)(2,1)} %copy-done.2), calls=%async_computation.1 | async-start | bytes 1048576 | tf_op jit(solution)/shard_map/all_to_all | solution.py:167
  134.8 9.4 %collective-permute-start.22 = (bf16[1,128,512]{2,1,0:T(8,128)(2,1)S(1)}, bf16[1,128,512]{2,1,0:T(8,128)(2,1)S(1)}, u32[]{:S(2)}, u32[]{:S(2)}) collective-permute-start(bf16[1,128,512]{2,1,0:T(8,128)(2,1)S(1)} %get-tuple-element.58), channel_id=1, source_target_pairs={{0,16},{8,24},{16,0},{24,8},{1,17},{9,25},{17,1},{25,9},{2,18},{10... | collective-permute-start | bytes 393224 | tf_op jit(solution)/shard_map/ppermute | solution.py:123
  136.2 9.5 %collective-permute-start.23 = (bf16[1,128,512]{2,1,0:T(8,128)(2,1)S(1)}, bf16[1,128,512]{2,1,0:T(8,128)(2,1)S(1)}, u32[]{:S(2)}, u32[]{:S(2)}) collective-permute-start(bf16[1,128,512]{2,1,0:T(8,128)(2,1)S(1)} %get-tuple-element.59), channel_id=1, source_target_pairs={{0,24},{8,16},{16,8},{24,0},{1,25},{9,17},{17,9},{25,1},{2,26},{10... | collective-permute-start | bytes 393224 | tf_op jit(solution)/shard_map/ppermute | solution.py:123
  147.4 20.6 %all-to-all-start.2 = ((bf16[32,64,128]{2,1,0:T(8,128)(2,1)}), bf16[32,64,128]{2,1,0:T(8,128)(2,1)S(1)}, u32[]{:S(2)}, u32[]{:S(2)}) async-start(bf16[32,64,128]{2,1,0:T(8,128)(2,1)} %get-tuple-element.62), calls=%async_computation.2 | async-start | bytes 1048576 | tf_op jit(solution)/shard_map/all_to_all | solution.py:167
  (8 other events, 49.6 us)

commit v8 on v5

--- a/solution.py
+++ b/solution.py
@@ -96,7 +96,7 @@
             swap = [(1, 2), (2, 1)]
             outward = [(1, 0), (2, 3)]
             x1 = along(w, [(a, a ^ 1) for a in range(nz)])
-            y2 = along(w, swap)
+            y2 = along(after(w, x1), swap)
         own = (w, across(w))
 
         blocks = pl.pallas_call(

time: 170 us -> 196 us (1.15)
  waiting for transfers between devices: 93.4 us -> 121 us
    all_to_all x1, waiting for transfers between devices: 24.1 us -> 38.7 us  [local(): panel = lax.all_to_all(blocks, 'col', 0, 0, tiled=True)]
    ppermute x5, waiting for transfers between devices: 23 us -> 36.2 us  [along(): lax.ppermute(x, 'col', [(2 * a + c, 2 * b + c) for a, b in pairs for c in...]
  transfers between devices with their start and end apart: 19 -> 19, of which waited for: 12 -> 10; matrix products, arithmetic and copies ran while one was open for 3% -> 2% of each run, Pallas kernels for 4% -> 3%
where the time goes in v8:
time: 196 us
  waiting for transfers between devices  121 us (62%)
  blocking collectives  33.2 us (17%)
  starting transfers between devices  25.5 us (13%)
  Pallas kernels  10.1 us (5%)
  local copies, waits for them, and re-layouts  3.78 us (2%)
  other arithmetic  2.04 us (1%)
    ppermute x9, waiting for transfers between devices, exchange(): lax.ppermute(parts[t], 'row', [(r, r ^ t) for r in range(nrow)])  46.3 us
    all_to_all x1, waiting for transfers between devices, local(): panel = lax.all_to_all(blocks, 'col', 0, 0, tiled=True)  38.7 us
    ppermute x5, waiting for transfers between devices, along(): lax.ppermute(x, 'col', [(2 * a + c, 2 * b + c) for a, b in pairs for c in...  36.2 us
    all_to_all x1, blocking collectives, local(): second = lax.all_to_all(turned, ('row', 'col'), 0, 0, tiled=True)  33.2 us
    ppermute x9, starting transfers between devices, exchange(): lax.ppermute(parts[t], 'row', [(r, r ^ t) for r in range(nrow)])  10.7 us
    ppermute x5, starting transfers between devices, along(): lax.ppermute(x, 'col', [(2 * a + c, 2 * b + c) for a, b in pairs for c in...  8.92 us
    pallas_call x3, Pallas kernels, product(): pl.pallas_call(functools.partial(product_kernel, len(pairs)), out_shape=[...  6.4 us
    all_to_all x1, starting transfers between devices, local(): panel = lax.all_to_all(blocks, 'col', 0, 0, tiled=True)  5.18 us
  transfers between devices with their start and end apart: 19, of which 10 were waited for; matrix products, arithmetic and copies ran while one was open for 2% of the time, Pallas kernels for 3%

profile of v8, /device:TPU:0, one launch (start us, length us, event | category | flops | bytes accessed | tf_op | source)
XLA Modules:
  0.0 196.0 jit_solution(1697939029230689923)
XLA Ops:
  0.0 3.0 %collective-permute-start.1 = (bf16[1024,512]{1,0:T(8,128)(2,1)}, bf16[1024,512]{1,0:T(8,128)(2,1)S(1)}, u32[]{:S(2)}, u32[]{:S(2)}) collective-permute-start(bf16[1024,512]{1,0:T(8,128)(2,1)} %bitcast.9), channel_id=1, source_target_pairs={{0,2},{1,3},{2,0},{3,1},{4,6},{5,7},{6,4},{7,5},{8,10},{9,11},{10,... | collective-permute-start | bytes 3145736 | tf_op jit(solution)/shard_map/ppermute | solution.py:78
  3.0 23.4 %collective-permute-done.1.refs_2_ = bf16[1024,512]{1,0:T(8,128)(2,1)S(1)} collective-permute-done((bf16[1024,512]{1,0:T(8,128)(2,1)}, bf16[1024,512]{1,0:T(8,128)(2,1)S(1)}, u32[]{:S(2)}, u32[]{:S(2)}) %collective-permute-start.1) | collective-permute-done | bytes 1048608 | tf_op jit(solution)/shard_map/ppermute | solution.py:78
  26.4 1.7 collective-permute-start.2
  29.3 1.3 shard_map.28
  30.6 5.2 %all-to-all-start = ((bf16[8,2,64,512]{3,2,1,0:T(8,128)(2,1)}), bf16[8,2,64,512]{3,2,1,0:T(8,128)(2,1)S(1)}, u32[]{:S(2)}, u32[]{:S(2)}) async-start(bf16[8,2,64,512]{3,2,1,0:T(8,128)(2,1)} %shard_map.28), calls=%async_computation | async-start | bytes 2097152 | tf_op jit(solution)/shard_map/all_to_all | solution.py:109
  37.6 1.7 collective-permute-start.12
  39.3 38.7 %all-to-all-done = bf16[8,2,64,512]{3,2,1,0:T(8,128)(2,1)S(1)} async-done(((bf16[8,2,64,512]{3,2,1,0:T(8,128)(2,1)}), bf16[8,2,64,512]{3,2,1,0:T(8,128)(2,1)S(1)}, u32[]{:S(2)}, u32[]{:S(2)}) %all-to-all-start) | async-done | bytes 1048608 | tf_op jit(solution)/shard_map/all_to_all | solution.py:109
  79.1 1.5 copy.5.panel_ref
  80.6 3.9 %shard_map.29 = (f32[4,128,512]{2,1,0:T(8,128)S(1)}, bf16[4,128,512]{2,1,0:T(8,128)(2,1)S(1)}, bf16[4,128,512]{2,1,0:T(8,128)(2,1)S(1)}, bf16[4,128,512]{2,1,0:T(8,128)(2,1)S(1)}) custom-call(s32[1]{0:T(128)} %bitcast.4.core_ref, bf16[512,1024]{1,0:T(8,128)(2,1)S(1)} %copy.5.panel_ref, bf16[1024,512]{1,0:T(8,128)(2,1)S(1)} %bitcast.12, ...), custom_call_target="tpu_custom_call" | custom-call | tf_op jit(solution)/shard_map/pallas_call | solution.py:115
  84.5 12.8 %collective-permute-done.7 = bf16[1024,512]{1,0:T(8,128)(2,1)} collective-permute-done((bf16[1024,512]{1,0:T(8,128)(2,1)}, bf16[1024,512]{1,0:T(8,128)(2,1)}, u32[]{:S(2)}, u32[]{:S(2)}) %collective-permute-start.7) | collective-permute-done | bytes 1048608 | tf_op jit(solution)/shard_map/ppermute | solution.py:78
  97.3 1.3 broadcast_select_fusion.1.refs_0_
  98.7 1.3 collective-permute-start.13
  100.0 2.5 %collective-permute-start.6 = (bf16[4,128,512]{2,1,0:T(8,128)(2,1)S(1)}, bf16[4,128,512]{2,1,0:T(8,128)(2,1)S(1)}, u32[]{:S(2)}, u32[]{:S(2)}) collective-permute-start(bf16[4,128,512]{2,1,0:T(8,128)(2,1)S(1)} %get-tuple-element.32), channel_id=1, source_target_pairs={{0,24},{8,16},{16,8},{24,0},{1,25},{9,17},{17,9},{25,1},{2,26},{10... | collective-permute-start | bytes 1572872 | tf_op jit(solution)/shard_map/ppermute | solution.py:125
  103.6 12.2 %collective-permute-done.6 = bf16[4,128,512]{2,1,0:T(8,128)(2,1)S(1)} collective-permute-done((bf16[4,128,512]{2,1,0:T(8,128)(2,1)S(1)}, bf16[4,128,512]{2,1,0:T(8,128)(2,1)S(1)}, u32[]{:S(2)}, u32[]{:S(2)}) %collective-permute-start.6) | collective-permute-done | bytes 524320 | tf_op jit(solution)/shard_map/ppermute | solution.py:125
  115.8 10.8 %collective-permute-done.5 = bf16[4,128,512]{2,1,0:T(8,128)(2,1)S(1)} collective-permute-done((bf16[4,128,512]{2,1,0:T(8,128)(2,1)S(1)}, bf16[4,128,512]{2,1,0:T(8,128)(2,1)S(1)}, u32[]{:S(2)}, u32[]{:S(2)}) %collective-permute-start.5) | collective-permute-done | bytes 524320 | tf_op jit(solution)/shard_map/ppermute | solution.py:125
  128.5 1.7 collective-permute-start.11
  130.2 1.3 collective-permute-start.10
  132.1 6.6 %collective-permute-done.11 = bf16[2,128,512]{2,1,0:T(8,128)(2,1)S(1)} collective-permute-done((bf16[2,128,512]{2,1,0:T(8,128)(2,1)S(1)}, bf16[2,128,512]{2,1,0:T(8,128)(2,1)S(1)}, u32[]{:S(2)}, u32[]{:S(2)}) %collective-permute-start.11) | collective-permute-done | bytes 262176 | tf_op jit(solution)/shard_map/ppermute | solution.py:125
  138.6 5.1 %collective-permute-done.10 = bf16[2,128,512]{2,1,0:T(8,128)(2,1)S(1)} collective-permute-done((bf16[2,128,512]{2,1,0:T(8,128)(2,1)S(1)}, bf16[2,128,512]{2,1,0:T(8,128)(2,1)S(1)}, u32[]{:S(2)}, u32[]{:S(2)}) %collective-permute-start.10) | collective-permute-done | bytes 262176 | tf_op jit(solution)/shard_map/ppermute | solution.py:125
  145.2 1.6 collective-permute-start.15
  148.8 5.6 %collective-permute-done.15.refs_3_ = bf16[2,128,512]{2,1,0:T(8,128)(2,1)S(1)} collective-permute-done((bf16[2,128,512]{2,1,0:T(8,128)(2,1)S(1)}, bf16[2,128,512]{2,1,0:T(8,128)(2,1)S(1)}, u32[]{:S(2)}, u32[]{:S(2)}) %collective-permute-start.15) | collective-permute-done | bytes 262176 | tf_op jit(solution)/shard_map/ppermute | solution.py:125
  154.4 5.9 %collective-permute-done.16.refs_4_ = bf16[2,128,512]{2,1,0:T(8,128)(2,1)S(1)} collective-permute-done((bf16[2,128,512]{2,1,0:T(8,128)(2,1)S(1)}, bf16[2,128,512]{2,1,0:T(8,128)(2,1)S(1)}, u32[]{:S(2)}, u32[]{:S(2)}) %collective-permute-start.16) | collective-permute-done | bytes 262176 | tf_op jit(solution)/shard_map/ppermute | solution.py:125
  161.3 33.2 %all_to_all.10.second_ref = bf16[32,2,64,128]{3,2,1,0:T(8,128)(2,1)S(1)} all-to-all(bf16[32,2,64,128]{3,2,1,0:T(8,128)(2,1)S(1)} %get-tuple-element.48), channel_id=1, replica_groups=mesh['row'=4,'col'=8] {'row','col'}, dimensions={0} | all-to-all | bytes 2097152 | tf_op jit(solution)/shard_map/all_to_all | solution.py:166
  194.5 1.5 shard_map.33
  (32 shorter events, 12.2 us)
Async XLA Ops:
  0.0 26.4 %collective-permute-start.1 = (bf16[1024,512]{1,0:T(8,128)(2,1)}, bf16[1024,512]{1,0:T(8,128)(2,1)S(1)}, u32[]{:S(2)}, u32[]{:S(2)}) collective-permute-start(bf16[1024,512]{1,0:T(8,128)(2,1)} %bitcast.9), channel_id=1, source_target_pairs={{0,2},{1,3},{2,0},{3,1},{4,6},{5,7},{6,4},{7,5},{8,10},{9,11},{10,... | collective-permute-start | bytes 3145736 | tf_op jit(solution)/shard_map/ppermute | solution.py:78
  26.4 9.9 %collective-permute-start.2 = (bf16[1024,512]{1,0:T(8,128)(2,1)}, bf16[1024,512]{1,0:T(8,128)(2,1)}, u32[]{:S(2)}, u32[]{:S(2)}) collective-permute-start(bf16[1024,512]{1,0:T(8,128)(2,1)} %bitcast.10), channel_id=1, source_target_pairs={{2,4},{3,5},{4,2},{5,3},{10,12},{11,13},{12,10},{13,11},{18,20},{1... | collective-permute-start | bytes 3145736 | tf_op jit(solution)/shard_map/ppermute | solution.py:78
  28.1 1.2 copy-start
  30.6 5.2 %copy-start.1 = (bf16[2,512,1,512]{3,1,2,0:T(8,128)(2,1)S(1)}, bf16[2,512,1,512]{3,1,2,0:T(8,128)(2,1)}, u32[]{:S(2)}) copy-start(bf16[2,512,1,512]{3,1,2,0:T(8,128)(2,1)} %param.3) | copy-start | bytes 3145732
  30.6 47.4 %all-to-all-start = ((bf16[8,2,64,512]{3,2,1,0:T(8,128)(2,1)}), bf16[8,2,64,512]{3,2,1,0:T(8,128)(2,1)S(1)}, u32[]{:S(2)}, u32[]{:S(2)}) async-start(bf16[8,2,64,512]{3,2,1,0:T(8,128)(2,1)} %shard_map.28), calls=%async_computation | async-start | bytes 2097152 | tf_op jit(solution)/shard_map/all_to_all | solution.py:109
  35.8 44.8 %collective-permute-start = (bf16[1024,512]{1,0:T(8,128)(2,1)S(1)}, bf16[1024,512]{1,0:T(8,128)(2,1)}, u32[]{:S(2)}, u32[]{:S(2)}) collective-permute-start(bf16[1024,512]{1,0:T(8,128)(2,1)S(1)} %bitcast.11), channel_id=1, source_target_pairs={{0,1},{1,0},{2,3},{3,2},{4,5},{5,4},{6,7},{7,6},{8,9},{9,8},{10,11... | collective-permute-start | bytes 3145736 | tf_op jit(solution)/shard_map/ppermute | solution.py:75
  36.3 44.3 %collective-permute-start.3 = (bf16[1024,512]{1,0:T(8,128)(2,1)S(1)}, bf16[1024,512]{1,0:T(8,128)(2,1)}, u32[]{:S(2)}, u32[]{:S(2)}) collective-permute-start(bf16[1024,512]{1,0:T(8,128)(2,1)S(1)} %collective-permute-done.1.refs_2_), channel_id=1, source_target_pairs={{0,1},{1,0},{2,3},{3,2},{4,5},{5,4},{6,7},{7,6},{8,9},{9,8},{10,11... | collective-permute-start | bytes 3145736 | tf_op jit(solution)/shard_map/ppermute | solution.py:75
  36.4 60.9 %collective-permute-start.7 = (bf16[1024,512]{1,0:T(8,128)(2,1)}, bf16[1024,512]{1,0:T(8,128)(2,1)}, u32[]{:S(2)}, u32[]{:S(2)}) collective-permute-start(bf16[1024,512]{1,0:T(8,128)(2,1)} %collective-permute-done.2), channel_id=1, source_target_pairs={{2,0},{3,1},{4,6},{5,7},{10,8},{11,9},{12,14},{13,15},{18,16},{19,... | collective-permute-start | bytes 3145736 | tf_op jit(solution)/shard_map/ppermute | solution.py:78
  37.6 61.1 %collective-permute-start.12 = (bf16[1024,512]{1,0:T(8,128)(2,1)S(1)}, bf16[1024,512]{1,0:T(8,128)(2,1)}, u32[]{:S(2)}, u32[]{:S(2)}) collective-permute-start(bf16[1024,512]{1,0:T(8,128)(2,1)S(1)} %collective-permute-done.1.refs_2_), channel_id=1, source_target_pairs={{2,4},{3,5},{4,2},{5,3},{10,12},{11,13},{12,10},{13,11},{18,20},{1... | collective-permute-start | bytes 3145736 | tf_op jit(solution)/shard_map/ppermute | solution.py:78
  98.6 28.3 %collective-permute-start.8 = (bf16[1024,512]{1,0:T(8,128)(2,1)S(1)}, bf16[1024,512]{1,0:T(8,128)(2,1)S(1)}, u32[]{:S(2)}, u32[]{:S(2)}) collective-permute-start(bf16[1024,512]{1,0:T(8,128)(2,1)S(1)} %broadcast_select_fusion.1.refs_0_), channel_id=1, source_target_pairs={{0,1},{1,0},{2,3},{3,2},{4,5},{5,4},{6,7},{7,6},{8,9},{9,8},{10,11... | collective-permute-start | bytes 3145736 | tf_op jit(solution)/shard_map/ppermute | solution.py:75
  98.7 29.5 %collective-permute-start.13 = (bf16[1024,512]{1,0:T(8,128)(2,1)}, bf16[1024,512]{1,0:T(8,128)(2,1)S(1)}, u32[]{:S(2)}, u32[]{:S(2)}) collective-permute-start(bf16[1024,512]{1,0:T(8,128)(2,1)} %collective-permute-done.12), channel_id=1, source_target_pairs={{2,0},{3,1},{4,6},{5,7},{10,8},{11,9},{12,14},{13,15},{18,16},{19,... | collective-permute-start | bytes 3145736 | tf_op jit(solution)/shard_map/ppermute | solution.py:78
  100.0 15.7 %collective-permute-start.6 = (bf16[4,128,512]{2,1,0:T(8,128)(2,1)S(1)}, bf16[4,128,512]{2,1,0:T(8,128)(2,1)S(1)}, u32[]{:S(2)}, u32[]{:S(2)}) collective-permute-start(bf16[4,128,512]{2,1,0:T(8,128)(2,1)S(1)} %get-tuple-element.32), channel_id=1, source_target_pairs={{0,24},{8,16},{16,8},{24,0},{1,25},{9,17},{17,9},{25,1},{2,26},{10... | collective-permute-start | bytes 1572872 | tf_op jit(solution)/shard_map/ppermute | solution.py:125
  102.5 24.0 %collective-permute-start.5 = (bf16[4,128,512]{2,1,0:T(8,128)(2,1)S(1)}, bf16[4,128,512]{2,1,0:T(8,128)(2,1)S(1)}, u32[]{:S(2)}, u32[]{:S(2)}) collective-permute-start(bf16[4,128,512]{2,1,0:T(8,128)(2,1)S(1)} %get-tuple-element.31), channel_id=1, source_target_pairs={{0,16},{8,24},{16,0},{24,8},{1,17},{9,25},{17,1},{25,9},{2,18},{10... | collective-permute-start | bytes 1572872 | tf_op jit(solution)/shard_map/ppermute | solution.py:125
  103.0 23.6 %collective-permute-start.4 = (bf16[4,128,512]{2,1,0:T(8,128)(2,1)S(1)}, bf16[4,128,512]{2,1,0:T(8,128)(2,1)S(1)}, u32[]{:S(2)}, u32[]{:S(2)}) collective-permute-start(bf16[4,128,512]{2,1,0:T(8,128)(2,1)S(1)} %get-tuple-element.30), channel_id=1, source_target_pairs={{0,8},{8,0},{16,24},{24,16},{1,9},{9,1},{17,25},{25,17},{2,10},{10... | collective-permute-start | bytes 1572872 | tf_op jit(solution)/shard_map/ppermute | solution.py:125
  128.4 15.5 %collective-permute-start.14 = (bf16[1024,512]{1,0:T(8,128)(2,1)S(1)}, bf16[1024,512]{1,0:T(8,128)(2,1)S(1)}, u32[]{:S(2)}, u32[]{:S(2)}) collective-permute-start(bf16[1024,512]{1,0:T(8,128)(2,1)S(1)} %broadcast_select_fusion.refs_0_), channel_id=1, source_target_pairs={{0,1},{1,0},{2,3},{3,2},{4,5},{5,4},{6,7},{7,6},{8,9},{9,8},{10,11... | collective-permute-start | bytes 3145736 | tf_op jit(solution)/shard_map/ppermute | solution.py:75
  128.5 10.1 %collective-permute-start.11 = (bf16[2,128,512]{2,1,0:T(8,128)(2,1)S(1)}, bf16[2,128,512]{2,1,0:T(8,128)(2,1)S(1)}, u32[]{:S(2)}, u32[]{:S(2)}) collective-permute-start(bf16[2,128,512]{2,1,0:T(8,128)(2,1)S(1)} %get-tuple-element.39), channel_id=1, source_target_pairs={{0,24},{8,16},{16,8},{24,0},{1,25},{9,17},{17,9},{25,1},{2,26},{10... | collective-permute-start | bytes 786440 | tf_op jit(solution)/shard_map/ppermute | solution.py:125
  130.2 13.5 %collective-permute-start.10 = (bf16[2,128,512]{2,1,0:T(8,128)(2,1)S(1)}, bf16[2,128,512]{2,1,0:T(8,128)(2,1)S(1)}, u32[]{:S(2)}, u32[]{:S(2)}) collective-permute-start(bf16[2,128,512]{2,1,0:T(8,128)(2,1)S(1)} %get-tuple-element.38), channel_id=1, source_target_pairs={{0,16},{8,24},{16,0},{24,8},{1,17},{9,25},{17,1},{25,9},{2,18},{10... | collective-permute-start | bytes 786440 | tf_op jit(solution)/shard_map/ppermute | solution.py:125
  131.5 12.2 %collective-permute-start.9 = (bf16[2,128,512]{2,1,0:T(8,128)(2,1)S(1)}, bf16[2,128,512]{2,1,0:T(8,128)(2,1)S(1)}, u32[]{:S(2)}, u32[]{:S(2)}) collective-permute-start(bf16[2,128,512]{2,1,0:T(8,128)(2,1)S(1)} %get-tuple-element.37), channel_id=1, source_target_pairs={{0,8},{8,0},{16,24},{24,16},{1,9},{9,1},{17,25},{25,17},{2,10},{10... | collective-permute-start | bytes 786440 | tf_op jit(solution)/shard_map/ppermute | solution.py:125
  145.2 9.2 %collective-permute-start.15 = (bf16[2,128,512]{2,1,0:T(8,128)(2,1)S(1)}, bf16[2,128,512]{2,1,0:T(8,128)(2,1)S(1)}, u32[]{:S(2)}, u32[]{:S(2)}) collective-permute-start(bf16[2,128,512]{2,1,0:T(8,128)(2,1)S(1)} %get-tuple-element.44), channel_id=1, source_target_pairs={{0,8},{8,0},{16,24},{24,16},{1,9},{9,1},{17,25},{25,17},{2,10},{10... | collective-permute-start | bytes 786440 | tf_op jit(solution)/shard_map/ppermute | solution.py:125
  146.7 13.6 %collective-permute-start.16 = (bf16[2,128,512]{2,1,0:T(8,128)(2,1)S(1)}, bf16[2,128,512]{2,1,0:T(8,128)(2,1)S(1)}, u32[]{:S(2)}, u32[]{:S(2)}) collective-permute-start(bf16[2,128,512]{2,1,0:T(8,128)(2,1)S(1)} %get-tuple-element.45), channel_id=1, source_target_pairs={{0,16},{8,24},{16,0},{24,8},{1,17},{9,25},{17,1},{25,9},{2,18},{10... | collective-permute-start | bytes 786440 | tf_op jit(solution)/shard_map/ppermute | solution.py:125
  147.4 12.9 %collective-permute-start.17 = (bf16[2,128,512]{2,1,0:T(8,128)(2,1)S(1)}, bf16[2,128,512]{2,1,0:T(8,128)(2,1)S(1)}, u32[]{:S(2)}, u32[]{:S(2)}) collective-permute-start(bf16[2,128,512]{2,1,0:T(8,128)(2,1)S(1)} %get-tuple-element.46), channel_id=1, source_target_pairs={{0,24},{8,16},{16,8},{24,0},{1,25},{9,17},{17,9},{25,1},{2,26},{10... | collective-permute-start | bytes 786440 | tf_op jit(solution)/shard_map/ppermute | solution.py:125

commit v9 on v5

--- a/solution.py
+++ b/solution.py
@@ -23,17 +23,18 @@
             out_ref[s, k] = jnp.concatenate(piece, axis=1)
 
 
-def product_kernel(count, core_ref, panel_ref, *refs):
-    blocks, outs = refs[: 2 * count], refs[2 * count :]
+def product_kernel(sets, core_ref, panel_ref, *refs):
+    core = core_ref[0]
+    blocks, outs = refs[: 2 * sets], refs[2 * sets :]
+    size = len(outs) // sets
     rows = outs[0].shape[1]
-    core = core_ref[0]
-    for m in range(count):
+    for m in range(sets):
+        to = outs[m * size : (m + 1) * size]
         for c in range(2):
-            n = 2 * m + (core ^ c)
             prod = jnp.dot(panel_ref[...], blocks[2 * m + c][...], preferred_element_type=F32)
-            outs[0][n] = prod[:rows]
-            for t in range(1, len(outs)):
-                outs[t][n] = prod[t * rows : (t + 1) * rows].astype(BF16)
+            to[0][core ^ c] = prod[:rows]
+            for t in range(1, size):
+                to[t][core ^ c] = prod[t * rows : (t + 1) * rows].astype(BF16)
 
 
 def turn_kernel(sizes, ncol, slot_ref, *refs):
@@ -109,16 +110,17 @@
         panel = lax.all_to_all(blocks, "col", 0, 0, tiled=True)
         panel = jnp.transpose(panel, (3, 1, 0, 2)).reshape(nrow * rows, kk * v)
 
-        def product(pairs):
-            n = 2 * len(pairs)
-            sent = [jax.ShapeDtypeStruct((n, rows, v), BF16)] * (nrow - 1)
-            return pl.pallas_call(
-                functools.partial(product_kernel, len(pairs)),
-                out_shape=[jax.ShapeDtypeStruct((n, rows, v), F32)] + sent,
-                in_specs=[SMEM] + [VMEM] * (1 + n),
-                out_specs=[VMEM] * nrow,
+        def product(*pairs):
+            sets = len(pairs)
+            sent = [jax.ShapeDtypeStruct((2, rows, v), BF16)] * (nrow - 1)
+            parts = pl.pallas_call(
+                functools.partial(product_kernel, sets),
+                out_shape=([jax.ShapeDtypeStruct((2, rows, v), F32)] + sent) * sets,
+                in_specs=[SMEM] + [VMEM] * (1 + 2 * sets),
+                out_specs=[VMEM] * (nrow * sets),
                 compiler_params=PARAMS,
             )(core, panel, *[x for pair in pairs for x in pair])
+            return [parts[m * nrow : (m + 1) * nrow] for m in range(sets)]
 
         def exchange(parts):
             return [parts[0]] + [
@@ -135,22 +137,25 @@
         if line:
             x1, y2, blocks = lax.optimization_barrier((x1, y2, blocks))
             y3, e2 = along(x1, swap), along(y2, outward)
-            parts = product([own, (x1, across(x1))])
-            groups = [exchange(parts)]
-            e3 = along(after(y3, *parts), outward)
-            for inner, outer in ((y2, e2), (y3, e3)):
-                groups[-1] = [summed(groups[-1])]
-                x = jnp.where(end, after(outer, *parts), inner)
-                parts = product([(after(x, groups[-1][0]), across(x))])
-                groups.append(exchange(parts))
+            parts, parts1 = product(own, (x1, across(x1)))
+            sums = [summed(exchange(parts))]
+            e3 = along(after(y3, sums[0]), outward)
+            sums.append(summed(exchange(parts1)))
+            x2 = jnp.where(end, e2, y2)
+            group = exchange(product((after(x2, sums[1]), across(x2)))[0])
+            sums.append(summed(group))
+            x3 = jnp.where(end, after(e3, *group[1:]), y3)
+            last = exchange(product((x3, across(x3)))[0])
             slots = [z, z ^ 1, jnp.where(end, z ^ 2, 3 - z), jnp.where(end, 3 - z, z ^ 2)]
         else:
-            groups = [exchange(product([own]))]
+            last = exchange(product(own)[0])
+            sums = []
             for m in range(1, nz):
-                groups[-1] = [summed(groups[-1])]
+                sums.append(summed(last))
                 x = along(w, [(a, a ^ m) for a in range(nz)])
-                groups.append(exchange(product([(after(x, groups[-1][0]), across(x))])))
+                last = exchange(product((after(x, sums[-1]), across(x)))[0])
             slots = [z ^ m for m in range(nz)]
+        groups = [[x] for x in sums] + [last]
 
         sizes = [len(g) for g in groups]
         first, turned = pl.pallas_call(

time: 170 us -> 163 us (0.959)
  waiting for transfers between devices: 93.4 us -> 83 us
  starting transfers between devices: 25 us -> 28.5 us
  blocking collectives: 35 us -> 32.8 us
    ppermute x9 -> x12, waiting for transfers between devices: 46.2 us -> 37.2 us  [exchange(): lax.ppermute(parts[t], 'row', [(r, r ^ t) for r in range(nrow)])]
    ppermute x5, waiting for transfers between devices: 23 us -> 19 us  [along(): lax.ppermute(x, 'col', [(2 * a + c, 2 * b + c) for a, b in pairs for c in...]
    ppermute x9 -> x12, starting transfers between devices: 10.7 us -> 14.2 us  [exchange(): lax.ppermute(parts[t], 'row', [(r, r ^ t) for r in range(nrow)])]
    ppermute x4, waiting for transfers between devices: 0.01 us -> 2.56 us  [across(): return lax.ppermute(x, 'col', [(s, s ^ 1) for s in range(ncol)])]
    all_to_all x1, blocking collectives: 35 us -> 32.8 us  [local(): second = lax.all_to_all(turned, ('row', 'col'), 0, 0, tiled=True)]
  transfers between devices with their start and end apart: 19 -> 22, of which waited for: 12 -> 15; matrix products, arithmetic and copies ran while one was open for 3% -> 3% of each run, Pallas kernels for 4% -> 4%
where the time goes in v9:
time: 163 us; the launch traced here: 162 us
  waiting for transfers between devices  83 us (51%)
  blocking collectives  32.8 us (20%)
  starting transfers between devices  28.5 us (17%)
  Pallas kernels  10.1 us (6%)
  local copies, waits for them, and re-layouts  5.21 us (3%)
  other arithmetic  2.7 us (2%)
    ppermute x12, waiting for transfers between devices, exchange(): lax.ppermute(parts[t], 'row', [(r, r ^ t) for r in range(nrow)])  37.2 us
    all_to_all x1, blocking collectives, local(): second = lax.all_to_all(turned, ('row', 'col'), 0, 0, tiled=True)  32.8 us
    all_to_all x1, waiting for transfers between devices, local(): panel = lax.all_to_all(blocks, 'col', 0, 0, tiled=True)  24.1 us
    ppermute x5, waiting for transfers between devices, along(): lax.ppermute(x, 'col', [(2 * a + c, 2 * b + c) for a, b in pairs for c in...  19 us
    ppermute x12, starting transfers between devices, exchange(): lax.ppermute(parts[t], 'row', [(r, r ^ t) for r in range(nrow)])  14.2 us
    ppermute x5, starting transfers between devices, along(): lax.ppermute(x, 'col', [(2 * a + c, 2 * b + c) for a, b in pairs for c in...  8.86 us
    pallas_call x3, Pallas kernels, product(): pl.pallas_call(functools.partial(product_kernel, sets), out_shape=([jax.S...  6.37 us
    all_to_all x1, starting transfers between devices, local(): panel = lax.all_to_all(blocks, 'col', 0, 0, tiled=True)  4.84 us
  transfers between devices with their start and end apart: 22, of which 15 were waited for; matrix products, arithmetic and copies ran while one was open for 3% of the time, Pallas kernels for 4%

profile of v9, /device:TPU:0, one launch (start us, length us, event | category | flops | bytes accessed | tf_op | source)
XLA Modules:
  0.0 162.4 jit_solution(3979862044465788825)
XLA Ops:
  0.0 3.0 %collective-permute-start.1 = (bf16[1024,512]{1,0:T(8,128)(2,1)}, bf16[1024,512]{1,0:T(8,128)(2,1)S(1)}, u32[]{:S(2)}, u32[]{:S(2)}) collective-permute-start(bf16[1024,512]{1,0:T(8,128)(2,1)} %bitcast.9), channel_id=1, source_target_pairs={{0,2},{1,3},{2,0},{3,1},{4,6},{5,7},{6,4},{7,5},{8,10},{9,11},{10,... | collective-permute-start | bytes 3145736 | tf_op jit(solution)/shard_map/ppermute | solution.py:79
  3.0 1.6 %collective-permute-start.2 = (bf16[1024,512]{1,0:T(8,128)(2,1)}, bf16[1024,512]{1,0:T(8,128)(2,1)}, u32[]{:S(2)}, u32[]{:S(2)}) collective-permute-start(bf16[1024,512]{1,0:T(8,128)(2,1)} %bitcast.10), channel_id=1, source_target_pairs={{2,4},{3,5},{4,2},{5,3},{10,12},{11,13},{12,10},{13,11},{18,20},{1... | collective-permute-start | bytes 3145736 | tf_op jit(solution)/shard_map/ppermute | solution.py:79
  7.2 4.8 %all-to-all-start = ((bf16[8,2,64,512]{3,2,1,0:T(8,128)(2,1)}), bf16[8,2,64,512]{3,2,1,0:T(8,128)(2,1)S(1)}, u32[]{:S(2)}, u32[]{:S(2)}) async-start(bf16[8,2,64,512]{3,2,1,0:T(8,128)(2,1)} %shard_map.28), calls=%async_computation | async-start | bytes 2097152 | tf_op jit(solution)/shard_map/all_to_all | solution.py:110
  12.5 14.7 %collective-permute-done.1.refs_2_ = bf16[1024,512]{1,0:T(8,128)(2,1)S(1)} collective-permute-done((bf16[1024,512]{1,0:T(8,128)(2,1)}, bf16[1024,512]{1,0:T(8,128)(2,1)S(1)}, u32[]{:S(2)}, u32[]{:S(2)}) %collective-permute-start.1) | collective-permute-done | bytes 1048608 | tf_op jit(solution)/shard_map/ppermute | solution.py:79
  28.5 1.6 %collective-permute-start.15 = (bf16[1024,512]{1,0:T(8,128)(2,1)S(1)}, bf16[1024,512]{1,0:T(8,128)(2,1)}, u32[]{:S(2)}, u32[]{:S(2)}) collective-permute-start(bf16[1024,512]{1,0:T(8,128)(2,1)S(1)} %collective-permute-done.1.refs_2_), channel_id=1, source_target_pairs={{2,4},{3,5},{4,2},{5,3},{10,12},{11,13},{12,10},{13,11},{18,20},{1... | collective-permute-start | bytes 3145736 | tf_op jit(solution)/shard_map/ppermute | solution.py:79
  30.2 24.1 %all-to-all-done = bf16[8,2,64,512]{3,2,1,0:T(8,128)(2,1)S(1)} async-done(((bf16[8,2,64,512]{3,2,1,0:T(8,128)(2,1)}), bf16[8,2,64,512]{3,2,1,0:T(8,128)(2,1)S(1)}, u32[]{:S(2)}, u32[]{:S(2)}) %all-to-all-start) | async-done | bytes 1048608 | tf_op jit(solution)/shard_map/all_to_all | solution.py:110
  55.3 1.5 copy.5.panel_ref
  56.8 3.9 %shard_map.29 = (f32[2,128,512]{2,1,0:T(8,128)S(1)}, bf16[2,128,512]{2,1,0:T(8,128)(2,1)S(1)}, bf16[2,128,512]{2,1,0:T(8,128)(2,1)S(1)}, bf16[2,128,512]{2,1,0:T...) custom-call(s32[1]{0:T(128)} %bitcast.4.core_ref, ...), custom_call_target="tpu_custom_call" | custom-call | tf_op jit(solution)/shard_map/pallas_call | solution.py:116
  60.7 2.5 %collective-permute-start.6 = (bf16[2,128,512]{2,1,0:T(8,128)(2,1)S(1)}, bf16[2,128,512]{2,1,0:T(8,128)(2,1)S(1)}, u32[]{:S(2)}, u32[]{:S(2)}) collective-permute-start(bf16[2,128,512]{2,1,0:T(8,128)(2,1)S(1)} %get-tuple-element.32), channel_id=1, source_target_pairs={{0,24},{8,16},{16,8},{24,0},{1,25},{9,17},{17,9},{25,1},{2,26},{10... | collective-permute-start | bytes 786440 | tf_op jit(solution)/shard_map/ppermute | solution.py:127
  64.3 4.4 %collective-permute-done.10 = bf16[1024,512]{1,0:T(8,128)(2,1)} collective-permute-done((bf16[1024,512]{1,0:T(8,128)(2,1)}, bf16[1024,512]{1,0:T(8,128)(2,1)}, u32[]{:S(2)}, u32[]{:S(2)}) %collective-permute-start.10) | collective-permute-done | bytes 1048608 | tf_op jit(solution)/shard_map/ppermute | solution.py:79
  70.6 2.8 %collective-permute-done.5 = bf16[2,128,512]{2,1,0:T(8,128)(2,1)S(1)} collective-permute-done((bf16[2,128,512]{2,1,0:T(8,128)(2,1)S(1)}, bf16[2,128,512]{2,1,0:T(8,128)(2,1)S(1)}, u32[]{:S(2)}, u32[]{:S(2)}) %collective-permute-start.5) | collective-permute-done | bytes 262176 | tf_op jit(solution)/shard_map/ppermute | solution.py:127
  74.9 1.7 %collective-permute-start.9 = (bf16[2,128,512]{2,1,0:T(8,128)(2,1)S(1)}, bf16[2,128,512]{2,1,0:T(8,128)(2,1)S(1)}, u32[]{:S(2)}, u32[]{:S(2)}) collective-permute-start(bf16[2,128,512]{2,1,0:T(8,128)(2,1)S(1)} %get-tuple-element.36), channel_id=1, source_target_pairs={{0,24},{8,16},{16,8},{24,0},{1,25},{9,17},{17,9},{25,1},{2,26},{10... | collective-permute-start | bytes 786440 | tf_op jit(solution)/shard_map/ppermute | solution.py:127
  78.4 6.7 %collective-permute-done.9 = bf16[2,128,512]{2,1,0:T(8,128)(2,1)S(1)} collective-permute-done((bf16[2,128,512]{2,1,0:T(8,128)(2,1)S(1)}, bf16[2,128,512]{2,1,0:T(8,128)(2,1)S(1)}, u32[]{:S(2)}, u32[]{:S(2)}) %collective-permute-start.9) | collective-permute-done | bytes 262176 | tf_op jit(solution)/shard_map/ppermute | solution.py:127
  85.1 3.3 %collective-permute-done.8 = bf16[2,128,512]{2,1,0:T(8,128)(2,1)S(1)} collective-permute-done((bf16[2,128,512]{2,1,0:T(8,128)(2,1)S(1)}, bf16[2,128,512]{2,1,0:T(8,128)(2,1)S(1)}, u32[]{:S(2)}, u32[]{:S(2)}) %collective-permute-start.8) | collective-permute-done | bytes 262176 | tf_op jit(solution)/shard_map/ppermute | solution.py:127
  92.0 1.4 collective-permute-start.14
  93.4 1.4 collective-permute-start.13
  95.5 6.7 %collective-permute-done.14 = bf16[2,128,512]{2,1,0:T(8,128)(2,1)S(1)} collective-permute-done((bf16[2,128,512]{2,1,0:T(8,128)(2,1)S(1)}, bf16[2,128,512]{2,1,0:T(8,128)(2,1)S(1)}, u32[]{:S(2)}, u32[]{:S(2)}) %collective-permute-start.14) | collective-permute-done | bytes 262176 | tf_op jit(solution)/shard_map/ppermute | solution.py:127
  102.2 3.9 %collective-permute-done.13 = bf16[2,128,512]{2,1,0:T(8,128)(2,1)S(1)} collective-permute-done((bf16[2,128,512]{2,1,0:T(8,128)(2,1)S(1)}, bf16[2,128,512]{2,1,0:T(8,128)(2,1)S(1)}, u32[]{:S(2)}, u32[]{:S(2)}) %collective-permute-start.13) | collective-permute-done | bytes 262176 | tf_op jit(solution)/shard_map/ppermute | solution.py:127
  107.6 2.6 %collective-permute-done.17.refs_1_ = bf16[1024,512]{1,0:T(8,128)(2,1)S(1)} collective-permute-done((bf16[1024,512]{1,0:T(8,128)(2,1)S(1)}, bf16[1024,512]{1,0:T(8,128)(2,1)S(1)}, u32[]{:S(2)}, u32[]{:S(2)}) %collective-permute-start.17) | collective-permute-done | bytes 1048608 | tf_op jit(solution)/shard_map/ppermute | solution.py:76
  111.4 2.0 %collective-permute-start.18 = (bf16[2,128,512]{2,1,0:T(8,128)(2,1)S(1)}, bf16[2,128,512]{2,1,0:T(8,128)(2,1)S(1)}, u32[]{:S(2)}, u32[]{:S(2)}) collective-permute-start(bf16[2,128,512]{2,1,0:T(8,128)(2,1)S(1)} %get-tuple-element.46), channel_id=1, source_target_pairs={{0,8},{8,0},{16,24},{24,16},{1,9},{9,1},{17,25},{25,17},{2,10},{10... | collective-permute-start | bytes 786440 | tf_op jit(solution)/shard_map/ppermute | solution.py:127
  115.2 5.4 %collective-permute-done.18.refs_4_ = bf16[2,128,512]{2,1,0:T(8,128)(2,1)S(1)} collective-permute-done((bf16[2,128,512]{2,1,0:T(8,128)(2,1)S(1)}, bf16[2,128,512]{2,1,0:T(8,128)(2,1)S(1)}, u32[]{:S(2)}, u32[]{:S(2)}) %collective-permute-start.18) | collective-permute-done | bytes 262176 | tf_op jit(solution)/shard_map/ppermute | solution.py:127
  120.6 6.5 %collective-permute-done.19.refs_5_ = bf16[2,128,512]{2,1,0:T(8,128)(2,1)S(1)} collective-permute-done((bf16[2,128,512]{2,1,0:T(8,128)(2,1)S(1)}, bf16[2,128,512]{2,1,0:T(8,128)(2,1)S(1)}, u32[]{:S(2)}, u32[]{:S(2)}) %collective-permute-start.19) | collective-permute-done | bytes 262176 | tf_op jit(solution)/shard_map/ppermute | solution.py:127
  128.1 32.8 %all_to_all.10.second_ref = bf16[32,2,64,128]{3,2,1,0:T(8,128)(2,1)S(1)} all-to-all(bf16[32,2,64,128]{3,2,1,0:T(8,128)(2,1)S(1)} %get-tuple-element.50), channel_id=1, replica_groups=mesh['row'=4,'col'=8] {'row','col'}, dimensions={0} | all-to-all | bytes 2097152 | tf_op jit(solution)/shard_map/all_to_all | solution.py:171
  160.9 1.5 shard_map.33
  (57 shorter events, 21.3 us)
Async XLA Ops:
  0.0 27.2 %collective-permute-start.1 = (bf16[1024,512]{1,0:T(8,128)(2,1)}, bf16[1024,512]{1,0:T(8,128)(2,1)S(1)}, u32[]{:S(2)}, u32[]{:S(2)}) collective-permute-start(bf16[1024,512]{1,0:T(8,128)(2,1)} %bitcast.9), channel_id=1, source_target_pairs={{0,2},{1,3},{2,0},{3,1},{4,6},{5,7},{6,4},{7,5},{8,10},{9,11},{10,... | collective-permute-start | bytes 3145736 | tf_op jit(solution)/shard_map/ppermute | solution.py:79
  3.0 24.2 %collective-permute-start.2 = (bf16[1024,512]{1,0:T(8,128)(2,1)}, bf16[1024,512]{1,0:T(8,128)(2,1)}, u32[]{:S(2)}, u32[]{:S(2)}) collective-permute-start(bf16[1024,512]{1,0:T(8,128)(2,1)} %bitcast.10), channel_id=1, source_target_pairs={{2,4},{3,5},{4,2},{5,3},{10,12},{11,13},{12,10},{13,11},{18,20},{1... | collective-permute-start | bytes 3145736 | tf_op jit(solution)/shard_map/ppermute | solution.py:79
  7.2 47.1 %all-to-all-start = ((bf16[8,2,64,512]{3,2,1,0:T(8,128)(2,1)}), bf16[8,2,64,512]{3,2,1,0:T(8,128)(2,1)S(1)}, u32[]{:S(2)}, u32[]{:S(2)}) async-start(bf16[8,2,64,512]{3,2,1,0:T(8,128)(2,1)} %shard_map.28), calls=%async_computation | async-start | bytes 2097152 | tf_op jit(solution)/shard_map/all_to_all | solution.py:110
  12.0 44.8 %collective-permute-start = (bf16[1024,512]{1,0:T(8,128)(2,1)S(1)}, bf16[1024,512]{1,0:T(8,128)(2,1)}, u32[]{:S(2)}, u32[]{:S(2)}) collective-permute-start(bf16[1024,512]{1,0:T(8,128)(2,1)S(1)} %bitcast.11), channel_id=1, source_target_pairs={{0,1},{1,0},{2,3},{3,2},{4,5},{5,4},{6,7},{7,6},{8,9},{9,8},{10,11... | collective-permute-start | bytes 3145736 | tf_op jit(solution)/shard_map/ppermute | solution.py:76
  27.2 29.6 %collective-permute-start.3 = (bf16[1024,512]{1,0:T(8,128)(2,1)S(1)}, bf16[1024,512]{1,0:T(8,128)(2,1)}, u32[]{:S(2)}, u32[]{:S(2)}) collective-permute-start(bf16[1024,512]{1,0:T(8,128)(2,1)S(1)} %collective-permute-done.1.refs_2_), channel_id=1, source_target_pairs={{0,1},{1,0},{2,3},{3,2},{4,5},{5,4},{6,7},{7,6},{8,9},{9,8},{10,11... | collective-permute-start | bytes 3145736 | tf_op jit(solution)/shard_map/ppermute | solution.py:76
  27.2 41.4 %collective-permute-start.10 = (bf16[1024,512]{1,0:T(8,128)(2,1)}, bf16[1024,512]{1,0:T(8,128)(2,1)}, u32[]{:S(2)}, u32[]{:S(2)}) collective-permute-start(bf16[1024,512]{1,0:T(8,128)(2,1)} %collective-permute-done.2), channel_id=1, source_target_pairs={{2,0},{3,1},{4,6},{5,7},{10,8},{11,9},{12,14},{13,15},{18,16},{19,... | collective-permute-start | bytes 3145736 | tf_op jit(solution)/shard_map/ppermute | solution.py:79
  28.5 45.1 %collective-permute-start.15 = (bf16[1024,512]{1,0:T(8,128)(2,1)S(1)}, bf16[1024,512]{1,0:T(8,128)(2,1)}, u32[]{:S(2)}, u32[]{:S(2)}) collective-permute-start(bf16[1024,512]{1,0:T(8,128)(2,1)S(1)} %collective-permute-done.1.refs_2_), channel_id=1, source_target_pairs={{2,4},{3,5},{4,2},{5,3},{10,12},{11,13},{12,10},{13,11},{18,20},{1... | collective-permute-start | bytes 3145736 | tf_op jit(solution)/shard_map/ppermute | solution.py:79
  60.7 9.8 %collective-permute-start.6 = (bf16[2,128,512]{2,1,0:T(8,128)(2,1)S(1)}, bf16[2,128,512]{2,1,0:T(8,128)(2,1)S(1)}, u32[]{:S(2)}, u32[]{:S(2)}) collective-permute-start(bf16[2,128,512]{2,1,0:T(8,128)(2,1)S(1)} %get-tuple-element.32), channel_id=1, source_target_pairs={{0,24},{8,16},{16,8},{24,0},{1,25},{9,17},{17,9},{25,1},{2,26},{10... | collective-permute-start | bytes 786440 | tf_op jit(solution)/shard_map/ppermute | solution.py:127
  63.2 10.1 %collective-permute-start.5 = (bf16[2,128,512]{2,1,0:T(8,128)(2,1)S(1)}, bf16[2,128,512]{2,1,0:T(8,128)(2,1)S(1)}, u32[]{:S(2)}, u32[]{:S(2)}) collective-permute-start(bf16[2,128,512]{2,1,0:T(8,128)(2,1)S(1)} %get-tuple-element.31), channel_id=1, source_target_pairs={{0,16},{8,24},{16,0},{24,8},{1,17},{9,25},{17,1},{25,9},{2,18},{10... | collective-permute-start | bytes 786440 | tf_op jit(solution)/shard_map/ppermute | solution.py:127
  63.7 9.7 %collective-permute-start.4 = (bf16[2,128,512]{2,1,0:T(8,128)(2,1)S(1)}, bf16[2,128,512]{2,1,0:T(8,128)(2,1)S(1)}, u32[]{:S(2)}, u32[]{:S(2)}) collective-permute-start(bf16[2,128,512]{2,1,0:T(8,128)(2,1)S(1)} %get-tuple-element.30), channel_id=1, source_target_pairs={{0,8},{8,0},{16,24},{24,16},{1,9},{9,1},{17,25},{25,17},{2,10},{10... | collective-permute-start | bytes 786440 | tf_op jit(solution)/shard_map/ppermute | solution.py:127
  70.0 20.0 %collective-permute-start.11 = (bf16[1024,512]{1,0:T(8,128)(2,1)S(1)}, bf16[1024,512]{1,0:T(8,128)(2,1)S(1)}, u32[]{:S(2)}, u32[]{:S(2)}) collective-permute-start(bf16[1024,512]{1,0:T(8,128)(2,1)S(1)} %broadcast_select_fusion.1.refs_0_), channel_id=1, source_target_pairs={{0,1},{1,0},{2,3},{3,2},{4,5},{5,4},{6,7},{7,6},{8,9},{9,8},{10,11... | collective-permute-start | bytes 3145736 | tf_op jit(solution)/shard_map/ppermute | solution.py:76
  73.6 33.3 %collective-permute-start.16 = (bf16[1024,512]{1,0:T(8,128)(2,1)}, bf16[1024,512]{1,0:T(8,128)(2,1)S(1)}, u32[]{:S(2)}, u32[]{:S(2)}) collective-permute-start(bf16[1024,512]{1,0:T(8,128)(2,1)} %collective-permute-done.15), channel_id=1, source_target_pairs={{2,0},{3,1},{4,6},{5,7},{10,8},{11,9},{12,14},{13,15},{18,16},{19,... | collective-permute-start | bytes 3145736 | tf_op jit(solution)/shard_map/ppermute | solution.py:79
  74.9 10.3 %collective-permute-start.9 = (bf16[2,128,512]{2,1,0:T(8,128)(2,1)S(1)}, bf16[2,128,512]{2,1,0:T(8,128)(2,1)S(1)}, u32[]{:S(2)}, u32[]{:S(2)}) collective-permute-start(bf16[2,128,512]{2,1,0:T(8,128)(2,1)S(1)} %get-tuple-element.36), channel_id=1, source_target_pairs={{0,24},{8,16},{16,8},{24,0},{1,25},{9,17},{17,9},{25,1},{2,26},{10... | collective-permute-start | bytes 786440 | tf_op jit(solution)/shard_map/ppermute | solution.py:127
  76.6 11.9 %collective-permute-start.8 = (bf16[2,128,512]{2,1,0:T(8,128)(2,1)S(1)}, bf16[2,128,512]{2,1,0:T(8,128)(2,1)S(1)}, u32[]{:S(2)}, u32[]{:S(2)}) collective-permute-start(bf16[2,128,512]{2,1,0:T(8,128)(2,1)S(1)} %get-tuple-element.35), channel_id=1, source_target_pairs={{0,16},{8,24},{16,0},{24,8},{1,17},{9,25},{17,1},{25,9},{2,18},{10... | collective-permute-start | bytes 786440 | tf_op jit(solution)/shard_map/ppermute | solution.py:127
  77.9 11.2 %collective-permute-start.7 = (bf16[2,128,512]{2,1,0:T(8,128)(2,1)S(1)}, bf16[2,128,512]{2,1,0:T(8,128)(2,1)S(1)}, u32[]{:S(2)}, u32[]{:S(2)}) collective-permute-start(bf16[2,128,512]{2,1,0:T(8,128)(2,1)S(1)} %get-tuple-element.34), channel_id=1, source_target_pairs={{0,8},{8,0},{16,24},{24,16},{1,9},{9,1},{17,25},{25,17},{2,10},{10... | collective-permute-start | bytes 786440 | tf_op jit(solution)/shard_map/ppermute | solution.py:127
  92.0 10.2 %collective-permute-start.14 = (bf16[2,128,512]{2,1,0:T(8,128)(2,1)S(1)}, bf16[2,128,512]{2,1,0:T(8,128)(2,1)S(1)}, u32[]{:S(2)}, u32[]{:S(2)}) collective-permute-start(bf16[2,128,512]{2,1,0:T(8,128)(2,1)S(1)} %get-tuple-element.42), channel_id=1, source_target_pairs={{0,24},{8,16},{16,8},{24,0},{1,25},{9,17},{17,9},{25,1},{2,26},{10... | collective-permute-start | bytes 786440 | tf_op jit(solution)/shard_map/ppermute | solution.py:127
  93.4 12.7 %collective-permute-start.13 = (bf16[2,128,512]{2,1,0:T(8,128)(2,1)S(1)}, bf16[2,128,512]{2,1,0:T(8,128)(2,1)S(1)}, u32[]{:S(2)}, u32[]{:S(2)}) collective-permute-start(bf16[2,128,512]{2,1,0:T(8,128)(2,1)S(1)} %get-tuple-element.41), channel_id=1, source_target_pairs={{0,16},{8,24},{16,0},{24,8},{1,17},{9,25},{17,1},{25,9},{2,18},{10... | collective-permute-start | bytes 786440 | tf_op jit(solution)/shard_map/ppermute | solution.py:127
  94.8 11.9 %collective-permute-start.12 = (bf16[2,128,512]{2,1,0:T(8,128)(2,1)S(1)}, bf16[2,128,512]{2,1,0:T(8,128)(2,1)S(1)}, u32[]{:S(2)}, u32[]{:S(2)}) collective-permute-start(bf16[2,128,512]{2,1,0:T(8,128)(2,1)S(1)} %get-tuple-element.40), channel_id=1, source_target_pairs={{0,8},{8,0},{16,24},{24,16},{1,9},{9,1},{17,25},{25,17},{2,10},{10... | collective-permute-start | bytes 786440 | tf_op jit(solution)/shard_map/ppermute | solution.py:127
  107.5 2.7 %collective-permute-start.17 = (bf16[1024,512]{1,0:T(8,128)(2,1)S(1)}, bf16[1024,512]{1,0:T(8,128)(2,1)S(1)}, u32[]{:S(2)}, u32[]{:S(2)}) collective-permute-start(bf16[1024,512]{1,0:T(8,128)(2,1)S(1)} %broadcast_select_fusion.refs_0_), channel_id=1, source_target_pairs={{0,1},{1,0},{2,3},{3,2},{4,5},{5,4},{6,7},{7,6},{8,9},{9,8},{10,11... | collective-permute-start | bytes 3145736 | tf_op jit(solution)/shard_map/ppermute | solution.py:76
  107.6 7.4 %copy-start.10 = (bf16[2,128,512]{2,1,0:T(8,128)(2,1)S(1)}, bf16[2,128,512]{2,1,0:T(8,128)(2,1)}, u32[]{:S(2)}) copy-start(bf16[2,128,512]{2,1,0:T(8,128)(2,1)} %copy-done.9) | copy-start | bytes 786436
  111.4 9.2 %collective-permute-start.18 = (bf16[2,128,512]{2,1,0:T(8,128)(2,1)S(1)}, bf16[2,128,512]{2,1,0:T(8,128)(2,1)S(1)}, u32[]{:S(2)}, u32[]{:S(2)}) collective-permute-start(bf16[2,128,512]{2,1,0:T(8,128)(2,1)S(1)} %get-tuple-element.46), channel_id=1, source_target_pairs={{0,8},{8,0},{16,24},{24,16},{1,9},{9,1},{17,25},{25,17},{2,10},{10... | collective-permute-start | bytes 786440 | tf_op jit(solution)/shard_map/ppermute | solution.py:127
  113.5 13.7 %collective-permute-start.19 = (bf16[2,128,512]{2,1,0:T(8,128)(2,1)S(1)}, bf16[2,128,512]{2,1,0:T(8,128)(2,1)S(1)}, u32[]{:S(2)}, u32[]{:S(2)}) collective-permute-start(bf16[2,128,512]{2,1,0:T(8,128)(2,1)S(1)} %get-tuple-element.47), channel_id=1, source_target_pairs={{0,16},{8,24},{16,0},{24,8},{1,17},{9,25},{17,1},{25,9},{2,18},{10... | collective-permute-start | bytes 786440 | tf_op jit(solution)/shard_map/ppermute | solution.py:127
  114.0 13.1 %collective-permute-start.20 = (bf16[2,128,512]{2,1,0:T(8,128)(2,1)S(1)}, bf16[2,128,512]{2,1,0:T(8,128)(2,1)S(1)}, u32[]{:S(2)}, u32[]{:S(2)}) collective-permute-start(bf16[2,128,512]{2,1,0:T(8,128)(2,1)S(1)} %get-tuple-element.48), channel_id=1, source_target_pairs={{0,24},{8,16},{16,8},{24,0},{1,25},{9,17},{17,9},{25,1},{2,26},{10... | collective-permute-start | bytes 786440 | tf_op jit(solution)/shard_map/ppermute | solution.py:127
  115.0 12.1 %copy-start.1 = (bf16[2,128,512]{2,1,0:T(8,128)(2,1)S(1)}, bf16[2,128,512]{2,1,0:T(8,128)(2,1)}, u32[]{:S(2)}) copy-start(bf16[2,128,512]{2,1,0:T(8,128)(2,1)} %add_convert_fusion.1.refs_1_) | copy-start | bytes 786436
  (9 other events, 35.0 us)

commit v10 on v9

--- a/solution.py
+++ b/solution.py
@@ -35,6 +35,15 @@
             to[0][core ^ c] = prod[:rows]
             for t in range(1, size):
                 to[t][core ^ c] = prod[t * rows : (t + 1) * rows].astype(BF16)
+
+
+def first_product_kernel(core_ref, raw_ref, here_ref, there_ref, panel_ref, *outs):
+    ncol, kk, cs, wide = raw_ref.shape
+    v = ncol * cs
+    for k in range(kk):
+        part = raw_ref[:, k].reshape(v, wide)
+        panel_ref[:, k * v : (k + 1) * v] = part.T
+    product_kernel(1, core_ref, panel_ref, here_ref, there_ref, *outs)
 
 
 def turn_kernel(sizes, ncol, slot_ref, *refs):
@@ -93,12 +102,14 @@
 
         w = intermediate.reshape(kk * v, v)
         line = nz == 4
+        own = (w, across(w))
         if line:
             swap = [(1, 2), (2, 1)]
             outward = [(1, 0), (2, 3)]
             x1 = along(w, [(a, a ^ 1) for a in range(nz)])
             y2 = along(w, swap)
-        own = (w, across(w))
+            pair1 = (x1, across(x1))
+            own = (w, after(own[1], pair1[1]))
 
         blocks = pl.pallas_call(
             functools.partial(spread_kernel, nrow, ncol),
@@ -107,20 +118,25 @@
             out_specs=VMEM,
             compiler_params=PARAMS,
         )(row, amplitudes)
-        panel = lax.all_to_all(blocks, "col", 0, 0, tiled=True)
-        panel = jnp.transpose(panel, (3, 1, 0, 2)).reshape(nrow * rows, kk * v)
-
-        def product(*pairs):
-            sets = len(pairs)
-            sent = [jax.ShapeDtypeStruct((2, rows, v), BF16)] * (nrow - 1)
-            parts = pl.pallas_call(
-                functools.partial(product_kernel, sets),
-                out_shape=([jax.ShapeDtypeStruct((2, rows, v), F32)] + sent) * sets,
-                in_specs=[SMEM] + [VMEM] * (1 + 2 * sets),
-                out_specs=[VMEM] * (nrow * sets),
+        raw = lax.all_to_all(blocks, "col", 0, 0, tiled=True)
+        sent = [jax.ShapeDtypeStruct((2, rows, v), BF16)] * (nrow - 1)
+        sent = [jax.ShapeDtypeStruct((2, rows, v), F32)] + sent
+        panel, *parts = pl.pallas_call(
+            first_product_kernel,
+            out_shape=[jax.ShapeDtypeStruct((nrow * rows, kk * v), BF16)] + sent,
+            in_specs=[SMEM] + [VMEM] * 3,
+            out_specs=[VMEM] * (1 + nrow),
+            compiler_params=PARAMS,
+        )(core, raw, *own)
+
+        def product(pair):
+            return pl.pallas_call(
+                functools.partial(product_kernel, 1),
+                out_shape=sent,
+                in_specs=[SMEM] + [VMEM] * 3,
+                out_specs=[VMEM] * nrow,
                 compiler_params=PARAMS,
-            )(core, panel, *[x for pair in pairs for x in pair])
-            return [parts[m * nrow : (m + 1) * nrow] for m in range(sets)]
+            )(core, panel, *pair)
 
         def exchange(parts):
             return [parts[0]] + [
@@ -137,23 +153,23 @@
         if line:
             x1, y2, blocks = lax.optimization_barrier((x1, y2, blocks))
             y3, e2 = along(x1, swap), along(y2, outward)
-            parts, parts1 = product(own, (x1, across(x1)))
             sums = [summed(exchange(parts))]
-            e3 = along(after(y3, sums[0]), outward)
-            sums.append(summed(exchange(parts1)))
+            parts = product(pair1)
+            e3 = along(after(y3, sums[0], *parts), outward)
+            sums.append(summed(exchange(parts)))
             x2 = jnp.where(end, e2, y2)
-            group = exchange(product((after(x2, sums[1]), across(x2)))[0])
+            group = exchange(product((after(x2, sums[1]), across(x2))))
             sums.append(summed(group))
             x3 = jnp.where(end, after(e3, *group[1:]), y3)
-            last = exchange(product((x3, across(x3)))[0])
+            last = exchange(product((x3, across(x3))))
             slots = [z, z ^ 1, jnp.where(end, z ^ 2, 3 - z), jnp.where(end, 3 - z, z ^ 2)]
         else:
-            last = exchange(product(own)[0])
+            last = exchange(parts)
             sums = []
             for m in range(1, nz):
                 sums.append(summed(last))
                 x = along(w, [(a, a ^ m) for a in range(nz)])
-                last = exchange(product((after(x, sums[-1]), across(x)))[0])
+                last = exchange(product((after(x, sums[-1]), across(x))))
             slots = [z ^ m for m in range(nz)]
         groups = [[x] for x in sums] + [last]
 

time: 163 us -> 163 us (level)
  blocking collectives: 32.8 us -> 35.4 us
  waiting for transfers between devices: 83 us -> 80.8 us
    all_to_all x1, blocking collectives: 32.8 us -> 35.4 us  [local(): second = lax.all_to_all(turned, ('row', 'col'), 0, 0, tiled=True)]
    ppermute x12, waiting for transfers between devices: 37.2 us -> 34.9 us  [exchange(): lax.ppermute(parts[t], 'row', [(r, r ^ t) for r in range(nrow)])]
    unnamed x22 -> x26, local copies, waits for them, and re-layouts: 2.66 us -> 4.19 us
    pallas_call x3 -> x4, Pallas kernels: 6.37 us -> 7.49 us  [the longest x3 4.99 us: product(): pl.pallas_call(functools.partial(product_kernel, 1), out_shape=sent, in_s...]
  transfers between devices with their start and end apart: 22 -> 22, of which waited for: 15 -> 12; matrix products, arithmetic and copies ran while one was open for 3% -> 2% of each run, Pallas kernels for 4% -> 5%
where the time goes in v10:
time: 163 us
  waiting for transfers between devices  80.8 us (50%)
  blocking collectives  35.4 us (22%)
  starting transfers between devices  28.5 us (17%)
  Pallas kernels  11.2 us (7%)
  local copies, waits for them, and re-layouts  4.19 us (3%)
  other arithmetic  2.7 us (2%)
    all_to_all x1, blocking collectives, local(): second = lax.all_to_all(turned, ('row', 'col'), 0, 0, tiled=True)  35.4 us
    ppermute x12, waiting for transfers between devices, exchange(): lax.ppermute(parts[t], 'row', [(r, r ^ t) for r in range(nrow)])  34.9 us
    all_to_all x1, waiting for transfers between devices, local(): raw = lax.all_to_all(blocks, 'col', 0, 0, tiled=True)  23 us
    ppermute x5, waiting for transfers between devices, along(): lax.ppermute(x, 'col', [(2 * a + c, 2 * b + c) for a, b in pairs for c in...  20.3 us
    ppermute x12, starting transfers between devices, exchange(): lax.ppermute(parts[t], 'row', [(r, r ^ t) for r in range(nrow)])  14.1 us
    ppermute x5, starting transfers between devices, along(): lax.ppermute(x, 'col', [(2 * a + c, 2 * b + c) for a, b in pairs for c in...  8.87 us
    pallas_call x3, Pallas kernels, product(): pl.pallas_call(functools.partial(product_kernel, 1), out_shape=sent, in_s...  4.99 us
    all_to_all x1, starting transfers between devices, local(): raw = lax.all_to_all(blocks, 'col', 0, 0, tiled=True)  4.84 us
  transfers between devices with their start and end apart: 22, of which 12 were waited for; matrix products, arithmetic and copies ran while one was open for 2% of the time, Pallas kernels for 5%

profile of v10, /device:TPU:0, one launch (start us, length us, event | category | flops | bytes accessed | tf_op | source)
XLA Modules:
  0.0 163.0 jit_solution(9360480052414178330)
XLA Ops:
  0.0 3.0 %collective-permute-start.1 = (bf16[1024,512]{1,0:T(8,128)(2,1)}, bf16[1024,512]{1,0:T(8,128)(2,1)}, u32[]{:S(2)}, u32[]{:S(2)}) collective-permute-start(bf16[1024,512]{1,0:T(8,128)(2,1)} %bitcast.7), channel_id=1, source_target_pairs={{0,2},{1,3},{2,0},{3,1},{4,6},{5,7},{6,4},{7,5},{8,10},{9,11},{10,... | collective-permute-start | bytes 3145736 | tf_op jit(solution)/shard_map/ppermute | solution.py:88
  3.0 1.6 %collective-permute-start.9 = (bf16[1024,512]{1,0:T(8,128)(2,1)}, bf16[1024,512]{1,0:T(8,128)(2,1)}, u32[]{:S(2)}, u32[]{:S(2)}) collective-permute-start(bf16[1024,512]{1,0:T(8,128)(2,1)} %bitcast.8), channel_id=1, source_target_pairs={{2,4},{3,5},{4,2},{5,3},{10,12},{11,13},{12,10},{13,11},{18,20},{1... | collective-permute-start | bytes 3145736 | tf_op jit(solution)/shard_map/ppermute | solution.py:88
  7.2 4.8 %all-to-all-start = ((bf16[8,2,64,512]{3,2,1,0:T(8,128)(2,1)}), bf16[8,2,64,512]{3,2,1,0:T(8,128)(2,1)S(1)}, u32[]{:S(2)}, u32[]{:S(2)}) async-start(bf16[8,2,64,512]{3,2,1,0:T(8,128)(2,1)} %shard_map.28), calls=%async_computation | async-start | bytes 2097152 | tf_op jit(solution)/shard_map/all_to_all | solution.py:121
  12.5 14.8 %collective-permute-done.1.refs_0_ = bf16[1024,512]{1,0:T(8,128)(2,1)} collective-permute-done((bf16[1024,512]{1,0:T(8,128)(2,1)}, bf16[1024,512]{1,0:T(8,128)(2,1)}, u32[]{:S(2)}, u32[]{:S(2)}) %collective-permute-start.1) | collective-permute-done | bytes 1048608 | tf_op jit(solution)/shard_map/ppermute | solution.py:88
  28.6 1.6 %collective-permute-start.15 = (bf16[1024,512]{1,0:T(8,128)(2,1)}, bf16[1024,512]{1,0:T(8,128)(2,1)}, u32[]{:S(2)}, u32[]{:S(2)}) collective-permute-start(bf16[1024,512]{1,0:T(8,128)(2,1)} %collective-permute-done.1.refs_0_), channel_id=1, source_target_pairs={{2,4},{3,5},{4,2},{5,3},{10,12},{11,13},{12,10},{13,11},{18,20},{1... | collective-permute-start | bytes 3145736 | tf_op jit(solution)/shard_map/ppermute | solution.py:88
  31.3 23.0 %all-to-all-done.raw_ref = bf16[8,2,64,512]{3,2,1,0:T(8,128)(2,1)S(1)} async-done(((bf16[8,2,64,512]{3,2,1,0:T(8,128)(2,1)}), bf16[8,2,64,512]{3,2,1,0:T(8,128)(2,1)S(1)}, u32[]{:S(2)}, u32[]{:S(2)}) %all-to-all-start) | async-done | bytes 1048608 | tf_op jit(solution)/shard_map/all_to_all | solution.py:121
  54.3 2.5 %shard_map.29 = (bf16[512,1024]{1,0:T(8,128)(2,1)S(1)}, f32[2,128,512]{2,1,0:T(8,128)S(1)}, bf16[2,128,512]{2,1,0:T(8,128)(2,1)S(1)}, bf16[2,128,512]{2,1,0:T(8,128)(2,1)S(1)}, bf16[2,128,512]{2,1,0:T(8,128)(2,1)S(1)}) custom-call(s32[1]{0:T(128)} %bitcast.4.core_ref, bf16[8,2,64,512]{3,2,1,0:T(8,128)(2,1)S(1)} %all-to-all-done.raw_ref, ...), custom_call_target="tpu_custom_call" | custom-call | tf_op jit(solution)/shard_map/pallas_call | solution.py:124
  56.8 2.5 %collective-permute-start.5 = (bf16[2,128,512]{2,1,0:T(8,128)(2,1)S(1)}, bf16[2,128,512]{2,1,0:T(8,128)(2,1)S(1)}, u32[]{:S(2)}, u32[]{:S(2)}) collective-permute-start(bf16[2,128,512]{2,1,0:T(8,128)(2,1)S(1)} %get-tuple-element.34), channel_id=1, source_target_pairs={{0,24},{8,16},{16,8},{24,0},{1,25},{9,17},{17,9},{25,1},{2,26},{10... | collective-permute-start | bytes 786440 | tf_op jit(solution)/shard_map/ppermute | solution.py:143
  60.3 5.5 %collective-permute-done.10 = bf16[1024,512]{1,0:T(8,128)(2,1)} collective-permute-done((bf16[1024,512]{1,0:T(8,128)(2,1)}, bf16[1024,512]{1,0:T(8,128)(2,1)}, u32[]{:S(2)}, u32[]{:S(2)}) %collective-permute-start.10) | collective-permute-done | bytes 1048608 | tf_op jit(solution)/shard_map/ppermute | solution.py:88
  67.3 2.5 %shard_map.30 = (f32[2,128,512]{2,1,0:T(8,128)S(1)}, bf16[2,128,512]{2,1,0:T(8,128)(2,1)S(1)}, bf16[2,128,512]{2,1,0:T(8,128)(2,1)S(1)}, bf16[2,128,512]{2,1,0:T(8,128)(2,1)S(1)}) custom-call(s32[1]{0:T(128)} %bitcast.4.core_ref, bf16[512,1024]{1,0:T(8,128)(2,1)S(1)} %get-tuple-element.35.panel_ref, bf16[1024,512]{1,0:T(8,128)(2,1)} %collective-permute-done.1.refs_0_, ...), custom_call_target="tpu_custom_call" | custom-call | tf_op jit(solution)/shard_map/pallas_call | solution.py:133
  71.2 2.7 %collective-permute-start.8 = (bf16[2,128,512]{2,1,0:T(8,128)(2,1)S(1)}, bf16[2,128,512]{2,1,0:T(8,128)(2,1)S(1)}, u32[]{:S(2)}, u32[]{:S(2)}) collective-permute-start(bf16[2,128,512]{2,1,0:T(8,128)(2,1)S(1)} %get-tuple-element.39), channel_id=1, source_target_pairs={{0,24},{8,16},{16,8},{24,0},{1,25},{9,17},{17,9},{25,1},{2,26},{10... | collective-permute-start | bytes 786440 | tf_op jit(solution)/shard_map/ppermute | solution.py:143
  74.8 6.6 %collective-permute-done.8 = bf16[2,128,512]{2,1,0:T(8,128)(2,1)S(1)} collective-permute-done((bf16[2,128,512]{2,1,0:T(8,128)(2,1)S(1)}, bf16[2,128,512]{2,1,0:T(8,128)(2,1)S(1)}, u32[]{:S(2)}, u32[]{:S(2)}) %collective-permute-start.8) | collective-permute-done | bytes 262176 | tf_op jit(solution)/shard_map/ppermute | solution.py:143
  81.3 5.2 %collective-permute-done.7 = bf16[2,128,512]{2,1,0:T(8,128)(2,1)S(1)} collective-permute-done((bf16[2,128,512]{2,1,0:T(8,128)(2,1)S(1)}, bf16[2,128,512]{2,1,0:T(8,128)(2,1)S(1)}, u32[]{:S(2)}, u32[]{:S(2)}) %collective-permute-start.7) | collective-permute-done | bytes 262176 | tf_op jit(solution)/shard_map/ppermute | solution.py:143
  89.7 1.5 collective-permute-start.14
  91.2 1.4 collective-permute-start.13
  93.2 6.7 %collective-permute-done.14 = bf16[2,128,512]{2,1,0:T(8,128)(2,1)S(1)} collective-permute-done((bf16[2,128,512]{2,1,0:T(8,128)(2,1)S(1)}, bf16[2,128,512]{2,1,0:T(8,128)(2,1)S(1)}, u32[]{:S(2)}, u32[]{:S(2)}) %collective-permute-start.14) | collective-permute-done | bytes 262176 | tf_op jit(solution)/shard_map/ppermute | solution.py:143
  99.9 4.4 %collective-permute-done.13 = bf16[2,128,512]{2,1,0:T(8,128)(2,1)S(1)} collective-permute-done((bf16[2,128,512]{2,1,0:T(8,128)(2,1)S(1)}, bf16[2,128,512]{2,1,0:T(8,128)(2,1)S(1)}, u32[]{:S(2)}, u32[]{:S(2)}) %collective-permute-start.13) | collective-permute-done | bytes 262176 | tf_op jit(solution)/shard_map/ppermute | solution.py:143
  105.9 2.5 %collective-permute-done.17.refs_1_ = bf16[1024,512]{1,0:T(8,128)(2,1)S(1)} collective-permute-done((bf16[1024,512]{1,0:T(8,128)(2,1)S(1)}, bf16[1024,512]{1,0:T(8,128)(2,1)S(1)}, u32[]{:S(2)}, u32[]{:S(2)}) %collective-permute-start.17) | collective-permute-done | bytes 1048608 | tf_op jit(solution)/shard_map/ppermute | solution.py:85
  109.7 1.7 %collective-permute-start.18 = (bf16[2,128,512]{2,1,0:T(8,128)(2,1)S(1)}, bf16[2,128,512]{2,1,0:T(8,128)(2,1)S(1)}, u32[]{:S(2)}, u32[]{:S(2)}) collective-permute-start(bf16[2,128,512]{2,1,0:T(8,128)(2,1)S(1)} %get-tuple-element.50), channel_id=1, source_target_pairs={{0,8},{8,0},{16,24},{24,16},{1,9},{9,1},{17,25},{25,17},{2,10},{10... | collective-permute-start | bytes 786440 | tf_op jit(solution)/shard_map/ppermute | solution.py:143
  111.7 1.6 collective-permute-start.20
  113.5 5.5 %collective-permute-done.18.refs_4_ = bf16[2,128,512]{2,1,0:T(8,128)(2,1)S(1)} collective-permute-done((bf16[2,128,512]{2,1,0:T(8,128)(2,1)S(1)}, bf16[2,128,512]{2,1,0:T(8,128)(2,1)S(1)}, u32[]{:S(2)}, u32[]{:S(2)}) %collective-permute-start.18) | collective-permute-done | bytes 262176 | tf_op jit(solution)/shard_map/ppermute | solution.py:143
  118.9 6.2 %collective-permute-done.19.refs_5_ = bf16[2,128,512]{2,1,0:T(8,128)(2,1)S(1)} collective-permute-done((bf16[2,128,512]{2,1,0:T(8,128)(2,1)S(1)}, bf16[2,128,512]{2,1,0:T(8,128)(2,1)S(1)}, u32[]{:S(2)}, u32[]{:S(2)}) %collective-permute-start.19) | collective-permute-done | bytes 262176 | tf_op jit(solution)/shard_map/ppermute | solution.py:143
  126.1 35.4 %all_to_all.10.second_ref = bf16[32,2,64,128]{3,2,1,0:T(8,128)(2,1)S(1)} all-to-all(bf16[32,2,64,128]{3,2,1,0:T(8,128)(2,1)S(1)} %get-tuple-element.54), channel_id=1, replica_groups=mesh['row'=4,'col'=8] {'row','col'}, dimensions={0} | all-to-all | bytes 2097152 | tf_op jit(solution)/shard_map/all_to_all | solution.py:187
  161.5 1.5 shard_map.34
  (60 shorter events, 18.2 us)
Async XLA Ops:
  0.0 27.3 %collective-permute-start.1 = (bf16[1024,512]{1,0:T(8,128)(2,1)}, bf16[1024,512]{1,0:T(8,128)(2,1)}, u32[]{:S(2)}, u32[]{:S(2)}) collective-permute-start(bf16[1024,512]{1,0:T(8,128)(2,1)} %bitcast.7), channel_id=1, source_target_pairs={{0,2},{1,3},{2,0},{3,1},{4,6},{5,7},{6,4},{7,5},{8,10},{9,11},{10,... | collective-permute-start | bytes 3145736 | tf_op jit(solution)/shard_map/ppermute | solution.py:88
  3.0 24.3 %collective-permute-start.9 = (bf16[1024,512]{1,0:T(8,128)(2,1)}, bf16[1024,512]{1,0:T(8,128)(2,1)}, u32[]{:S(2)}, u32[]{:S(2)}) collective-permute-start(bf16[1024,512]{1,0:T(8,128)(2,1)} %bitcast.8), channel_id=1, source_target_pairs={{2,4},{3,5},{4,2},{5,3},{10,12},{11,13},{12,10},{13,11},{18,20},{1... | collective-permute-start | bytes 3145736 | tf_op jit(solution)/shard_map/ppermute | solution.py:88
  7.2 47.1 %all-to-all-start = ((bf16[8,2,64,512]{3,2,1,0:T(8,128)(2,1)}), bf16[8,2,64,512]{3,2,1,0:T(8,128)(2,1)S(1)}, u32[]{:S(2)}, u32[]{:S(2)}) async-start(bf16[8,2,64,512]{3,2,1,0:T(8,128)(2,1)} %shard_map.28), calls=%async_computation | async-start | bytes 2097152 | tf_op jit(solution)/shard_map/all_to_all | solution.py:121
  12.0 18.2 %collective-permute-start = (bf16[1024,512]{1,0:T(8,128)(2,1)S(1)}, bf16[1024,512]{1,0:T(8,128)(2,1)}, u32[]{:S(2)}, u32[]{:S(2)}) collective-permute-start(bf16[1024,512]{1,0:T(8,128)(2,1)S(1)} %bitcast.9), channel_id=1, source_target_pairs={{0,1},{1,0},{2,3},{3,2},{4,5},{5,4},{6,7},{7,6},{8,9},{9,8},{10,11... | collective-permute-start | bytes 3145736 | tf_op jit(solution)/shard_map/ppermute | solution.py:85
  27.3 2.9 %collective-permute-start.2 = (bf16[1024,512]{1,0:T(8,128)(2,1)}, bf16[1024,512]{1,0:T(8,128)(2,1)S(1)}, u32[]{:S(2)}, u32[]{:S(2)}) collective-permute-start(bf16[1024,512]{1,0:T(8,128)(2,1)} %collective-permute-done.1.refs_0_), channel_id=1, source_target_pairs={{0,1},{1,0},{2,3},{3,2},{4,5},{5,4},{6,7},{7,6},{8,9},{9,8},{10,11... | collective-permute-start | bytes 3145736 | tf_op jit(solution)/shard_map/ppermute | solution.py:85
  27.3 38.5 %collective-permute-start.10 = (bf16[1024,512]{1,0:T(8,128)(2,1)}, bf16[1024,512]{1,0:T(8,128)(2,1)}, u32[]{:S(2)}, u32[]{:S(2)}) collective-permute-start(bf16[1024,512]{1,0:T(8,128)(2,1)} %collective-permute-done.9), channel_id=1, source_target_pairs={{2,0},{3,1},{4,6},{5,7},{10,8},{11,9},{12,14},{13,15},{18,16},{19,... | collective-permute-start | bytes 3145736 | tf_op jit(solution)/shard_map/ppermute | solution.py:88
  28.6 41.3 %collective-permute-start.15 = (bf16[1024,512]{1,0:T(8,128)(2,1)}, bf16[1024,512]{1,0:T(8,128)(2,1)}, u32[]{:S(2)}, u32[]{:S(2)}) collective-permute-start(bf16[1024,512]{1,0:T(8,128)(2,1)} %collective-permute-done.1.refs_0_), channel_id=1, source_target_pairs={{2,4},{3,5},{4,2},{5,3},{10,12},{11,13},{12,10},{13,11},{18,20},{1... | collective-permute-start | bytes 3145736 | tf_op jit(solution)/shard_map/ppermute | solution.py:88
  56.8 13.0 %collective-permute-start.5 = (bf16[2,128,512]{2,1,0:T(8,128)(2,1)S(1)}, bf16[2,128,512]{2,1,0:T(8,128)(2,1)S(1)}, u32[]{:S(2)}, u32[]{:S(2)}) collective-permute-start(bf16[2,128,512]{2,1,0:T(8,128)(2,1)S(1)} %get-tuple-element.34), channel_id=1, source_target_pairs={{0,24},{8,16},{16,8},{24,0},{1,25},{9,17},{17,9},{25,1},{2,26},{10... | collective-permute-start | bytes 786440 | tf_op jit(solution)/shard_map/ppermute | solution.py:143
  59.3 10.5 %collective-permute-start.4 = (bf16[2,128,512]{2,1,0:T(8,128)(2,1)S(1)}, bf16[2,128,512]{2,1,0:T(8,128)(2,1)S(1)}, u32[]{:S(2)}, u32[]{:S(2)}) collective-permute-start(bf16[2,128,512]{2,1,0:T(8,128)(2,1)S(1)} %get-tuple-element.33), channel_id=1, source_target_pairs={{0,16},{8,24},{16,0},{24,8},{1,17},{9,25},{17,1},{25,9},{2,18},{10... | collective-permute-start | bytes 786440 | tf_op jit(solution)/shard_map/ppermute | solution.py:143
  59.8 7.5 %copy-start.3 = (bf16[1024,512]{1,0:T(8,128)(2,1)S(1)}, bf16[1024,512]{1,0:T(8,128)(2,1)}, u32[]{:S(2)}) copy-start(bf16[1024,512]{1,0:T(8,128)(2,1)} %copy-done.2) | copy-start | bytes 3145732
  59.8 10.0 %collective-permute-start.3 = (bf16[2,128,512]{2,1,0:T(8,128)(2,1)S(1)}, bf16[2,128,512]{2,1,0:T(8,128)(2,1)S(1)}, u32[]{:S(2)}, u32[]{:S(2)}) collective-permute-start(bf16[2,128,512]{2,1,0:T(8,128)(2,1)S(1)} %get-tuple-element.32), channel_id=1, source_target_pairs={{0,8},{8,0},{16,24},{24,16},{1,9},{9,1},{17,25},{25,17},{2,10},{10... | collective-permute-start | bytes 786440 | tf_op jit(solution)/shard_map/ppermute | solution.py:143
  67.2 20.5 %collective-permute-start.11 = (bf16[1024,512]{1,0:T(8,128)(2,1)S(1)}, bf16[1024,512]{1,0:T(8,128)(2,1)S(1)}, u32[]{:S(2)}, u32[]{:S(2)}) collective-permute-start(bf16[1024,512]{1,0:T(8,128)(2,1)S(1)} %broadcast_select_fusion.1.refs_0_), channel_id=1, source_target_pairs={{0,1},{1,0},{2,3},{3,2},{4,5},{5,4},{6,7},{7,6},{8,9},{9,8},{10,11... | collective-permute-start | bytes 3145736 | tf_op jit(solution)/shard_map/ppermute | solution.py:85
  69.9 35.0 %collective-permute-start.16 = (bf16[1024,512]{1,0:T(8,128)(2,1)}, bf16[1024,512]{1,0:T(8,128)(2,1)S(1)}, u32[]{:S(2)}, u32[]{:S(2)}) collective-permute-start(bf16[1024,512]{1,0:T(8,128)(2,1)} %collective-permute-done.15), channel_id=1, source_target_pairs={{2,0},{3,1},{4,6},{5,7},{10,8},{11,9},{12,14},{13,15},{18,16},{19,... | collective-permute-start | bytes 3145736 | tf_op jit(solution)/shard_map/ppermute | solution.py:88
  71.2 10.1 %collective-permute-start.8 = (bf16[2,128,512]{2,1,0:T(8,128)(2,1)S(1)}, bf16[2,128,512]{2,1,0:T(8,128)(2,1)S(1)}, u32[]{:S(2)}, u32[]{:S(2)}) collective-permute-start(bf16[2,128,512]{2,1,0:T(8,128)(2,1)S(1)} %get-tuple-element.39), channel_id=1, source_target_pairs={{0,24},{8,16},{16,8},{24,0},{1,25},{9,17},{17,9},{25,1},{2,26},{10... | collective-permute-start | bytes 786440 | tf_op jit(solution)/shard_map/ppermute | solution.py:143
  73.9 12.6 %collective-permute-start.7 = (bf16[2,128,512]{2,1,0:T(8,128)(2,1)S(1)}, bf16[2,128,512]{2,1,0:T(8,128)(2,1)S(1)}, u32[]{:S(2)}, u32[]{:S(2)}) collective-permute-start(bf16[2,128,512]{2,1,0:T(8,128)(2,1)S(1)} %get-tuple-element.38), channel_id=1, source_target_pairs={{0,16},{8,24},{16,0},{24,8},{1,17},{9,25},{17,1},{25,9},{2,18},{10... | collective-permute-start | bytes 786440 | tf_op jit(solution)/shard_map/ppermute | solution.py:143
  74.4 12.4 %collective-permute-start.6 = (bf16[2,128,512]{2,1,0:T(8,128)(2,1)S(1)}, bf16[2,128,512]{2,1,0:T(8,128)(2,1)S(1)}, u32[]{:S(2)}, u32[]{:S(2)}) collective-permute-start(bf16[2,128,512]{2,1,0:T(8,128)(2,1)S(1)} %get-tuple-element.37), channel_id=1, source_target_pairs={{0,8},{8,0},{16,24},{24,16},{1,9},{9,1},{17,25},{25,17},{2,10},{10... | collective-permute-start | bytes 786440 | tf_op jit(solution)/shard_map/ppermute | solution.py:143
  89.7 10.1 %collective-permute-start.14 = (bf16[2,128,512]{2,1,0:T(8,128)(2,1)S(1)}, bf16[2,128,512]{2,1,0:T(8,128)(2,1)S(1)}, u32[]{:S(2)}, u32[]{:S(2)}) collective-permute-start(bf16[2,128,512]{2,1,0:T(8,128)(2,1)S(1)} %get-tuple-element.45), channel_id=1, source_target_pairs={{0,24},{8,16},{16,8},{24,0},{1,25},{9,17},{17,9},{25,1},{2,26},{10... | collective-permute-start | bytes 786440 | tf_op jit(solution)/shard_map/ppermute | solution.py:143
  91.2 13.0 %collective-permute-start.13 = (bf16[2,128,512]{2,1,0:T(8,128)(2,1)S(1)}, bf16[2,128,512]{2,1,0:T(8,128)(2,1)S(1)}, u32[]{:S(2)}, u32[]{:S(2)}) collective-permute-start(bf16[2,128,512]{2,1,0:T(8,128)(2,1)S(1)} %get-tuple-element.44), channel_id=1, source_target_pairs={{0,16},{8,24},{16,0},{24,8},{1,17},{9,25},{17,1},{25,9},{2,18},{10... | collective-permute-start | bytes 786440 | tf_op jit(solution)/shard_map/ppermute | solution.py:143
  92.7 11.8 %collective-permute-start.12 = (bf16[2,128,512]{2,1,0:T(8,128)(2,1)S(1)}, bf16[2,128,512]{2,1,0:T(8,128)(2,1)S(1)}, u32[]{:S(2)}, u32[]{:S(2)}) collective-permute-start(bf16[2,128,512]{2,1,0:T(8,128)(2,1)S(1)} %get-tuple-element.43), channel_id=1, source_target_pairs={{0,8},{8,0},{16,24},{24,16},{1,9},{9,1},{17,25},{25,17},{2,10},{10... | collective-permute-start | bytes 786440 | tf_op jit(solution)/shard_map/ppermute | solution.py:143
  105.7 2.7 %collective-permute-start.17 = (bf16[1024,512]{1,0:T(8,128)(2,1)S(1)}, bf16[1024,512]{1,0:T(8,128)(2,1)S(1)}, u32[]{:S(2)}, u32[]{:S(2)}) collective-permute-start(bf16[1024,512]{1,0:T(8,128)(2,1)S(1)} %broadcast_select_fusion.refs_0_), channel_id=1, source_target_pairs={{0,1},{1,0},{2,3},{3,2},{4,5},{5,4},{6,7},{7,6},{8,9},{9,8},{10,11... | collective-permute-start | bytes 3145736 | tf_op jit(solution)/shard_map/ppermute | solution.py:85
  109.7 9.2 %collective-permute-start.18 = (bf16[2,128,512]{2,1,0:T(8,128)(2,1)S(1)}, bf16[2,128,512]{2,1,0:T(8,128)(2,1)S(1)}, u32[]{:S(2)}, u32[]{:S(2)}) collective-permute-start(bf16[2,128,512]{2,1,0:T(8,128)(2,1)S(1)} %get-tuple-element.50), channel_id=1, source_target_pairs={{0,8},{8,0},{16,24},{24,16},{1,9},{9,1},{17,25},{25,17},{2,10},{10... | collective-permute-start | bytes 786440 | tf_op jit(solution)/shard_map/ppermute | solution.py:143
  111.4 13.7 %collective-permute-start.19 = (bf16[2,128,512]{2,1,0:T(8,128)(2,1)S(1)}, bf16[2,128,512]{2,1,0:T(8,128)(2,1)S(1)}, u32[]{:S(2)}, u32[]{:S(2)}) collective-permute-start(bf16[2,128,512]{2,1,0:T(8,128)(2,1)S(1)} %get-tuple-element.51), channel_id=1, source_target_pairs={{0,16},{8,24},{16,0},{24,8},{1,17},{9,25},{17,1},{25,9},{2,18},{10... | collective-permute-start | bytes 786440 | tf_op jit(solution)/shard_map/ppermute | solution.py:143
  111.7 13.4 %collective-permute-start.20 = (bf16[2,128,512]{2,1,0:T(8,128)(2,1)S(1)}, bf16[2,128,512]{2,1,0:T(8,128)(2,1)S(1)}, u32[]{:S(2)}, u32[]{:S(2)}) collective-permute-start(bf16[2,128,512]{2,1,0:T(8,128)(2,1)S(1)} %get-tuple-element.52), channel_id=1, source_target_pairs={{0,24},{8,16},{16,8},{24,0},{1,25},{9,17},{17,9},{25,1},{2,26},{10... | collective-permute-start | bytes 786440 | tf_op jit(solution)/shard_map/ppermute | solution.py:143
  113.3 11.8 %copy-start.4 = (bf16[2,128,512]{2,1,0:T(8,128)(2,1)S(1)}, bf16[2,128,512]{2,1,0:T(8,128)(2,1)}, u32[]{:S(2)}) copy-start(bf16[2,128,512]{2,1,0:T(8,128)(2,1)} %add_convert_fusion.1.refs_1_) | copy-start | bytes 786436
  (11 other events, 43.4 us)

commit v11 on v5

--- a/solution.py
+++ b/solution.py
@@ -13,27 +13,41 @@
 PARAMS = pltpu.CompilerParams(vmem_limit_bytes=16 * 1024 * 1024)
 
 
-def spread_kernel(nrow, ncol, row_ref, a_ref, out_ref):
+def spread_kernel(nrow, ncol, row_ref, a_ref, *out_refs):
     kk, occ, _, v = a_ref.shape
     ai, vs = occ // nrow, v // ncol
+    for odd, out_ref in enumerate(out_refs):
+        for k in range(kk):
+            tiles = [
+                a_ref[k, (row_ref[0] ^ t) * ai + i] for t in range(odd, nrow, 2) for i in range(ai)
+            ]
+            for s in range(ncol):
+                piece = [tile[:, s * vs : (s + 1) * vs] for tile in tiles]
+                out_ref[s, k] = jnp.concatenate(piece, axis=1)
+
+
+def multiply(core, panel_ref, blocks, outs):
+    rows = outs[0].shape[1]
+    for m, block in enumerate(blocks):
+        n = m - m % 2 + ((m % 2) ^ core)
+        prod = jnp.dot(panel_ref[...], block[...], preferred_element_type=F32)
+        for o, out in enumerate(outs):
+            out[n] = prod[o * rows : (o + 1) * rows].astype(out.dtype)
+
+
+def opening_kernel(count, core_ref, raw_ref, *refs):
+    panel_ref = refs[count]
+    ncol, kk, cs, wide = raw_ref.shape
+    v = ncol * cs
     for k in range(kk):
-        tiles = [a_ref[k, (row_ref[0] ^ t) * ai + i] for t in range(nrow) for i in range(ai)]
-        for s in range(ncol):
-            piece = [tile[:, s * vs : (s + 1) * vs] for tile in tiles]
-            out_ref[s, k] = jnp.concatenate(piece, axis=1)
-
-
-def product_kernel(count, core_ref, panel_ref, *refs):
-    blocks, outs = refs[: 2 * count], refs[2 * count :]
-    rows = outs[0].shape[1]
-    core = core_ref[0]
-    for m in range(count):
-        for c in range(2):
-            n = 2 * m + (core ^ c)
-            prod = jnp.dot(panel_ref[...], blocks[2 * m + c][...], preferred_element_type=F32)
-            outs[0][n] = prod[:rows]
-            for t in range(1, len(outs)):
-                outs[t][n] = prod[t * rows : (t + 1) * rows].astype(BF16)
+        panel_ref[:, k * v : (k + 1) * v] = raw_ref[:, k].reshape(v, wide).T
+    multiply(core_ref[0], panel_ref, refs[:count], refs[count + 1 :])
+
+
+def product_kernel(core_ref, even_ref, odd_ref, here_ref, there_ref, *outs):
+    half = len(outs) // 2
+    for panel_ref, part in ((even_ref, outs[:half]), (odd_ref, outs[half:])):
+        multiply(core_ref[0], panel_ref, (here_ref, there_ref), part)
 
 
 def turn_kernel(sizes, ncol, slot_ref, *refs):
@@ -92,39 +106,57 @@
 
         w = intermediate.reshape(kk * v, v)
         line = nz == 4
+        first_blocks = [w, across(w)]
         if line:
             swap = [(1, 2), (2, 1)]
             outward = [(1, 0), (2, 3)]
             x1 = along(w, [(a, a ^ 1) for a in range(nz)])
             y2 = along(w, swap)
-        own = (w, across(w))
-
-        blocks = pl.pallas_call(
+            first_blocks += [x1, across(x1)]
+
+        wide = occ * vs // 2
+        even, odd = pl.pallas_call(
             functools.partial(spread_kernel, nrow, ncol),
-            out_shape=jax.ShapeDtypeStruct((ncol, kk, cs, occ * vs), BF16),
+            out_shape=[jax.ShapeDtypeStruct((ncol, kk, cs, wide), BF16)] * 2,
             in_specs=[SMEM, VMEM],
-            out_specs=VMEM,
+            out_specs=[VMEM] * 2,
             compiler_params=PARAMS,
         )(row, amplitudes)
-        panel = lax.all_to_all(blocks, "col", 0, 0, tiled=True)
-        panel = jnp.transpose(panel, (3, 1, 0, 2)).reshape(nrow * rows, kk * v)
-
-        def product(pairs):
-            n = 2 * len(pairs)
-            sent = [jax.ShapeDtypeStruct((n, rows, v), BF16)] * (nrow - 1)
+
+        def shapes(n, kinds):
+            return [jax.ShapeDtypeStruct((n, rows, v), kind) for kind in kinds]
+
+        def opening(raw, kinds):
+            count = len(first_blocks)
+            panel, *parts = pl.pallas_call(
+                functools.partial(opening_kernel, count),
+                out_shape=[jax.ShapeDtypeStruct((wide, kk * v), BF16)] + shapes(count, kinds),
+                in_specs=[SMEM] + [VMEM] * (1 + count),
+                out_specs=[VMEM] * (1 + len(kinds)),
+                compiler_params=PARAMS,
+            )(core, raw, *first_blocks)
+            return panel, parts
+
+        half = nrow // 2
+        kinds = [F32] + [BF16] * (half - 1)
+
+        def product(here, there):
             return pl.pallas_call(
-                functools.partial(product_kernel, len(pairs)),
-                out_shape=[jax.ShapeDtypeStruct((n, rows, v), F32)] + sent,
-                in_specs=[SMEM] + [VMEM] * (1 + n),
+                product_kernel,
+                out_shape=shapes(2, kinds + [BF16] * half),
+                in_specs=[SMEM] + [VMEM] * 4,
                 out_specs=[VMEM] * nrow,
                 compiler_params=PARAMS,
-            )(core, panel, *[x for pair in pairs for x in pair])
+            )(core, even, odd, here, there)
+
+        def to_owner(parts, start):
+            return [
+                lax.ppermute(part, "row", [(r, r ^ (start + 2 * n)) for r in range(nrow)])
+                for n, part in enumerate(parts)
+            ]
 
         def exchange(parts):
-            return [parts[0]] + [
-                lax.ppermute(parts[t], "row", [(r, r ^ t) for r in range(nrow)])
-                for t in range(1, nrow)
-            ]
+            return [parts[0]] + to_owner(parts[1:half], 2) + to_owner(parts[half:], 1)
 
         def summed(group):
             total = group[0]
@@ -132,25 +164,31 @@
                 total = total + part.astype(F32)
             return total.astype(BF16)
 
+        odd = lax.all_to_all(odd, "col", 0, 0, tiled=True)
         if line:
-            x1, y2, blocks = lax.optimization_barrier((x1, y2, blocks))
+            x1, y2, odd = lax.optimization_barrier((x1, y2, odd))
             y3, e2 = along(x1, swap), along(y2, outward)
-            parts = product([own, (x1, across(x1))])
-            groups = [exchange(parts)]
-            e3 = along(after(y3, *parts), outward)
-            for inner, outer in ((y2, e2), (y3, e3)):
-                groups[-1] = [summed(groups[-1])]
-                x = jnp.where(end, after(outer, *parts), inner)
-                parts = product([(after(x, groups[-1][0]), across(x))])
-                groups.append(exchange(parts))
+        even = lax.all_to_all(after(even, odd), "col", 0, 0, tiled=True)
+        odd, parts = opening(odd, [BF16] * half)
+        odd_sums = to_owner(parts, 1)
+        even, parts = opening(even, kinds)
+        sums = [summed([parts[0]] + to_owner(parts[1:], 2) + odd_sums)]
+        if line:
+            e3 = along(after(y3, *odd_sums, *parts), outward)
+            x2 = jnp.where(end, e2, y2)
+            group = exchange(product(after(x2, sums[0]), across(x2)))
+            sums.append(summed(group))
+            x3 = jnp.where(end, after(e3, *group[1:]), y3)
+            last = exchange(product(x3, across(x3)))
             slots = [z, z ^ 1, jnp.where(end, z ^ 2, 3 - z), jnp.where(end, 3 - z, z ^ 2)]
         else:
-            groups = [exchange(product([own]))]
             for m in range(1, nz):
-                groups[-1] = [summed(groups[-1])]
                 x = along(w, [(a, a ^ m) for a in range(nz)])
-                groups.append(exchange(product([(after(x, groups[-1][0]), across(x))])))
+                last = exchange(product(after(x, sums[-1]), across(x)))
+                if m < nz - 1:
+                    sums.append(summed(last))
             slots = [z ^ m for m in range(nz)]
+        groups = [[x] for x in sums] + [last]
 
         sizes = [len(g) for g in groups]
         first, turned = pl.pallas_call(

time: 170 us -> 174 us (1.024)
  starting transfers between devices: 25 us -> 32.9 us
  waiting for transfers between devices: 93.4 us -> 86.7 us
  Pallas kernels: 10.1 us -> 15.3 us
  blocking collectives: 35 us -> 31.8 us
  other arithmetic: 2.03 us -> 4.22 us
    ppermute x9, waiting for transfers between devices: 46.2 us -> 32.4 us  [to_owner(): lax.ppermute(part, 'row', [(r, r ^ start + 2 * n) for r in range(nrow)])]
    all_to_all x1 -> x2, starting transfers between devices: 4.81 us -> 11.6 us  [the longest x1 6.91 us: local(): even = lax.all_to_all(after(even, odd), 'col', 0, 0, tiled=True)]
    ppermute x5, waiting for transfers between devices: 23 us -> 28.3 us  [along(): lax.ppermute(x, 'col', [(2 * a + c, 2 * b + c) for a, b in pairs for c in...]
    pallas_call x4 -> x5, Pallas kernels: 7.7 us -> 12.8 us  [the longest x2 6.4 us: opening(): pl.pallas_call(functools.partial(opening_kernel, count), out_shape=[jax.S...]
    all_to_all x1, blocking collectives: 35 us -> 31.8 us  [local(): second = lax.all_to_all(turned, ('row', 'col'), 0, 0, tiled=True)]
    ppermute x4, waiting for transfers between devices: 0.01 us -> 2.69 us  [across(): return lax.ppermute(x, 'col', [(s, s ^ 1) for s in range(ncol)])]
    all_to_all x1 -> x2, waiting for transfers between devices: 24.1 us -> 23.3 us  [the longest x1 14.7 us: local(): odd = lax.all_to_all(odd, 'col', 0, 0, tiled=True)]
  transfers between devices with their start and end apart: 19 -> 20, of which waited for: 12 -> 12; matrix products, arithmetic and copies ran while one was open for 3% -> 2% of each run, Pallas kernels for 4% -> 6%
where the time goes in v11:
time: 174 us
  waiting for transfers between devices  86.7 us (50%)
  starting transfers between devices  32.9 us (19%)
  blocking collectives  31.8 us (18%)
  Pallas kernels  15.3 us (9%)
  other arithmetic  4.22 us (2%)
  local copies, waits for them, and re-layouts  2.75 us (2%)
    ppermute x9, waiting for transfers between devices, to_owner(): lax.ppermute(part, 'row', [(r, r ^ start + 2 * n) for r in range(nrow)])  32.4 us
    all_to_all x1, blocking collectives, local(): second = lax.all_to_all(turned, ('row', 'col'), 0, 0, tiled=True)  31.8 us
    ppermute x5, waiting for transfers between devices, along(): lax.ppermute(x, 'col', [(2 * a + c, 2 * b + c) for a, b in pairs for c in...  28.3 us
    all_to_all x1, waiting for transfers between devices, local(): odd = lax.all_to_all(odd, 'col', 0, 0, tiled=True)  14.7 us
    ppermute x9, starting transfers between devices, to_owner(): lax.ppermute(part, 'row', [(r, r ^ start + 2 * n) for r in range(nrow)])  11.7 us
    ppermute x5, starting transfers between devices, along(): lax.ppermute(x, 'col', [(2 * a + c, 2 * b + c) for a, b in pairs for c in...  9.01 us
    all_to_all x1, waiting for transfers between devices, local(): even = lax.all_to_all(after(even, odd), 'col', 0, 0, tiled=True)  8.56 us
    all_to_all x1, starting transfers between devices, local(): even = lax.all_to_all(after(even, odd), 'col', 0, 0, tiled=True)  6.91 us
  transfers between devices with their start and end apart: 20, of which 12 were waited for; matrix products, arithmetic and copies ran while one was open for 2% of the time, Pallas kernels for 6%

profile of v11, /device:TPU:0, one launch (start us, length us, event | category | flops | bytes accessed | tf_op | source)
XLA Modules:
  0.0 173.7 jit_solution(7534761968227132890)
XLA Ops:
  0.0 3.0 %collective-permute-start = (bf16[1024,512]{1,0:T(8,128)(2,1)}, bf16[1024,512]{1,0:T(8,128)(2,1)S(1)}, u32[]{:S(2)}, u32[]{:S(2)}) collective-permute-start(bf16[1024,512]{1,0:T(8,128)(2,1)} %bitcast.7), channel_id=1, source_target_pairs={{0,2},{1,3},{2,0},{3,1},{4,6},{5,7},{6,4},{7,5},{8,10},{9,11},{10,... | collective-permute-start | bytes 3145736 | tf_op jit(solution)/shard_map/ppermute | solution.py:92
  3.0 1.6 collective-permute-start.1
  7.8 4.7 %all-to-all-start = ((bf16[8,2,64,256]{3,2,1,0:T(8,128)(2,1)}), bf16[8,2,64,256]{3,2,1,0:T(8,128)(2,1)}, u32[]{:S(2)}, u32[]{:S(2)}) async-start(bf16[8,2,64,256]{3,2,1,0:T(8,128)(2,1)} %get-tuple-element.31), calls=%async_computation | async-start | bytes 1048576 | tf_op jit(solution)/shard_map/all_to_all | solution.py:167
  13.0 14.2 %collective-permute-done.refs_2_ = bf16[1024,512]{1,0:T(8,128)(2,1)S(1)} collective-permute-done((bf16[1024,512]{1,0:T(8,128)(2,1)}, bf16[1024,512]{1,0:T(8,128)(2,1)S(1)}, u32[]{:S(2)}, u32[]{:S(2)}) %collective-permute-start) | collective-permute-done | bytes 1048608 | tf_op jit(solution)/shard_map/ppermute | solution.py:92
  27.2 14.7 %all-to-all-done.raw_ref = bf16[8,2,64,256]{3,2,1,0:T(8,128)(2,1)} async-done(((bf16[8,2,64,256]{3,2,1,0:T(8,128)(2,1)}), bf16[8,2,64,256]{3,2,1,0:T(8,128)(2,1)}, u32[]{:S(2)}, u32[]{:S(2)}) %all-to-all-start) | async-done | bytes 524320 | tf_op jit(solution)/shard_map/all_to_all | solution.py:167
  43.2 1.6 collective-permute-start.12
  44.9 6.9 %all-to-all-start.1 = ((bf16[8,2,64,256]{3,2,1,0:T(8,128)(2,1)}), bf16[8,2,64,256]{3,2,1,0:T(8,128)(2,1)}, u32[]{:S(2)}, u32[]{:S(2)}) async-start(bf16[8,2,64,256]{3,2,1,0:T(8,128)(2,1)} %copy-done.6), calls=%async_computation.1 | async-start | bytes 1048576 | tf_op jit(solution)/shard_map/all_to_all | solution.py:171
  51.8 3.7 %shard_map.30 = (bf16[256,1024]{1,0:T(8,128)(2,1)S(1)}, bf16[4,128,512]{2,1,0:T(8,128)(2,1)}, bf16[4,128,512]{2,1,0:T(8,128)(2,1)}) custom-call(s32[1]{0:T(128)} %bitcast.4.core_ref, bf16[8,2,64,256]{3,2,1,0:T(8,128)(2,1)} %all-to-all-done.raw_ref, bf16[1024,512]{1,0:T(8,128)(2,1)S(1)} %bitcast.10, bf16[1024,512]{1,0:T(8,128)(2,1)S(1)} %collective-permute-done.2.refs_1_, ...), custom_call_target="tpu_custom_call" | custom-call | tf_op jit(solution)/shard_map/pallas_call | solution.py:131
  58.5 14.1 %collective-permute-done.7 = bf16[1024,512]{1,0:T(8,128)(2,1)} collective-permute-done((bf16[1024,512]{1,0:T(8,128)(2,1)}, bf16[1024,512]{1,0:T(8,128)(2,1)}, u32[]{:S(2)}, u32[]{:S(2)}) %collective-permute-start.7) | collective-permute-done | bytes 1048608 | tf_op jit(solution)/shard_map/ppermute | solution.py:92
  72.5 2.3 %broadcast_select_fusion.1.here_ref = bf16[1024,512]{1,0:T(8,128)(2,1)} fusion(bf16[1024,512]{1,0:T(8,128)(2,1)} %collective-permute-done.7, bf16[1024,512]{1,0:T(8,128)(2,1)} %collective-permute-done.1, pred[]{:T(512)S(6)} %or.3), kind=kLoop, calls=%fused_computation.2 | loop fusion | flops 524288 | bytes 3145729 | tf_op jit(solution)/shard_map/jit(_where)/select_n | solution.py:178
  74.8 8.6 %all-to-all-done.1.raw_ref = bf16[8,2,64,256]{3,2,1,0:T(8,128)(2,1)} async-done(((bf16[8,2,64,256]{3,2,1,0:T(8,128)(2,1)}), bf16[8,2,64,256]{3,2,1,0:T(8,128)(2,1)}, u32[]{:S(2)}, u32[]{:S(2)}) %all-to-all-start.1) | async-done | bytes 524320 | tf_op jit(solution)/shard_map/all_to_all | solution.py:171
  83.4 2.7 %shard_map.29 = (bf16[256,1024]{1,0:T(8,128)(2,1)S(1)}, f32[4,128,512]{2,1,0:T(8,128)S(1)}, bf16[4,128,512]{2,1,0:T(8,128)(2,1)S(1)}) custom-call(s32[1]{0:T(128)} %bitcast.4.core_ref, bf16[8,2,64,256]{3,2,1,0:T(8,128)(2,1)} %all-to-all-done.1.raw_ref, bf16[1024,512]{1,0:T(8,128)(2,1)S(1)} %bitcast.11, bf16[1024,512]{1,0:T(8,128)(2,1)S(1)} %collective-permute-done.2.refs_1_, ...), custom_call_target="tpu_custom_call" | custom-call | tf_op jit(solution)/shard_map/pallas_call | solution.py:131
  86.1 1.6 collective-permute-start.4
  89.2 10.0 %collective-permute-done.4 = bf16[4,128,512]{2,1,0:T(8,128)(2,1)S(1)} collective-permute-done((bf16[4,128,512]{2,1,0:T(8,128)(2,1)S(1)}, bf16[4,128,512]{2,1,0:T(8,128)(2,1)S(1)}, u32[]{:S(2)}, u32[]{:S(2)}) %collective-permute-start.4) | collective-permute-done | bytes 524320 | tf_op jit(solution)/shard_map/ppermute | solution.py:154
  99.2 1.5 add_convert_fusion.refs_0_
  100.7 2.8 %shard_map.31 = (f32[2,128,512]{2,1,0:T(8,128)S(1)}, bf16[2,128,512]{2,1,0:T(8,128)(2,1)S(1)}, bf16[2,128,512]{2,1,0:T(8,128)(2,1)S(1)}, bf16[2,128,512]{2,1,0:T(8,128)(2,1)S(1)}) custom-call(s32[1]{0:T(128)} %bitcast.4.core_ref, bf16[256,1024]{1,0:T(8,128)(2,1)S(1)} %get-tuple-element.38.even_ref, bf16[256,1024]{1,0:T(8,128)(2,1)S(1)} %copy-done.2, ...), custom_call_target="tpu_custom_call" | custom-call | tf_op jit(solution)/shard_map/pallas_call | solution.py:144
  103.5 1.6 collective-permute-start.10
  107.1 5.7 %collective-permute-done.10 = bf16[2,128,512]{2,1,0:T(8,128)(2,1)S(1)} collective-permute-done((bf16[2,128,512]{2,1,0:T(8,128)(2,1)S(1)}, bf16[2,128,512]{2,1,0:T(8,128)(2,1)S(1)}, u32[]{:S(2)}, u32[]{:S(2)}) %collective-permute-start.10) | collective-permute-done | bytes 262176 | tf_op jit(solution)/shard_map/ppermute | solution.py:154
  112.8 3.8 %collective-permute-done.11 = bf16[2,128,512]{2,1,0:T(8,128)(2,1)S(1)} collective-permute-done((bf16[2,128,512]{2,1,0:T(8,128)(2,1)S(1)}, bf16[2,128,512]{2,1,0:T(8,128)(2,1)S(1)}, u32[]{:S(2)}, u32[]{:S(2)}) %collective-permute-start.11) | collective-permute-done | bytes 262176 | tf_op jit(solution)/shard_map/ppermute | solution.py:154
  119.1 2.7 %collective-permute-done.14.there_ref = bf16[1024,512]{1,0:T(8,128)(2,1)} collective-permute-done((bf16[1024,512]{1,0:T(8,128)(2,1)S(1)}, bf16[1024,512]{1,0:T(8,128)(2,1)}, u32[]{:S(2)}, u32[]{:S(2)}) %collective-permute-start.14) | collective-permute-done | bytes 1048608 | tf_op jit(solution)/shard_map/ppermute | solution.py:89
  121.8 2.5 %shard_map.32 = (f32[2,128,512]{2,1,0:T(8,128)S(1)}, bf16[2,128,512]{2,1,0:T(8,128)(2,1)S(1)}, bf16[2,128,512]{2,1,0:T(8,128)(2,1)S(1)}, bf16[2,128,512]{2,1,0:T(8,128)(2,1)S(1)}) custom-call(s32[1]{0:T(128)} %bitcast.4.core_ref, bf16[256,1024]{1,0:T(8,128)(2,1)S(1)} %copy-done.4, bf16[256,1024]{1,0:T(8,128)(2,1)S(1)} %copy-done.2, ...), custom_call_target="tpu_custom_call" | custom-call | tf_op jit(solution)/shard_map/pallas_call | solution.py:144
  128.0 4.7 %collective-permute-done.15.refs_3_ = bf16[2,128,512]{2,1,0:T(8,128)(2,1)S(1)} collective-permute-done((bf16[2,128,512]{2,1,0:T(8,128)(2,1)S(1)}, bf16[2,128,512]{2,1,0:T(8,128)(2,1)S(1)}, u32[]{:S(2)}, u32[]{:S(2)}) %collective-permute-start.15) | collective-permute-done | bytes 262176 | tf_op jit(solution)/shard_map/ppermute | solution.py:154
  134.0 5.4 %collective-permute-done.17.refs_5_ = bf16[2,128,512]{2,1,0:T(8,128)(2,1)S(1)} collective-permute-done((bf16[2,128,512]{2,1,0:T(8,128)(2,1)S(1)}, bf16[2,128,512]{2,1,0:T(8,128)(2,1)S(1)}, u32[]{:S(2)}, u32[]{:S(2)}) %collective-permute-start.17) | collective-permute-done | bytes 262176 | tf_op jit(solution)/shard_map/ppermute | solution.py:154
  140.4 31.8 %all_to_all.15.second_ref = bf16[32,2,64,128]{3,2,1,0:T(8,128)(2,1)S(1)} all-to-all(bf16[32,2,64,128]{3,2,1,0:T(8,128)(2,1)S(1)} %get-tuple-element.54), channel_id=1, replica_groups=mesh['row'=4,'col'=8] {'row','col'}, dimensions={0} | all-to-all | bytes 2097152 | tf_op jit(solution)/shard_map/all_to_all | solution.py:204
  (51 shorter events, 21.3 us)
Async XLA Ops:
  0.0 27.2 %collective-permute-start = (bf16[1024,512]{1,0:T(8,128)(2,1)}, bf16[1024,512]{1,0:T(8,128)(2,1)S(1)}, u32[]{:S(2)}, u32[]{:S(2)}) collective-permute-start(bf16[1024,512]{1,0:T(8,128)(2,1)} %bitcast.7), channel_id=1, source_target_pairs={{0,2},{1,3},{2,0},{3,1},{4,6},{5,7},{6,4},{7,5},{8,10},{9,11},{10,... | collective-permute-start | bytes 3145736 | tf_op jit(solution)/shard_map/ppermute | solution.py:92
  3.0 38.9 %collective-permute-start.1 = (bf16[1024,512]{1,0:T(8,128)(2,1)}, bf16[1024,512]{1,0:T(8,128)(2,1)}, u32[]{:S(2)}, u32[]{:S(2)}) collective-permute-start(bf16[1024,512]{1,0:T(8,128)(2,1)} %bitcast.8), channel_id=1, source_target_pairs={{2,4},{3,5},{4,2},{5,3},{10,12},{11,13},{12,10},{13,11},{18,20},{1... | collective-permute-start | bytes 3145736 | tf_op jit(solution)/shard_map/ppermute | solution.py:92
  7.8 34.1 %all-to-all-start = ((bf16[8,2,64,256]{3,2,1,0:T(8,128)(2,1)}), bf16[8,2,64,256]{3,2,1,0:T(8,128)(2,1)}, u32[]{:S(2)}, u32[]{:S(2)}) async-start(bf16[8,2,64,256]{3,2,1,0:T(8,128)(2,1)} %get-tuple-element.31), calls=%async_computation | async-start | bytes 1048576 | tf_op jit(solution)/shard_map/all_to_all | solution.py:167
  12.5 39.2 %collective-permute-start.2 = (bf16[1024,512]{1,0:T(8,128)(2,1)S(1)}, bf16[1024,512]{1,0:T(8,128)(2,1)S(1)}, u32[]{:S(2)}, u32[]{:S(2)}) collective-permute-start(bf16[1024,512]{1,0:T(8,128)(2,1)S(1)} %bitcast.9), channel_id=1, source_target_pairs={{0,1},{1,0},{2,3},{3,2},{4,5},{5,4},{6,7},{7,6},{8,9},{9,8},{10,11... | collective-permute-start | bytes 3145736 | tf_op jit(solution)/shard_map/ppermute | solution.py:89
  27.2 24.6 %collective-permute-start.3 = (bf16[1024,512]{1,0:T(8,128)(2,1)S(1)}, bf16[1024,512]{1,0:T(8,128)(2,1)}, u32[]{:S(2)}, u32[]{:S(2)}) collective-permute-start(bf16[1024,512]{1,0:T(8,128)(2,1)S(1)} %collective-permute-done.refs_2_), channel_id=1, source_target_pairs={{0,1},{1,0},{2,3},{3,2},{4,5},{5,4},{6,7},{7,6},{8,9},{9,8},{10,11... | collective-permute-start | bytes 3145736 | tf_op jit(solution)/shard_map/ppermute | solution.py:89
  41.9 30.6 %collective-permute-start.7 = (bf16[1024,512]{1,0:T(8,128)(2,1)}, bf16[1024,512]{1,0:T(8,128)(2,1)}, u32[]{:S(2)}, u32[]{:S(2)}) collective-permute-start(bf16[1024,512]{1,0:T(8,128)(2,1)} %collective-permute-done.1), channel_id=1, source_target_pairs={{2,0},{3,1},{4,6},{5,7},{10,8},{11,9},{12,14},{13,15},{18,16},{19,... | collective-permute-start | bytes 3145736 | tf_op jit(solution)/shard_map/ppermute | solution.py:92
  43.2 44.5 %collective-permute-start.12 = (bf16[1024,512]{1,0:T(8,128)(2,1)S(1)}, bf16[1024,512]{1,0:T(8,128)(2,1)}, u32[]{:S(2)}, u32[]{:S(2)}) collective-permute-start(bf16[1024,512]{1,0:T(8,128)(2,1)S(1)} %collective-permute-done.refs_2_), channel_id=1, source_target_pairs={{2,4},{3,5},{4,2},{5,3},{10,12},{11,13},{12,10},{13,11},{18,20},{1... | collective-permute-start | bytes 3145736 | tf_op jit(solution)/shard_map/ppermute | solution.py:92
  44.9 38.5 %all-to-all-start.1 = ((bf16[8,2,64,256]{3,2,1,0:T(8,128)(2,1)}), bf16[8,2,64,256]{3,2,1,0:T(8,128)(2,1)}, u32[]{:S(2)}, u32[]{:S(2)}) async-start(bf16[8,2,64,256]{3,2,1,0:T(8,128)(2,1)} %copy-done.6), calls=%async_computation.1 | async-start | bytes 1048576 | tf_op jit(solution)/shard_map/all_to_all | solution.py:171
  55.5 19.4 %copy-start.1 = (bf16[256,1024]{1,0:T(8,128)(2,1)}, bf16[256,1024]{1,0:T(8,128)(2,1)S(1)}, u32[]{:S(2)}) copy-start(bf16[256,1024]{1,0:T(8,128)(2,1)S(1)} %get-tuple-element.39.odd_ref) | copy-start | bytes 1572868
  55.5 32.2 %collective-permute-start.5 = (bf16[4,128,512]{2,1,0:T(8,128)(2,1)}, bf16[4,128,512]{2,1,0:T(8,128)(2,1)}, u32[]{:S(2)}, u32[]{:S(2)}) collective-permute-start(bf16[4,128,512]{2,1,0:T(8,128)(2,1)} %get-tuple-element.36), channel_id=1, source_target_pairs={{0,8},{8,0},{16,24},{24,16},{1,9},{9,1},{17,25},{25,17},{2,10},{10... | collective-permute-start | bytes 1572872 | tf_op jit(solution)/shard_map/ppermute | solution.py:154
  57.0 30.8 %collective-permute-start.6 = (bf16[4,128,512]{2,1,0:T(8,128)(2,1)}, bf16[4,128,512]{2,1,0:T(8,128)(2,1)}, u32[]{:S(2)}, u32[]{:S(2)}) collective-permute-start(bf16[4,128,512]{2,1,0:T(8,128)(2,1)} %get-tuple-element.37), channel_id=1, source_target_pairs={{0,24},{8,16},{16,8},{24,0},{1,25},{9,17},{17,9},{25,1},{2,26},{10... | collective-permute-start | bytes 1572872 | tf_op jit(solution)/shard_map/ppermute | solution.py:154
  74.8 25.9 %collective-permute-start.8 = (bf16[1024,512]{1,0:T(8,128)(2,1)}, bf16[1024,512]{1,0:T(8,128)(2,1)}, u32[]{:S(2)}, u32[]{:S(2)}) collective-permute-start(bf16[1024,512]{1,0:T(8,128)(2,1)} %broadcast_select_fusion.1.here_ref), channel_id=1, source_target_pairs={{0,1},{1,0},{2,3},{3,2},{4,5},{5,4},{6,7},{7,6},{8,9},{9,8},{10,11... | collective-permute-start | bytes 3145736 | tf_op jit(solution)/shard_map/ppermute | solution.py:89
  86.1 14.6 %copy-start.3 = (bf16[256,1024]{1,0:T(8,128)(2,1)}, bf16[256,1024]{1,0:T(8,128)(2,1)S(1)}, u32[]{:S(2)}) copy-start(bf16[256,1024]{1,0:T(8,128)(2,1)S(1)} %get-tuple-element.38.even_ref) | copy-start | bytes 1572868
  86.1 13.0 %collective-permute-start.4 = (bf16[4,128,512]{2,1,0:T(8,128)(2,1)S(1)}, bf16[4,128,512]{2,1,0:T(8,128)(2,1)S(1)}, u32[]{:S(2)}, u32[]{:S(2)}) collective-permute-start(bf16[4,128,512]{2,1,0:T(8,128)(2,1)S(1)} %get-tuple-element.35), channel_id=1, source_target_pairs={{0,16},{8,24},{16,0},{24,8},{1,17},{9,25},{17,1},{25,9},{2,18},{10... | collective-permute-start | bytes 1572872 | tf_op jit(solution)/shard_map/ppermute | solution.py:154
  87.7 13.0 %copy-start.2 = (bf16[256,1024]{1,0:T(8,128)(2,1)S(1)}, bf16[256,1024]{1,0:T(8,128)(2,1)}, u32[]{:S(2)}) copy-start(bf16[256,1024]{1,0:T(8,128)(2,1)} %copy-done.1) | copy-start | bytes 1572868
  87.7 31.0 %collective-permute-start.13 = (bf16[1024,512]{1,0:T(8,128)(2,1)}, bf16[1024,512]{1,0:T(8,128)(2,1)S(1)}, u32[]{:S(2)}, u32[]{:S(2)}) collective-permute-start(bf16[1024,512]{1,0:T(8,128)(2,1)} %collective-permute-done.12), channel_id=1, source_target_pairs={{2,0},{3,1},{4,6},{5,7},{10,8},{11,9},{12,14},{13,15},{18,16},{19,... | collective-permute-start | bytes 3145736 | tf_op jit(solution)/shard_map/ppermute | solution.py:92
  103.5 9.3 %collective-permute-start.10 = (bf16[2,128,512]{2,1,0:T(8,128)(2,1)S(1)}, bf16[2,128,512]{2,1,0:T(8,128)(2,1)S(1)}, u32[]{:S(2)}, u32[]{:S(2)}) collective-permute-start(bf16[2,128,512]{2,1,0:T(8,128)(2,1)S(1)} %get-tuple-element.44), channel_id=1, source_target_pairs={{0,8},{8,0},{16,24},{24,16},{1,9},{9,1},{17,25},{25,17},{2,10},{10... | collective-permute-start | bytes 786440 | tf_op jit(solution)/shard_map/ppermute | solution.py:154
  105.1 11.6 %collective-permute-start.11 = (bf16[2,128,512]{2,1,0:T(8,128)(2,1)S(1)}, bf16[2,128,512]{2,1,0:T(8,128)(2,1)S(1)}, u32[]{:S(2)}, u32[]{:S(2)}) collective-permute-start(bf16[2,128,512]{2,1,0:T(8,128)(2,1)S(1)} %get-tuple-element.45), channel_id=1, source_target_pairs={{0,24},{8,16},{16,8},{24,0},{1,25},{9,17},{17,9},{25,1},{2,26},{10... | collective-permute-start | bytes 786440 | tf_op jit(solution)/shard_map/ppermute | solution.py:154
  106.6 15.2 %copy-start.4 = (bf16[256,1024]{1,0:T(8,128)(2,1)S(1)}, bf16[256,1024]{1,0:T(8,128)(2,1)}, u32[]{:S(2)}) copy-start(bf16[256,1024]{1,0:T(8,128)(2,1)} %copy-done.3) | copy-start | bytes 1572868
  106.6 11.5 %collective-permute-start.9 = (bf16[2,128,512]{2,1,0:T(8,128)(2,1)S(1)}, bf16[2,128,512]{2,1,0:T(8,128)(2,1)S(1)}, u32[]{:S(2)}, u32[]{:S(2)}) collective-permute-start(bf16[2,128,512]{2,1,0:T(8,128)(2,1)S(1)} %get-tuple-element.43), channel_id=1, source_target_pairs={{0,16},{8,24},{16,0},{24,8},{1,17},{9,25},{17,1},{25,9},{2,18},{10... | collective-permute-start | bytes 786440 | tf_op jit(solution)/shard_map/ppermute | solution.py:154
  118.9 2.9 %collective-permute-start.14 = (bf16[1024,512]{1,0:T(8,128)(2,1)S(1)}, bf16[1024,512]{1,0:T(8,128)(2,1)}, u32[]{:S(2)}, u32[]{:S(2)}) collective-permute-start(bf16[1024,512]{1,0:T(8,128)(2,1)S(1)} %broadcast_select_fusion.here_ref), channel_id=1, source_target_pairs={{0,1},{1,0},{2,3},{3,2},{4,5},{5,4},{6,7},{7,6},{8,9},{9,8},{10,11... | collective-permute-start | bytes 3145736 | tf_op jit(solution)/shard_map/ppermute | solution.py:89
  124.3 8.4 %collective-permute-start.15 = (bf16[2,128,512]{2,1,0:T(8,128)(2,1)S(1)}, bf16[2,128,512]{2,1,0:T(8,128)(2,1)S(1)}, u32[]{:S(2)}, u32[]{:S(2)}) collective-permute-start(bf16[2,128,512]{2,1,0:T(8,128)(2,1)S(1)} %get-tuple-element.50), channel_id=1, source_target_pairs={{0,16},{8,24},{16,0},{24,8},{1,17},{9,25},{17,1},{25,9},{2,18},{10... | collective-permute-start | bytes 786440 | tf_op jit(solution)/shard_map/ppermute | solution.py:154
  124.8 9.2 %collective-permute-start.16 = (bf16[2,128,512]{2,1,0:T(8,128)(2,1)S(1)}, bf16[2,128,512]{2,1,0:T(8,128)(2,1)S(1)}, u32[]{:S(2)}, u32[]{:S(2)}) collective-permute-start(bf16[2,128,512]{2,1,0:T(8,128)(2,1)S(1)} %get-tuple-element.51), channel_id=1, source_target_pairs={{0,8},{8,0},{16,24},{24,16},{1,9},{9,1},{17,25},{25,17},{2,10},{10... | collective-permute-start | bytes 786440 | tf_op jit(solution)/shard_map/ppermute | solution.py:154
  126.3 13.2 %collective-permute-start.17 = (bf16[2,128,512]{2,1,0:T(8,128)(2,1)S(1)}, bf16[2,128,512]{2,1,0:T(8,128)(2,1)S(1)}, u32[]{:S(2)}, u32[]{:S(2)}) collective-permute-start(bf16[2,128,512]{2,1,0:T(8,128)(2,1)S(1)} %get-tuple-element.52), channel_id=1, source_target_pairs={{0,24},{8,16},{16,8},{24,0},{1,25},{9,17},{17,9},{25,1},{2,26},{10... | collective-permute-start | bytes 786440 | tf_op jit(solution)/shard_map/ppermute | solution.py:154
  (7 other events, 29.1 us)

commit v12 on v10

--- a/solution.py
+++ b/solution.py
@@ -155,12 +155,13 @@
             y3, e2 = along(x1, swap), along(y2, outward)
             sums = [summed(exchange(parts))]
             parts = product(pair1)
-            e3 = along(after(y3, sums[0], *parts), outward)
-            sums.append(summed(exchange(parts)))
+            group = exchange(parts)
+            e3 = along(after(y3, sums[0], group[-1]), outward)
+            sums.append(summed(group))
             x2 = jnp.where(end, e2, y2)
             group = exchange(product((after(x2, sums[1]), across(x2))))
             sums.append(summed(group))
-            x3 = jnp.where(end, after(e3, *group[1:]), y3)
+            x3 = jnp.where(end, after(e3, group[-1]), y3)
             last = exchange(product((x3, across(x3))))
             slots = [z, z ^ 1, jnp.where(end, z ^ 2, 3 - z), jnp.where(end, 3 - z, z ^ 2)]
         else:

time: 163 us -> 156 us (0.957)
  waiting for transfers between devices: 80.8 us -> 72.6 us
  blocking collectives: 35.4 us -> 32 us
  starting transfers between devices: 28.5 us -> 31.7 us
    ppermute x12, waiting for transfers between devices: 34.9 us -> 27.9 us  [exchange(): lax.ppermute(parts[t], 'row', [(r, r ^ t) for r in range(nrow)])]
    all_to_all x1, blocking collectives: 35.4 us -> 32 us  [local(): second = lax.all_to_all(turned, ('row', 'col'), 0, 0, tiled=True)]
    ppermute x12, starting transfers between devices: 14.1 us -> 17.3 us  [exchange(): lax.ppermute(parts[t], 'row', [(r, r ^ t) for r in range(nrow)])]
    ppermute x4, waiting for transfers between devices: 2.55 us -> 0.01 us  [across(): return lax.ppermute(x, 'col', [(s, s ^ 1) for s in range(ncol)])]
    unnamed x26 -> x18, local copies, waits for them, and re-layouts: 4.19 us -> 3.76 us
  transfers between devices with their start and end apart: 22 -> 22, of which waited for: 12 -> 13; matrix products, arithmetic and copies ran while one was open for 2% -> 2% of each run, Pallas kernels for 5% -> 6%
where the time goes in v12:
time: 156 us
  waiting for transfers between devices  72.6 us (47%)
  blocking collectives  32 us (21%)
  starting transfers between devices  31.7 us (20%)
  Pallas kernels  12.1 us (8%)
  other arithmetic  3.77 us (2%)
  local copies, waits for them, and re-layouts  3.76 us (2%)
    all_to_all x1, blocking collectives, local(): second = lax.all_to_all(turned, ('row', 'col'), 0, 0, tiled=True)  32 us
    ppermute x12, waiting for transfers between devices, exchange(): lax.ppermute(parts[t], 'row', [(r, r ^ t) for r in range(nrow)])  27.9 us
    all_to_all x1, waiting for transfers between devices, local(): raw = lax.all_to_all(blocks, 'col', 0, 0, tiled=True)  23 us
    ppermute x5, waiting for transfers between devices, along(): lax.ppermute(x, 'col', [(2 * a + c, 2 * b + c) for a, b in pairs for c in...  21.7 us
    ppermute x12, starting transfers between devices, exchange(): lax.ppermute(parts[t], 'row', [(r, r ^ t) for r in range(nrow)])  17.3 us
    ppermute x5, starting transfers between devices, along(): lax.ppermute(x, 'col', [(2 * a + c, 2 * b + c) for a, b in pairs for c in...  8.85 us
    pallas_call x3, Pallas kernels, product(): pl.pallas_call(functools.partial(product_kernel, 1), out_shape=sent, in_s...  5.72 us
    all_to_all x1, starting transfers between devices, local(): raw = lax.all_to_all(blocks, 'col', 0, 0, tiled=True)  4.83 us
  transfers between devices with their start and end apart: 22, of which 13 were waited for; matrix products, arithmetic and copies ran while one was open for 2% of the time, Pallas kernels for 6%

profile of v12, /device:TPU:0, one launch (start us, length us, event | category | flops | bytes accessed | tf_op | source)
XLA Modules:
  0.0 156.0 jit_solution(13880804181728550771)
XLA Ops:
  0.0 3.0 %collective-permute-start.1 = (bf16[1024,512]{1,0:T(8,128)(2,1)}, bf16[1024,512]{1,0:T(8,128)(2,1)}, u32[]{:S(2)}, u32[]{:S(2)}) collective-permute-start(bf16[1024,512]{1,0:T(8,128)(2,1)} %bitcast.7), channel_id=1, source_target_pairs={{0,2},{1,3},{2,0},{3,1},{4,6},{5,7},{6,4},{7,5},{8,10},{9,11},{10,... | collective-permute-start | bytes 3145736 | tf_op jit(solution)/shard_map/ppermute | solution.py:88
  3.0 1.6 %collective-permute-start.9 = (bf16[1024,512]{1,0:T(8,128)(2,1)}, bf16[1024,512]{1,0:T(8,128)(2,1)}, u32[]{:S(2)}, u32[]{:S(2)}) collective-permute-start(bf16[1024,512]{1,0:T(8,128)(2,1)} %bitcast.8), channel_id=1, source_target_pairs={{2,4},{3,5},{4,2},{5,3},{10,12},{11,13},{12,10},{13,11},{18,20},{1... | collective-permute-start | bytes 3145736 | tf_op jit(solution)/shard_map/ppermute | solution.py:88
  7.2 4.8 %all-to-all-start = ((bf16[8,2,64,512]{3,2,1,0:T(8,128)(2,1)}), bf16[8,2,64,512]{3,2,1,0:T(8,128)(2,1)S(1)}, u32[]{:S(2)}, u32[]{:S(2)}) async-start(bf16[8,2,64,512]{3,2,1,0:T(8,128)(2,1)} %shard_map.28), calls=%async_computation | async-start | bytes 2097152 | tf_op jit(solution)/shard_map/all_to_all | solution.py:121
  12.5 14.8 %collective-permute-done.1.refs_0_ = bf16[1024,512]{1,0:T(8,128)(2,1)} collective-permute-done((bf16[1024,512]{1,0:T(8,128)(2,1)}, bf16[1024,512]{1,0:T(8,128)(2,1)}, u32[]{:S(2)}, u32[]{:S(2)}) %collective-permute-start.1) | collective-permute-done | bytes 1048608 | tf_op jit(solution)/shard_map/ppermute | solution.py:88
  28.6 1.6 %collective-permute-start.15 = (bf16[1024,512]{1,0:T(8,128)(2,1)}, bf16[1024,512]{1,0:T(8,128)(2,1)}, u32[]{:S(2)}, u32[]{:S(2)}) collective-permute-start(bf16[1024,512]{1,0:T(8,128)(2,1)} %collective-permute-done.1.refs_0_), channel_id=1, source_target_pairs={{2,4},{3,5},{4,2},{5,3},{10,12},{11,13},{12,10},{13,11},{18,20},{1... | collective-permute-start | bytes 3145736 | tf_op jit(solution)/shard_map/ppermute | solution.py:88
  31.3 23.0 %all-to-all-done.raw_ref = bf16[8,2,64,512]{3,2,1,0:T(8,128)(2,1)S(1)} async-done(((bf16[8,2,64,512]{3,2,1,0:T(8,128)(2,1)}), bf16[8,2,64,512]{3,2,1,0:T(8,128)(2,1)S(1)}, u32[]{:S(2)}, u32[]{:S(2)}) %all-to-all-start) | async-done | bytes 1048608 | tf_op jit(solution)/shard_map/all_to_all | solution.py:121
  54.3 2.6 %shard_map.29 = (bf16[512,1024]{1,0:T(8,128)(2,1)S(1)}, f32[2,128,512]{2,1,0:T(8,128)S(1)}, bf16[2,128,512]{2,1,0:T(8,128)(2,1)S(1)}, bf16[2,128,512]{2,1,0:T(8,128)(2,1)S(1)}, bf16[2,128,512]{2,1,0:T(8,128)(2,1)S(1)}) custom-call(s32[1]{0:T(128)} %bitcast.4.core_ref, bf16[8,2,64,512]{3,2,1,0:T(8,128)(2,1)S(1)} %all-to-all-done.raw_ref, ...), custom_call_target="tpu_custom_call" | custom-call | tf_op jit(solution)/shard_map/pallas_call | solution.py:124
  56.9 2.5 %collective-permute-start.5 = (bf16[2,128,512]{2,1,0:T(8,128)(2,1)S(1)}, bf16[2,128,512]{2,1,0:T(8,128)(2,1)S(1)}, u32[]{:S(2)}, u32[]{:S(2)}) collective-permute-start(bf16[2,128,512]{2,1,0:T(8,128)(2,1)S(1)} %get-tuple-element.34), channel_id=1, source_target_pairs={{0,24},{8,16},{16,8},{24,0},{1,25},{9,17},{17,9},{25,1},{2,26},{10... | collective-permute-start | bytes 786440 | tf_op jit(solution)/shard_map/ppermute | solution.py:143
  60.4 2.5 %shard_map.30 = (f32[2,128,512]{2,1,0:T(8,128)S(1)}, bf16[2,128,512]{2,1,0:T(8,128)(2,1)S(1)}, bf16[2,128,512]{2,1,0:T(8,128)(2,1)S(1)}, bf16[2,128,512]{2,1,0:T(8,128)(2,1)S(1)}) custom-call(s32[1]{0:T(128)} %bitcast.4.core_ref, bf16[512,1024]{1,0:T(8,128)(2,1)S(1)} %get-tuple-element.35.panel_ref, bf16[1024,512]{1,0:T(8,128)(2,1)} %collective-permute-done.1.refs_0_, ...), custom_call_target="tpu_custom_call" | custom-call | tf_op jit(solution)/shard_map/pallas_call | solution.py:133
  62.9 2.9 %collective-permute-done.10 = bf16[1024,512]{1,0:T(8,128)(2,1)} collective-permute-done((bf16[1024,512]{1,0:T(8,128)(2,1)}, bf16[1024,512]{1,0:T(8,128)(2,1)}, u32[]{:S(2)}, u32[]{:S(2)}) %collective-permute-start.10) | collective-permute-done | bytes 1048608 | tf_op jit(solution)/shard_map/ppermute | solution.py:88
  65.8 2.6 %collective-permute-start.8 = (bf16[2,128,512]{2,1,0:T(8,128)(2,1)S(1)}, bf16[2,128,512]{2,1,0:T(8,128)(2,1)S(1)}, u32[]{:S(2)}, u32[]{:S(2)}) collective-permute-start(bf16[2,128,512]{2,1,0:T(8,128)(2,1)S(1)} %get-tuple-element.39), channel_id=1, source_target_pairs={{0,24},{8,16},{16,8},{24,0},{1,25},{9,17},{17,9},{25,1},{2,26},{10... | collective-permute-start | bytes 786440 | tf_op jit(solution)/shard_map/ppermute | solution.py:143
  69.9 2.4 %collective-permute-done.4 = bf16[2,128,512]{2,1,0:T(8,128)(2,1)S(1)} collective-permute-done((bf16[2,128,512]{2,1,0:T(8,128)(2,1)S(1)}, bf16[2,128,512]{2,1,0:T(8,128)(2,1)S(1)}, u32[]{:S(2)}, u32[]{:S(2)}) %collective-permute-start.4) | collective-permute-done | bytes 262176 | tf_op jit(solution)/shard_map/ppermute | solution.py:143
  72.5 2.6 %collective-permute-done.8 = bf16[2,128,512]{2,1,0:T(8,128)(2,1)S(1)} collective-permute-done((bf16[2,128,512]{2,1,0:T(8,128)(2,1)S(1)}, bf16[2,128,512]{2,1,0:T(8,128)(2,1)S(1)}, u32[]{:S(2)}, u32[]{:S(2)}) %collective-permute-start.8) | collective-permute-done | bytes 262176 | tf_op jit(solution)/shard_map/ppermute | solution.py:143
  76.4 1.6 %collective-permute-start.7 = (bf16[2,128,512]{2,1,0:T(8,128)(2,1)S(1)}, bf16[2,128,512]{2,1,0:T(8,128)(2,1)S(1)}, u32[]{:S(2)}, u32[]{:S(2)}) collective-permute-start(bf16[2,128,512]{2,1,0:T(8,128)(2,1)S(1)} %get-tuple-element.38), channel_id=1, source_target_pairs={{0,16},{8,24},{16,0},{24,8},{1,17},{9,25},{17,1},{25,9},{2,18},{10... | collective-permute-start | bytes 786440 | tf_op jit(solution)/shard_map/ppermute | solution.py:143
  79.5 3.3 %collective-permute-done.7 = bf16[2,128,512]{2,1,0:T(8,128)(2,1)S(1)} collective-permute-done((bf16[2,128,512]{2,1,0:T(8,128)(2,1)S(1)}, bf16[2,128,512]{2,1,0:T(8,128)(2,1)S(1)}, u32[]{:S(2)}, u32[]{:S(2)}) %collective-permute-start.7) | collective-permute-done | bytes 262176 | tf_op jit(solution)/shard_map/ppermute | solution.py:143
  82.8 1.6 collective-permute-done.6
  85.2 2.0 %shard_map.31 = (f32[2,128,512]{2,1,0:T(8,128)S(1)}, bf16[2,128,512]{2,1,0:T(8,128)(2,1)}, bf16[2,128,512]{2,1,0:T(8,128)(2,1)}, bf16[2,128,512]{2,1,0:T(8,128)(2,1)S(1)}) custom-call(s32[1]{0:T(128)} %bitcast.4.core_ref, bf16[512,1024]{1,0:T(8,128)(2,1)S(1)} %get-tuple-element.35.panel_ref, bf16[1024,512]{1,0:T(8,128)(2,1)S(1)} %broadcast_select_fusion.1.refs_0_, ...), custom_call_target="tpu_custom_call" | custom-call | tf_op jit(solution)/shard_map/pallas_call | solution.py:133
  89.4 5.8 %collective-permute-done.14 = bf16[2,128,512]{2,1,0:T(8,128)(2,1)S(1)} collective-permute-done((bf16[2,128,512]{2,1,0:T(8,128)(2,1)S(1)}, bf16[2,128,512]{2,1,0:T(8,128)(2,1)S(1)}, u32[]{:S(2)}, u32[]{:S(2)}) %collective-permute-start.14) | collective-permute-done | bytes 262176 | tf_op jit(solution)/shard_map/ppermute | solution.py:143
  96.0 4.0 %collective-permute-done.16 = bf16[1024,512]{1,0:T(8,128)(2,1)S(1)} collective-permute-done((bf16[1024,512]{1,0:T(8,128)(2,1)}, bf16[1024,512]{1,0:T(8,128)(2,1)S(1)}, u32[]{:S(2)}, u32[]{:S(2)}) %collective-permute-start.16) | collective-permute-done | bytes 1048608 | tf_op jit(solution)/shard_map/ppermute | solution.py:88
  100.2 1.6 %collective-permute-start.13 = (bf16[2,128,512]{2,1,0:T(8,128)(2,1)}, bf16[2,128,512]{2,1,0:T(8,128)(2,1)}, u32[]{:S(2)}, u32[]{:S(2)}) collective-permute-start(bf16[2,128,512]{2,1,0:T(8,128)(2,1)} %get-tuple-element.44), channel_id=1, source_target_pairs={{0,16},{8,24},{16,0},{24,8},{1,17},{9,25},{17,1},{25,9},{2,18},{10... | collective-permute-start | bytes 786440 | tf_op jit(solution)/shard_map/ppermute | solution.py:143
  109.7 1.6 %collective-permute-done.12 = bf16[2,128,512]{2,1,0:T(8,128)(2,1)} collective-permute-done((bf16[2,128,512]{2,1,0:T(8,128)(2,1)}, bf16[2,128,512]{2,1,0:T(8,128)(2,1)}, u32[]{:S(2)}, u32[]{:S(2)}) %collective-permute-start.12) | collective-permute-done | bytes 262176 | tf_op jit(solution)/shard_map/ppermute | solution.py:143
  112.5 4.3 %collective-permute-done.18.refs_4_ = bf16[2,128,512]{2,1,0:T(8,128)(2,1)S(1)} collective-permute-done((bf16[2,128,512]{2,1,0:T(8,128)(2,1)S(1)}, bf16[2,128,512]{2,1,0:T(8,128)(2,1)S(1)}, u32[]{:S(2)}, u32[]{:S(2)}) %collective-permute-start.18) | collective-permute-done | bytes 262176 | tf_op jit(solution)/shard_map/ppermute | solution.py:143
  116.8 4.8 %collective-permute-done.20.refs_6_ = bf16[2,128,512]{2,1,0:T(8,128)(2,1)S(1)} collective-permute-done((bf16[2,128,512]{2,1,0:T(8,128)(2,1)S(1)}, bf16[2,128,512]{2,1,0:T(8,128)(2,1)S(1)}, u32[]{:S(2)}, u32[]{:S(2)}) %collective-permute-start.20) | collective-permute-done | bytes 262176 | tf_op jit(solution)/shard_map/ppermute | solution.py:143
  122.5 32.0 %all_to_all.10.second_ref = bf16[32,2,64,128]{3,2,1,0:T(8,128)(2,1)S(1)} all-to-all(bf16[32,2,64,128]{3,2,1,0:T(8,128)(2,1)S(1)} %get-tuple-element.54), channel_id=1, replica_groups=mesh['row'=4,'col'=8] {'row','col'}, dimensions={0} | all-to-all | bytes 2097152 | tf_op jit(solution)/shard_map/all_to_all | solution.py:188
  (52 shorter events, 26.3 us)
Async XLA Ops:
  0.0 27.3 %collective-permute-start.1 = (bf16[1024,512]{1,0:T(8,128)(2,1)}, bf16[1024,512]{1,0:T(8,128)(2,1)}, u32[]{:S(2)}, u32[]{:S(2)}) collective-permute-start(bf16[1024,512]{1,0:T(8,128)(2,1)} %bitcast.7), channel_id=1, source_target_pairs={{0,2},{1,3},{2,0},{3,1},{4,6},{5,7},{6,4},{7,5},{8,10},{9,11},{10,... | collective-permute-start | bytes 3145736 | tf_op jit(solution)/shard_map/ppermute | solution.py:88
  3.0 24.3 %collective-permute-start.9 = (bf16[1024,512]{1,0:T(8,128)(2,1)}, bf16[1024,512]{1,0:T(8,128)(2,1)}, u32[]{:S(2)}, u32[]{:S(2)}) collective-permute-start(bf16[1024,512]{1,0:T(8,128)(2,1)} %bitcast.8), channel_id=1, source_target_pairs={{2,4},{3,5},{4,2},{5,3},{10,12},{11,13},{12,10},{13,11},{18,20},{1... | collective-permute-start | bytes 3145736 | tf_op jit(solution)/shard_map/ppermute | solution.py:88
  7.2 47.1 %all-to-all-start = ((bf16[8,2,64,512]{3,2,1,0:T(8,128)(2,1)}), bf16[8,2,64,512]{3,2,1,0:T(8,128)(2,1)S(1)}, u32[]{:S(2)}, u32[]{:S(2)}) async-start(bf16[8,2,64,512]{3,2,1,0:T(8,128)(2,1)} %shard_map.28), calls=%async_computation | async-start | bytes 2097152 | tf_op jit(solution)/shard_map/all_to_all | solution.py:121
  12.0 18.2 %collective-permute-start = (bf16[1024,512]{1,0:T(8,128)(2,1)S(1)}, bf16[1024,512]{1,0:T(8,128)(2,1)}, u32[]{:S(2)}, u32[]{:S(2)}) collective-permute-start(bf16[1024,512]{1,0:T(8,128)(2,1)S(1)} %bitcast.9), channel_id=1, source_target_pairs={{0,1},{1,0},{2,3},{3,2},{4,5},{5,4},{6,7},{7,6},{8,9},{9,8},{10,11... | collective-permute-start | bytes 3145736 | tf_op jit(solution)/shard_map/ppermute | solution.py:85
  27.3 2.9 %collective-permute-start.2 = (bf16[1024,512]{1,0:T(8,128)(2,1)}, bf16[1024,512]{1,0:T(8,128)(2,1)S(1)}, u32[]{:S(2)}, u32[]{:S(2)}) collective-permute-start(bf16[1024,512]{1,0:T(8,128)(2,1)} %collective-permute-done.1.refs_0_), channel_id=1, source_target_pairs={{0,1},{1,0},{2,3},{3,2},{4,5},{5,4},{6,7},{7,6},{8,9},{9,8},{10,11... | collective-permute-start | bytes 3145736 | tf_op jit(solution)/shard_map/ppermute | solution.py:85
  27.3 38.5 %collective-permute-start.10 = (bf16[1024,512]{1,0:T(8,128)(2,1)}, bf16[1024,512]{1,0:T(8,128)(2,1)}, u32[]{:S(2)}, u32[]{:S(2)}) collective-permute-start(bf16[1024,512]{1,0:T(8,128)(2,1)} %collective-permute-done.9), channel_id=1, source_target_pairs={{2,0},{3,1},{4,6},{5,7},{10,8},{11,9},{12,14},{13,15},{18,16},{19,... | collective-permute-start | bytes 3145736 | tf_op jit(solution)/shard_map/ppermute | solution.py:88
  28.6 43.9 %collective-permute-start.15 = (bf16[1024,512]{1,0:T(8,128)(2,1)}, bf16[1024,512]{1,0:T(8,128)(2,1)}, u32[]{:S(2)}, u32[]{:S(2)}) collective-permute-start(bf16[1024,512]{1,0:T(8,128)(2,1)} %collective-permute-done.1.refs_0_), channel_id=1, source_target_pairs={{2,4},{3,5},{4,2},{5,3},{10,12},{11,13},{12,10},{13,11},{18,20},{1... | collective-permute-start | bytes 3145736 | tf_op jit(solution)/shard_map/ppermute | solution.py:88
  56.9 12.9 %collective-permute-start.5 = (bf16[2,128,512]{2,1,0:T(8,128)(2,1)S(1)}, bf16[2,128,512]{2,1,0:T(8,128)(2,1)S(1)}, u32[]{:S(2)}, u32[]{:S(2)}) collective-permute-start(bf16[2,128,512]{2,1,0:T(8,128)(2,1)S(1)} %get-tuple-element.34), channel_id=1, source_target_pairs={{0,24},{8,16},{16,8},{24,0},{1,25},{9,17},{17,9},{25,1},{2,26},{10... | collective-permute-start | bytes 786440 | tf_op jit(solution)/shard_map/ppermute | solution.py:143
  59.4 12.9 %collective-permute-start.4 = (bf16[2,128,512]{2,1,0:T(8,128)(2,1)S(1)}, bf16[2,128,512]{2,1,0:T(8,128)(2,1)S(1)}, u32[]{:S(2)}, u32[]{:S(2)}) collective-permute-start(bf16[2,128,512]{2,1,0:T(8,128)(2,1)S(1)} %get-tuple-element.33), channel_id=1, source_target_pairs={{0,16},{8,24},{16,0},{24,8},{1,17},{9,25},{17,1},{25,9},{2,18},{10... | collective-permute-start | bytes 786440 | tf_op jit(solution)/shard_map/ppermute | solution.py:143
  59.9 12.4 %collective-permute-start.3 = (bf16[2,128,512]{2,1,0:T(8,128)(2,1)S(1)}, bf16[2,128,512]{2,1,0:T(8,128)(2,1)S(1)}, u32[]{:S(2)}, u32[]{:S(2)}) collective-permute-start(bf16[2,128,512]{2,1,0:T(8,128)(2,1)S(1)} %get-tuple-element.32), channel_id=1, source_target_pairs={{0,8},{8,0},{16,24},{24,16},{1,9},{9,1},{17,25},{25,17},{2,10},{10... | collective-permute-start | bytes 786440 | tf_op jit(solution)/shard_map/ppermute | solution.py:143
  65.8 9.3 %collective-permute-start.8 = (bf16[2,128,512]{2,1,0:T(8,128)(2,1)S(1)}, bf16[2,128,512]{2,1,0:T(8,128)(2,1)S(1)}, u32[]{:S(2)}, u32[]{:S(2)}) collective-permute-start(bf16[2,128,512]{2,1,0:T(8,128)(2,1)S(1)} %get-tuple-element.39), channel_id=1, source_target_pairs={{0,24},{8,16},{16,8},{24,0},{1,25},{9,17},{17,9},{25,1},{2,26},{10... | collective-permute-start | bytes 786440 | tf_op jit(solution)/shard_map/ppermute | solution.py:143
  69.8 15.4 %collective-permute-start.11 = (bf16[1024,512]{1,0:T(8,128)(2,1)S(1)}, bf16[1024,512]{1,0:T(8,128)(2,1)S(1)}, u32[]{:S(2)}, u32[]{:S(2)}) collective-permute-start(bf16[1024,512]{1,0:T(8,128)(2,1)S(1)} %broadcast_select_fusion.1.refs_0_), channel_id=1, source_target_pairs={{0,1},{1,0},{2,3},{3,2},{4,5},{5,4},{6,7},{7,6},{8,9},{9,8},{10,11... | collective-permute-start | bytes 3145736 | tf_op jit(solution)/shard_map/ppermute | solution.py:85
  75.1 24.9 %collective-permute-start.16 = (bf16[1024,512]{1,0:T(8,128)(2,1)}, bf16[1024,512]{1,0:T(8,128)(2,1)S(1)}, u32[]{:S(2)}, u32[]{:S(2)}) collective-permute-start(bf16[1024,512]{1,0:T(8,128)(2,1)} %collective-permute-done.15), channel_id=1, source_target_pairs={{2,0},{3,1},{4,6},{5,7},{10,8},{11,9},{12,14},{13,15},{18,16},{19,... | collective-permute-start | bytes 3145736 | tf_op jit(solution)/shard_map/ppermute | solution.py:88
  76.4 6.4 %collective-permute-start.7 = (bf16[2,128,512]{2,1,0:T(8,128)(2,1)S(1)}, bf16[2,128,512]{2,1,0:T(8,128)(2,1)S(1)}, u32[]{:S(2)}, u32[]{:S(2)}) collective-permute-start(bf16[2,128,512]{2,1,0:T(8,128)(2,1)S(1)} %get-tuple-element.38), channel_id=1, source_target_pairs={{0,16},{8,24},{16,0},{24,8},{1,17},{9,25},{17,1},{25,9},{2,18},{10... | collective-permute-start | bytes 786440 | tf_op jit(solution)/shard_map/ppermute | solution.py:143
  78.0 6.4 %collective-permute-start.6 = (bf16[2,128,512]{2,1,0:T(8,128)(2,1)S(1)}, bf16[2,128,512]{2,1,0:T(8,128)(2,1)S(1)}, u32[]{:S(2)}, u32[]{:S(2)}) collective-permute-start(bf16[2,128,512]{2,1,0:T(8,128)(2,1)S(1)} %get-tuple-element.37), channel_id=1, source_target_pairs={{0,8},{8,0},{16,24},{24,16},{1,9},{9,1},{17,25},{25,17},{2,10},{10... | collective-permute-start | bytes 786440 | tf_op jit(solution)/shard_map/ppermute | solution.py:143
  88.0 7.3 %collective-permute-start.14 = (bf16[2,128,512]{2,1,0:T(8,128)(2,1)S(1)}, bf16[2,128,512]{2,1,0:T(8,128)(2,1)S(1)}, u32[]{:S(2)}, u32[]{:S(2)}) collective-permute-start(bf16[2,128,512]{2,1,0:T(8,128)(2,1)S(1)} %get-tuple-element.45), channel_id=1, source_target_pairs={{0,24},{8,16},{16,8},{24,0},{1,25},{9,17},{17,9},{25,1},{2,26},{10... | collective-permute-start | bytes 786440 | tf_op jit(solution)/shard_map/ppermute | solution.py:143
  100.1 3.2 %collective-permute-start.17 = (bf16[1024,512]{1,0:T(8,128)(2,1)S(1)}, bf16[1024,512]{1,0:T(8,128)(2,1)S(1)}, u32[]{:S(2)}, u32[]{:S(2)}) collective-permute-start(bf16[1024,512]{1,0:T(8,128)(2,1)S(1)} %broadcast_select_fusion.refs_0_), channel_id=1, source_target_pairs={{0,1},{1,0},{2,3},{3,2},{4,5},{5,4},{6,7},{7,6},{8,9},{9,8},{10,11... | collective-permute-start | bytes 3145736 | tf_op jit(solution)/shard_map/ppermute | solution.py:85
  100.2 9.5 %collective-permute-start.13 = (bf16[2,128,512]{2,1,0:T(8,128)(2,1)}, bf16[2,128,512]{2,1,0:T(8,128)(2,1)}, u32[]{:S(2)}, u32[]{:S(2)}) collective-permute-start(bf16[2,128,512]{2,1,0:T(8,128)(2,1)} %get-tuple-element.44), channel_id=1, source_target_pairs={{0,16},{8,24},{16,0},{24,8},{1,17},{9,25},{17,1},{25,9},{2,18},{10... | collective-permute-start | bytes 786440 | tf_op jit(solution)/shard_map/ppermute | solution.py:143
  101.8 9.5 %collective-permute-start.12 = (bf16[2,128,512]{2,1,0:T(8,128)(2,1)}, bf16[2,128,512]{2,1,0:T(8,128)(2,1)}, u32[]{:S(2)}, u32[]{:S(2)}) collective-permute-start(bf16[2,128,512]{2,1,0:T(8,128)(2,1)} %get-tuple-element.43), channel_id=1, source_target_pairs={{0,8},{8,0},{16,24},{24,16},{1,9},{9,1},{17,25},{25,17},{2,10},{10... | collective-permute-start | bytes 786440 | tf_op jit(solution)/shard_map/ppermute | solution.py:143
  103.4 7.9 %copy-start.8 = (bf16[2,128,512]{2,1,0:T(8,128)(2,1)S(1)}, bf16[2,128,512]{2,1,0:T(8,128)(2,1)}, u32[]{:S(2)}) copy-start(bf16[2,128,512]{2,1,0:T(8,128)(2,1)} %copy-done.7) | copy-start | bytes 786436
  104.6 12.1 %collective-permute-start.18 = (bf16[2,128,512]{2,1,0:T(8,128)(2,1)S(1)}, bf16[2,128,512]{2,1,0:T(8,128)(2,1)S(1)}, u32[]{:S(2)}, u32[]{:S(2)}) collective-permute-start(bf16[2,128,512]{2,1,0:T(8,128)(2,1)S(1)} %get-tuple-element.50), channel_id=1, source_target_pairs={{0,8},{8,0},{16,24},{24,16},{1,9},{9,1},{17,25},{25,17},{2,10},{10... | collective-permute-start | bytes 786440 | tf_op jit(solution)/shard_map/ppermute | solution.py:143
  105.7 11.1 %collective-permute-start.19 = (bf16[2,128,512]{2,1,0:T(8,128)(2,1)S(1)}, bf16[2,128,512]{2,1,0:T(8,128)(2,1)S(1)}, u32[]{:S(2)}, u32[]{:S(2)}) collective-permute-start(bf16[2,128,512]{2,1,0:T(8,128)(2,1)S(1)} %get-tuple-element.51), channel_id=1, source_target_pairs={{0,16},{8,24},{16,0},{24,8},{1,17},{9,25},{17,1},{25,9},{2,18},{10... | collective-permute-start | bytes 786440 | tf_op jit(solution)/shard_map/ppermute | solution.py:143
  107.2 14.4 %collective-permute-start.20 = (bf16[2,128,512]{2,1,0:T(8,128)(2,1)S(1)}, bf16[2,128,512]{2,1,0:T(8,128)(2,1)S(1)}, u32[]{:S(2)}, u32[]{:S(2)}) collective-permute-start(bf16[2,128,512]{2,1,0:T(8,128)(2,1)S(1)} %get-tuple-element.52), channel_id=1, source_target_pairs={{0,24},{8,16},{16,8},{24,0},{1,25},{9,17},{17,9},{25,1},{2,26},{10... | collective-permute-start | bytes 786440 | tf_op jit(solution)/shard_map/ppermute | solution.py:143
  111.3 10.3 %copy-start.4 = (bf16[2,128,512]{2,1,0:T(8,128)(2,1)S(1)}, bf16[2,128,512]{2,1,0:T(8,128)(2,1)}, u32[]{:S(2)}) copy-start(bf16[2,128,512]{2,1,0:T(8,128)(2,1)} %add_convert_fusion.1.refs_1_) | copy-start | bytes 786436
  (7 other events, 22.6 us)

commit v13 on v12

--- a/solution.py
+++ b/solution.py
@@ -161,7 +161,7 @@
             x2 = jnp.where(end, e2, y2)
             group = exchange(product((after(x2, sums[1]), across(x2))))
             sums.append(summed(group))
-            x3 = jnp.where(end, after(e3, group[-1]), y3)
+            x3 = jnp.where(end, after(e3, *group[nrow // 2 :]), y3)
             last = exchange(product((x3, across(x3))))
             slots = [z, z ^ 1, jnp.where(end, z ^ 2, 3 - z), jnp.where(end, 3 - z, z ^ 2)]
         else:

time: 156 us -> 156 us (level)
    ppermute x5, waiting for transfers between devices: 21.7 us -> 18.1 us  [along(): lax.ppermute(x, 'col', [(2 * a + c, 2 * b + c) for a, b in pairs for c in...]
    ppermute x12, waiting for transfers between devices: 27.9 us -> 30.4 us  [exchange(): lax.ppermute(parts[t], 'row', [(r, r ^ t) for r in range(nrow)])]
    unnamed x18 -> x22, local copies, waits for them, and re-layouts: 3.76 us -> 3.74 us
  transfers between devices with their start and end apart: 22 -> 22, of which waited for: 13 -> 14; matrix products, arithmetic and copies ran while one was open for 2% -> 2% of each run, Pallas kernels for 6% -> 6%
where the time goes in v13:
time: 156 us
  waiting for transfers between devices  72.5 us (46%)
  blocking collectives  32.2 us (21%)
  starting transfers between devices  31.7 us (20%)
  Pallas kernels  12 us (8%)
  local copies, waits for them, and re-layouts  3.74 us (2%)
  other arithmetic  3.7 us (2%)
    all_to_all x1, blocking collectives, local(): second = lax.all_to_all(turned, ('row', 'col'), 0, 0, tiled=True)  32.2 us
    ppermute x12, waiting for transfers between devices, exchange(): lax.ppermute(parts[t], 'row', [(r, r ^ t) for r in range(nrow)])  30.4 us
    all_to_all x1, waiting for transfers between devices, local(): raw = lax.all_to_all(blocks, 'col', 0, 0, tiled=True)  23 us
    ppermute x5, waiting for transfers between devices, along(): lax.ppermute(x, 'col', [(2 * a + c, 2 * b + c) for a, b in pairs for c in...  18.1 us
    ppermute x12, starting transfers between devices, exchange(): lax.ppermute(parts[t], 'row', [(r, r ^ t) for r in range(nrow)])  17.3 us
    ppermute x5, starting transfers between devices, along(): lax.ppermute(x, 'col', [(2 * a + c, 2 * b + c) for a, b in pairs for c in...  8.88 us
    pallas_call x3, Pallas kernels, product(): pl.pallas_call(functools.partial(product_kernel, 1), out_shape=sent, in_s...  5.62 us
    all_to_all x1, starting transfers between devices, local(): raw = lax.all_to_all(blocks, 'col', 0, 0, tiled=True)  4.83 us
  transfers between devices with their start and end apart: 22, of which 14 were waited for; matrix products, arithmetic and copies ran while one was open for 2% of the time, Pallas kernels for 6%

profile of v13, /device:TPU:0, one launch (start us, length us, event | category | flops | bytes accessed | tf_op | source)
XLA Modules:
  0.0 155.9 jit_solution(646618887708565946)
XLA Ops:
  0.0 3.0 %collective-permute-start.1 = (bf16[1024,512]{1,0:T(8,128)(2,1)}, bf16[1024,512]{1,0:T(8,128)(2,1)}, u32[]{:S(2)}, u32[]{:S(2)}) collective-permute-start(bf16[1024,512]{1,0:T(8,128)(2,1)} %bitcast.7), channel_id=1, source_target_pairs={{0,2},{1,3},{2,0},{3,1},{4,6},{5,7},{6,4},{7,5},{8,10},{9,11},{10,... | collective-permute-start | bytes 3145736 | tf_op jit(solution)/shard_map/ppermute | solution.py:88
  3.0 1.6 %collective-permute-start.9 = (bf16[1024,512]{1,0:T(8,128)(2,1)}, bf16[1024,512]{1,0:T(8,128)(2,1)}, u32[]{:S(2)}, u32[]{:S(2)}) collective-permute-start(bf16[1024,512]{1,0:T(8,128)(2,1)} %bitcast.8), channel_id=1, source_target_pairs={{2,4},{3,5},{4,2},{5,3},{10,12},{11,13},{12,10},{13,11},{18,20},{1... | collective-permute-start | bytes 3145736 | tf_op jit(solution)/shard_map/ppermute | solution.py:88
  7.2 4.8 %all-to-all-start = ((bf16[8,2,64,512]{3,2,1,0:T(8,128)(2,1)}), bf16[8,2,64,512]{3,2,1,0:T(8,128)(2,1)S(1)}, u32[]{:S(2)}, u32[]{:S(2)}) async-start(bf16[8,2,64,512]{3,2,1,0:T(8,128)(2,1)} %shard_map.28), calls=%async_computation | async-start | bytes 2097152 | tf_op jit(solution)/shard_map/all_to_all | solution.py:121
  12.5 14.8 %collective-permute-done.1.refs_0_ = bf16[1024,512]{1,0:T(8,128)(2,1)} collective-permute-done((bf16[1024,512]{1,0:T(8,128)(2,1)}, bf16[1024,512]{1,0:T(8,128)(2,1)}, u32[]{:S(2)}, u32[]{:S(2)}) %collective-permute-start.1) | collective-permute-done | bytes 1048608 | tf_op jit(solution)/shard_map/ppermute | solution.py:88
  28.6 1.7 %collective-permute-start.15 = (bf16[1024,512]{1,0:T(8,128)(2,1)}, bf16[1024,512]{1,0:T(8,128)(2,1)}, u32[]{:S(2)}, u32[]{:S(2)}) collective-permute-start(bf16[1024,512]{1,0:T(8,128)(2,1)} %collective-permute-done.1.refs_0_), channel_id=1, source_target_pairs={{2,4},{3,5},{4,2},{5,3},{10,12},{11,13},{12,10},{13,11},{18,20},{1... | collective-permute-start | bytes 3145736 | tf_op jit(solution)/shard_map/ppermute | solution.py:88
  31.3 23.0 %all-to-all-done.raw_ref = bf16[8,2,64,512]{3,2,1,0:T(8,128)(2,1)S(1)} async-done(((bf16[8,2,64,512]{3,2,1,0:T(8,128)(2,1)}), bf16[8,2,64,512]{3,2,1,0:T(8,128)(2,1)S(1)}, u32[]{:S(2)}, u32[]{:S(2)}) %all-to-all-start) | async-done | bytes 1048608 | tf_op jit(solution)/shard_map/all_to_all | solution.py:121
  54.3 2.6 %shard_map.29 = (bf16[512,1024]{1,0:T(8,128)(2,1)S(1)}, f32[2,128,512]{2,1,0:T(8,128)S(1)}, bf16[2,128,512]{2,1,0:T(8,128)(2,1)S(1)}, bf16[2,128,512]{2,1,0:T(8,128)(2,1)S(1)}, bf16[2,128,512]{2,1,0:T(8,128)(2,1)S(1)}) custom-call(s32[1]{0:T(128)} %bitcast.4.core_ref, bf16[8,2,64,512]{3,2,1,0:T(8,128)(2,1)S(1)} %all-to-all-done.raw_ref, ...), custom_call_target="tpu_custom_call" | custom-call | tf_op jit(solution)/shard_map/pallas_call | solution.py:124
  56.9 2.5 %collective-permute-start.5 = (bf16[2,128,512]{2,1,0:T(8,128)(2,1)S(1)}, bf16[2,128,512]{2,1,0:T(8,128)(2,1)S(1)}, u32[]{:S(2)}, u32[]{:S(2)}) collective-permute-start(bf16[2,128,512]{2,1,0:T(8,128)(2,1)S(1)} %get-tuple-element.34), channel_id=1, source_target_pairs={{0,24},{8,16},{16,8},{24,0},{1,25},{9,17},{17,9},{25,1},{2,26},{10... | collective-permute-start | bytes 786440 | tf_op jit(solution)/shard_map/ppermute | solution.py:143
  60.4 2.5 %shard_map.30 = (f32[2,128,512]{2,1,0:T(8,128)S(1)}, bf16[2,128,512]{2,1,0:T(8,128)(2,1)S(1)}, bf16[2,128,512]{2,1,0:T(8,128)(2,1)S(1)}, bf16[2,128,512]{2,1,0:T(8,128)(2,1)S(1)}) custom-call(s32[1]{0:T(128)} %bitcast.4.core_ref, bf16[512,1024]{1,0:T(8,128)(2,1)S(1)} %get-tuple-element.35.panel_ref, bf16[1024,512]{1,0:T(8,128)(2,1)} %collective-permute-done.1.refs_0_, ...), custom_call_target="tpu_custom_call" | custom-call | tf_op jit(solution)/shard_map/pallas_call | solution.py:133
  62.9 2.9 %collective-permute-done.10 = bf16[1024,512]{1,0:T(8,128)(2,1)} collective-permute-done((bf16[1024,512]{1,0:T(8,128)(2,1)}, bf16[1024,512]{1,0:T(8,128)(2,1)}, u32[]{:S(2)}, u32[]{:S(2)}) %collective-permute-start.10) | collective-permute-done | bytes 1048608 | tf_op jit(solution)/shard_map/ppermute | solution.py:88
  65.8 2.6 %collective-permute-start.8 = (bf16[2,128,512]{2,1,0:T(8,128)(2,1)S(1)}, bf16[2,128,512]{2,1,0:T(8,128)(2,1)S(1)}, u32[]{:S(2)}, u32[]{:S(2)}) collective-permute-start(bf16[2,128,512]{2,1,0:T(8,128)(2,1)S(1)} %get-tuple-element.39), channel_id=1, source_target_pairs={{0,24},{8,16},{16,8},{24,0},{1,25},{9,17},{17,9},{25,1},{2,26},{10... | collective-permute-start | bytes 786440 | tf_op jit(solution)/shard_map/ppermute | solution.py:143
  69.9 2.4 %collective-permute-done.4 = bf16[2,128,512]{2,1,0:T(8,128)(2,1)S(1)} collective-permute-done((bf16[2,128,512]{2,1,0:T(8,128)(2,1)S(1)}, bf16[2,128,512]{2,1,0:T(8,128)(2,1)S(1)}, u32[]{:S(2)}, u32[]{:S(2)}) %collective-permute-start.4) | collective-permute-done | bytes 262176 | tf_op jit(solution)/shard_map/ppermute | solution.py:143
  72.5 2.6 %collective-permute-done.8 = bf16[2,128,512]{2,1,0:T(8,128)(2,1)S(1)} collective-permute-done((bf16[2,128,512]{2,1,0:T(8,128)(2,1)S(1)}, bf16[2,128,512]{2,1,0:T(8,128)(2,1)S(1)}, u32[]{:S(2)}, u32[]{:S(2)}) %collective-permute-start.8) | collective-permute-done | bytes 262176 | tf_op jit(solution)/shard_map/ppermute | solution.py:143
  76.4 1.6 %collective-permute-start.7 = (bf16[2,128,512]{2,1,0:T(8,128)(2,1)S(1)}, bf16[2,128,512]{2,1,0:T(8,128)(2,1)S(1)}, u32[]{:S(2)}, u32[]{:S(2)}) collective-permute-start(bf16[2,128,512]{2,1,0:T(8,128)(2,1)S(1)} %get-tuple-element.38), channel_id=1, source_target_pairs={{0,16},{8,24},{16,0},{24,8},{1,17},{9,25},{17,1},{25,9},{2,18},{10... | collective-permute-start | bytes 786440 | tf_op jit(solution)/shard_map/ppermute | solution.py:143
  79.5 3.3 %collective-permute-done.7 = bf16[2,128,512]{2,1,0:T(8,128)(2,1)S(1)} collective-permute-done((bf16[2,128,512]{2,1,0:T(8,128)(2,1)S(1)}, bf16[2,128,512]{2,1,0:T(8,128)(2,1)S(1)}, u32[]{:S(2)}, u32[]{:S(2)}) %collective-permute-start.7) | collective-permute-done | bytes 262176 | tf_op jit(solution)/shard_map/ppermute | solution.py:143
  85.2 1.9 %shard_map.31 = (f32[2,128,512]{2,1,0:T(8,128)S(1)}, bf16[2,128,512]{2,1,0:T(8,128)(2,1)}, bf16[2,128,512]{2,1,0:T(8,128)(2,1)S(1)}, bf16[2,128,512]{2,1,0:T(8,128)(2,1)S(1)}) custom-call(s32[1]{0:T(128)} %bitcast.4.core_ref, bf16[512,1024]{1,0:T(8,128)(2,1)S(1)} %get-tuple-element.35.panel_ref, bf16[1024,512]{1,0:T(8,128)(2,1)S(1)} %broadcast_select_fusion.1.refs_0_, ...), custom_call_target="tpu_custom_call" | custom-call | tf_op jit(solution)/shard_map/pallas_call | solution.py:133
  90.9 4.4 %collective-permute-done.14 = bf16[2,128,512]{2,1,0:T(8,128)(2,1)S(1)} collective-permute-done((bf16[2,128,512]{2,1,0:T(8,128)(2,1)S(1)}, bf16[2,128,512]{2,1,0:T(8,128)(2,1)S(1)}, u32[]{:S(2)}, u32[]{:S(2)}) %collective-permute-start.14) | collective-permute-done | bytes 262176 | tf_op jit(solution)/shard_map/ppermute | solution.py:143
  95.3 3.6 %collective-permute-done.13 = bf16[2,128,512]{2,1,0:T(8,128)(2,1)S(1)} collective-permute-done((bf16[2,128,512]{2,1,0:T(8,128)(2,1)S(1)}, bf16[2,128,512]{2,1,0:T(8,128)(2,1)S(1)}, u32[]{:S(2)}, u32[]{:S(2)}) %collective-permute-start.13) | collective-permute-done | bytes 262176 | tf_op jit(solution)/shard_map/ppermute | solution.py:143
  100.2 1.6 collective-permute-start.12
  104.1 1.6 collective-permute-start.18
  107.7 2.0 %collective-permute-done.12 = bf16[2,128,512]{2,1,0:T(8,128)(2,1)} collective-permute-done((bf16[2,128,512]{2,1,0:T(8,128)(2,1)}, bf16[2,128,512]{2,1,0:T(8,128)(2,1)}, u32[]{:S(2)}, u32[]{:S(2)}) %collective-permute-start.12) | collective-permute-done | bytes 262176 | tf_op jit(solution)/shard_map/ppermute | solution.py:143
  110.9 4.3 %collective-permute-done.18.refs_4_ = bf16[2,128,512]{2,1,0:T(8,128)(2,1)S(1)} collective-permute-done((bf16[2,128,512]{2,1,0:T(8,128)(2,1)S(1)}, bf16[2,128,512]{2,1,0:T(8,128)(2,1)S(1)}, u32[]{:S(2)}, u32[]{:S(2)}) %collective-permute-start.18) | collective-permute-done | bytes 262176 | tf_op jit(solution)/shard_map/ppermute | solution.py:143
  115.2 6.1 %collective-permute-done.20.refs_6_ = bf16[2,128,512]{2,1,0:T(8,128)(2,1)S(1)} collective-permute-done((bf16[2,128,512]{2,1,0:T(8,128)(2,1)S(1)}, bf16[2,128,512]{2,1,0:T(8,128)(2,1)S(1)}, u32[]{:S(2)}, u32[]{:S(2)}) %collective-permute-start.20) | collective-permute-done | bytes 262176 | tf_op jit(solution)/shard_map/ppermute | solution.py:143
  122.3 32.2 %all_to_all.10.second_ref = bf16[32,2,64,128]{3,2,1,0:T(8,128)(2,1)S(1)} all-to-all(bf16[32,2,64,128]{3,2,1,0:T(8,128)(2,1)S(1)} %get-tuple-element.54), channel_id=1, replica_groups=mesh['row'=4,'col'=8] {'row','col'}, dimensions={0} | all-to-all | bytes 2097152 | tf_op jit(solution)/shard_map/all_to_all | solution.py:188
  (56 shorter events, 26.2 us)
Async XLA Ops:
  0.0 27.3 %collective-permute-start.1 = (bf16[1024,512]{1,0:T(8,128)(2,1)}, bf16[1024,512]{1,0:T(8,128)(2,1)}, u32[]{:S(2)}, u32[]{:S(2)}) collective-permute-start(bf16[1024,512]{1,0:T(8,128)(2,1)} %bitcast.7), channel_id=1, source_target_pairs={{0,2},{1,3},{2,0},{3,1},{4,6},{5,7},{6,4},{7,5},{8,10},{9,11},{10,... | collective-permute-start | bytes 3145736 | tf_op jit(solution)/shard_map/ppermute | solution.py:88
  3.0 24.3 %collective-permute-start.9 = (bf16[1024,512]{1,0:T(8,128)(2,1)}, bf16[1024,512]{1,0:T(8,128)(2,1)}, u32[]{:S(2)}, u32[]{:S(2)}) collective-permute-start(bf16[1024,512]{1,0:T(8,128)(2,1)} %bitcast.8), channel_id=1, source_target_pairs={{2,4},{3,5},{4,2},{5,3},{10,12},{11,13},{12,10},{13,11},{18,20},{1... | collective-permute-start | bytes 3145736 | tf_op jit(solution)/shard_map/ppermute | solution.py:88
  7.2 47.1 %all-to-all-start = ((bf16[8,2,64,512]{3,2,1,0:T(8,128)(2,1)}), bf16[8,2,64,512]{3,2,1,0:T(8,128)(2,1)S(1)}, u32[]{:S(2)}, u32[]{:S(2)}) async-start(bf16[8,2,64,512]{3,2,1,0:T(8,128)(2,1)} %shard_map.28), calls=%async_computation | async-start | bytes 2097152 | tf_op jit(solution)/shard_map/all_to_all | solution.py:121
  12.0 18.2 %collective-permute-start = (bf16[1024,512]{1,0:T(8,128)(2,1)S(1)}, bf16[1024,512]{1,0:T(8,128)(2,1)}, u32[]{:S(2)}, u32[]{:S(2)}) collective-permute-start(bf16[1024,512]{1,0:T(8,128)(2,1)S(1)} %bitcast.9), channel_id=1, source_target_pairs={{0,1},{1,0},{2,3},{3,2},{4,5},{5,4},{6,7},{7,6},{8,9},{9,8},{10,11... | collective-permute-start | bytes 3145736 | tf_op jit(solution)/shard_map/ppermute | solution.py:85
  27.3 3.0 %collective-permute-start.2 = (bf16[1024,512]{1,0:T(8,128)(2,1)}, bf16[1024,512]{1,0:T(8,128)(2,1)S(1)}, u32[]{:S(2)}, u32[]{:S(2)}) collective-permute-start(bf16[1024,512]{1,0:T(8,128)(2,1)} %collective-permute-done.1.refs_0_), channel_id=1, source_target_pairs={{0,1},{1,0},{2,3},{3,2},{4,5},{5,4},{6,7},{7,6},{8,9},{9,8},{10,11... | collective-permute-start | bytes 3145736 | tf_op jit(solution)/shard_map/ppermute | solution.py:85
  27.3 38.5 %collective-permute-start.10 = (bf16[1024,512]{1,0:T(8,128)(2,1)}, bf16[1024,512]{1,0:T(8,128)(2,1)}, u32[]{:S(2)}, u32[]{:S(2)}) collective-permute-start(bf16[1024,512]{1,0:T(8,128)(2,1)} %collective-permute-done.9), channel_id=1, source_target_pairs={{2,0},{3,1},{4,6},{5,7},{10,8},{11,9},{12,14},{13,15},{18,16},{19,... | collective-permute-start | bytes 3145736 | tf_op jit(solution)/shard_map/ppermute | solution.py:88
  28.6 43.9 %collective-permute-start.15 = (bf16[1024,512]{1,0:T(8,128)(2,1)}, bf16[1024,512]{1,0:T(8,128)(2,1)}, u32[]{:S(2)}, u32[]{:S(2)}) collective-permute-start(bf16[1024,512]{1,0:T(8,128)(2,1)} %collective-permute-done.1.refs_0_), channel_id=1, source_target_pairs={{2,4},{3,5},{4,2},{5,3},{10,12},{11,13},{12,10},{13,11},{18,20},{1... | collective-permute-start | bytes 3145736 | tf_op jit(solution)/shard_map/ppermute | solution.py:88
  56.9 12.9 %collective-permute-start.5 = (bf16[2,128,512]{2,1,0:T(8,128)(2,1)S(1)}, bf16[2,128,512]{2,1,0:T(8,128)(2,1)S(1)}, u32[]{:S(2)}, u32[]{:S(2)}) collective-permute-start(bf16[2,128,512]{2,1,0:T(8,128)(2,1)S(1)} %get-tuple-element.34), channel_id=1, source_target_pairs={{0,24},{8,16},{16,8},{24,0},{1,25},{9,17},{17,9},{25,1},{2,26},{10... | collective-permute-start | bytes 786440 | tf_op jit(solution)/shard_map/ppermute | solution.py:143
  59.4 12.9 %collective-permute-start.4 = (bf16[2,128,512]{2,1,0:T(8,128)(2,1)S(1)}, bf16[2,128,512]{2,1,0:T(8,128)(2,1)S(1)}, u32[]{:S(2)}, u32[]{:S(2)}) collective-permute-start(bf16[2,128,512]{2,1,0:T(8,128)(2,1)S(1)} %get-tuple-element.33), channel_id=1, source_target_pairs={{0,16},{8,24},{16,0},{24,8},{1,17},{9,25},{17,1},{25,9},{2,18},{10... | collective-permute-start | bytes 786440 | tf_op jit(solution)/shard_map/ppermute | solution.py:143
  59.9 12.4 %collective-permute-start.3 = (bf16[2,128,512]{2,1,0:T(8,128)(2,1)S(1)}, bf16[2,128,512]{2,1,0:T(8,128)(2,1)S(1)}, u32[]{:S(2)}, u32[]{:S(2)}) collective-permute-start(bf16[2,128,512]{2,1,0:T(8,128)(2,1)S(1)} %get-tuple-element.32), channel_id=1, source_target_pairs={{0,8},{8,0},{16,24},{24,16},{1,9},{9,1},{17,25},{25,17},{2,10},{10... | collective-permute-start | bytes 786440 | tf_op jit(solution)/shard_map/ppermute | solution.py:143
  65.8 9.3 %collective-permute-start.8 = (bf16[2,128,512]{2,1,0:T(8,128)(2,1)S(1)}, bf16[2,128,512]{2,1,0:T(8,128)(2,1)S(1)}, u32[]{:S(2)}, u32[]{:S(2)}) collective-permute-start(bf16[2,128,512]{2,1,0:T(8,128)(2,1)S(1)} %get-tuple-element.39), channel_id=1, source_target_pairs={{0,24},{8,16},{16,8},{24,0},{1,25},{9,17},{17,9},{25,1},{2,26},{10... | collective-permute-start | bytes 786440 | tf_op jit(solution)/shard_map/ppermute | solution.py:143
  69.8 15.4 %collective-permute-start.11 = (bf16[1024,512]{1,0:T(8,128)(2,1)S(1)}, bf16[1024,512]{1,0:T(8,128)(2,1)S(1)}, u32[]{:S(2)}, u32[]{:S(2)}) collective-permute-start(bf16[1024,512]{1,0:T(8,128)(2,1)S(1)} %broadcast_select_fusion.1.refs_0_), channel_id=1, source_target_pairs={{0,1},{1,0},{2,3},{3,2},{4,5},{5,4},{6,7},{7,6},{8,9},{9,8},{10,11... | collective-permute-start | bytes 3145736 | tf_op jit(solution)/shard_map/ppermute | solution.py:85
  75.1 24.9 %collective-permute-start.16 = (bf16[1024,512]{1,0:T(8,128)(2,1)}, bf16[1024,512]{1,0:T(8,128)(2,1)S(1)}, u32[]{:S(2)}, u32[]{:S(2)}) collective-permute-start(bf16[1024,512]{1,0:T(8,128)(2,1)} %collective-permute-done.15), channel_id=1, source_target_pairs={{2,0},{3,1},{4,6},{5,7},{10,8},{11,9},{12,14},{13,15},{18,16},{19,... | collective-permute-start | bytes 3145736 | tf_op jit(solution)/shard_map/ppermute | solution.py:88
  76.4 6.4 %collective-permute-start.7 = (bf16[2,128,512]{2,1,0:T(8,128)(2,1)S(1)}, bf16[2,128,512]{2,1,0:T(8,128)(2,1)S(1)}, u32[]{:S(2)}, u32[]{:S(2)}) collective-permute-start(bf16[2,128,512]{2,1,0:T(8,128)(2,1)S(1)} %get-tuple-element.38), channel_id=1, source_target_pairs={{0,16},{8,24},{16,0},{24,8},{1,17},{9,25},{17,1},{25,9},{2,18},{10... | collective-permute-start | bytes 786440 | tf_op jit(solution)/shard_map/ppermute | solution.py:143
  78.0 6.4 %collective-permute-start.6 = (bf16[2,128,512]{2,1,0:T(8,128)(2,1)S(1)}, bf16[2,128,512]{2,1,0:T(8,128)(2,1)S(1)}, u32[]{:S(2)}, u32[]{:S(2)}) collective-permute-start(bf16[2,128,512]{2,1,0:T(8,128)(2,1)S(1)} %get-tuple-element.37), channel_id=1, source_target_pairs={{0,8},{8,0},{16,24},{24,16},{1,9},{9,1},{17,25},{25,17},{2,10},{10... | collective-permute-start | bytes 786440 | tf_op jit(solution)/shard_map/ppermute | solution.py:143
  87.9 7.4 %collective-permute-start.14 = (bf16[2,128,512]{2,1,0:T(8,128)(2,1)S(1)}, bf16[2,128,512]{2,1,0:T(8,128)(2,1)S(1)}, u32[]{:S(2)}, u32[]{:S(2)}) collective-permute-start(bf16[2,128,512]{2,1,0:T(8,128)(2,1)S(1)} %get-tuple-element.45), channel_id=1, source_target_pairs={{0,24},{8,16},{16,8},{24,0},{1,25},{9,17},{17,9},{25,1},{2,26},{10... | collective-permute-start | bytes 786440 | tf_op jit(solution)/shard_map/ppermute | solution.py:143
  89.3 9.5 %collective-permute-start.13 = (bf16[2,128,512]{2,1,0:T(8,128)(2,1)S(1)}, bf16[2,128,512]{2,1,0:T(8,128)(2,1)S(1)}, u32[]{:S(2)}, u32[]{:S(2)}) collective-permute-start(bf16[2,128,512]{2,1,0:T(8,128)(2,1)S(1)} %get-tuple-element.44), channel_id=1, source_target_pairs={{0,16},{8,24},{16,0},{24,8},{1,17},{9,25},{17,1},{25,9},{2,18},{10... | collective-permute-start | bytes 786440 | tf_op jit(solution)/shard_map/ppermute | solution.py:143
  100.1 2.7 %collective-permute-start.17 = (bf16[1024,512]{1,0:T(8,128)(2,1)S(1)}, bf16[1024,512]{1,0:T(8,128)(2,1)S(1)}, u32[]{:S(2)}, u32[]{:S(2)}) collective-permute-start(bf16[1024,512]{1,0:T(8,128)(2,1)S(1)} %broadcast_select_fusion.refs_0_), channel_id=1, source_target_pairs={{0,1},{1,0},{2,3},{3,2},{4,5},{5,4},{6,7},{7,6},{8,9},{9,8},{10,11... | collective-permute-start | bytes 3145736 | tf_op jit(solution)/shard_map/ppermute | solution.py:85
  100.2 9.5 %collective-permute-start.12 = (bf16[2,128,512]{2,1,0:T(8,128)(2,1)}, bf16[2,128,512]{2,1,0:T(8,128)(2,1)}, u32[]{:S(2)}, u32[]{:S(2)}) collective-permute-start(bf16[2,128,512]{2,1,0:T(8,128)(2,1)} %get-tuple-element.43), channel_id=1, source_target_pairs={{0,8},{8,0},{16,24},{24,16},{1,9},{9,1},{17,25},{25,17},{2,10},{10... | collective-permute-start | bytes 786440 | tf_op jit(solution)/shard_map/ppermute | solution.py:143
  101.8 7.9 %copy-start.10 = (bf16[2,128,512]{2,1,0:T(8,128)(2,1)S(1)}, bf16[2,128,512]{2,1,0:T(8,128)(2,1)}, u32[]{:S(2)}) copy-start(bf16[2,128,512]{2,1,0:T(8,128)(2,1)} %copy-done.9) | copy-start | bytes 786436
  104.1 11.1 %collective-permute-start.18 = (bf16[2,128,512]{2,1,0:T(8,128)(2,1)S(1)}, bf16[2,128,512]{2,1,0:T(8,128)(2,1)S(1)}, u32[]{:S(2)}, u32[]{:S(2)}) collective-permute-start(bf16[2,128,512]{2,1,0:T(8,128)(2,1)S(1)} %get-tuple-element.50), channel_id=1, source_target_pairs={{0,8},{8,0},{16,24},{24,16},{1,9},{9,1},{17,25},{25,17},{2,10},{10... | collective-permute-start | bytes 786440 | tf_op jit(solution)/shard_map/ppermute | solution.py:143
  105.7 9.6 %collective-permute-start.19 = (bf16[2,128,512]{2,1,0:T(8,128)(2,1)S(1)}, bf16[2,128,512]{2,1,0:T(8,128)(2,1)S(1)}, u32[]{:S(2)}, u32[]{:S(2)}) collective-permute-start(bf16[2,128,512]{2,1,0:T(8,128)(2,1)S(1)} %get-tuple-element.51), channel_id=1, source_target_pairs={{0,16},{8,24},{16,0},{24,8},{1,17},{9,25},{17,1},{25,9},{2,18},{10... | collective-permute-start | bytes 786440 | tf_op jit(solution)/shard_map/ppermute | solution.py:143
  107.2 14.1 %collective-permute-start.20 = (bf16[2,128,512]{2,1,0:T(8,128)(2,1)S(1)}, bf16[2,128,512]{2,1,0:T(8,128)(2,1)S(1)}, u32[]{:S(2)}, u32[]{:S(2)}) collective-permute-start(bf16[2,128,512]{2,1,0:T(8,128)(2,1)S(1)} %get-tuple-element.52), channel_id=1, source_target_pairs={{0,24},{8,16},{16,8},{24,0},{1,25},{9,17},{17,9},{25,1},{2,26},{10... | collective-permute-start | bytes 786440 | tf_op jit(solution)/shard_map/ppermute | solution.py:143
  109.7 11.6 %copy-start.4 = (bf16[2,128,512]{2,1,0:T(8,128)(2,1)S(1)}, bf16[2,128,512]{2,1,0:T(8,128)(2,1)}, u32[]{:S(2)}) copy-start(bf16[2,128,512]{2,1,0:T(8,128)(2,1)} %add_convert_fusion.1.refs_1_) | copy-start | bytes 786436
  (9 other events, 34.0 us)

commit v14 on v13

--- a/solution.py
+++ b/solution.py
@@ -139,10 +139,10 @@
             )(core, panel, *pair)
 
         def exchange(parts):
-            return [parts[0]] + [
-                lax.ppermute(parts[t], "row", [(r, r ^ t) for r in range(nrow)])
-                for t in range(1, nrow)
-            ]
+            sent = {}
+            for t in range(nrow - 1, 0, -1):
+                sent[t] = lax.ppermute(parts[t], "row", [(r, r ^ t) for r in range(nrow)])
+            return [parts[0]] + [sent[t] for t in range(1, nrow)]
 
         def summed(group):
             total = group[0]
@@ -163,6 +163,7 @@
             sums.append(summed(group))
             x3 = jnp.where(end, after(e3, *group[nrow // 2 :]), y3)
             last = exchange(product((x3, across(x3))))
+            last = [last[0]] + last[:0:-1]
             slots = [z, z ^ 1, jnp.where(end, z ^ 2, 3 - z), jnp.where(end, 3 - z, z ^ 2)]
         else:
             last = exchange(parts)

time: 156 us -> 156 us (level)
  transfers between devices with their start and end apart: 22 -> 22, of which waited for: 14 -> 15; matrix products, arithmetic and copies ran while one was open for 2% -> 2% of each run, Pallas kernels for 6% -> 6%
where the time goes in v14:
time: 156 us
  waiting for transfers between devices  71.6 us (46%)
  blocking collectives  32.8 us (21%)
  starting transfers between devices  31.7 us (20%)
  Pallas kernels  12 us (8%)
  local copies, waits for them, and re-layouts  3.74 us (2%)
  other arithmetic  3.7 us (2%)
    all_to_all x1, blocking collectives, local(): second = lax.all_to_all(turned, ('row', 'col'), 0, 0, tiled=True)  32.8 us
    ppermute x12, waiting for transfers between devices, exchange(): sent[t] = lax.ppermute(parts[t], 'row', [(r, r ^ t) for r in range(nrow)])  29.5 us
    all_to_all x1, waiting for transfers between devices, local(): raw = lax.all_to_all(blocks, 'col', 0, 0, tiled=True)  23 us
    ppermute x5, waiting for transfers between devices, along(): lax.ppermute(x, 'col', [(2 * a + c, 2 * b + c) for a, b in pairs for c in...  18.1 us
    ppermute x12, starting transfers between devices, exchange(): sent[t] = lax.ppermute(parts[t], 'row', [(r, r ^ t) for r in range(nrow)])  17.4 us
    ppermute x5, starting transfers between devices, along(): lax.ppermute(x, 'col', [(2 * a + c, 2 * b + c) for a, b in pairs for c in...  8.88 us
    pallas_call x3, Pallas kernels, product(): pl.pallas_call(functools.partial(product_kernel, 1), out_shape=sent, in_s...  5.62 us
    all_to_all x1, starting transfers between devices, local(): raw = lax.all_to_all(blocks, 'col', 0, 0, tiled=True)  4.83 us
  transfers between devices with their start and end apart: 22, of which 15 were waited for; matrix products, arithmetic and copies ran while one was open for 2% of the time, Pallas kernels for 6%

profile of v14, /device:TPU:0, one launch (start us, length us, event | category | flops | bytes accessed | tf_op | source)
XLA Modules:
  0.0 155.6 jit_solution(3229109498098486842)
XLA Ops:
  0.0 3.0 %collective-permute-start.1 = (bf16[1024,512]{1,0:T(8,128)(2,1)}, bf16[1024,512]{1,0:T(8,128)(2,1)}, u32[]{:S(2)}, u32[]{:S(2)}) collective-permute-start(bf16[1024,512]{1,0:T(8,128)(2,1)} %bitcast.7), channel_id=1, source_target_pairs={{0,2},{1,3},{2,0},{3,1},{4,6},{5,7},{6,4},{7,5},{8,10},{9,11},{10,... | collective-permute-start | bytes 3145736 | tf_op jit(solution)/shard_map/ppermute | solution.py:88
  3.0 1.6 %collective-permute-start.9 = (bf16[1024,512]{1,0:T(8,128)(2,1)}, bf16[1024,512]{1,0:T(8,128)(2,1)}, u32[]{:S(2)}, u32[]{:S(2)}) collective-permute-start(bf16[1024,512]{1,0:T(8,128)(2,1)} %bitcast.8), channel_id=1, source_target_pairs={{2,4},{3,5},{4,2},{5,3},{10,12},{11,13},{12,10},{13,11},{18,20},{1... | collective-permute-start | bytes 3145736 | tf_op jit(solution)/shard_map/ppermute | solution.py:88
  7.2 4.8 %all-to-all-start = ((bf16[8,2,64,512]{3,2,1,0:T(8,128)(2,1)}), bf16[8,2,64,512]{3,2,1,0:T(8,128)(2,1)S(1)}, u32[]{:S(2)}, u32[]{:S(2)}) async-start(bf16[8,2,64,512]{3,2,1,0:T(8,128)(2,1)} %shard_map.28), calls=%async_computation | async-start | bytes 2097152 | tf_op jit(solution)/shard_map/all_to_all | solution.py:121
  12.5 14.8 %collective-permute-done.1.refs_0_ = bf16[1024,512]{1,0:T(8,128)(2,1)} collective-permute-done((bf16[1024,512]{1,0:T(8,128)(2,1)}, bf16[1024,512]{1,0:T(8,128)(2,1)}, u32[]{:S(2)}, u32[]{:S(2)}) %collective-permute-start.1) | collective-permute-done | bytes 1048608 | tf_op jit(solution)/shard_map/ppermute | solution.py:88
  28.6 1.7 %collective-permute-start.15 = (bf16[1024,512]{1,0:T(8,128)(2,1)}, bf16[1024,512]{1,0:T(8,128)(2,1)}, u32[]{:S(2)}, u32[]{:S(2)}) collective-permute-start(bf16[1024,512]{1,0:T(8,128)(2,1)} %collective-permute-done.1.refs_0_), channel_id=1, source_target_pairs={{2,4},{3,5},{4,2},{5,3},{10,12},{11,13},{12,10},{13,11},{18,20},{1... | collective-permute-start | bytes 3145736 | tf_op jit(solution)/shard_map/ppermute | solution.py:88
  31.3 23.0 %all-to-all-done.raw_ref = bf16[8,2,64,512]{3,2,1,0:T(8,128)(2,1)S(1)} async-done(((bf16[8,2,64,512]{3,2,1,0:T(8,128)(2,1)}), bf16[8,2,64,512]{3,2,1,0:T(8,128)(2,1)S(1)}, u32[]{:S(2)}, u32[]{:S(2)}) %all-to-all-start) | async-done | bytes 1048608 | tf_op jit(solution)/shard_map/all_to_all | solution.py:121
  54.3 2.6 %shard_map.29 = (bf16[512,1024]{1,0:T(8,128)(2,1)S(1)}, f32[2,128,512]{2,1,0:T(8,128)S(1)}, bf16[2,128,512]{2,1,0:T(8,128)(2,1)S(1)}, bf16[2,128,512]{2,1,0:T(8,128)(2,1)S(1)}, bf16[2,128,512]{2,1,0:T(8,128)(2,1)S(1)}) custom-call(s32[1]{0:T(128)} %bitcast.4.core_ref, bf16[8,2,64,512]{3,2,1,0:T(8,128)(2,1)S(1)} %all-to-all-done.raw_ref, ...), custom_call_target="tpu_custom_call" | custom-call | tf_op jit(solution)/shard_map/pallas_call | solution.py:124
  56.9 2.5 %collective-permute-start.5 = (bf16[2,128,512]{2,1,0:T(8,128)(2,1)S(1)}, bf16[2,128,512]{2,1,0:T(8,128)(2,1)S(1)}, u32[]{:S(2)}, u32[]{:S(2)}) collective-permute-start(bf16[2,128,512]{2,1,0:T(8,128)(2,1)S(1)} %get-tuple-element.34), channel_id=1, source_target_pairs={{0,24},{8,16},{16,8},{24,0},{1,25},{9,17},{17,9},{25,1},{2,26},{10... | collective-permute-start | bytes 786440 | tf_op jit(solution)/shard_map/ppermute | solution.py:144
  60.4 2.5 %shard_map.30 = (f32[2,128,512]{2,1,0:T(8,128)S(1)}, bf16[2,128,512]{2,1,0:T(8,128)(2,1)S(1)}, bf16[2,128,512]{2,1,0:T(8,128)(2,1)S(1)}, bf16[2,128,512]{2,1,0:T(8,128)(2,1)S(1)}) custom-call(s32[1]{0:T(128)} %bitcast.4.core_ref, bf16[512,1024]{1,0:T(8,128)(2,1)S(1)} %get-tuple-element.35.panel_ref, bf16[1024,512]{1,0:T(8,128)(2,1)} %collective-permute-done.1.refs_0_, ...), custom_call_target="tpu_custom_call" | custom-call | tf_op jit(solution)/shard_map/pallas_call | solution.py:133
  62.9 2.9 %collective-permute-done.10 = bf16[1024,512]{1,0:T(8,128)(2,1)} collective-permute-done((bf16[1024,512]{1,0:T(8,128)(2,1)}, bf16[1024,512]{1,0:T(8,128)(2,1)}, u32[]{:S(2)}, u32[]{:S(2)}) %collective-permute-start.10) | collective-permute-done | bytes 1048608 | tf_op jit(solution)/shard_map/ppermute | solution.py:88
  65.8 2.6 %collective-permute-start.8 = (bf16[2,128,512]{2,1,0:T(8,128)(2,1)S(1)}, bf16[2,128,512]{2,1,0:T(8,128)(2,1)S(1)}, u32[]{:S(2)}, u32[]{:S(2)}) collective-permute-start(bf16[2,128,512]{2,1,0:T(8,128)(2,1)S(1)} %get-tuple-element.39), channel_id=1, source_target_pairs={{0,24},{8,16},{16,8},{24,0},{1,25},{9,17},{17,9},{25,1},{2,26},{10... | collective-permute-start | bytes 786440 | tf_op jit(solution)/shard_map/ppermute | solution.py:144
  69.9 2.4 %collective-permute-done.4 = bf16[2,128,512]{2,1,0:T(8,128)(2,1)S(1)} collective-permute-done((bf16[2,128,512]{2,1,0:T(8,128)(2,1)S(1)}, bf16[2,128,512]{2,1,0:T(8,128)(2,1)S(1)}, u32[]{:S(2)}, u32[]{:S(2)}) %collective-permute-start.4) | collective-permute-done | bytes 262176 | tf_op jit(solution)/shard_map/ppermute | solution.py:144
  72.5 2.6 %collective-permute-done.8 = bf16[2,128,512]{2,1,0:T(8,128)(2,1)S(1)} collective-permute-done((bf16[2,128,512]{2,1,0:T(8,128)(2,1)S(1)}, bf16[2,128,512]{2,1,0:T(8,128)(2,1)S(1)}, u32[]{:S(2)}, u32[]{:S(2)}) %collective-permute-start.8) | collective-permute-done | bytes 262176 | tf_op jit(solution)/shard_map/ppermute | solution.py:144
  76.4 1.6 %collective-permute-start.7 = (bf16[2,128,512]{2,1,0:T(8,128)(2,1)S(1)}, bf16[2,128,512]{2,1,0:T(8,128)(2,1)S(1)}, u32[]{:S(2)}, u32[]{:S(2)}) collective-permute-start(bf16[2,128,512]{2,1,0:T(8,128)(2,1)S(1)} %get-tuple-element.38), channel_id=1, source_target_pairs={{0,16},{8,24},{16,0},{24,8},{1,17},{9,25},{17,1},{25,9},{2,18},{10... | collective-permute-start | bytes 786440 | tf_op jit(solution)/shard_map/ppermute | solution.py:144
  79.5 3.3 %collective-permute-done.7 = bf16[2,128,512]{2,1,0:T(8,128)(2,1)S(1)} collective-permute-done((bf16[2,128,512]{2,1,0:T(8,128)(2,1)S(1)}, bf16[2,128,512]{2,1,0:T(8,128)(2,1)S(1)}, u32[]{:S(2)}, u32[]{:S(2)}) %collective-permute-start.7) | collective-permute-done | bytes 262176 | tf_op jit(solution)/shard_map/ppermute | solution.py:144
  85.2 1.9 %shard_map.31 = (f32[2,128,512]{2,1,0:T(8,128)S(1)}, bf16[2,128,512]{2,1,0:T(8,128)(2,1)}, bf16[2,128,512]{2,1,0:T(8,128)(2,1)S(1)}, bf16[2,128,512]{2,1,0:T(8,128)(2,1)S(1)}) custom-call(s32[1]{0:T(128)} %bitcast.4.core_ref, bf16[512,1024]{1,0:T(8,128)(2,1)S(1)} %get-tuple-element.35.panel_ref, bf16[1024,512]{1,0:T(8,128)(2,1)S(1)} %broadcast_select_fusion.1.refs_0_, ...), custom_call_target="tpu_custom_call" | custom-call | tf_op jit(solution)/shard_map/pallas_call | solution.py:133
  90.9 4.4 %collective-permute-done.14 = bf16[2,128,512]{2,1,0:T(8,128)(2,1)S(1)} collective-permute-done((bf16[2,128,512]{2,1,0:T(8,128)(2,1)S(1)}, bf16[2,128,512]{2,1,0:T(8,128)(2,1)S(1)}, u32[]{:S(2)}, u32[]{:S(2)}) %collective-permute-start.14) | collective-permute-done | bytes 262176 | tf_op jit(solution)/shard_map/ppermute | solution.py:144
  95.3 3.6 %collective-permute-done.13 = bf16[2,128,512]{2,1,0:T(8,128)(2,1)S(1)} collective-permute-done((bf16[2,128,512]{2,1,0:T(8,128)(2,1)S(1)}, bf16[2,128,512]{2,1,0:T(8,128)(2,1)S(1)}, u32[]{:S(2)}, u32[]{:S(2)}) %collective-permute-start.13) | collective-permute-done | bytes 262176 | tf_op jit(solution)/shard_map/ppermute | solution.py:144
  100.2 1.6 collective-permute-start.12
  104.1 2.5 %collective-permute-start.18 = (bf16[2,128,512]{2,1,0:T(8,128)(2,1)S(1)}, bf16[2,128,512]{2,1,0:T(8,128)(2,1)S(1)}, u32[]{:S(2)}, u32[]{:S(2)}) collective-permute-start(bf16[2,128,512]{2,1,0:T(8,128)(2,1)S(1)} %get-tuple-element.50), channel_id=1, source_target_pairs={{0,24},{8,16},{16,8},{24,0},{1,25},{9,17},{17,9},{25,1},{2,26},{10... | collective-permute-start | bytes 786440 | tf_op jit(solution)/shard_map/ppermute | solution.py:144
  107.7 2.0 %collective-permute-done.12 = bf16[2,128,512]{2,1,0:T(8,128)(2,1)} collective-permute-done((bf16[2,128,512]{2,1,0:T(8,128)(2,1)}, bf16[2,128,512]{2,1,0:T(8,128)(2,1)}, u32[]{:S(2)}, u32[]{:S(2)}) %collective-permute-start.12) | collective-permute-done | bytes 262176 | tf_op jit(solution)/shard_map/ppermute | solution.py:144
  110.9 5.3 %collective-permute-done.18.refs_4_ = bf16[2,128,512]{2,1,0:T(8,128)(2,1)S(1)} collective-permute-done((bf16[2,128,512]{2,1,0:T(8,128)(2,1)S(1)}, bf16[2,128,512]{2,1,0:T(8,128)(2,1)S(1)}, u32[]{:S(2)}, u32[]{:S(2)}) %collective-permute-start.18) | collective-permute-done | bytes 262176 | tf_op jit(solution)/shard_map/ppermute | solution.py:144
  116.2 4.1 %collective-permute-done.19.refs_5_ = bf16[2,128,512]{2,1,0:T(8,128)(2,1)S(1)} collective-permute-done((bf16[2,128,512]{2,1,0:T(8,128)(2,1)S(1)}, bf16[2,128,512]{2,1,0:T(8,128)(2,1)S(1)}, u32[]{:S(2)}, u32[]{:S(2)}) %collective-permute-start.19) | collective-permute-done | bytes 262176 | tf_op jit(solution)/shard_map/ppermute | solution.py:144
  121.4 32.8 %all_to_all.10.second_ref = bf16[32,2,64,128]{3,2,1,0:T(8,128)(2,1)S(1)} all-to-all(bf16[32,2,64,128]{3,2,1,0:T(8,128)(2,1)S(1)} %get-tuple-element.54), channel_id=1, replica_groups=mesh['row'=4,'col'=8] {'row','col'}, dimensions={0} | all-to-all | bytes 2097152 | tf_op jit(solution)/shard_map/all_to_all | solution.py:189
  (56 shorter events, 25.3 us)
Async XLA Ops:
  0.0 27.3 %collective-permute-start.1 = (bf16[1024,512]{1,0:T(8,128)(2,1)}, bf16[1024,512]{1,0:T(8,128)(2,1)}, u32[]{:S(2)}, u32[]{:S(2)}) collective-permute-start(bf16[1024,512]{1,0:T(8,128)(2,1)} %bitcast.7), channel_id=1, source_target_pairs={{0,2},{1,3},{2,0},{3,1},{4,6},{5,7},{6,4},{7,5},{8,10},{9,11},{10,... | collective-permute-start | bytes 3145736 | tf_op jit(solution)/shard_map/ppermute | solution.py:88
  3.0 24.3 %collective-permute-start.9 = (bf16[1024,512]{1,0:T(8,128)(2,1)}, bf16[1024,512]{1,0:T(8,128)(2,1)}, u32[]{:S(2)}, u32[]{:S(2)}) collective-permute-start(bf16[1024,512]{1,0:T(8,128)(2,1)} %bitcast.8), channel_id=1, source_target_pairs={{2,4},{3,5},{4,2},{5,3},{10,12},{11,13},{12,10},{13,11},{18,20},{1... | collective-permute-start | bytes 3145736 | tf_op jit(solution)/shard_map/ppermute | solution.py:88
  7.2 47.1 %all-to-all-start = ((bf16[8,2,64,512]{3,2,1,0:T(8,128)(2,1)}), bf16[8,2,64,512]{3,2,1,0:T(8,128)(2,1)S(1)}, u32[]{:S(2)}, u32[]{:S(2)}) async-start(bf16[8,2,64,512]{3,2,1,0:T(8,128)(2,1)} %shard_map.28), calls=%async_computation | async-start | bytes 2097152 | tf_op jit(solution)/shard_map/all_to_all | solution.py:121
  12.0 18.2 %collective-permute-start = (bf16[1024,512]{1,0:T(8,128)(2,1)S(1)}, bf16[1024,512]{1,0:T(8,128)(2,1)}, u32[]{:S(2)}, u32[]{:S(2)}) collective-permute-start(bf16[1024,512]{1,0:T(8,128)(2,1)S(1)} %bitcast.9), channel_id=1, source_target_pairs={{0,1},{1,0},{2,3},{3,2},{4,5},{5,4},{6,7},{7,6},{8,9},{9,8},{10,11... | collective-permute-start | bytes 3145736 | tf_op jit(solution)/shard_map/ppermute | solution.py:85
  27.3 3.0 %collective-permute-start.2 = (bf16[1024,512]{1,0:T(8,128)(2,1)}, bf16[1024,512]{1,0:T(8,128)(2,1)S(1)}, u32[]{:S(2)}, u32[]{:S(2)}) collective-permute-start(bf16[1024,512]{1,0:T(8,128)(2,1)} %collective-permute-done.1.refs_0_), channel_id=1, source_target_pairs={{0,1},{1,0},{2,3},{3,2},{4,5},{5,4},{6,7},{7,6},{8,9},{9,8},{10,11... | collective-permute-start | bytes 3145736 | tf_op jit(solution)/shard_map/ppermute | solution.py:85
  27.3 38.5 %collective-permute-start.10 = (bf16[1024,512]{1,0:T(8,128)(2,1)}, bf16[1024,512]{1,0:T(8,128)(2,1)}, u32[]{:S(2)}, u32[]{:S(2)}) collective-permute-start(bf16[1024,512]{1,0:T(8,128)(2,1)} %collective-permute-done.9), channel_id=1, source_target_pairs={{2,0},{3,1},{4,6},{5,7},{10,8},{11,9},{12,14},{13,15},{18,16},{19,... | collective-permute-start | bytes 3145736 | tf_op jit(solution)/shard_map/ppermute | solution.py:88
  28.6 43.9 %collective-permute-start.15 = (bf16[1024,512]{1,0:T(8,128)(2,1)}, bf16[1024,512]{1,0:T(8,128)(2,1)}, u32[]{:S(2)}, u32[]{:S(2)}) collective-permute-start(bf16[1024,512]{1,0:T(8,128)(2,1)} %collective-permute-done.1.refs_0_), channel_id=1, source_target_pairs={{2,4},{3,5},{4,2},{5,3},{10,12},{11,13},{12,10},{13,11},{18,20},{1... | collective-permute-start | bytes 3145736 | tf_op jit(solution)/shard_map/ppermute | solution.py:88
  56.9 12.9 %collective-permute-start.5 = (bf16[2,128,512]{2,1,0:T(8,128)(2,1)S(1)}, bf16[2,128,512]{2,1,0:T(8,128)(2,1)S(1)}, u32[]{:S(2)}, u32[]{:S(2)}) collective-permute-start(bf16[2,128,512]{2,1,0:T(8,128)(2,1)S(1)} %get-tuple-element.34), channel_id=1, source_target_pairs={{0,24},{8,16},{16,8},{24,0},{1,25},{9,17},{17,9},{25,1},{2,26},{10... | collective-permute-start | bytes 786440 | tf_op jit(solution)/shard_map/ppermute | solution.py:144
  59.4 12.9 %collective-permute-start.4 = (bf16[2,128,512]{2,1,0:T(8,128)(2,1)S(1)}, bf16[2,128,512]{2,1,0:T(8,128)(2,1)S(1)}, u32[]{:S(2)}, u32[]{:S(2)}) collective-permute-start(bf16[2,128,512]{2,1,0:T(8,128)(2,1)S(1)} %get-tuple-element.33), channel_id=1, source_target_pairs={{0,16},{8,24},{16,0},{24,8},{1,17},{9,25},{17,1},{25,9},{2,18},{10... | collective-permute-start | bytes 786440 | tf_op jit(solution)/shard_map/ppermute | solution.py:144
  59.9 12.4 %collective-permute-start.3 = (bf16[2,128,512]{2,1,0:T(8,128)(2,1)S(1)}, bf16[2,128,512]{2,1,0:T(8,128)(2,1)S(1)}, u32[]{:S(2)}, u32[]{:S(2)}) collective-permute-start(bf16[2,128,512]{2,1,0:T(8,128)(2,1)S(1)} %get-tuple-element.32), channel_id=1, source_target_pairs={{0,8},{8,0},{16,24},{24,16},{1,9},{9,1},{17,25},{25,17},{2,10},{10... | collective-permute-start | bytes 786440 | tf_op jit(solution)/shard_map/ppermute | solution.py:144
  65.8 9.3 %collective-permute-start.8 = (bf16[2,128,512]{2,1,0:T(8,128)(2,1)S(1)}, bf16[2,128,512]{2,1,0:T(8,128)(2,1)S(1)}, u32[]{:S(2)}, u32[]{:S(2)}) collective-permute-start(bf16[2,128,512]{2,1,0:T(8,128)(2,1)S(1)} %get-tuple-element.39), channel_id=1, source_target_pairs={{0,24},{8,16},{16,8},{24,0},{1,25},{9,17},{17,9},{25,1},{2,26},{10... | collective-permute-start | bytes 786440 | tf_op jit(solution)/shard_map/ppermute | solution.py:144
  69.8 15.4 %collective-permute-start.11 = (bf16[1024,512]{1,0:T(8,128)(2,1)S(1)}, bf16[1024,512]{1,0:T(8,128)(2,1)S(1)}, u32[]{:S(2)}, u32[]{:S(2)}) collective-permute-start(bf16[1024,512]{1,0:T(8,128)(2,1)S(1)} %broadcast_select_fusion.1.refs_0_), channel_id=1, source_target_pairs={{0,1},{1,0},{2,3},{3,2},{4,5},{5,4},{6,7},{7,6},{8,9},{9,8},{10,11... | collective-permute-start | bytes 3145736 | tf_op jit(solution)/shard_map/ppermute | solution.py:85
  75.1 24.9 %collective-permute-start.16 = (bf16[1024,512]{1,0:T(8,128)(2,1)}, bf16[1024,512]{1,0:T(8,128)(2,1)S(1)}, u32[]{:S(2)}, u32[]{:S(2)}) collective-permute-start(bf16[1024,512]{1,0:T(8,128)(2,1)} %collective-permute-done.15), channel_id=1, source_target_pairs={{2,0},{3,1},{4,6},{5,7},{10,8},{11,9},{12,14},{13,15},{18,16},{19,... | collective-permute-start | bytes 3145736 | tf_op jit(solution)/shard_map/ppermute | solution.py:88
  76.4 6.4 %collective-permute-start.7 = (bf16[2,128,512]{2,1,0:T(8,128)(2,1)S(1)}, bf16[2,128,512]{2,1,0:T(8,128)(2,1)S(1)}, u32[]{:S(2)}, u32[]{:S(2)}) collective-permute-start(bf16[2,128,512]{2,1,0:T(8,128)(2,1)S(1)} %get-tuple-element.38), channel_id=1, source_target_pairs={{0,16},{8,24},{16,0},{24,8},{1,17},{9,25},{17,1},{25,9},{2,18},{10... | collective-permute-start | bytes 786440 | tf_op jit(solution)/shard_map/ppermute | solution.py:144
  78.0 6.4 %collective-permute-start.6 = (bf16[2,128,512]{2,1,0:T(8,128)(2,1)S(1)}, bf16[2,128,512]{2,1,0:T(8,128)(2,1)S(1)}, u32[]{:S(2)}, u32[]{:S(2)}) collective-permute-start(bf16[2,128,512]{2,1,0:T(8,128)(2,1)S(1)} %get-tuple-element.37), channel_id=1, source_target_pairs={{0,8},{8,0},{16,24},{24,16},{1,9},{9,1},{17,25},{25,17},{2,10},{10... | collective-permute-start | bytes 786440 | tf_op jit(solution)/shard_map/ppermute | solution.py:144
  87.9 7.4 %collective-permute-start.14 = (bf16[2,128,512]{2,1,0:T(8,128)(2,1)S(1)}, bf16[2,128,512]{2,1,0:T(8,128)(2,1)S(1)}, u32[]{:S(2)}, u32[]{:S(2)}) collective-permute-start(bf16[2,128,512]{2,1,0:T(8,128)(2,1)S(1)} %get-tuple-element.45), channel_id=1, source_target_pairs={{0,24},{8,16},{16,8},{24,0},{1,25},{9,17},{17,9},{25,1},{2,26},{10... | collective-permute-start | bytes 786440 | tf_op jit(solution)/shard_map/ppermute | solution.py:144
  89.3 9.5 %collective-permute-start.13 = (bf16[2,128,512]{2,1,0:T(8,128)(2,1)S(1)}, bf16[2,128,512]{2,1,0:T(8,128)(2,1)S(1)}, u32[]{:S(2)}, u32[]{:S(2)}) collective-permute-start(bf16[2,128,512]{2,1,0:T(8,128)(2,1)S(1)} %get-tuple-element.44), channel_id=1, source_target_pairs={{0,16},{8,24},{16,0},{24,8},{1,17},{9,25},{17,1},{25,9},{2,18},{10... | collective-permute-start | bytes 786440 | tf_op jit(solution)/shard_map/ppermute | solution.py:144
  100.1 2.7 %collective-permute-start.17 = (bf16[1024,512]{1,0:T(8,128)(2,1)S(1)}, bf16[1024,512]{1,0:T(8,128)(2,1)S(1)}, u32[]{:S(2)}, u32[]{:S(2)}) collective-permute-start(bf16[1024,512]{1,0:T(8,128)(2,1)S(1)} %broadcast_select_fusion.refs_0_), channel_id=1, source_target_pairs={{0,1},{1,0},{2,3},{3,2},{4,5},{5,4},{6,7},{7,6},{8,9},{9,8},{10,11... | collective-permute-start | bytes 3145736 | tf_op jit(solution)/shard_map/ppermute | solution.py:85
  100.2 9.5 %collective-permute-start.12 = (bf16[2,128,512]{2,1,0:T(8,128)(2,1)}, bf16[2,128,512]{2,1,0:T(8,128)(2,1)}, u32[]{:S(2)}, u32[]{:S(2)}) collective-permute-start(bf16[2,128,512]{2,1,0:T(8,128)(2,1)} %get-tuple-element.43), channel_id=1, source_target_pairs={{0,8},{8,0},{16,24},{24,16},{1,9},{9,1},{17,25},{25,17},{2,10},{10... | collective-permute-start | bytes 786440 | tf_op jit(solution)/shard_map/ppermute | solution.py:144
  101.8 7.9 %copy-start.10 = (bf16[2,128,512]{2,1,0:T(8,128)(2,1)S(1)}, bf16[2,128,512]{2,1,0:T(8,128)(2,1)}, u32[]{:S(2)}) copy-start(bf16[2,128,512]{2,1,0:T(8,128)(2,1)} %copy-done.9) | copy-start | bytes 786436
  104.1 12.1 %collective-permute-start.18 = (bf16[2,128,512]{2,1,0:T(8,128)(2,1)S(1)}, bf16[2,128,512]{2,1,0:T(8,128)(2,1)S(1)}, u32[]{:S(2)}, u32[]{:S(2)}) collective-permute-start(bf16[2,128,512]{2,1,0:T(8,128)(2,1)S(1)} %get-tuple-element.50), channel_id=1, source_target_pairs={{0,24},{8,16},{16,8},{24,0},{1,25},{9,17},{17,9},{25,1},{2,26},{10... | collective-permute-start | bytes 786440 | tf_op jit(solution)/shard_map/ppermute | solution.py:144
  106.6 13.7 %collective-permute-start.19 = (bf16[2,128,512]{2,1,0:T(8,128)(2,1)S(1)}, bf16[2,128,512]{2,1,0:T(8,128)(2,1)S(1)}, u32[]{:S(2)}, u32[]{:S(2)}) collective-permute-start(bf16[2,128,512]{2,1,0:T(8,128)(2,1)S(1)} %get-tuple-element.51), channel_id=1, source_target_pairs={{0,16},{8,24},{16,0},{24,8},{1,17},{9,25},{17,1},{25,9},{2,18},{10... | collective-permute-start | bytes 786440 | tf_op jit(solution)/shard_map/ppermute | solution.py:144
  107.1 13.3 %collective-permute-start.20 = (bf16[2,128,512]{2,1,0:T(8,128)(2,1)S(1)}, bf16[2,128,512]{2,1,0:T(8,128)(2,1)S(1)}, u32[]{:S(2)}, u32[]{:S(2)}) collective-permute-start(bf16[2,128,512]{2,1,0:T(8,128)(2,1)S(1)} %get-tuple-element.52), channel_id=1, source_target_pairs={{0,8},{8,0},{16,24},{24,16},{1,9},{9,1},{17,25},{25,17},{2,10},{10... | collective-permute-start | bytes 786440 | tf_op jit(solution)/shard_map/ppermute | solution.py:144
  109.7 10.7 %copy-start.4 = (bf16[2,128,512]{2,1,0:T(8,128)(2,1)S(1)}, bf16[2,128,512]{2,1,0:T(8,128)(2,1)}, u32[]{:S(2)}) copy-start(bf16[2,128,512]{2,1,0:T(8,128)(2,1)} %add_convert_fusion.1.refs_1_) | copy-start | bytes 786436
  (9 other events, 34.0 us)

commit v15 on v14

--- a/solution.py
+++ b/solution.py
@@ -140,9 +140,9 @@
 
         def exchange(parts):
             sent = {}
-            for t in range(nrow - 1, 0, -1):
+            for t in range(len(parts) - 1, 0, -1):
                 sent[t] = lax.ppermute(parts[t], "row", [(r, r ^ t) for r in range(nrow)])
-            return [parts[0]] + [sent[t] for t in range(1, nrow)]
+            return [parts[0]] + [sent[t] for t in range(1, len(parts))]
 
         def summed(group):
             total = group[0]
@@ -155,9 +155,11 @@
             y3, e2 = along(x1, swap), along(y2, outward)
             sums = [summed(exchange(parts))]
             parts = product(pair1)
-            group = exchange(parts)
-            e3 = along(after(y3, sums[0], group[-1]), outward)
-            sums.append(summed(group))
+            far = [(r, r ^ (nrow - 1)) for r in range(nrow)]
+            lead = lax.ppermute(parts[-1][:1], "row", far)
+            rest = lax.ppermute(parts[-1][1:], "row", far)
+            e3 = along(after(y3, sums[0], lead), outward)
+            sums.append(summed(exchange(parts[:-1]) + [jnp.concatenate([lead, rest])]))
             x2 = jnp.where(end, e2, y2)
             group = exchange(product((after(x2, sums[1]), across(x2))))
             sums.append(summed(group))

time: 156 us -> 159 us (1.019)
  blocking collectives: 32.8 us -> 36 us
    ppermute x12 -> x11, waiting for transfers between devices: 29.5 us -> 21.1 us  [exchange(): sent[t] = lax.ppermute(parts[t], 'row', [(r, r ^ t) for r in range(nrow)])]
    ppermute x0 -> x2, waiting for transfers between devices: none -> 8.14 us  [the longest x1 7.01 us: local(): rest = lax.ppermute(parts[-1][1:], 'row', far)]
    all_to_all x1, blocking collectives: 32.8 us -> 36 us  [local(): second = lax.all_to_all(turned, ('row', 'col'), 0, 0, tiled=True)]
    ppermute x0 -> x2, starting transfers between devices: none -> 3.05 us  [the longest x1 2.61 us: local(): lead = lax.ppermute(parts[-1][:1], 'row', far)]
    ppermute x12 -> x11, starting transfers between devices: 17.4 us -> 14.6 us  [exchange(): sent[t] = lax.ppermute(parts[t], 'row', [(r, r ^ t) for r in range(nrow)])]
  transfers between devices with their start and end apart: 22 -> 23, of which waited for: 15 -> 15; matrix products, arithmetic and copies ran while one was open for 2% -> 2% of each run, Pallas kernels for 6% -> 6%
where the time goes in v15:
time: 159 us
  waiting for transfers between devices  71.3 us (45%)
  blocking collectives  36 us (23%)
  starting transfers between devices  32 us (20%)
  Pallas kernels  12 us (8%)
  local copies, waits for them, and re-layouts  3.77 us (2%)
  other arithmetic  3.72 us (2%)
    all_to_all x1, blocking collectives, local(): second = lax.all_to_all(turned, ('row', 'col'), 0, 0, tiled=True)  36 us
    all_to_all x1, waiting for transfers between devices, local(): raw = lax.all_to_all(blocks, 'col', 0, 0, tiled=True)  23 us
    ppermute x11, waiting for transfers between devices, exchange(): sent[t] = lax.ppermute(parts[t], 'row', [(r, r ^ t) for r in range(nrow)])  21.1 us
    ppermute x5, waiting for transfers between devices, along(): lax.ppermute(x, 'col', [(2 * a + c, 2 * b + c) for a, b in pairs for c in...  18 us
    ppermute x11, starting transfers between devices, exchange(): sent[t] = lax.ppermute(parts[t], 'row', [(r, r ^ t) for r in range(nrow)])  14.6 us
    ppermute x5, starting transfers between devices, along(): lax.ppermute(x, 'col', [(2 * a + c, 2 * b + c) for a, b in pairs for c in...  8.86 us
    ppermute x1, waiting for transfers between devices, local(): rest = lax.ppermute(parts[-1][1:], 'row', far)  7.01 us
    pallas_call x3, Pallas kernels, product(): pl.pallas_call(functools.partial(product_kernel, 1), out_shape=sent, in_s...  5.62 us
  transfers between devices with their start and end apart: 23, of which 15 were waited for; matrix products, arithmetic and copies ran while one was open for 2% of the time, Pallas kernels for 6%

profile of v15, /device:TPU:0, one launch (start us, length us, event | category | flops | bytes accessed | tf_op | source)
XLA Modules:
  0.0 158.9 jit_solution(18213059216377377917)
XLA Ops:
  0.0 3.0 %collective-permute-start.1 = (bf16[1024,512]{1,0:T(8,128)(2,1)}, bf16[1024,512]{1,0:T(8,128)(2,1)}, u32[]{:S(2)}, u32[]{:S(2)}) collective-permute-start(bf16[1024,512]{1,0:T(8,128)(2,1)} %bitcast.7), channel_id=1, source_target_pairs={{0,2},{1,3},{2,0},{3,1},{4,6},{5,7},{6,4},{7,5},{8,10},{9,11},{10,... | collective-permute-start | bytes 3145736 | tf_op jit(solution)/shard_map/ppermute | solution.py:88
  3.0 1.6 %collective-permute-start.10 = (bf16[1024,512]{1,0:T(8,128)(2,1)}, bf16[1024,512]{1,0:T(8,128)(2,1)}, u32[]{:S(2)}, u32[]{:S(2)}) collective-permute-start(bf16[1024,512]{1,0:T(8,128)(2,1)} %bitcast.8), channel_id=1, source_target_pairs={{2,4},{3,5},{4,2},{5,3},{10,12},{11,13},{12,10},{13,11},{18,20},{1... | collective-permute-start | bytes 3145736 | tf_op jit(solution)/shard_map/ppermute | solution.py:88
  7.2 4.8 %all-to-all-start = ((bf16[8,2,64,512]{3,2,1,0:T(8,128)(2,1)}), bf16[8,2,64,512]{3,2,1,0:T(8,128)(2,1)S(1)}, u32[]{:S(2)}, u32[]{:S(2)}) async-start(bf16[8,2,64,512]{3,2,1,0:T(8,128)(2,1)} %shard_map.28), calls=%async_computation | async-start | bytes 2097152 | tf_op jit(solution)/shard_map/all_to_all | solution.py:121
  12.5 14.8 %collective-permute-done.1.refs_0_ = bf16[1024,512]{1,0:T(8,128)(2,1)} collective-permute-done((bf16[1024,512]{1,0:T(8,128)(2,1)}, bf16[1024,512]{1,0:T(8,128)(2,1)}, u32[]{:S(2)}, u32[]{:S(2)}) %collective-permute-start.1) | collective-permute-done | bytes 1048608 | tf_op jit(solution)/shard_map/ppermute | solution.py:88
  28.6 1.6 %collective-permute-start.16 = (bf16[1024,512]{1,0:T(8,128)(2,1)}, bf16[1024,512]{1,0:T(8,128)(2,1)}, u32[]{:S(2)}, u32[]{:S(2)}) collective-permute-start(bf16[1024,512]{1,0:T(8,128)(2,1)} %collective-permute-done.1.refs_0_), channel_id=1, source_target_pairs={{2,4},{3,5},{4,2},{5,3},{10,12},{11,13},{12,10},{13,11},{18,20},{1... | collective-permute-start | bytes 3145736 | tf_op jit(solution)/shard_map/ppermute | solution.py:88
  31.3 23.0 %all-to-all-done.raw_ref = bf16[8,2,64,512]{3,2,1,0:T(8,128)(2,1)S(1)} async-done(((bf16[8,2,64,512]{3,2,1,0:T(8,128)(2,1)}), bf16[8,2,64,512]{3,2,1,0:T(8,128)(2,1)S(1)}, u32[]{:S(2)}, u32[]{:S(2)}) %all-to-all-start) | async-done | bytes 1048608 | tf_op jit(solution)/shard_map/all_to_all | solution.py:121
  54.3 2.6 %shard_map.29 = (bf16[512,1024]{1,0:T(8,128)(2,1)S(1)}, f32[2,128,512]{2,1,0:T(8,128)S(1)}, bf16[2,128,512]{2,1,0:T(8,128)(2,1)S(1)}, bf16[2,128,512]{2,1,0:T(8,128)(2,1)S(1)}, bf16[2,128,512]{2,1,0:T(8,128)(2,1)S(1)}) custom-call(s32[1]{0:T(128)} %bitcast.4.core_ref, bf16[8,2,64,512]{3,2,1,0:T(8,128)(2,1)S(1)} %all-to-all-done.raw_ref, ...), custom_call_target="tpu_custom_call" | custom-call | tf_op jit(solution)/shard_map/pallas_call | solution.py:124
  56.9 2.5 %collective-permute-start.5 = (bf16[2,128,512]{2,1,0:T(8,128)(2,1)S(1)}, bf16[2,128,512]{2,1,0:T(8,128)(2,1)S(1)}, u32[]{:S(2)}, u32[]{:S(2)}) collective-permute-start(bf16[2,128,512]{2,1,0:T(8,128)(2,1)S(1)} %get-tuple-element.34), channel_id=1, source_target_pairs={{0,24},{8,16},{16,8},{24,0},{1,25},{9,17},{17,9},{25,1},{2,26},{10... | collective-permute-start | bytes 786440 | tf_op jit(solution)/shard_map/ppermute | solution.py:144
  60.4 2.5 %shard_map.30 = (f32[2,128,512]{2,1,0:T(8,128)S(1)}, bf16[2,128,512]{2,1,0:T(8,128)(2,1)S(1)}, bf16[2,128,512]{2,1,0:T(8,128)(2,1)S(1)}, bf16[2,128,512]{2,1,0:T(8,128)(2,1)S(1)}) custom-call(s32[1]{0:T(128)} %bitcast.4.core_ref, bf16[512,1024]{1,0:T(8,128)(2,1)S(1)} %get-tuple-element.35.panel_ref, bf16[1024,512]{1,0:T(8,128)(2,1)} %collective-permute-done.1.refs_0_, ...), custom_call_target="tpu_custom_call" | custom-call | tf_op jit(solution)/shard_map/pallas_call | solution.py:133
  62.9 2.9 %collective-permute-done.11 = bf16[1024,512]{1,0:T(8,128)(2,1)} collective-permute-done((bf16[1024,512]{1,0:T(8,128)(2,1)}, bf16[1024,512]{1,0:T(8,128)(2,1)}, u32[]{:S(2)}, u32[]{:S(2)}) %collective-permute-start.11) | collective-permute-done | bytes 1048608 | tf_op jit(solution)/shard_map/ppermute | solution.py:88
  65.8 2.6 %collective-permute-start.8 = (bf16[1,128,512]{2,1,0:T(8,128)(2,1)S(1)}, bf16[1,128,512]{2,1,0:T(8,128)(2,1)S(1)}, u32[]{:S(2)}, u32[]{:S(2)}) collective-permute-start(bf16[1,128,512]{2,1,0:T(8,128)(2,1)S(1)} %get-tuple-element.55), channel_id=1, source_target_pairs={{0,24},{8,16},{16,8},{24,0},{1,25},{9,17},{17,9},{25,1},{2,26},{10... | collective-permute-start | bytes 393224 | tf_op jit(solution)/shard_map/ppermute | solution.py:159
  73.6 1.6 %collective-permute-start.7 = (bf16[2,128,512]{2,1,0:T(8,128)(2,1)S(1)}, bf16[2,128,512]{2,1,0:T(8,128)(2,1)S(1)}, u32[]{:S(2)}, u32[]{:S(2)}) collective-permute-start(bf16[2,128,512]{2,1,0:T(8,128)(2,1)S(1)} %get-tuple-element.38), channel_id=1, source_target_pairs={{0,16},{8,24},{16,0},{24,8},{1,17},{9,25},{17,1},{25,9},{2,18},{10... | collective-permute-start | bytes 786440 | tf_op jit(solution)/shard_map/ppermute | solution.py:144
  75.2 1.5 collective-permute-start.6
  77.1 7.0 %collective-permute-done.9 = bf16[1,128,512]{2,1,0:T(8,128)(2,1)S(1)} collective-permute-done((bf16[1,128,512]{2,1,0:T(8,128)(2,1)S(1)}, bf16[1,128,512]{2,1,0:T(8,128)(2,1)S(1)}, u32[]{:S(2)}, u32[]{:S(2)}) %collective-permute-start.9) | collective-permute-done | bytes 131104 | tf_op jit(solution)/shard_map/ppermute | solution.py:160
  85.0 1.9 %shard_map.31 = (f32[2,128,512]{2,1,0:T(8,128)S(1)}, bf16[2,128,512]{2,1,0:T(8,128)(2,1)}, bf16[2,128,512]{2,1,0:T(8,128)(2,1)S(1)}, bf16[2,128,512]{2,1,0:T(8,128)(2,1)S(1)}) custom-call(s32[1]{0:T(128)} %bitcast.4.core_ref, bf16[512,1024]{1,0:T(8,128)(2,1)S(1)} %get-tuple-element.35.panel_ref, bf16[1024,512]{1,0:T(8,128)(2,1)S(1)} %broadcast_select_fusion.1.refs_0_, ...), custom_call_target="tpu_custom_call" | custom-call | tf_op jit(solution)/shard_map/pallas_call | solution.py:133
  89.0 1.5 collective-permute-start.14
  90.5 4.5 %collective-permute-done.15 = bf16[2,128,512]{2,1,0:T(8,128)(2,1)S(1)} collective-permute-done((bf16[2,128,512]{2,1,0:T(8,128)(2,1)S(1)}, bf16[2,128,512]{2,1,0:T(8,128)(2,1)S(1)}, u32[]{:S(2)}, u32[]{:S(2)}) %collective-permute-start.15) | collective-permute-done | bytes 262176 | tf_op jit(solution)/shard_map/ppermute | solution.py:144
  95.1 3.9 %collective-permute-done.14 = bf16[2,128,512]{2,1,0:T(8,128)(2,1)S(1)} collective-permute-done((bf16[2,128,512]{2,1,0:T(8,128)(2,1)S(1)}, bf16[2,128,512]{2,1,0:T(8,128)(2,1)S(1)}, u32[]{:S(2)}, u32[]{:S(2)}) %collective-permute-start.14) | collective-permute-done | bytes 262176 | tf_op jit(solution)/shard_map/ppermute | solution.py:144
  100.2 1.6 collective-permute-start.13
  104.1 2.5 %collective-permute-start.19 = (bf16[2,128,512]{2,1,0:T(8,128)(2,1)S(1)}, bf16[2,128,512]{2,1,0:T(8,128)(2,1)S(1)}, u32[]{:S(2)}, u32[]{:S(2)}) collective-permute-start(bf16[2,128,512]{2,1,0:T(8,128)(2,1)S(1)} %get-tuple-element.50), channel_id=1, source_target_pairs={{0,24},{8,16},{16,8},{24,0},{1,25},{9,17},{17,9},{25,1},{2,26},{10... | collective-permute-start | bytes 786440 | tf_op jit(solution)/shard_map/ppermute | solution.py:144
  107.7 2.0 %collective-permute-done.13 = bf16[2,128,512]{2,1,0:T(8,128)(2,1)} collective-permute-done((bf16[2,128,512]{2,1,0:T(8,128)(2,1)}, bf16[2,128,512]{2,1,0:T(8,128)(2,1)}, u32[]{:S(2)}, u32[]{:S(2)}) %collective-permute-start.13) | collective-permute-done | bytes 262176 | tf_op jit(solution)/shard_map/ppermute | solution.py:144
  110.9 5.3 %collective-permute-done.19.refs_4_ = bf16[2,128,512]{2,1,0:T(8,128)(2,1)S(1)} collective-permute-done((bf16[2,128,512]{2,1,0:T(8,128)(2,1)S(1)}, bf16[2,128,512]{2,1,0:T(8,128)(2,1)S(1)}, u32[]{:S(2)}, u32[]{:S(2)}) %collective-permute-start.19) | collective-permute-done | bytes 262176 | tf_op jit(solution)/shard_map/ppermute | solution.py:144
  116.2 4.1 %collective-permute-done.20.refs_5_ = bf16[2,128,512]{2,1,0:T(8,128)(2,1)S(1)} collective-permute-done((bf16[2,128,512]{2,1,0:T(8,128)(2,1)S(1)}, bf16[2,128,512]{2,1,0:T(8,128)(2,1)S(1)}, u32[]{:S(2)}, u32[]{:S(2)}) %collective-permute-start.20) | collective-permute-done | bytes 262176 | tf_op jit(solution)/shard_map/ppermute | solution.py:144
  121.4 36.0 %all_to_all.10.second_ref = bf16[32,2,64,128]{3,2,1,0:T(8,128)(2,1)S(1)} all-to-all(bf16[32,2,64,128]{3,2,1,0:T(8,128)(2,1)S(1)} %get-tuple-element.54), channel_id=1, replica_groups=mesh['row'=4,'col'=8] {'row','col'}, dimensions={0} | all-to-all | bytes 2097152 | tf_op jit(solution)/shard_map/all_to_all | solution.py:191
  (59 shorter events, 23.3 us)
Async XLA Ops:
  0.0 27.3 %collective-permute-start.1 = (bf16[1024,512]{1,0:T(8,128)(2,1)}, bf16[1024,512]{1,0:T(8,128)(2,1)}, u32[]{:S(2)}, u32[]{:S(2)}) collective-permute-start(bf16[1024,512]{1,0:T(8,128)(2,1)} %bitcast.7), channel_id=1, source_target_pairs={{0,2},{1,3},{2,0},{3,1},{4,6},{5,7},{6,4},{7,5},{8,10},{9,11},{10,... | collective-permute-start | bytes 3145736 | tf_op jit(solution)/shard_map/ppermute | solution.py:88
  3.0 24.3 %collective-permute-start.10 = (bf16[1024,512]{1,0:T(8,128)(2,1)}, bf16[1024,512]{1,0:T(8,128)(2,1)}, u32[]{:S(2)}, u32[]{:S(2)}) collective-permute-start(bf16[1024,512]{1,0:T(8,128)(2,1)} %bitcast.8), channel_id=1, source_target_pairs={{2,4},{3,5},{4,2},{5,3},{10,12},{11,13},{12,10},{13,11},{18,20},{1... | collective-permute-start | bytes 3145736 | tf_op jit(solution)/shard_map/ppermute | solution.py:88
  7.2 47.1 %all-to-all-start = ((bf16[8,2,64,512]{3,2,1,0:T(8,128)(2,1)}), bf16[8,2,64,512]{3,2,1,0:T(8,128)(2,1)S(1)}, u32[]{:S(2)}, u32[]{:S(2)}) async-start(bf16[8,2,64,512]{3,2,1,0:T(8,128)(2,1)} %shard_map.28), calls=%async_computation | async-start | bytes 2097152 | tf_op jit(solution)/shard_map/all_to_all | solution.py:121
  12.0 18.2 %collective-permute-start = (bf16[1024,512]{1,0:T(8,128)(2,1)S(1)}, bf16[1024,512]{1,0:T(8,128)(2,1)}, u32[]{:S(2)}, u32[]{:S(2)}) collective-permute-start(bf16[1024,512]{1,0:T(8,128)(2,1)S(1)} %bitcast.9), channel_id=1, source_target_pairs={{0,1},{1,0},{2,3},{3,2},{4,5},{5,4},{6,7},{7,6},{8,9},{9,8},{10,11... | collective-permute-start | bytes 3145736 | tf_op jit(solution)/shard_map/ppermute | solution.py:85
  27.3 2.9 %collective-permute-start.2 = (bf16[1024,512]{1,0:T(8,128)(2,1)}, bf16[1024,512]{1,0:T(8,128)(2,1)S(1)}, u32[]{:S(2)}, u32[]{:S(2)}) collective-permute-start(bf16[1024,512]{1,0:T(8,128)(2,1)} %collective-permute-done.1.refs_0_), channel_id=1, source_target_pairs={{0,1},{1,0},{2,3},{3,2},{4,5},{5,4},{6,7},{7,6},{8,9},{9,8},{10,11... | collective-permute-start | bytes 3145736 | tf_op jit(solution)/shard_map/ppermute | solution.py:85
  27.3 38.5 %collective-permute-start.11 = (bf16[1024,512]{1,0:T(8,128)(2,1)}, bf16[1024,512]{1,0:T(8,128)(2,1)}, u32[]{:S(2)}, u32[]{:S(2)}) collective-permute-start(bf16[1024,512]{1,0:T(8,128)(2,1)} %collective-permute-done.10), channel_id=1, source_target_pairs={{2,0},{3,1},{4,6},{5,7},{10,8},{11,9},{12,14},{13,15},{18,16},{19,... | collective-permute-start | bytes 3145736 | tf_op jit(solution)/shard_map/ppermute | solution.py:88
  28.6 42.5 %collective-permute-start.16 = (bf16[1024,512]{1,0:T(8,128)(2,1)}, bf16[1024,512]{1,0:T(8,128)(2,1)}, u32[]{:S(2)}, u32[]{:S(2)}) collective-permute-start(bf16[1024,512]{1,0:T(8,128)(2,1)} %collective-permute-done.1.refs_0_), channel_id=1, source_target_pairs={{2,4},{3,5},{4,2},{5,3},{10,12},{11,13},{12,10},{13,11},{18,20},{1... | collective-permute-start | bytes 3145736 | tf_op jit(solution)/shard_map/ppermute | solution.py:88
  56.9 12.9 %collective-permute-start.5 = (bf16[2,128,512]{2,1,0:T(8,128)(2,1)S(1)}, bf16[2,128,512]{2,1,0:T(8,128)(2,1)S(1)}, u32[]{:S(2)}, u32[]{:S(2)}) collective-permute-start(bf16[2,128,512]{2,1,0:T(8,128)(2,1)S(1)} %get-tuple-element.34), channel_id=1, source_target_pairs={{0,24},{8,16},{16,8},{24,0},{1,25},{9,17},{17,9},{25,1},{2,26},{10... | collective-permute-start | bytes 786440 | tf_op jit(solution)/shard_map/ppermute | solution.py:144
  59.4 11.5 %collective-permute-start.4 = (bf16[2,128,512]{2,1,0:T(8,128)(2,1)S(1)}, bf16[2,128,512]{2,1,0:T(8,128)(2,1)S(1)}, u32[]{:S(2)}, u32[]{:S(2)}) collective-permute-start(bf16[2,128,512]{2,1,0:T(8,128)(2,1)S(1)} %get-tuple-element.33), channel_id=1, source_target_pairs={{0,16},{8,24},{16,0},{24,8},{1,17},{9,25},{17,1},{25,9},{2,18},{10... | collective-permute-start | bytes 786440 | tf_op jit(solution)/shard_map/ppermute | solution.py:144
  59.9 11.1 %collective-permute-start.3 = (bf16[2,128,512]{2,1,0:T(8,128)(2,1)S(1)}, bf16[2,128,512]{2,1,0:T(8,128)(2,1)S(1)}, u32[]{:S(2)}, u32[]{:S(2)}) collective-permute-start(bf16[2,128,512]{2,1,0:T(8,128)(2,1)S(1)} %get-tuple-element.32), channel_id=1, source_target_pairs={{0,8},{8,0},{16,24},{24,16},{1,9},{9,1},{17,25},{25,17},{2,10},{10... | collective-permute-start | bytes 786440 | tf_op jit(solution)/shard_map/ppermute | solution.py:144
  65.8 6.5 %collective-permute-start.8 = (bf16[1,128,512]{2,1,0:T(8,128)(2,1)S(1)}, bf16[1,128,512]{2,1,0:T(8,128)(2,1)S(1)}, u32[]{:S(2)}, u32[]{:S(2)}) collective-permute-start(bf16[1,128,512]{2,1,0:T(8,128)(2,1)S(1)} %get-tuple-element.55), channel_id=1, source_target_pairs={{0,24},{8,16},{16,8},{24,0},{1,25},{9,17},{17,9},{25,1},{2,26},{10... | collective-permute-start | bytes 393224 | tf_op jit(solution)/shard_map/ppermute | solution.py:159
  69.8 15.2 %collective-permute-start.12 = (bf16[1024,512]{1,0:T(8,128)(2,1)S(1)}, bf16[1024,512]{1,0:T(8,128)(2,1)S(1)}, u32[]{:S(2)}, u32[]{:S(2)}) collective-permute-start(bf16[1024,512]{1,0:T(8,128)(2,1)S(1)} %broadcast_select_fusion.1.refs_0_), channel_id=1, source_target_pairs={{0,1},{1,0},{2,3},{3,2},{4,5},{5,4},{6,7},{7,6},{8,9},{9,8},{10,11... | collective-permute-start | bytes 3145736 | tf_op jit(solution)/shard_map/ppermute | solution.py:85
  72.3 27.7 %collective-permute-start.17 = (bf16[1024,512]{1,0:T(8,128)(2,1)}, bf16[1024,512]{1,0:T(8,128)(2,1)S(1)}, u32[]{:S(2)}, u32[]{:S(2)}) collective-permute-start(bf16[1024,512]{1,0:T(8,128)(2,1)} %collective-permute-done.16), channel_id=1, source_target_pairs={{2,0},{3,1},{4,6},{5,7},{10,8},{11,9},{12,14},{13,15},{18,16},{19,... | collective-permute-start | bytes 3145736 | tf_op jit(solution)/shard_map/ppermute | solution.py:88
  73.6 10.6 %collective-permute-start.7 = (bf16[2,128,512]{2,1,0:T(8,128)(2,1)S(1)}, bf16[2,128,512]{2,1,0:T(8,128)(2,1)S(1)}, u32[]{:S(2)}, u32[]{:S(2)}) collective-permute-start(bf16[2,128,512]{2,1,0:T(8,128)(2,1)S(1)} %get-tuple-element.38), channel_id=1, source_target_pairs={{0,16},{8,24},{16,0},{24,8},{1,17},{9,25},{17,1},{25,9},{2,18},{10... | collective-permute-start | bytes 786440 | tf_op jit(solution)/shard_map/ppermute | solution.py:144
  75.2 9.0 %collective-permute-start.6 = (bf16[2,128,512]{2,1,0:T(8,128)(2,1)S(1)}, bf16[2,128,512]{2,1,0:T(8,128)(2,1)S(1)}, u32[]{:S(2)}, u32[]{:S(2)}) collective-permute-start(bf16[2,128,512]{2,1,0:T(8,128)(2,1)S(1)} %get-tuple-element.37), channel_id=1, source_target_pairs={{0,8},{8,0},{16,24},{24,16},{1,9},{9,1},{17,25},{25,17},{2,10},{10... | collective-permute-start | bytes 786440 | tf_op jit(solution)/shard_map/ppermute | solution.py:144
  76.7 7.4 %collective-permute-start.9 = (bf16[1,128,512]{2,1,0:T(8,128)(2,1)S(1)}, bf16[1,128,512]{2,1,0:T(8,128)(2,1)S(1)}, u32[]{:S(2)}, u32[]{:S(2)}) collective-permute-start(bf16[1,128,512]{2,1,0:T(8,128)(2,1)S(1)} %get-tuple-element.56), channel_id=1, source_target_pairs={{0,24},{8,16},{16,8},{24,0},{1,25},{9,17},{17,9},{25,1},{2,26},{10... | collective-permute-start | bytes 393224 | tf_op jit(solution)/shard_map/ppermute | solution.py:160
  87.7 7.4 %collective-permute-start.15 = (bf16[2,128,512]{2,1,0:T(8,128)(2,1)S(1)}, bf16[2,128,512]{2,1,0:T(8,128)(2,1)S(1)}, u32[]{:S(2)}, u32[]{:S(2)}) collective-permute-start(bf16[2,128,512]{2,1,0:T(8,128)(2,1)S(1)} %get-tuple-element.45), channel_id=1, source_target_pairs={{0,24},{8,16},{16,8},{24,0},{1,25},{9,17},{17,9},{25,1},{2,26},{10... | collective-permute-start | bytes 786440 | tf_op jit(solution)/shard_map/ppermute | solution.py:144
  89.0 10.0 %collective-permute-start.14 = (bf16[2,128,512]{2,1,0:T(8,128)(2,1)S(1)}, bf16[2,128,512]{2,1,0:T(8,128)(2,1)S(1)}, u32[]{:S(2)}, u32[]{:S(2)}) collective-permute-start(bf16[2,128,512]{2,1,0:T(8,128)(2,1)S(1)} %get-tuple-element.44), channel_id=1, source_target_pairs={{0,16},{8,24},{16,0},{24,8},{1,17},{9,25},{17,1},{25,9},{2,18},{10... | collective-permute-start | bytes 786440 | tf_op jit(solution)/shard_map/ppermute | solution.py:144
  100.1 2.7 %collective-permute-start.18 = (bf16[1024,512]{1,0:T(8,128)(2,1)S(1)}, bf16[1024,512]{1,0:T(8,128)(2,1)S(1)}, u32[]{:S(2)}, u32[]{:S(2)}) collective-permute-start(bf16[1024,512]{1,0:T(8,128)(2,1)S(1)} %broadcast_select_fusion.refs_0_), channel_id=1, source_target_pairs={{0,1},{1,0},{2,3},{3,2},{4,5},{5,4},{6,7},{7,6},{8,9},{9,8},{10,11... | collective-permute-start | bytes 3145736 | tf_op jit(solution)/shard_map/ppermute | solution.py:85
  100.2 9.5 %collective-permute-start.13 = (bf16[2,128,512]{2,1,0:T(8,128)(2,1)}, bf16[2,128,512]{2,1,0:T(8,128)(2,1)}, u32[]{:S(2)}, u32[]{:S(2)}) collective-permute-start(bf16[2,128,512]{2,1,0:T(8,128)(2,1)} %get-tuple-element.43), channel_id=1, source_target_pairs={{0,8},{8,0},{16,24},{24,16},{1,9},{9,1},{17,25},{25,17},{2,10},{10... | collective-permute-start | bytes 786440 | tf_op jit(solution)/shard_map/ppermute | solution.py:144
  104.1 12.1 %collective-permute-start.19 = (bf16[2,128,512]{2,1,0:T(8,128)(2,1)S(1)}, bf16[2,128,512]{2,1,0:T(8,128)(2,1)S(1)}, u32[]{:S(2)}, u32[]{:S(2)}) collective-permute-start(bf16[2,128,512]{2,1,0:T(8,128)(2,1)S(1)} %get-tuple-element.50), channel_id=1, source_target_pairs={{0,24},{8,16},{16,8},{24,0},{1,25},{9,17},{17,9},{25,1},{2,26},{10... | collective-permute-start | bytes 786440 | tf_op jit(solution)/shard_map/ppermute | solution.py:144
  106.6 13.7 %collective-permute-start.20 = (bf16[2,128,512]{2,1,0:T(8,128)(2,1)S(1)}, bf16[2,128,512]{2,1,0:T(8,128)(2,1)S(1)}, u32[]{:S(2)}, u32[]{:S(2)}) collective-permute-start(bf16[2,128,512]{2,1,0:T(8,128)(2,1)S(1)} %get-tuple-element.51), channel_id=1, source_target_pairs={{0,16},{8,24},{16,0},{24,8},{1,17},{9,25},{17,1},{25,9},{2,18},{10... | collective-permute-start | bytes 786440 | tf_op jit(solution)/shard_map/ppermute | solution.py:144
  107.1 13.3 %collective-permute-start.21 = (bf16[2,128,512]{2,1,0:T(8,128)(2,1)S(1)}, bf16[2,128,512]{2,1,0:T(8,128)(2,1)S(1)}, u32[]{:S(2)}, u32[]{:S(2)}) collective-permute-start(bf16[2,128,512]{2,1,0:T(8,128)(2,1)S(1)} %get-tuple-element.52), channel_id=1, source_target_pairs={{0,8},{8,0},{16,24},{24,16},{1,9},{9,1},{17,25},{25,17},{2,10},{10... | collective-permute-start | bytes 786440 | tf_op jit(solution)/shard_map/ppermute | solution.py:144
  109.7 10.7 %copy-start.4 = (bf16[2,128,512]{2,1,0:T(8,128)(2,1)S(1)}, bf16[2,128,512]{2,1,0:T(8,128)(2,1)}, u32[]{:S(2)}) copy-start(bf16[2,128,512]{2,1,0:T(8,128)(2,1)} %add_convert_fusion.1.refs_1_) | copy-start | bytes 786436
  (10 other events, 42.2 us)

commit v16 on v14

--- a/solution.py
+++ b/solution.py
@@ -161,7 +161,7 @@
             x2 = jnp.where(end, e2, y2)
             group = exchange(product((after(x2, sums[1]), across(x2))))
             sums.append(summed(group))
-            x3 = jnp.where(end, after(e3, *group[nrow // 2 :]), y3)
+            x3 = jnp.where(end, after(e3, group[-1]), y3)
             last = exchange(product((x3, across(x3))))
             last = [last[0]] + last[:0:-1]
             slots = [z, z ^ 1, jnp.where(end, z ^ 2, 3 - z), jnp.where(end, 3 - z, z ^ 2)]

time: 156 us -> 156 us (level)
  blocking collectives: 32.8 us -> 31 us
    ppermute x5, waiting for transfers between devices: 18.1 us -> 21.7 us  [along(): lax.ppermute(x, 'col', [(2 * a + c, 2 * b + c) for a, b in pairs for c in...]
    all_to_all x1, blocking collectives: 32.8 us -> 31 us  [local(): second = lax.all_to_all(turned, ('row', 'col'), 0, 0, tiled=True)]
    unnamed x22 -> x18, local copies, waits for them, and re-layouts: 3.74 us -> 3.76 us
  transfers between devices with their start and end apart: 22 -> 22, of which waited for: 15 -> 14; matrix products, arithmetic and copies ran while one was open for 2% -> 2% of each run, Pallas kernels for 6% -> 6%
where the time goes in v16:
time: 156 us; the launch traced here: 155 us
  waiting for transfers between devices  72.7 us (47%)
  starting transfers between devices  31.7 us (20%)
  blocking collectives  31 us (20%)
  Pallas kernels  12.1 us (8%)
  other arithmetic  3.77 us (2%)
  local copies, waits for them, and re-layouts  3.76 us (2%)
    all_to_all x1, blocking collectives, local(): second = lax.all_to_all(turned, ('row', 'col'), 0, 0, tiled=True)  31 us
    ppermute x12, waiting for transfers between devices, exchange(): sent[t] = lax.ppermute(parts[t], 'row', [(r, r ^ t) for r in range(nrow)])  28 us
    all_to_all x1, waiting for transfers between devices, local(): raw = lax.all_to_all(blocks, 'col', 0, 0, tiled=True)  23 us
    ppermute x5, waiting for transfers between devices, along(): lax.ppermute(x, 'col', [(2 * a + c, 2 * b + c) for a, b in pairs for c in...  21.7 us
    ppermute x12, starting transfers between devices, exchange(): sent[t] = lax.ppermute(parts[t], 'row', [(r, r ^ t) for r in range(nrow)])  17.3 us
    ppermute x5, starting transfers between devices, along(): lax.ppermute(x, 'col', [(2 * a + c, 2 * b + c) for a, b in pairs for c in...  8.85 us
    pallas_call x3, Pallas kernels, product(): pl.pallas_call(functools.partial(product_kernel, 1), out_shape=sent, in_s...  5.72 us
    all_to_all x1, starting transfers between devices, local(): raw = lax.all_to_all(blocks, 'col', 0, 0, tiled=True)  4.83 us
  transfers between devices with their start and end apart: 22, of which 14 were waited for; matrix products, arithmetic and copies ran while one was open for 2% of the time, Pallas kernels for 6%

profile of v16, /device:TPU:0, one launch (start us, length us, event | category | flops | bytes accessed | tf_op | source)
XLA Modules:
  0.0 155.1 jit_solution(8372386209731605081)
XLA Ops:
  0.0 3.0 %collective-permute-start.1 = (bf16[1024,512]{1,0:T(8,128)(2,1)}, bf16[1024,512]{1,0:T(8,128)(2,1)}, u32[]{:S(2)}, u32[]{:S(2)}) collective-permute-start(bf16[1024,512]{1,0:T(8,128)(2,1)} %bitcast.7), channel_id=1, source_target_pairs={{0,2},{1,3},{2,0},{3,1},{4,6},{5,7},{6,4},{7,5},{8,10},{9,11},{10,... | collective-permute-start | bytes 3145736 | tf_op jit(solution)/shard_map/ppermute | solution.py:88
  3.0 1.6 %collective-permute-start.9 = (bf16[1024,512]{1,0:T(8,128)(2,1)}, bf16[1024,512]{1,0:T(8,128)(2,1)}, u32[]{:S(2)}, u32[]{:S(2)}) collective-permute-start(bf16[1024,512]{1,0:T(8,128)(2,1)} %bitcast.8), channel_id=1, source_target_pairs={{2,4},{3,5},{4,2},{5,3},{10,12},{11,13},{12,10},{13,11},{18,20},{1... | collective-permute-start | bytes 3145736 | tf_op jit(solution)/shard_map/ppermute | solution.py:88
  7.2 4.8 %all-to-all-start = ((bf16[8,2,64,512]{3,2,1,0:T(8,128)(2,1)}), bf16[8,2,64,512]{3,2,1,0:T(8,128)(2,1)S(1)}, u32[]{:S(2)}, u32[]{:S(2)}) async-start(bf16[8,2,64,512]{3,2,1,0:T(8,128)(2,1)} %shard_map.28), calls=%async_computation | async-start | bytes 2097152 | tf_op jit(solution)/shard_map/all_to_all | solution.py:121
  12.5 14.8 %collective-permute-done.1.refs_0_ = bf16[1024,512]{1,0:T(8,128)(2,1)} collective-permute-done((bf16[1024,512]{1,0:T(8,128)(2,1)}, bf16[1024,512]{1,0:T(8,128)(2,1)}, u32[]{:S(2)}, u32[]{:S(2)}) %collective-permute-start.1) | collective-permute-done | bytes 1048608 | tf_op jit(solution)/shard_map/ppermute | solution.py:88
  28.6 1.6 %collective-permute-start.15 = (bf16[1024,512]{1,0:T(8,128)(2,1)}, bf16[1024,512]{1,0:T(8,128)(2,1)}, u32[]{:S(2)}, u32[]{:S(2)}) collective-permute-start(bf16[1024,512]{1,0:T(8,128)(2,1)} %collective-permute-done.1.refs_0_), channel_id=1, source_target_pairs={{2,4},{3,5},{4,2},{5,3},{10,12},{11,13},{12,10},{13,11},{18,20},{1... | collective-permute-start | bytes 3145736 | tf_op jit(solution)/shard_map/ppermute | solution.py:88
  31.3 23.0 %all-to-all-done.raw_ref = bf16[8,2,64,512]{3,2,1,0:T(8,128)(2,1)S(1)} async-done(((bf16[8,2,64,512]{3,2,1,0:T(8,128)(2,1)}), bf16[8,2,64,512]{3,2,1,0:T(8,128)(2,1)S(1)}, u32[]{:S(2)}, u32[]{:S(2)}) %all-to-all-start) | async-done | bytes 1048608 | tf_op jit(solution)/shard_map/all_to_all | solution.py:121
  54.3 2.6 %shard_map.29 = (bf16[512,1024]{1,0:T(8,128)(2,1)S(1)}, f32[2,128,512]{2,1,0:T(8,128)S(1)}, bf16[2,128,512]{2,1,0:T(8,128)(2,1)S(1)}, bf16[2,128,512]{2,1,0:T(8,128)(2,1)S(1)}, bf16[2,128,512]{2,1,0:T(8,128)(2,1)S(1)}) custom-call(s32[1]{0:T(128)} %bitcast.4.core_ref, bf16[8,2,64,512]{3,2,1,0:T(8,128)(2,1)S(1)} %all-to-all-done.raw_ref, ...), custom_call_target="tpu_custom_call" | custom-call | tf_op jit(solution)/shard_map/pallas_call | solution.py:124
  56.9 2.5 %collective-permute-start.5 = (bf16[2,128,512]{2,1,0:T(8,128)(2,1)S(1)}, bf16[2,128,512]{2,1,0:T(8,128)(2,1)S(1)}, u32[]{:S(2)}, u32[]{:S(2)}) collective-permute-start(bf16[2,128,512]{2,1,0:T(8,128)(2,1)S(1)} %get-tuple-element.34), channel_id=1, source_target_pairs={{0,24},{8,16},{16,8},{24,0},{1,25},{9,17},{17,9},{25,1},{2,26},{10... | collective-permute-start | bytes 786440 | tf_op jit(solution)/shard_map/ppermute | solution.py:144
  60.4 2.5 %shard_map.30 = (f32[2,128,512]{2,1,0:T(8,128)S(1)}, bf16[2,128,512]{2,1,0:T(8,128)(2,1)S(1)}, bf16[2,128,512]{2,1,0:T(8,128)(2,1)S(1)}, bf16[2,128,512]{2,1,0:T(8,128)(2,1)S(1)}) custom-call(s32[1]{0:T(128)} %bitcast.4.core_ref, bf16[512,1024]{1,0:T(8,128)(2,1)S(1)} %get-tuple-element.35.panel_ref, bf16[1024,512]{1,0:T(8,128)(2,1)} %collective-permute-done.1.refs_0_, ...), custom_call_target="tpu_custom_call" | custom-call | tf_op jit(solution)/shard_map/pallas_call | solution.py:133
  62.9 2.9 %collective-permute-done.10 = bf16[1024,512]{1,0:T(8,128)(2,1)} collective-permute-done((bf16[1024,512]{1,0:T(8,128)(2,1)}, bf16[1024,512]{1,0:T(8,128)(2,1)}, u32[]{:S(2)}, u32[]{:S(2)}) %collective-permute-start.10) | collective-permute-done | bytes 1048608 | tf_op jit(solution)/shard_map/ppermute | solution.py:88
  65.8 2.6 %collective-permute-start.8 = (bf16[2,128,512]{2,1,0:T(8,128)(2,1)S(1)}, bf16[2,128,512]{2,1,0:T(8,128)(2,1)S(1)}, u32[]{:S(2)}, u32[]{:S(2)}) collective-permute-start(bf16[2,128,512]{2,1,0:T(8,128)(2,1)S(1)} %get-tuple-element.39), channel_id=1, source_target_pairs={{0,24},{8,16},{16,8},{24,0},{1,25},{9,17},{17,9},{25,1},{2,26},{10... | collective-permute-start | bytes 786440 | tf_op jit(solution)/shard_map/ppermute | solution.py:144
  69.9 2.4 %collective-permute-done.4 = bf16[2,128,512]{2,1,0:T(8,128)(2,1)S(1)} collective-permute-done((bf16[2,128,512]{2,1,0:T(8,128)(2,1)S(1)}, bf16[2,128,512]{2,1,0:T(8,128)(2,1)S(1)}, u32[]{:S(2)}, u32[]{:S(2)}) %collective-permute-start.4) | collective-permute-done | bytes 262176 | tf_op jit(solution)/shard_map/ppermute | solution.py:144
  72.5 2.6 %collective-permute-done.8 = bf16[2,128,512]{2,1,0:T(8,128)(2,1)S(1)} collective-permute-done((bf16[2,128,512]{2,1,0:T(8,128)(2,1)S(1)}, bf16[2,128,512]{2,1,0:T(8,128)(2,1)S(1)}, u32[]{:S(2)}, u32[]{:S(2)}) %collective-permute-start.8) | collective-permute-done | bytes 262176 | tf_op jit(solution)/shard_map/ppermute | solution.py:144
  76.4 1.6 %collective-permute-start.7 = (bf16[2,128,512]{2,1,0:T(8,128)(2,1)S(1)}, bf16[2,128,512]{2,1,0:T(8,128)(2,1)S(1)}, u32[]{:S(2)}, u32[]{:S(2)}) collective-permute-start(bf16[2,128,512]{2,1,0:T(8,128)(2,1)S(1)} %get-tuple-element.38), channel_id=1, source_target_pairs={{0,16},{8,24},{16,0},{24,8},{1,17},{9,25},{17,1},{25,9},{2,18},{10... | collective-permute-start | bytes 786440 | tf_op jit(solution)/shard_map/ppermute | solution.py:144
  79.5 3.3 %collective-permute-done.7 = bf16[2,128,512]{2,1,0:T(8,128)(2,1)S(1)} collective-permute-done((bf16[2,128,512]{2,1,0:T(8,128)(2,1)S(1)}, bf16[2,128,512]{2,1,0:T(8,128)(2,1)S(1)}, u32[]{:S(2)}, u32[]{:S(2)}) %collective-permute-start.7) | collective-permute-done | bytes 262176 | tf_op jit(solution)/shard_map/ppermute | solution.py:144
  85.2 2.0 %shard_map.31 = (f32[2,128,512]{2,1,0:T(8,128)S(1)}, bf16[2,128,512]{2,1,0:T(8,128)(2,1)}, bf16[2,128,512]{2,1,0:T(8,128)(2,1)}, bf16[2,128,512]{2,1,0:T(8,128)(2,1)S(1)}) custom-call(s32[1]{0:T(128)} %bitcast.4.core_ref, bf16[512,1024]{1,0:T(8,128)(2,1)S(1)} %get-tuple-element.35.panel_ref, bf16[1024,512]{1,0:T(8,128)(2,1)S(1)} %broadcast_select_fusion.1.refs_0_, ...), custom_call_target="tpu_custom_call" | custom-call | tf_op jit(solution)/shard_map/pallas_call | solution.py:133
  89.4 5.8 %collective-permute-done.14 = bf16[2,128,512]{2,1,0:T(8,128)(2,1)S(1)} collective-permute-done((bf16[2,128,512]{2,1,0:T(8,128)(2,1)S(1)}, bf16[2,128,512]{2,1,0:T(8,128)(2,1)S(1)}, u32[]{:S(2)}, u32[]{:S(2)}) %collective-permute-start.14) | collective-permute-done | bytes 262176 | tf_op jit(solution)/shard_map/ppermute | solution.py:144
  96.0 4.0 %collective-permute-done.16 = bf16[1024,512]{1,0:T(8,128)(2,1)S(1)} collective-permute-done((bf16[1024,512]{1,0:T(8,128)(2,1)}, bf16[1024,512]{1,0:T(8,128)(2,1)S(1)}, u32[]{:S(2)}, u32[]{:S(2)}) %collective-permute-start.16) | collective-permute-done | bytes 1048608 | tf_op jit(solution)/shard_map/ppermute | solution.py:88
  100.2 1.6 %collective-permute-start.13 = (bf16[2,128,512]{2,1,0:T(8,128)(2,1)}, bf16[2,128,512]{2,1,0:T(8,128)(2,1)}, u32[]{:S(2)}, u32[]{:S(2)}) collective-permute-start(bf16[2,128,512]{2,1,0:T(8,128)(2,1)} %get-tuple-element.44), channel_id=1, source_target_pairs={{0,16},{8,24},{16,0},{24,8},{1,17},{9,25},{17,1},{25,9},{2,18},{10... | collective-permute-start | bytes 786440 | tf_op jit(solution)/shard_map/ppermute | solution.py:144
  104.6 2.0 %collective-permute-start.18 = (bf16[2,128,512]{2,1,0:T(8,128)(2,1)S(1)}, bf16[2,128,512]{2,1,0:T(8,128)(2,1)S(1)}, u32[]{:S(2)}, u32[]{:S(2)}) collective-permute-start(bf16[2,128,512]{2,1,0:T(8,128)(2,1)S(1)} %get-tuple-element.50), channel_id=1, source_target_pairs={{0,24},{8,16},{16,8},{24,0},{1,25},{9,17},{17,9},{25,1},{2,26},{10... | collective-permute-start | bytes 786440 | tf_op jit(solution)/shard_map/ppermute | solution.py:144
  109.3 2.0 %collective-permute-done.12 = bf16[2,128,512]{2,1,0:T(8,128)(2,1)} collective-permute-done((bf16[2,128,512]{2,1,0:T(8,128)(2,1)}, bf16[2,128,512]{2,1,0:T(8,128)(2,1)}, u32[]{:S(2)}, u32[]{:S(2)}) %collective-permute-start.12) | collective-permute-done | bytes 262176 | tf_op jit(solution)/shard_map/ppermute | solution.py:144
  112.5 4.3 %collective-permute-done.18.refs_4_ = bf16[2,128,512]{2,1,0:T(8,128)(2,1)S(1)} collective-permute-done((bf16[2,128,512]{2,1,0:T(8,128)(2,1)S(1)}, bf16[2,128,512]{2,1,0:T(8,128)(2,1)S(1)}, u32[]{:S(2)}, u32[]{:S(2)}) %collective-permute-start.18) | collective-permute-done | bytes 262176 | tf_op jit(solution)/shard_map/ppermute | solution.py:144
  116.8 3.6 %collective-permute-done.19.refs_5_ = bf16[2,128,512]{2,1,0:T(8,128)(2,1)S(1)} collective-permute-done((bf16[2,128,512]{2,1,0:T(8,128)(2,1)S(1)}, bf16[2,128,512]{2,1,0:T(8,128)(2,1)S(1)}, u32[]{:S(2)}, u32[]{:S(2)}) %collective-permute-start.19) | collective-permute-done | bytes 262176 | tf_op jit(solution)/shard_map/ppermute | solution.py:144
  122.6 31.0 %all_to_all.10.second_ref = bf16[32,2,64,128]{3,2,1,0:T(8,128)(2,1)S(1)} all-to-all(bf16[32,2,64,128]{3,2,1,0:T(8,128)(2,1)S(1)} %get-tuple-element.54), channel_id=1, replica_groups=mesh['row'=4,'col'=8] {'row','col'}, dimensions={0} | all-to-all | bytes 2097152 | tf_op jit(solution)/shard_map/all_to_all | solution.py:189
  (52 shorter events, 26.7 us)
Async XLA Ops:
  0.0 27.3 %collective-permute-start.1 = (bf16[1024,512]{1,0:T(8,128)(2,1)}, bf16[1024,512]{1,0:T(8,128)(2,1)}, u32[]{:S(2)}, u32[]{:S(2)}) collective-permute-start(bf16[1024,512]{1,0:T(8,128)(2,1)} %bitcast.7), channel_id=1, source_target_pairs={{0,2},{1,3},{2,0},{3,1},{4,6},{5,7},{6,4},{7,5},{8,10},{9,11},{10,... | collective-permute-start | bytes 3145736 | tf_op jit(solution)/shard_map/ppermute | solution.py:88
  3.0 24.3 %collective-permute-start.9 = (bf16[1024,512]{1,0:T(8,128)(2,1)}, bf16[1024,512]{1,0:T(8,128)(2,1)}, u32[]{:S(2)}, u32[]{:S(2)}) collective-permute-start(bf16[1024,512]{1,0:T(8,128)(2,1)} %bitcast.8), channel_id=1, source_target_pairs={{2,4},{3,5},{4,2},{5,3},{10,12},{11,13},{12,10},{13,11},{18,20},{1... | collective-permute-start | bytes 3145736 | tf_op jit(solution)/shard_map/ppermute | solution.py:88
  7.2 47.1 %all-to-all-start = ((bf16[8,2,64,512]{3,2,1,0:T(8,128)(2,1)}), bf16[8,2,64,512]{3,2,1,0:T(8,128)(2,1)S(1)}, u32[]{:S(2)}, u32[]{:S(2)}) async-start(bf16[8,2,64,512]{3,2,1,0:T(8,128)(2,1)} %shard_map.28), calls=%async_computation | async-start | bytes 2097152 | tf_op jit(solution)/shard_map/all_to_all | solution.py:121
  12.0 18.2 %collective-permute-start = (bf16[1024,512]{1,0:T(8,128)(2,1)S(1)}, bf16[1024,512]{1,0:T(8,128)(2,1)}, u32[]{:S(2)}, u32[]{:S(2)}) collective-permute-start(bf16[1024,512]{1,0:T(8,128)(2,1)S(1)} %bitcast.9), channel_id=1, source_target_pairs={{0,1},{1,0},{2,3},{3,2},{4,5},{5,4},{6,7},{7,6},{8,9},{9,8},{10,11... | collective-permute-start | bytes 3145736 | tf_op jit(solution)/shard_map/ppermute | solution.py:85
  27.3 2.9 %collective-permute-start.2 = (bf16[1024,512]{1,0:T(8,128)(2,1)}, bf16[1024,512]{1,0:T(8,128)(2,1)S(1)}, u32[]{:S(2)}, u32[]{:S(2)}) collective-permute-start(bf16[1024,512]{1,0:T(8,128)(2,1)} %collective-permute-done.1.refs_0_), channel_id=1, source_target_pairs={{0,1},{1,0},{2,3},{3,2},{4,5},{5,4},{6,7},{7,6},{8,9},{9,8},{10,11... | collective-permute-start | bytes 3145736 | tf_op jit(solution)/shard_map/ppermute | solution.py:85
  27.3 38.5 %collective-permute-start.10 = (bf16[1024,512]{1,0:T(8,128)(2,1)}, bf16[1024,512]{1,0:T(8,128)(2,1)}, u32[]{:S(2)}, u32[]{:S(2)}) collective-permute-start(bf16[1024,512]{1,0:T(8,128)(2,1)} %collective-permute-done.9), channel_id=1, source_target_pairs={{2,0},{3,1},{4,6},{5,7},{10,8},{11,9},{12,14},{13,15},{18,16},{19,... | collective-permute-start | bytes 3145736 | tf_op jit(solution)/shard_map/ppermute | solution.py:88
  28.6 43.9 %collective-permute-start.15 = (bf16[1024,512]{1,0:T(8,128)(2,1)}, bf16[1024,512]{1,0:T(8,128)(2,1)}, u32[]{:S(2)}, u32[]{:S(2)}) collective-permute-start(bf16[1024,512]{1,0:T(8,128)(2,1)} %collective-permute-done.1.refs_0_), channel_id=1, source_target_pairs={{2,4},{3,5},{4,2},{5,3},{10,12},{11,13},{12,10},{13,11},{18,20},{1... | collective-permute-start | bytes 3145736 | tf_op jit(solution)/shard_map/ppermute | solution.py:88
  56.9 12.9 %collective-permute-start.5 = (bf16[2,128,512]{2,1,0:T(8,128)(2,1)S(1)}, bf16[2,128,512]{2,1,0:T(8,128)(2,1)S(1)}, u32[]{:S(2)}, u32[]{:S(2)}) collective-permute-start(bf16[2,128,512]{2,1,0:T(8,128)(2,1)S(1)} %get-tuple-element.34), channel_id=1, source_target_pairs={{0,24},{8,16},{16,8},{24,0},{1,25},{9,17},{17,9},{25,1},{2,26},{10... | collective-permute-start | bytes 786440 | tf_op jit(solution)/shard_map/ppermute | solution.py:144
  59.4 12.9 %collective-permute-start.4 = (bf16[2,128,512]{2,1,0:T(8,128)(2,1)S(1)}, bf16[2,128,512]{2,1,0:T(8,128)(2,1)S(1)}, u32[]{:S(2)}, u32[]{:S(2)}) collective-permute-start(bf16[2,128,512]{2,1,0:T(8,128)(2,1)S(1)} %get-tuple-element.33), channel_id=1, source_target_pairs={{0,16},{8,24},{16,0},{24,8},{1,17},{9,25},{17,1},{25,9},{2,18},{10... | collective-permute-start | bytes 786440 | tf_op jit(solution)/shard_map/ppermute | solution.py:144
  59.9 12.4 %collective-permute-start.3 = (bf16[2,128,512]{2,1,0:T(8,128)(2,1)S(1)}, bf16[2,128,512]{2,1,0:T(8,128)(2,1)S(1)}, u32[]{:S(2)}, u32[]{:S(2)}) collective-permute-start(bf16[2,128,512]{2,1,0:T(8,128)(2,1)S(1)} %get-tuple-element.32), channel_id=1, source_target_pairs={{0,8},{8,0},{16,24},{24,16},{1,9},{9,1},{17,25},{25,17},{2,10},{10... | collective-permute-start | bytes 786440 | tf_op jit(solution)/shard_map/ppermute | solution.py:144
  65.8 9.3 %collective-permute-start.8 = (bf16[2,128,512]{2,1,0:T(8,128)(2,1)S(1)}, bf16[2,128,512]{2,1,0:T(8,128)(2,1)S(1)}, u32[]{:S(2)}, u32[]{:S(2)}) collective-permute-start(bf16[2,128,512]{2,1,0:T(8,128)(2,1)S(1)} %get-tuple-element.39), channel_id=1, source_target_pairs={{0,24},{8,16},{16,8},{24,0},{1,25},{9,17},{17,9},{25,1},{2,26},{10... | collective-permute-start | bytes 786440 | tf_op jit(solution)/shard_map/ppermute | solution.py:144
  69.8 15.4 %collective-permute-start.11 = (bf16[1024,512]{1,0:T(8,128)(2,1)S(1)}, bf16[1024,512]{1,0:T(8,128)(2,1)S(1)}, u32[]{:S(2)}, u32[]{:S(2)}) collective-permute-start(bf16[1024,512]{1,0:T(8,128)(2,1)S(1)} %broadcast_select_fusion.1.refs_0_), channel_id=1, source_target_pairs={{0,1},{1,0},{2,3},{3,2},{4,5},{5,4},{6,7},{7,6},{8,9},{9,8},{10,11... | collective-permute-start | bytes 3145736 | tf_op jit(solution)/shard_map/ppermute | solution.py:85
  75.1 24.9 %collective-permute-start.16 = (bf16[1024,512]{1,0:T(8,128)(2,1)}, bf16[1024,512]{1,0:T(8,128)(2,1)S(1)}, u32[]{:S(2)}, u32[]{:S(2)}) collective-permute-start(bf16[1024,512]{1,0:T(8,128)(2,1)} %collective-permute-done.15), channel_id=1, source_target_pairs={{2,0},{3,1},{4,6},{5,7},{10,8},{11,9},{12,14},{13,15},{18,16},{19,... | collective-permute-start | bytes 3145736 | tf_op jit(solution)/shard_map/ppermute | solution.py:88
  76.4 6.4 %collective-permute-start.7 = (bf16[2,128,512]{2,1,0:T(8,128)(2,1)S(1)}, bf16[2,128,512]{2,1,0:T(8,128)(2,1)S(1)}, u32[]{:S(2)}, u32[]{:S(2)}) collective-permute-start(bf16[2,128,512]{2,1,0:T(8,128)(2,1)S(1)} %get-tuple-element.38), channel_id=1, source_target_pairs={{0,16},{8,24},{16,0},{24,8},{1,17},{9,25},{17,1},{25,9},{2,18},{10... | collective-permute-start | bytes 786440 | tf_op jit(solution)/shard_map/ppermute | solution.py:144
  78.0 6.4 %collective-permute-start.6 = (bf16[2,128,512]{2,1,0:T(8,128)(2,1)S(1)}, bf16[2,128,512]{2,1,0:T(8,128)(2,1)S(1)}, u32[]{:S(2)}, u32[]{:S(2)}) collective-permute-start(bf16[2,128,512]{2,1,0:T(8,128)(2,1)S(1)} %get-tuple-element.37), channel_id=1, source_target_pairs={{0,8},{8,0},{16,24},{24,16},{1,9},{9,1},{17,25},{25,17},{2,10},{10... | collective-permute-start | bytes 786440 | tf_op jit(solution)/shard_map/ppermute | solution.py:144
  88.0 7.3 %collective-permute-start.14 = (bf16[2,128,512]{2,1,0:T(8,128)(2,1)S(1)}, bf16[2,128,512]{2,1,0:T(8,128)(2,1)S(1)}, u32[]{:S(2)}, u32[]{:S(2)}) collective-permute-start(bf16[2,128,512]{2,1,0:T(8,128)(2,1)S(1)} %get-tuple-element.45), channel_id=1, source_target_pairs={{0,24},{8,16},{16,8},{24,0},{1,25},{9,17},{17,9},{25,1},{2,26},{10... | collective-permute-start | bytes 786440 | tf_op jit(solution)/shard_map/ppermute | solution.py:144
  100.1 3.2 %collective-permute-start.17 = (bf16[1024,512]{1,0:T(8,128)(2,1)S(1)}, bf16[1024,512]{1,0:T(8,128)(2,1)S(1)}, u32[]{:S(2)}, u32[]{:S(2)}) collective-permute-start(bf16[1024,512]{1,0:T(8,128)(2,1)S(1)} %broadcast_select_fusion.refs_0_), channel_id=1, source_target_pairs={{0,1},{1,0},{2,3},{3,2},{4,5},{5,4},{6,7},{7,6},{8,9},{9,8},{10,11... | collective-permute-start | bytes 3145736 | tf_op jit(solution)/shard_map/ppermute | solution.py:85
  100.2 9.0 %collective-permute-start.13 = (bf16[2,128,512]{2,1,0:T(8,128)(2,1)}, bf16[2,128,512]{2,1,0:T(8,128)(2,1)}, u32[]{:S(2)}, u32[]{:S(2)}) collective-permute-start(bf16[2,128,512]{2,1,0:T(8,128)(2,1)} %get-tuple-element.44), channel_id=1, source_target_pairs={{0,16},{8,24},{16,0},{24,8},{1,17},{9,25},{17,1},{25,9},{2,18},{10... | collective-permute-start | bytes 786440 | tf_op jit(solution)/shard_map/ppermute | solution.py:144
  101.8 9.5 %collective-permute-start.12 = (bf16[2,128,512]{2,1,0:T(8,128)(2,1)}, bf16[2,128,512]{2,1,0:T(8,128)(2,1)}, u32[]{:S(2)}, u32[]{:S(2)}) collective-permute-start(bf16[2,128,512]{2,1,0:T(8,128)(2,1)} %get-tuple-element.43), channel_id=1, source_target_pairs={{0,8},{8,0},{16,24},{24,16},{1,9},{9,1},{17,25},{25,17},{2,10},{10... | collective-permute-start | bytes 786440 | tf_op jit(solution)/shard_map/ppermute | solution.py:144
  103.4 7.9 %copy-start.8 = (bf16[2,128,512]{2,1,0:T(8,128)(2,1)S(1)}, bf16[2,128,512]{2,1,0:T(8,128)(2,1)}, u32[]{:S(2)}) copy-start(bf16[2,128,512]{2,1,0:T(8,128)(2,1)} %copy-done.7) | copy-start | bytes 786436
  104.6 12.1 %collective-permute-start.18 = (bf16[2,128,512]{2,1,0:T(8,128)(2,1)S(1)}, bf16[2,128,512]{2,1,0:T(8,128)(2,1)S(1)}, u32[]{:S(2)}, u32[]{:S(2)}) collective-permute-start(bf16[2,128,512]{2,1,0:T(8,128)(2,1)S(1)} %get-tuple-element.50), channel_id=1, source_target_pairs={{0,24},{8,16},{16,8},{24,0},{1,25},{9,17},{17,9},{25,1},{2,26},{10... | collective-permute-start | bytes 786440 | tf_op jit(solution)/shard_map/ppermute | solution.py:144
  106.6 13.8 %collective-permute-start.19 = (bf16[2,128,512]{2,1,0:T(8,128)(2,1)S(1)}, bf16[2,128,512]{2,1,0:T(8,128)(2,1)S(1)}, u32[]{:S(2)}, u32[]{:S(2)}) collective-permute-start(bf16[2,128,512]{2,1,0:T(8,128)(2,1)S(1)} %get-tuple-element.51), channel_id=1, source_target_pairs={{0,16},{8,24},{16,0},{24,8},{1,17},{9,25},{17,1},{25,9},{2,18},{10... | collective-permute-start | bytes 786440 | tf_op jit(solution)/shard_map/ppermute | solution.py:144
  107.1 14.5 %collective-permute-start.20 = (bf16[2,128,512]{2,1,0:T(8,128)(2,1)S(1)}, bf16[2,128,512]{2,1,0:T(8,128)(2,1)S(1)}, u32[]{:S(2)}, u32[]{:S(2)}) collective-permute-start(bf16[2,128,512]{2,1,0:T(8,128)(2,1)S(1)} %get-tuple-element.52), channel_id=1, source_target_pairs={{0,8},{8,0},{16,24},{24,16},{1,9},{9,1},{17,25},{25,17},{2,10},{10... | collective-permute-start | bytes 786440 | tf_op jit(solution)/shard_map/ppermute | solution.py:144
  111.3 10.4 %copy-start.4 = (bf16[2,128,512]{2,1,0:T(8,128)(2,1)S(1)}, bf16[2,128,512]{2,1,0:T(8,128)(2,1)}, u32[]{:S(2)}) copy-start(bf16[2,128,512]{2,1,0:T(8,128)(2,1)} %add_convert_fusion.1.refs_1_) | copy-start | bytes 786436
  (7 other events, 22.6 us)

commit v17 on v16

--- a/solution.py
+++ b/solution.py
@@ -159,7 +159,7 @@
             e3 = along(after(y3, sums[0], group[-1]), outward)
             sums.append(summed(group))
             x2 = jnp.where(end, e2, y2)
-            group = exchange(product((after(x2, sums[1]), across(x2))))
+            group = exchange(product((after(x2, *group[1:]), across(x2))))
             sums.append(summed(group))
             x3 = jnp.where(end, after(e3, group[-1]), y3)
             last = exchange(product((x3, across(x3))))

time: 156 us -> 156 us (level)
  local copies, waits for them, and re-layouts: 3.76 us -> 5.94 us
    unnamed x18 -> x26, local copies, waits for them, and re-layouts: 3.76 us -> 5.94 us
  transfers between devices with their start and end apart: 22 -> 22, of which waited for: 14 -> 13; matrix products, arithmetic and copies ran while one was open for 2% -> 2% of each run, Pallas kernels for 6% -> 6%
where the time goes in v17:
time: 156 us; the launch traced here: 155 us
  waiting for transfers between devices  71.9 us (46%)
  starting transfers between devices  31.6 us (20%)
  blocking collectives  31 us (20%)
  Pallas kernels  11.3 us (7%)
  local copies, waits for them, and re-layouts  5.94 us (4%)
  other arithmetic  3.24 us (2%)
    all_to_all x1, blocking collectives, local(): second = lax.all_to_all(turned, ('row', 'col'), 0, 0, tiled=True)  31 us
    ppermute x12, waiting for transfers between devices, exchange(): sent[t] = lax.ppermute(parts[t], 'row', [(r, r ^ t) for r in range(nrow)])  27.9 us
    all_to_all x1, waiting for transfers between devices, local(): raw = lax.all_to_all(blocks, 'col', 0, 0, tiled=True)  23 us
    ppermute x5, waiting for transfers between devices, along(): lax.ppermute(x, 'col', [(2 * a + c, 2 * b + c) for a, b in pairs for c in...  21 us
    ppermute x12, starting transfers between devices, exchange(): sent[t] = lax.ppermute(parts[t], 'row', [(r, r ^ t) for r in range(nrow)])  17.3 us
    ppermute x5, starting transfers between devices, along(): lax.ppermute(x, 'col', [(2 * a + c, 2 * b + c) for a, b in pairs for c in...  8.86 us
    unnamed x26, local copies, waits for them, and re-layouts  5.94 us
    pallas_call x3, Pallas kernels, product(): pl.pallas_call(functools.partial(product_kernel, 1), out_shape=sent, in_s...  4.98 us
  transfers between devices with their start and end apart: 22, of which 13 were waited for; matrix products, arithmetic and copies ran while one was open for 2% of the time, Pallas kernels for 6%

profile of v17, /device:TPU:0, one launch (start us, length us, event | category | flops | bytes accessed | tf_op | source)
XLA Modules:
  0.0 155.2 jit_solution(7799745291995458219)
XLA Ops:
  0.0 3.0 %collective-permute-start.1 = (bf16[1024,512]{1,0:T(8,128)(2,1)}, bf16[1024,512]{1,0:T(8,128)(2,1)}, u32[]{:S(2)}, u32[]{:S(2)}) collective-permute-start(bf16[1024,512]{1,0:T(8,128)(2,1)} %bitcast.7), channel_id=1, source_target_pairs={{0,2},{1,3},{2,0},{3,1},{4,6},{5,7},{6,4},{7,5},{8,10},{9,11},{10,... | collective-permute-start | bytes 3145736 | tf_op jit(solution)/shard_map/ppermute | solution.py:88
  3.0 1.6 %collective-permute-start.9 = (bf16[1024,512]{1,0:T(8,128)(2,1)}, bf16[1024,512]{1,0:T(8,128)(2,1)}, u32[]{:S(2)}, u32[]{:S(2)}) collective-permute-start(bf16[1024,512]{1,0:T(8,128)(2,1)} %bitcast.8), channel_id=1, source_target_pairs={{2,4},{3,5},{4,2},{5,3},{10,12},{11,13},{12,10},{13,11},{18,20},{1... | collective-permute-start | bytes 3145736 | tf_op jit(solution)/shard_map/ppermute | solution.py:88
  7.2 4.8 %all-to-all-start = ((bf16[8,2,64,512]{3,2,1,0:T(8,128)(2,1)}), bf16[8,2,64,512]{3,2,1,0:T(8,128)(2,1)S(1)}, u32[]{:S(2)}, u32[]{:S(2)}) async-start(bf16[8,2,64,512]{3,2,1,0:T(8,128)(2,1)} %shard_map.28), calls=%async_computation | async-start | bytes 2097152 | tf_op jit(solution)/shard_map/all_to_all | solution.py:121
  12.5 14.8 %collective-permute-done.1.refs_0_ = bf16[1024,512]{1,0:T(8,128)(2,1)} collective-permute-done((bf16[1024,512]{1,0:T(8,128)(2,1)}, bf16[1024,512]{1,0:T(8,128)(2,1)}, u32[]{:S(2)}, u32[]{:S(2)}) %collective-permute-start.1) | collective-permute-done | bytes 1048608 | tf_op jit(solution)/shard_map/ppermute | solution.py:88
  28.6 1.6 %collective-permute-start.15 = (bf16[1024,512]{1,0:T(8,128)(2,1)}, bf16[1024,512]{1,0:T(8,128)(2,1)}, u32[]{:S(2)}, u32[]{:S(2)}) collective-permute-start(bf16[1024,512]{1,0:T(8,128)(2,1)} %collective-permute-done.1.refs_0_), channel_id=1, source_target_pairs={{2,4},{3,5},{4,2},{5,3},{10,12},{11,13},{12,10},{13,11},{18,20},{1... | collective-permute-start | bytes 3145736 | tf_op jit(solution)/shard_map/ppermute | solution.py:88
  31.3 23.0 %all-to-all-done.raw_ref = bf16[8,2,64,512]{3,2,1,0:T(8,128)(2,1)S(1)} async-done(((bf16[8,2,64,512]{3,2,1,0:T(8,128)(2,1)}), bf16[8,2,64,512]{3,2,1,0:T(8,128)(2,1)S(1)}, u32[]{:S(2)}, u32[]{:S(2)}) %all-to-all-start) | async-done | bytes 1048608 | tf_op jit(solution)/shard_map/all_to_all | solution.py:121
  54.3 2.6 %shard_map.29 = (bf16[512,1024]{1,0:T(8,128)(2,1)S(1)}, f32[2,128,512]{2,1,0:T(8,128)S(1)}, bf16[2,128,512]{2,1,0:T(8,128)(2,1)S(1)}, bf16[2,128,512]{2,1,0:T(8,128)(2,1)S(1)}, bf16[2,128,512]{2,1,0:T(8,128)(2,1)S(1)}) custom-call(s32[1]{0:T(128)} %bitcast.4.core_ref, bf16[8,2,64,512]{3,2,1,0:T(8,128)(2,1)S(1)} %all-to-all-done.raw_ref, ...), custom_call_target="tpu_custom_call" | custom-call | tf_op jit(solution)/shard_map/pallas_call | solution.py:124
  56.9 2.5 %collective-permute-start.5 = (bf16[2,128,512]{2,1,0:T(8,128)(2,1)S(1)}, bf16[2,128,512]{2,1,0:T(8,128)(2,1)S(1)}, u32[]{:S(2)}, u32[]{:S(2)}) collective-permute-start(bf16[2,128,512]{2,1,0:T(8,128)(2,1)S(1)} %get-tuple-element.34), channel_id=1, source_target_pairs={{0,24},{8,16},{16,8},{24,0},{1,25},{9,17},{17,9},{25,1},{2,26},{10... | collective-permute-start | bytes 786440 | tf_op jit(solution)/shard_map/ppermute | solution.py:144
  60.4 2.5 %shard_map.30 = (f32[2,128,512]{2,1,0:T(8,128)S(1)}, bf16[2,128,512]{2,1,0:T(8,128)(2,1)S(1)}, bf16[2,128,512]{2,1,0:T(8,128)(2,1)S(1)}, bf16[2,128,512]{2,1,0:T(8,128)(2,1)S(1)}) custom-call(s32[1]{0:T(128)} %bitcast.4.core_ref, bf16[512,1024]{1,0:T(8,128)(2,1)S(1)} %get-tuple-element.35.panel_ref, bf16[1024,512]{1,0:T(8,128)(2,1)} %collective-permute-done.1.refs_0_, ...), custom_call_target="tpu_custom_call" | custom-call | tf_op jit(solution)/shard_map/pallas_call | solution.py:133
  63.7 2.1 %collective-permute-done.10 = bf16[1024,512]{1,0:T(8,128)(2,1)} collective-permute-done((bf16[1024,512]{1,0:T(8,128)(2,1)}, bf16[1024,512]{1,0:T(8,128)(2,1)}, u32[]{:S(2)}, u32[]{:S(2)}) %collective-permute-start.10) | collective-permute-done | bytes 1048608 | tf_op jit(solution)/shard_map/ppermute | solution.py:88
  65.8 2.6 %collective-permute-start.8 = (bf16[2,128,512]{2,1,0:T(8,128)(2,1)S(1)}, bf16[2,128,512]{2,1,0:T(8,128)(2,1)}, u32[]{:S(2)}, u32[]{:S(2)}) collective-permute-start(bf16[2,128,512]{2,1,0:T(8,128)(2,1)S(1)} %get-tuple-element.39), channel_id=1, source_target_pairs={{0,24},{8,16},{16,8},{24,0},{1,25},{9,17},{17,9},{25,1},{2,26},{10... | collective-permute-start | bytes 786440 | tf_op jit(solution)/shard_map/ppermute | solution.py:144
  69.9 2.4 %collective-permute-done.4 = bf16[2,128,512]{2,1,0:T(8,128)(2,1)S(1)} collective-permute-done((bf16[2,128,512]{2,1,0:T(8,128)(2,1)S(1)}, bf16[2,128,512]{2,1,0:T(8,128)(2,1)S(1)}, u32[]{:S(2)}, u32[]{:S(2)}) %collective-permute-start.4) | collective-permute-done | bytes 262176 | tf_op jit(solution)/shard_map/ppermute | solution.py:144
  72.4 2.7 %collective-permute-done.8 = bf16[2,128,512]{2,1,0:T(8,128)(2,1)} collective-permute-done((bf16[2,128,512]{2,1,0:T(8,128)(2,1)S(1)}, bf16[2,128,512]{2,1,0:T(8,128)(2,1)}, u32[]{:S(2)}, u32[]{:S(2)}) %collective-permute-start.8) | collective-permute-done | bytes 262176 | tf_op jit(solution)/shard_map/ppermute | solution.py:144
  76.5 1.6 %collective-permute-start.7 = (bf16[2,128,512]{2,1,0:T(8,128)(2,1)S(1)}, bf16[2,128,512]{2,1,0:T(8,128)(2,1)S(1)}, u32[]{:S(2)}, u32[]{:S(2)}) collective-permute-start(bf16[2,128,512]{2,1,0:T(8,128)(2,1)S(1)} %get-tuple-element.38), channel_id=1, source_target_pairs={{0,16},{8,24},{16,0},{24,8},{1,17},{9,25},{17,1},{25,9},{2,18},{10... | collective-permute-start | bytes 786440 | tf_op jit(solution)/shard_map/ppermute | solution.py:144
  78.1 1.5 collective-permute-start.6
  79.6 3.3 %collective-permute-done.7 = bf16[2,128,512]{2,1,0:T(8,128)(2,1)S(1)} collective-permute-done((bf16[2,128,512]{2,1,0:T(8,128)(2,1)S(1)}, bf16[2,128,512]{2,1,0:T(8,128)(2,1)S(1)}, u32[]{:S(2)}, u32[]{:S(2)}) %collective-permute-start.7) | collective-permute-done | bytes 262176 | tf_op jit(solution)/shard_map/ppermute | solution.py:144
  82.9 1.6 collective-permute-done.6
  89.4 5.8 %collective-permute-done.14 = bf16[2,128,512]{2,1,0:T(8,128)(2,1)S(1)} collective-permute-done((bf16[2,128,512]{2,1,0:T(8,128)(2,1)S(1)}, bf16[2,128,512]{2,1,0:T(8,128)(2,1)S(1)}, u32[]{:S(2)}, u32[]{:S(2)}) %collective-permute-start.14) | collective-permute-done | bytes 262176 | tf_op jit(solution)/shard_map/ppermute | solution.py:144
  95.9 4.1 %collective-permute-done.16 = bf16[1024,512]{1,0:T(8,128)(2,1)S(1)} collective-permute-done((bf16[1024,512]{1,0:T(8,128)(2,1)}, bf16[1024,512]{1,0:T(8,128)(2,1)S(1)}, u32[]{:S(2)}, u32[]{:S(2)}) %collective-permute-start.16) | collective-permute-done | bytes 1048608 | tf_op jit(solution)/shard_map/ppermute | solution.py:88
  100.3 1.5 collective-permute-start.13
  109.6 1.6 %collective-permute-done.12 = bf16[2,128,512]{2,1,0:T(8,128)(2,1)S(1)} collective-permute-done((bf16[2,128,512]{2,1,0:T(8,128)(2,1)}, bf16[2,128,512]{2,1,0:T(8,128)(2,1)S(1)}, u32[]{:S(2)}, u32[]{:S(2)}) %collective-permute-start.12) | collective-permute-done | bytes 262176 | tf_op jit(solution)/shard_map/ppermute | solution.py:144
  111.4 5.5 %collective-permute-done.18.refs_4_ = bf16[2,128,512]{2,1,0:T(8,128)(2,1)S(1)} collective-permute-done((bf16[2,128,512]{2,1,0:T(8,128)(2,1)S(1)}, bf16[2,128,512]{2,1,0:T(8,128)(2,1)S(1)}, u32[]{:S(2)}, u32[]{:S(2)}) %collective-permute-start.18) | collective-permute-done | bytes 262176 | tf_op jit(solution)/shard_map/ppermute | solution.py:144
  116.8 3.7 %collective-permute-done.19.refs_5_ = bf16[2,128,512]{2,1,0:T(8,128)(2,1)S(1)} collective-permute-done((bf16[2,128,512]{2,1,0:T(8,128)(2,1)S(1)}, bf16[2,128,512]{2,1,0:T(8,128)(2,1)S(1)}, u32[]{:S(2)}, u32[]{:S(2)}) %collective-permute-start.19) | collective-permute-done | bytes 262176 | tf_op jit(solution)/shard_map/ppermute | solution.py:144
  122.7 31.0 %all_to_all.10.second_ref = bf16[32,2,64,128]{3,2,1,0:T(8,128)(2,1)S(1)} all-to-all(bf16[32,2,64,128]{3,2,1,0:T(8,128)(2,1)S(1)} %get-tuple-element.54), channel_id=1, replica_groups=mesh['row'=4,'col'=8] {'row','col'}, dimensions={0} | all-to-all | bytes 2097152 | tf_op jit(solution)/shard_map/all_to_all | solution.py:189
  (60 shorter events, 27.5 us)
Async XLA Ops:
  0.0 27.3 %collective-permute-start.1 = (bf16[1024,512]{1,0:T(8,128)(2,1)}, bf16[1024,512]{1,0:T(8,128)(2,1)}, u32[]{:S(2)}, u32[]{:S(2)}) collective-permute-start(bf16[1024,512]{1,0:T(8,128)(2,1)} %bitcast.7), channel_id=1, source_target_pairs={{0,2},{1,3},{2,0},{3,1},{4,6},{5,7},{6,4},{7,5},{8,10},{9,11},{10,... | collective-permute-start | bytes 3145736 | tf_op jit(solution)/shard_map/ppermute | solution.py:88
  3.0 24.3 %collective-permute-start.9 = (bf16[1024,512]{1,0:T(8,128)(2,1)}, bf16[1024,512]{1,0:T(8,128)(2,1)}, u32[]{:S(2)}, u32[]{:S(2)}) collective-permute-start(bf16[1024,512]{1,0:T(8,128)(2,1)} %bitcast.8), channel_id=1, source_target_pairs={{2,4},{3,5},{4,2},{5,3},{10,12},{11,13},{12,10},{13,11},{18,20},{1... | collective-permute-start | bytes 3145736 | tf_op jit(solution)/shard_map/ppermute | solution.py:88
  7.2 47.1 %all-to-all-start = ((bf16[8,2,64,512]{3,2,1,0:T(8,128)(2,1)}), bf16[8,2,64,512]{3,2,1,0:T(8,128)(2,1)S(1)}, u32[]{:S(2)}, u32[]{:S(2)}) async-start(bf16[8,2,64,512]{3,2,1,0:T(8,128)(2,1)} %shard_map.28), calls=%async_computation | async-start | bytes 2097152 | tf_op jit(solution)/shard_map/all_to_all | solution.py:121
  12.0 18.2 %collective-permute-start = (bf16[1024,512]{1,0:T(8,128)(2,1)S(1)}, bf16[1024,512]{1,0:T(8,128)(2,1)}, u32[]{:S(2)}, u32[]{:S(2)}) collective-permute-start(bf16[1024,512]{1,0:T(8,128)(2,1)S(1)} %bitcast.9), channel_id=1, source_target_pairs={{0,1},{1,0},{2,3},{3,2},{4,5},{5,4},{6,7},{7,6},{8,9},{9,8},{10,11... | collective-permute-start | bytes 3145736 | tf_op jit(solution)/shard_map/ppermute | solution.py:85
  27.3 2.9 %collective-permute-start.2 = (bf16[1024,512]{1,0:T(8,128)(2,1)}, bf16[1024,512]{1,0:T(8,128)(2,1)S(1)}, u32[]{:S(2)}, u32[]{:S(2)}) collective-permute-start(bf16[1024,512]{1,0:T(8,128)(2,1)} %collective-permute-done.1.refs_0_), channel_id=1, source_target_pairs={{0,1},{1,0},{2,3},{3,2},{4,5},{5,4},{6,7},{7,6},{8,9},{9,8},{10,11... | collective-permute-start | bytes 3145736 | tf_op jit(solution)/shard_map/ppermute | solution.py:85
  27.3 38.5 %collective-permute-start.10 = (bf16[1024,512]{1,0:T(8,128)(2,1)}, bf16[1024,512]{1,0:T(8,128)(2,1)}, u32[]{:S(2)}, u32[]{:S(2)}) collective-permute-start(bf16[1024,512]{1,0:T(8,128)(2,1)} %collective-permute-done.9), channel_id=1, source_target_pairs={{2,0},{3,1},{4,6},{5,7},{10,8},{11,9},{12,14},{13,15},{18,16},{19,... | collective-permute-start | bytes 3145736 | tf_op jit(solution)/shard_map/ppermute | solution.py:88
  28.6 43.8 %collective-permute-start.15 = (bf16[1024,512]{1,0:T(8,128)(2,1)}, bf16[1024,512]{1,0:T(8,128)(2,1)}, u32[]{:S(2)}, u32[]{:S(2)}) collective-permute-start(bf16[1024,512]{1,0:T(8,128)(2,1)} %collective-permute-done.1.refs_0_), channel_id=1, source_target_pairs={{2,4},{3,5},{4,2},{5,3},{10,12},{11,13},{12,10},{13,11},{18,20},{1... | collective-permute-start | bytes 3145736 | tf_op jit(solution)/shard_map/ppermute | solution.py:88
  56.9 12.9 %collective-permute-start.5 = (bf16[2,128,512]{2,1,0:T(8,128)(2,1)S(1)}, bf16[2,128,512]{2,1,0:T(8,128)(2,1)S(1)}, u32[]{:S(2)}, u32[]{:S(2)}) collective-permute-start(bf16[2,128,512]{2,1,0:T(8,128)(2,1)S(1)} %get-tuple-element.34), channel_id=1, source_target_pairs={{0,24},{8,16},{16,8},{24,0},{1,25},{9,17},{17,9},{25,1},{2,26},{10... | collective-permute-start | bytes 786440 | tf_op jit(solution)/shard_map/ppermute | solution.py:144
  59.4 12.9 %collective-permute-start.4 = (bf16[2,128,512]{2,1,0:T(8,128)(2,1)S(1)}, bf16[2,128,512]{2,1,0:T(8,128)(2,1)S(1)}, u32[]{:S(2)}, u32[]{:S(2)}) collective-permute-start(bf16[2,128,512]{2,1,0:T(8,128)(2,1)S(1)} %get-tuple-element.33), channel_id=1, source_target_pairs={{0,16},{8,24},{16,0},{24,8},{1,17},{9,25},{17,1},{25,9},{2,18},{10... | collective-permute-start | bytes 786440 | tf_op jit(solution)/shard_map/ppermute | solution.py:144
  59.9 12.4 %collective-permute-start.3 = (bf16[2,128,512]{2,1,0:T(8,128)(2,1)S(1)}, bf16[2,128,512]{2,1,0:T(8,128)(2,1)S(1)}, u32[]{:S(2)}, u32[]{:S(2)}) collective-permute-start(bf16[2,128,512]{2,1,0:T(8,128)(2,1)S(1)} %get-tuple-element.32), channel_id=1, source_target_pairs={{0,8},{8,0},{16,24},{24,16},{1,9},{9,1},{17,25},{25,17},{2,10},{10... | collective-permute-start | bytes 786440 | tf_op jit(solution)/shard_map/ppermute | solution.py:144
  65.8 9.4 %collective-permute-start.8 = (bf16[2,128,512]{2,1,0:T(8,128)(2,1)S(1)}, bf16[2,128,512]{2,1,0:T(8,128)(2,1)}, u32[]{:S(2)}, u32[]{:S(2)}) collective-permute-start(bf16[2,128,512]{2,1,0:T(8,128)(2,1)S(1)} %get-tuple-element.39), channel_id=1, source_target_pairs={{0,24},{8,16},{16,8},{24,0},{1,25},{9,17},{17,9},{25,1},{2,26},{10... | collective-permute-start | bytes 786440 | tf_op jit(solution)/shard_map/ppermute | solution.py:144
  69.8 14.7 %collective-permute-start.11 = (bf16[1024,512]{1,0:T(8,128)(2,1)S(1)}, bf16[1024,512]{1,0:T(8,128)(2,1)S(1)}, u32[]{:S(2)}, u32[]{:S(2)}) collective-permute-start(bf16[1024,512]{1,0:T(8,128)(2,1)S(1)} %broadcast_select_fusion.1.refs_0_), channel_id=1, source_target_pairs={{0,1},{1,0},{2,3},{3,2},{4,5},{5,4},{6,7},{7,6},{8,9},{9,8},{10,11... | collective-permute-start | bytes 3145736 | tf_op jit(solution)/shard_map/ppermute | solution.py:85
  75.2 24.8 %collective-permute-start.16 = (bf16[1024,512]{1,0:T(8,128)(2,1)}, bf16[1024,512]{1,0:T(8,128)(2,1)S(1)}, u32[]{:S(2)}, u32[]{:S(2)}) collective-permute-start(bf16[1024,512]{1,0:T(8,128)(2,1)} %collective-permute-done.15), channel_id=1, source_target_pairs={{2,0},{3,1},{4,6},{5,7},{10,8},{11,9},{12,14},{13,15},{18,16},{19,... | collective-permute-start | bytes 3145736 | tf_op jit(solution)/shard_map/ppermute | solution.py:88
  76.5 6.4 %collective-permute-start.7 = (bf16[2,128,512]{2,1,0:T(8,128)(2,1)S(1)}, bf16[2,128,512]{2,1,0:T(8,128)(2,1)S(1)}, u32[]{:S(2)}, u32[]{:S(2)}) collective-permute-start(bf16[2,128,512]{2,1,0:T(8,128)(2,1)S(1)} %get-tuple-element.38), channel_id=1, source_target_pairs={{0,16},{8,24},{16,0},{24,8},{1,17},{9,25},{17,1},{25,9},{2,18},{10... | collective-permute-start | bytes 786440 | tf_op jit(solution)/shard_map/ppermute | solution.py:144
  78.1 6.4 %collective-permute-start.6 = (bf16[2,128,512]{2,1,0:T(8,128)(2,1)S(1)}, bf16[2,128,512]{2,1,0:T(8,128)(2,1)S(1)}, u32[]{:S(2)}, u32[]{:S(2)}) collective-permute-start(bf16[2,128,512]{2,1,0:T(8,128)(2,1)S(1)} %get-tuple-element.37), channel_id=1, source_target_pairs={{0,8},{8,0},{16,24},{24,16},{1,9},{9,1},{17,25},{25,17},{2,10},{10... | collective-permute-start | bytes 786440 | tf_op jit(solution)/shard_map/ppermute | solution.py:144
  88.0 7.3 %collective-permute-start.14 = (bf16[2,128,512]{2,1,0:T(8,128)(2,1)S(1)}, bf16[2,128,512]{2,1,0:T(8,128)(2,1)S(1)}, u32[]{:S(2)}, u32[]{:S(2)}) collective-permute-start(bf16[2,128,512]{2,1,0:T(8,128)(2,1)S(1)} %get-tuple-element.45), channel_id=1, source_target_pairs={{0,24},{8,16},{16,8},{24,0},{1,25},{9,17},{17,9},{25,1},{2,26},{10... | collective-permute-start | bytes 786440 | tf_op jit(solution)/shard_map/ppermute | solution.py:144
  100.2 4.6 %collective-permute-start.17 = (bf16[1024,512]{1,0:T(8,128)(2,1)S(1)}, bf16[1024,512]{1,0:T(8,128)(2,1)S(1)}, u32[]{:S(2)}, u32[]{:S(2)}) collective-permute-start(bf16[1024,512]{1,0:T(8,128)(2,1)S(1)} %broadcast_select_fusion.refs_0_), channel_id=1, source_target_pairs={{0,1},{1,0},{2,3},{3,2},{4,5},{5,4},{6,7},{7,6},{8,9},{9,8},{10,11... | collective-permute-start | bytes 3145736 | tf_op jit(solution)/shard_map/ppermute | solution.py:85
  100.3 9.3 %collective-permute-start.13 = (bf16[2,128,512]{2,1,0:T(8,128)(2,1)}, bf16[2,128,512]{2,1,0:T(8,128)(2,1)S(1)}, u32[]{:S(2)}, u32[]{:S(2)}) collective-permute-start(bf16[2,128,512]{2,1,0:T(8,128)(2,1)} %copy-done.8), channel_id=1, source_target_pairs={{0,16},{8,24},{16,0},{24,8},{1,17},{9,25},{17,1},{25,9},{2,18},{10... | collective-permute-start | bytes 786440 | tf_op jit(solution)/shard_map/ppermute | solution.py:144
  101.9 9.4 %collective-permute-start.12 = (bf16[2,128,512]{2,1,0:T(8,128)(2,1)}, bf16[2,128,512]{2,1,0:T(8,128)(2,1)S(1)}, u32[]{:S(2)}, u32[]{:S(2)}) collective-permute-start(bf16[2,128,512]{2,1,0:T(8,128)(2,1)} %copy-done.7), channel_id=1, source_target_pairs={{0,8},{8,0},{16,24},{24,16},{1,9},{9,1},{17,25},{25,17},{2,10},{10... | collective-permute-start | bytes 786440 | tf_op jit(solution)/shard_map/ppermute | solution.py:144
  104.8 6.5 %copy-start.6 = (f32[2,128,512]{2,1,0:T(8,128)S(1)}, f32[2,128,512]{2,1,0:T(8,128)}, u32[]{:S(2)}) copy-start(f32[2,128,512]{2,1,0:T(8,128)} %copy-done.5) | copy-start | bytes 1572868
  104.8 6.5 %copy-start.10 = (bf16[2,128,512]{2,1,0:T(8,128)(2,1)S(1)}, bf16[2,128,512]{2,1,0:T(8,128)(2,1)}, u32[]{:S(2)}) copy-start(bf16[2,128,512]{2,1,0:T(8,128)(2,1)} %copy-done.9) | copy-start | bytes 786436
  106.0 10.8 %collective-permute-start.18 = (bf16[2,128,512]{2,1,0:T(8,128)(2,1)S(1)}, bf16[2,128,512]{2,1,0:T(8,128)(2,1)S(1)}, u32[]{:S(2)}, u32[]{:S(2)}) collective-permute-start(bf16[2,128,512]{2,1,0:T(8,128)(2,1)S(1)} %get-tuple-element.50), channel_id=1, source_target_pairs={{0,24},{8,16},{16,8},{24,0},{1,25},{9,17},{17,9},{25,1},{2,26},{10... | collective-permute-start | bytes 786440 | tf_op jit(solution)/shard_map/ppermute | solution.py:144
  106.7 13.8 %collective-permute-start.19 = (bf16[2,128,512]{2,1,0:T(8,128)(2,1)S(1)}, bf16[2,128,512]{2,1,0:T(8,128)(2,1)S(1)}, u32[]{:S(2)}, u32[]{:S(2)}) collective-permute-start(bf16[2,128,512]{2,1,0:T(8,128)(2,1)S(1)} %get-tuple-element.51), channel_id=1, source_target_pairs={{0,16},{8,24},{16,0},{24,8},{1,17},{9,25},{17,1},{25,9},{2,18},{10... | collective-permute-start | bytes 786440 | tf_op jit(solution)/shard_map/ppermute | solution.py:144
  108.1 13.7 %collective-permute-start.20 = (bf16[2,128,512]{2,1,0:T(8,128)(2,1)S(1)}, bf16[2,128,512]{2,1,0:T(8,128)(2,1)S(1)}, u32[]{:S(2)}, u32[]{:S(2)}) collective-permute-start(bf16[2,128,512]{2,1,0:T(8,128)(2,1)S(1)} %get-tuple-element.52), channel_id=1, source_target_pairs={{0,8},{8,0},{16,24},{24,16},{1,9},{9,1},{17,25},{25,17},{2,10},{10... | collective-permute-start | bytes 786440 | tf_op jit(solution)/shard_map/ppermute | solution.py:144
  (11 other events, 21.0 us)

commit v18 on v17

--- a/solution.py
+++ b/solution.py
@@ -153,10 +153,11 @@
         if line:
             x1, y2, blocks = lax.optimization_barrier((x1, y2, blocks))
             y3, e2 = along(x1, swap), along(y2, outward)
-            sums = [summed(exchange(parts))]
+            group0 = exchange(parts)
+            sums = [summed(group0)]
             parts = product(pair1)
             group = exchange(parts)
-            e3 = along(after(y3, sums[0], group[-1]), outward)
+            e3 = along(after(y3, *group0[1:], group[-1]), outward)
             sums.append(summed(group))
             x2 = jnp.where(end, e2, y2)
             group = exchange(product((after(x2, *group[1:]), across(x2))))

time: 156 us -> 165 us (1.058)
  waiting for transfers between devices: 71.9 us -> 80.3 us
    ppermute x5, waiting for transfers between devices: 21 us -> 25.5 us  [along(): lax.ppermute(x, 'col', [(2 * a + c, 2 * b + c) for a, b in pairs for c in...]
    ppermute x12, waiting for transfers between devices: 27.9 us -> 31.8 us  [exchange(): sent[t] = lax.ppermute(parts[t], 'row', [(r, r ^ t) for r in range(nrow)])]
    unnamed x26 -> x44, local copies, waits for them, and re-layouts: 5.94 us -> 5.25 us
  transfers between devices with their start and end apart: 22 -> 22, of which waited for: 13 -> 13; matrix products, arithmetic and copies ran while one was open for 2% -> 2% of each run, Pallas kernels for 6% -> 5%
where the time goes in v18:
time: 165 us; the launch traced here: 164 us
  waiting for transfers between devices  80.3 us (49%)
  starting transfers between devices  32.3 us (20%)
  blocking collectives  31.6 us (19%)
  Pallas kernels  11.2 us (7%)
  local copies, waits for them, and re-layouts  5.25 us (3%)
  other arithmetic  3.39 us (2%)
    ppermute x12, waiting for transfers between devices, exchange(): sent[t] = lax.ppermute(parts[t], 'row', [(r, r ^ t) for r in range(nrow)])  31.8 us
    all_to_all x1, blocking collectives, local(): second = lax.all_to_all(turned, ('row', 'col'), 0, 0, tiled=True)  31.6 us
    ppermute x5, waiting for transfers between devices, along(): lax.ppermute(x, 'col', [(2 * a + c, 2 * b + c) for a, b in pairs for c in...  25.5 us
    all_to_all x1, waiting for transfers between devices, local(): raw = lax.all_to_all(blocks, 'col', 0, 0, tiled=True)  23 us
    ppermute x12, starting transfers between devices, exchange(): sent[t] = lax.ppermute(parts[t], 'row', [(r, r ^ t) for r in range(nrow)])  17.9 us
    ppermute x5, starting transfers between devices, along(): lax.ppermute(x, 'col', [(2 * a + c, 2 * b + c) for a, b in pairs for c in...  8.88 us
    unnamed x44, local copies, waits for them, and re-layouts  5.25 us
    pallas_call x3, Pallas kernels, product(): pl.pallas_call(functools.partial(product_kernel, 1), out_shape=sent, in_s...  4.98 us
  transfers between devices with their start and end apart: 22, of which 13 were waited for; matrix products, arithmetic and copies ran while one was open for 2% of the time, Pallas kernels for 5%

profile of v18, /device:TPU:0, one launch (start us, length us, event | category | flops | bytes accessed | tf_op | source)
XLA Modules:
  0.0 164.3 jit_solution(16807413458500203969)
XLA Ops:
  0.0 3.0 %collective-permute-start.1 = (bf16[1024,512]{1,0:T(8,128)(2,1)}, bf16[1024,512]{1,0:T(8,128)(2,1)}, u32[]{:S(2)}, u32[]{:S(2)}) collective-permute-start(bf16[1024,512]{1,0:T(8,128)(2,1)} %bitcast.7), channel_id=1, source_target_pairs={{0,2},{1,3},{2,0},{3,1},{4,6},{5,7},{6,4},{7,5},{8,10},{9,11},{10,... | collective-permute-start | bytes 3145736 | tf_op jit(solution)/shard_map/ppermute | solution.py:88
  3.0 1.6 collective-permute-start.9
  7.2 4.8 %all-to-all-start = ((bf16[8,2,64,512]{3,2,1,0:T(8,128)(2,1)}), bf16[8,2,64,512]{3,2,1,0:T(8,128)(2,1)S(1)}, u32[]{:S(2)}, u32[]{:S(2)}) async-start(bf16[8,2,64,512]{3,2,1,0:T(8,128)(2,1)} %shard_map.28), calls=%async_computation | async-start | bytes 2097152 | tf_op jit(solution)/shard_map/all_to_all | solution.py:121
  12.5 14.8 %collective-permute-done.1.refs_0_ = bf16[1024,512]{1,0:T(8,128)(2,1)} collective-permute-done((bf16[1024,512]{1,0:T(8,128)(2,1)}, bf16[1024,512]{1,0:T(8,128)(2,1)}, u32[]{:S(2)}, u32[]{:S(2)}) %collective-permute-start.1) | collective-permute-done | bytes 1048608 | tf_op jit(solution)/shard_map/ppermute | solution.py:88
  28.6 1.7 %collective-permute-start.15 = (bf16[1024,512]{1,0:T(8,128)(2,1)}, bf16[1024,512]{1,0:T(8,128)(2,1)}, u32[]{:S(2)}, u32[]{:S(2)}) collective-permute-start(bf16[1024,512]{1,0:T(8,128)(2,1)} %collective-permute-done.1.refs_0_), channel_id=1, source_target_pairs={{2,4},{3,5},{4,2},{5,3},{10,12},{11,13},{12,10},{13,11},{18,20},{1... | collective-permute-start | bytes 3145736 | tf_op jit(solution)/shard_map/ppermute | solution.py:88
  31.3 23.0 %all-to-all-done.raw_ref = bf16[8,2,64,512]{3,2,1,0:T(8,128)(2,1)S(1)} async-done(((bf16[8,2,64,512]{3,2,1,0:T(8,128)(2,1)}), bf16[8,2,64,512]{3,2,1,0:T(8,128)(2,1)S(1)}, u32[]{:S(2)}, u32[]{:S(2)}) %all-to-all-start) | async-done | bytes 1048608 | tf_op jit(solution)/shard_map/all_to_all | solution.py:121
  54.3 2.5 %shard_map.29 = (bf16[512,1024]{1,0:T(8,128)(2,1)S(1)}, f32[2,128,512]{2,1,0:T(8,128)S(1)}, bf16[2,128,512]{2,1,0:T(8,128)(2,1)S(1)}, bf16[2,128,512]{2,1,0:T(8,128)(2,1)S(1)}, bf16[2,128,512]{2,1,0:T(8,128)(2,1)S(1)}) custom-call(s32[1]{0:T(128)} %bitcast.4.core_ref, bf16[8,2,64,512]{3,2,1,0:T(8,128)(2,1)S(1)} %all-to-all-done.raw_ref, ...), custom_call_target="tpu_custom_call" | custom-call | tf_op jit(solution)/shard_map/pallas_call | solution.py:124
  57.6 2.4 %collective-permute-start.5 = (bf16[2,128,512]{2,1,0:T(8,128)(2,1)S(1)}, bf16[2,128,512]{2,1,0:T(8,128)(2,1)S(1)}, u32[]{:S(2)}, u32[]{:S(2)}) collective-permute-start(bf16[2,128,512]{2,1,0:T(8,128)(2,1)S(1)} %get-tuple-element.34), channel_id=1, source_target_pairs={{0,24},{8,16},{16,8},{24,0},{1,25},{9,17},{17,9},{25,1},{2,26},{10... | collective-permute-start | bytes 786440 | tf_op jit(solution)/shard_map/ppermute | solution.py:144
  61.1 4.8 %collective-permute-done.10 = bf16[1024,512]{1,0:T(8,128)(2,1)} collective-permute-done((bf16[1024,512]{1,0:T(8,128)(2,1)}, bf16[1024,512]{1,0:T(8,128)(2,1)}, u32[]{:S(2)}, u32[]{:S(2)}) %collective-permute-start.10) | collective-permute-done | bytes 1048608 | tf_op jit(solution)/shard_map/ppermute | solution.py:88
  67.3 2.5 %shard_map.30 = (f32[2,128,512]{2,1,0:T(8,128)S(1)}, bf16[2,128,512]{2,1,0:T(8,128)(2,1)S(1)}, bf16[2,128,512]{2,1,0:T(8,128)(2,1)S(1)}, bf16[2,128,512]{2,1,0:T(8,128)(2,1)S(1)}) custom-call(s32[1]{0:T(128)} %bitcast.4.core_ref, bf16[512,1024]{1,0:T(8,128)(2,1)S(1)} %get-tuple-element.35.panel_ref, bf16[1024,512]{1,0:T(8,128)(2,1)} %collective-permute-done.1.refs_0_, ...), custom_call_target="tpu_custom_call" | custom-call | tf_op jit(solution)/shard_map/pallas_call | solution.py:133
  69.8 2.7 %collective-permute-start.8 = (bf16[2,128,512]{2,1,0:T(8,128)(2,1)S(1)}, bf16[2,128,512]{2,1,0:T(8,128)(2,1)S(1)}, u32[]{:S(2)}, u32[]{:S(2)}) collective-permute-start(bf16[2,128,512]{2,1,0:T(8,128)(2,1)S(1)} %get-tuple-element.39), channel_id=1, source_target_pairs={{0,24},{8,16},{16,8},{24,0},{1,25},{9,17},{17,9},{25,1},{2,26},{10... | collective-permute-start | bytes 786440 | tf_op jit(solution)/shard_map/ppermute | solution.py:144
  72.5 6.9 %collective-permute-done.8 = bf16[2,128,512]{2,1,0:T(8,128)(2,1)S(1)} collective-permute-done((bf16[2,128,512]{2,1,0:T(8,128)(2,1)S(1)}, bf16[2,128,512]{2,1,0:T(8,128)(2,1)S(1)}, u32[]{:S(2)}, u32[]{:S(2)}) %collective-permute-start.8) | collective-permute-done | bytes 262176 | tf_op jit(solution)/shard_map/ppermute | solution.py:144
  80.7 1.8 %collective-permute-start.7 = (bf16[2,128,512]{2,1,0:T(8,128)(2,1)S(1)}, bf16[2,128,512]{2,1,0:T(8,128)(2,1)S(1)}, u32[]{:S(2)}, u32[]{:S(2)}) collective-permute-start(bf16[2,128,512]{2,1,0:T(8,128)(2,1)S(1)} %get-tuple-element.38), channel_id=1, source_target_pairs={{0,16},{8,24},{16,0},{24,8},{1,17},{9,25},{17,1},{25,9},{2,18},{10... | collective-permute-start | bytes 786440 | tf_op jit(solution)/shard_map/ppermute | solution.py:144
  84.0 4.7 %collective-permute-done.7 = bf16[2,128,512]{2,1,0:T(8,128)(2,1)S(1)} collective-permute-done((bf16[2,128,512]{2,1,0:T(8,128)(2,1)S(1)}, bf16[2,128,512]{2,1,0:T(8,128)(2,1)S(1)}, u32[]{:S(2)}, u32[]{:S(2)}) %collective-permute-start.7) | collective-permute-done | bytes 262176 | tf_op jit(solution)/shard_map/ppermute | solution.py:144
  92.9 1.9 %collective-permute-start.14 = (bf16[2,128,512]{2,1,0:T(8,128)(2,1)S(1)}, bf16[2,128,512]{2,1,0:T(8,128)(2,1)S(1)}, u32[]{:S(2)}, u32[]{:S(2)}) collective-permute-start(bf16[2,128,512]{2,1,0:T(8,128)(2,1)S(1)} %get-tuple-element.45), channel_id=1, source_target_pairs={{0,24},{8,16},{16,8},{24,0},{1,25},{9,17},{17,9},{25,1},{2,26},{10... | collective-permute-start | bytes 786440 | tf_op jit(solution)/shard_map/ppermute | solution.py:144
  94.9 5.7 %collective-permute-done.14 = bf16[2,128,512]{2,1,0:T(8,128)(2,1)S(1)} collective-permute-done((bf16[2,128,512]{2,1,0:T(8,128)(2,1)S(1)}, bf16[2,128,512]{2,1,0:T(8,128)(2,1)S(1)}, u32[]{:S(2)}, u32[]{:S(2)}) %collective-permute-start.14) | collective-permute-done | bytes 262176 | tf_op jit(solution)/shard_map/ppermute | solution.py:144
  101.3 5.9 %collective-permute-done.16 = bf16[1024,512]{1,0:T(8,128)(2,1)S(1)} collective-permute-done((bf16[1024,512]{1,0:T(8,128)(2,1)}, bf16[1024,512]{1,0:T(8,128)(2,1)S(1)}, u32[]{:S(2)}, u32[]{:S(2)}) %collective-permute-start.16) | collective-permute-done | bytes 1048608 | tf_op jit(solution)/shard_map/ppermute | solution.py:88
  107.5 1.5 add_convert_fusion.2.refs_0_
  109.0 1.6 collective-permute-start.13
  114.1 1.5 collective-permute-start.19
  118.2 1.6 collective-permute-done.12
  119.9 5.5 %collective-permute-done.18.refs_4_ = bf16[2,128,512]{2,1,0:T(8,128)(2,1)S(1)} collective-permute-done((bf16[2,128,512]{2,1,0:T(8,128)(2,1)S(1)}, bf16[2,128,512]{2,1,0:T(8,128)(2,1)S(1)}, u32[]{:S(2)}, u32[]{:S(2)}) %collective-permute-start.18) | collective-permute-done | bytes 262176 | tf_op jit(solution)/shard_map/ppermute | solution.py:144
  125.4 3.7 %collective-permute-done.19.refs_5_ = bf16[2,128,512]{2,1,0:T(8,128)(2,1)S(1)} collective-permute-done((bf16[2,128,512]{2,1,0:T(8,128)(2,1)S(1)}, bf16[2,128,512]{2,1,0:T(8,128)(2,1)S(1)}, u32[]{:S(2)}, u32[]{:S(2)}) %collective-permute-start.19) | collective-permute-done | bytes 262176 | tf_op jit(solution)/shard_map/ppermute | solution.py:144
  131.3 31.6 %all_to_all.10.second_ref = bf16[32,2,64,128]{3,2,1,0:T(8,128)(2,1)S(1)} all-to-all(bf16[32,2,64,128]{3,2,1,0:T(8,128)(2,1)S(1)} %get-tuple-element.54), channel_id=1, replica_groups=mesh['row'=4,'col'=8] {'row','col'}, dimensions={0} | all-to-all | bytes 2097152 | tf_op jit(solution)/shard_map/all_to_all | solution.py:190
  (78 shorter events, 26.4 us)
Async XLA Ops:
  0.0 27.3 %collective-permute-start.1 = (bf16[1024,512]{1,0:T(8,128)(2,1)}, bf16[1024,512]{1,0:T(8,128)(2,1)}, u32[]{:S(2)}, u32[]{:S(2)}) collective-permute-start(bf16[1024,512]{1,0:T(8,128)(2,1)} %bitcast.7), channel_id=1, source_target_pairs={{0,2},{1,3},{2,0},{3,1},{4,6},{5,7},{6,4},{7,5},{8,10},{9,11},{10,... | collective-permute-start | bytes 3145736 | tf_op jit(solution)/shard_map/ppermute | solution.py:88
  3.0 24.3 %collective-permute-start.9 = (bf16[1024,512]{1,0:T(8,128)(2,1)}, bf16[1024,512]{1,0:T(8,128)(2,1)}, u32[]{:S(2)}, u32[]{:S(2)}) collective-permute-start(bf16[1024,512]{1,0:T(8,128)(2,1)} %bitcast.8), channel_id=1, source_target_pairs={{2,4},{3,5},{4,2},{5,3},{10,12},{11,13},{12,10},{13,11},{18,20},{1... | collective-permute-start | bytes 3145736 | tf_op jit(solution)/shard_map/ppermute | solution.py:88
  7.2 47.1 %all-to-all-start = ((bf16[8,2,64,512]{3,2,1,0:T(8,128)(2,1)}), bf16[8,2,64,512]{3,2,1,0:T(8,128)(2,1)S(1)}, u32[]{:S(2)}, u32[]{:S(2)}) async-start(bf16[8,2,64,512]{3,2,1,0:T(8,128)(2,1)} %shard_map.28), calls=%async_computation | async-start | bytes 2097152 | tf_op jit(solution)/shard_map/all_to_all | solution.py:121
  12.0 18.3 %collective-permute-start = (bf16[1024,512]{1,0:T(8,128)(2,1)S(1)}, bf16[1024,512]{1,0:T(8,128)(2,1)}, u32[]{:S(2)}, u32[]{:S(2)}) collective-permute-start(bf16[1024,512]{1,0:T(8,128)(2,1)S(1)} %bitcast.9), channel_id=1, source_target_pairs={{0,1},{1,0},{2,3},{3,2},{4,5},{5,4},{6,7},{7,6},{8,9},{9,8},{10,11... | collective-permute-start | bytes 3145736 | tf_op jit(solution)/shard_map/ppermute | solution.py:85
  27.3 3.0 %collective-permute-start.2 = (bf16[1024,512]{1,0:T(8,128)(2,1)}, bf16[1024,512]{1,0:T(8,128)(2,1)S(1)}, u32[]{:S(2)}, u32[]{:S(2)}) collective-permute-start(bf16[1024,512]{1,0:T(8,128)(2,1)} %collective-permute-done.1.refs_0_), channel_id=1, source_target_pairs={{0,1},{1,0},{2,3},{3,2},{4,5},{5,4},{6,7},{7,6},{8,9},{9,8},{10,11... | collective-permute-start | bytes 3145736 | tf_op jit(solution)/shard_map/ppermute | solution.py:85
  27.3 38.5 %collective-permute-start.10 = (bf16[1024,512]{1,0:T(8,128)(2,1)}, bf16[1024,512]{1,0:T(8,128)(2,1)}, u32[]{:S(2)}, u32[]{:S(2)}) collective-permute-start(bf16[1024,512]{1,0:T(8,128)(2,1)} %collective-permute-done.9), channel_id=1, source_target_pairs={{2,0},{3,1},{4,6},{5,7},{10,8},{11,9},{12,14},{13,15},{18,16},{19,... | collective-permute-start | bytes 3145736 | tf_op jit(solution)/shard_map/ppermute | solution.py:88
  28.6 41.1 %collective-permute-start.15 = (bf16[1024,512]{1,0:T(8,128)(2,1)}, bf16[1024,512]{1,0:T(8,128)(2,1)}, u32[]{:S(2)}, u32[]{:S(2)}) collective-permute-start(bf16[1024,512]{1,0:T(8,128)(2,1)} %collective-permute-done.1.refs_0_), channel_id=1, source_target_pairs={{2,4},{3,5},{4,2},{5,3},{10,12},{11,13},{12,10},{13,11},{18,20},{1... | collective-permute-start | bytes 3145736 | tf_op jit(solution)/shard_map/ppermute | solution.py:88
  57.6 14.9 %collective-permute-start.5 = (bf16[2,128,512]{2,1,0:T(8,128)(2,1)S(1)}, bf16[2,128,512]{2,1,0:T(8,128)(2,1)S(1)}, u32[]{:S(2)}, u32[]{:S(2)}) collective-permute-start(bf16[2,128,512]{2,1,0:T(8,128)(2,1)S(1)} %get-tuple-element.34), channel_id=1, source_target_pairs={{0,24},{8,16},{16,8},{24,0},{1,25},{9,17},{17,9},{25,1},{2,26},{10... | collective-permute-start | bytes 786440 | tf_op jit(solution)/shard_map/ppermute | solution.py:144
  60.0 12.4 %collective-permute-start.4 = (bf16[2,128,512]{2,1,0:T(8,128)(2,1)S(1)}, bf16[2,128,512]{2,1,0:T(8,128)(2,1)S(1)}, u32[]{:S(2)}, u32[]{:S(2)}) collective-permute-start(bf16[2,128,512]{2,1,0:T(8,128)(2,1)S(1)} %get-tuple-element.33), channel_id=1, source_target_pairs={{0,16},{8,24},{16,0},{24,8},{1,17},{9,25},{17,1},{25,9},{2,18},{10... | collective-permute-start | bytes 786440 | tf_op jit(solution)/shard_map/ppermute | solution.py:144
  60.5 11.9 %collective-permute-start.3 = (bf16[2,128,512]{2,1,0:T(8,128)(2,1)S(1)}, bf16[2,128,512]{2,1,0:T(8,128)(2,1)S(1)}, u32[]{:S(2)}, u32[]{:S(2)}) collective-permute-start(bf16[2,128,512]{2,1,0:T(8,128)(2,1)S(1)} %get-tuple-element.32), channel_id=1, source_target_pairs={{0,8},{8,0},{16,24},{24,16},{1,9},{9,1},{17,25},{25,17},{2,10},{10... | collective-permute-start | bytes 786440 | tf_op jit(solution)/shard_map/ppermute | solution.py:144
  67.2 22.9 %collective-permute-start.11 = (bf16[1024,512]{1,0:T(8,128)(2,1)S(1)}, bf16[1024,512]{1,0:T(8,128)(2,1)S(1)}, u32[]{:S(2)}, u32[]{:S(2)}) collective-permute-start(bf16[1024,512]{1,0:T(8,128)(2,1)S(1)} %broadcast_select_fusion.1.refs_0_), channel_id=1, source_target_pairs={{0,1},{1,0},{2,3},{3,2},{4,5},{5,4},{6,7},{7,6},{8,9},{9,8},{10,11... | collective-permute-start | bytes 3145736 | tf_op jit(solution)/shard_map/ppermute | solution.py:85
  69.7 21.6 %copy-start.5 = (f32[2,128,512]{2,1,0:T(8,128)}, f32[2,128,512]{2,1,0:T(8,128)S(1)}, u32[]{:S(2)}) copy-start(f32[2,128,512]{2,1,0:T(8,128)S(1)} %get-tuple-element.36) | copy-start | bytes 1572868
  69.8 9.7 %collective-permute-start.8 = (bf16[2,128,512]{2,1,0:T(8,128)(2,1)S(1)}, bf16[2,128,512]{2,1,0:T(8,128)(2,1)S(1)}, u32[]{:S(2)}, u32[]{:S(2)}) collective-permute-start(bf16[2,128,512]{2,1,0:T(8,128)(2,1)S(1)} %get-tuple-element.39), channel_id=1, source_target_pairs={{0,24},{8,16},{16,8},{24,0},{1,25},{9,17},{17,9},{25,1},{2,26},{10... | collective-permute-start | bytes 786440 | tf_op jit(solution)/shard_map/ppermute | solution.py:144
  72.4 18.9 %copy-start.12 = (bf16[2,128,512]{2,1,0:T(8,128)(2,1)}, bf16[2,128,512]{2,1,0:T(8,128)(2,1)S(1)}, u32[]{:S(2)}) copy-start(bf16[2,128,512]{2,1,0:T(8,128)(2,1)S(1)} %collective-permute-done.4) | copy-start | bytes 786436
  79.4 27.7 %collective-permute-start.16 = (bf16[1024,512]{1,0:T(8,128)(2,1)}, bf16[1024,512]{1,0:T(8,128)(2,1)S(1)}, u32[]{:S(2)}, u32[]{:S(2)}) collective-permute-start(bf16[1024,512]{1,0:T(8,128)(2,1)} %collective-permute-done.15), channel_id=1, source_target_pairs={{2,0},{3,1},{4,6},{5,7},{10,8},{11,9},{12,14},{13,15},{18,16},{19,... | collective-permute-start | bytes 3145736 | tf_op jit(solution)/shard_map/ppermute | solution.py:88
  80.7 8.0 %collective-permute-start.7 = (bf16[2,128,512]{2,1,0:T(8,128)(2,1)S(1)}, bf16[2,128,512]{2,1,0:T(8,128)(2,1)S(1)}, u32[]{:S(2)}, u32[]{:S(2)}) collective-permute-start(bf16[2,128,512]{2,1,0:T(8,128)(2,1)S(1)} %get-tuple-element.38), channel_id=1, source_target_pairs={{0,16},{8,24},{16,0},{24,8},{1,17},{9,25},{17,1},{25,9},{2,18},{10... | collective-permute-start | bytes 786440 | tf_op jit(solution)/shard_map/ppermute | solution.py:144
  82.5 7.6 %collective-permute-start.6 = (bf16[2,128,512]{2,1,0:T(8,128)(2,1)S(1)}, bf16[2,128,512]{2,1,0:T(8,128)(2,1)S(1)}, u32[]{:S(2)}, u32[]{:S(2)}) collective-permute-start(bf16[2,128,512]{2,1,0:T(8,128)(2,1)S(1)} %get-tuple-element.37), channel_id=1, source_target_pairs={{0,8},{8,0},{16,24},{24,16},{1,9},{9,1},{17,25},{25,17},{2,10},{10... | collective-permute-start | bytes 786440 | tf_op jit(solution)/shard_map/ppermute | solution.py:144
  92.9 7.6 %collective-permute-start.14 = (bf16[2,128,512]{2,1,0:T(8,128)(2,1)S(1)}, bf16[2,128,512]{2,1,0:T(8,128)(2,1)S(1)}, u32[]{:S(2)}, u32[]{:S(2)}) collective-permute-start(bf16[2,128,512]{2,1,0:T(8,128)(2,1)S(1)} %get-tuple-element.45), channel_id=1, source_target_pairs={{0,24},{8,16},{16,8},{24,0},{1,25},{9,17},{17,9},{25,1},{2,26},{10... | collective-permute-start | bytes 786440 | tf_op jit(solution)/shard_map/ppermute | solution.py:144
  107.3 5.0 %collective-permute-start.17 = (bf16[1024,512]{1,0:T(8,128)(2,1)S(1)}, bf16[1024,512]{1,0:T(8,128)(2,1)S(1)}, u32[]{:S(2)}, u32[]{:S(2)}) collective-permute-start(bf16[1024,512]{1,0:T(8,128)(2,1)S(1)} %broadcast_select_fusion.refs_0_), channel_id=1, source_target_pairs={{0,1},{1,0},{2,3},{3,2},{4,5},{5,4},{6,7},{7,6},{8,9},{9,8},{10,11... | collective-permute-start | bytes 3145736 | tf_op jit(solution)/shard_map/ppermute | solution.py:85
  109.0 9.2 %collective-permute-start.13 = (bf16[2,128,512]{2,1,0:T(8,128)(2,1)S(1)}, bf16[2,128,512]{2,1,0:T(8,128)(2,1)S(1)}, u32[]{:S(2)}, u32[]{:S(2)}) collective-permute-start(bf16[2,128,512]{2,1,0:T(8,128)(2,1)S(1)} %copy-done.10), channel_id=1, source_target_pairs={{0,16},{8,24},{16,0},{24,8},{1,17},{9,25},{17,1},{25,9},{2,18},{10... | collective-permute-start | bytes 786440 | tf_op jit(solution)/shard_map/ppermute | solution.py:144
  110.6 9.1 %collective-permute-start.12 = (bf16[2,128,512]{2,1,0:T(8,128)(2,1)S(1)}, bf16[2,128,512]{2,1,0:T(8,128)(2,1)S(1)}, u32[]{:S(2)}, u32[]{:S(2)}) collective-permute-start(bf16[2,128,512]{2,1,0:T(8,128)(2,1)S(1)} %get-tuple-element.43), channel_id=1, source_target_pairs={{0,8},{8,0},{16,24},{24,16},{1,9},{9,1},{17,25},{25,17},{2,10},{10... | collective-permute-start | bytes 786440 | tf_op jit(solution)/shard_map/ppermute | solution.py:144
  113.6 11.8 %collective-permute-start.18 = (bf16[2,128,512]{2,1,0:T(8,128)(2,1)S(1)}, bf16[2,128,512]{2,1,0:T(8,128)(2,1)S(1)}, u32[]{:S(2)}, u32[]{:S(2)}) collective-permute-start(bf16[2,128,512]{2,1,0:T(8,128)(2,1)S(1)} %get-tuple-element.50), channel_id=1, source_target_pairs={{0,24},{8,16},{16,8},{24,0},{1,25},{9,17},{17,9},{25,1},{2,26},{10... | collective-permute-start | bytes 786440 | tf_op jit(solution)/shard_map/ppermute | solution.py:144
  114.1 14.9 %collective-permute-start.19 = (bf16[2,128,512]{2,1,0:T(8,128)(2,1)S(1)}, bf16[2,128,512]{2,1,0:T(8,128)(2,1)S(1)}, u32[]{:S(2)}, u32[]{:S(2)}) collective-permute-start(bf16[2,128,512]{2,1,0:T(8,128)(2,1)S(1)} %get-tuple-element.51), channel_id=1, source_target_pairs={{0,16},{8,24},{16,0},{24,8},{1,17},{9,25},{17,1},{25,9},{2,18},{10... | collective-permute-start | bytes 786440 | tf_op jit(solution)/shard_map/ppermute | solution.py:144
  115.7 14.7 %collective-permute-start.20 = (bf16[2,128,512]{2,1,0:T(8,128)(2,1)S(1)}, bf16[2,128,512]{2,1,0:T(8,128)(2,1)S(1)}, u32[]{:S(2)}, u32[]{:S(2)}) collective-permute-start(bf16[2,128,512]{2,1,0:T(8,128)(2,1)S(1)} %get-tuple-element.52), channel_id=1, source_target_pairs={{0,8},{8,0},{16,24},{24,16},{1,9},{9,1},{17,25},{25,17},{2,10},{10... | collective-permute-start | bytes 786440 | tf_op jit(solution)/shard_map/ppermute | solution.py:144
  (20 other events, 103.1 us)
